TPU v7x, 32 devices: a whole 2x2x4 slice. The times are simulated.
32 devices in a mesh: sub: 2 (over y), rng: 16 (over z, x, core).
Axes of the slice: x: 2, y: 2, z: 4, core: 2. Of those that a mesh axis runs over, the one named last changes fastest.
Arguments:
- echoes: bfloat16 [2, 1024, 8192], P(None, ('sub', 'rng')), may hold values from -6 to 6
- fore_flag: int32 [1, 2, 16], P(None, None, 'rng'), may hold values from 0 to 1, as said below
- band_offset: int32 [1, 2, 16], P(None, None, 'rng'), may hold values from -16 to 16, as said below
- angle_interp: bfloat16 [1, 2, 512, 256], replicated, may hold values from -1 to 1
- range_kernel: bfloat16 [1, 544, 512], replicated, may hold values from -1 to 2, as said below
- center_shift: float32 [1, 2], replicated, may hold values from -6 to 6
Outputs:
- focused_image: float32 [2, 1024, 8192], P(None, 'sub', 'rng')
Inputs may be any that keep to these rules, and one draw needn't show every extreme that they name: fore_flag[l, g, b] + fore_flag[l, g XOR 2**l, b] = 1 for every level l, group g and block b. `band_offset`: in every level both -16 and 16 occur. range_kernel[l, w, r] = 0 wherever |w - 16 - r| > 16.
All inputs are finite; a program needn't handle non-finite values.
Results may differ from a plain program's by a relative error of at most 0.0076.
Values may be sent and summed in bfloat16 or wider, within the bound.
No kernel may reach another device: no remote copies, remote signals or barrier semaphores. Data moves between devices by JAX's collectives and lax.ppermute only.
A program may use at most 64 MiB of HBM per device.

v0:
```python
import functools
import math

import jax
import jax.numpy as jnp
from jax import lax
from jax.experimental import pallas as pl
from jax.experimental.pallas import tpu as pltpu
from jax.sharding import PartitionSpec as P

MAX_SHIFT = 16
LANES = 128
MIB = 2**20
JOIN_COST = 10**11
SIDE = jax.ShapeDtypeStruct((8, LANES), jnp.float32)
VMEM = pl.BlockSpec(memory_space=pltpu.VMEM)
SMEM = pl.BlockSpec(memory_space=pltpu.SMEM)
ANY = pl.BlockSpec(memory_space=pl.ANY)
F32 = jnp.float32
BF16 = jnp.bfloat16


def dot(a, b):
    return jnp.dot(a, b, preferred_element_type=F32)


def params(mib):
    return pltpu.CompilerParams(vmem_limit_bytes=mib * MIB)


def series(square, first, count):
    coefs = [
        (-1) ** i * math.pi ** (2 * i + first) / math.factorial(2 * i + first)
        for i in range(count)
    ]
    total = jnp.full_like(square, coefs[-1])
    for coef in coefs[-2::-1]:
        total = total * square + coef
    return total


def cos_sin_pi(v):
    turns = jnp.floor(v + 0.5)
    rest = v - turns
    sign = 1.0 - 2.0 * (turns - 2.0 * jnp.floor(turns * 0.5))
    square = rest * rest
    return series(square, 0, 8) * sign, series(square, 1, 7) * rest * sign


def rotated(pair, step):
    return pair[0] * step[0] - pair[1] * step[1], pair[0] * step[1] + pair[1] * step[0]


def mixed(left, right):
    lane = lax.broadcasted_iota(jnp.int32, left.shape, 1)
    return jnp.where(lane < LANES // 2, left.astype(F32), right.astype(F32)).astype(BF16)


def place_kernel(echoes_ref, far_ref, near_ref, inner_ref):
    devices, _, count = inner_ref.shape
    bins = count + LANES
    half = devices // 2
    base = lax.axis_index("rng") // half * half

    def tile(device, first):
        return echoes_ref[:, pl.ds(pl.multiple_of(device * bins + first, LANES), LANES)]

    for ref, start in ((far_ref, half - base), (near_ref, base)):
        for i in range(half):
            ref[i] = mixed(tile(start + i, 0), tile(start + i, bins - LANES))
    for device in range(devices):
        begin = device * bins
        inner_ref[device, :, :LANES] = mixed(tile(device, bins - LANES), tile(device, 0))
        inner_ref[device, :, LANES:] = echoes_ref[:, begin + LANES : begin + bins - LANES]


def placed(echoes, devices):
    rows, columns = echoes.shape
    outer = jax.ShapeDtypeStruct((devices // 2, rows, LANES), BF16)
    inner = jax.ShapeDtypeStruct((devices, rows, columns // devices - LANES), BF16)
    return pl.pallas_call(
        place_kernel,
        out_shape=[outer, outer, inner],
        in_specs=[VMEM],
        out_specs=[VMEM] * 3,
        compiler_params=params(8),
        cost_estimate=pl.CostEstimate(flops=0, bytes_accessed=2 * MIB, transcendentals=0),
    )(echoes)


def join_kernel(near_ref, relay_ref, *refs):
    me = lax.axis_index("rng") % len(refs)
    rows = near_ref.shape[1]
    for d, out_ref in enumerate(refs):
        out_ref[:rows] = near_ref[me ^ d]
        out_ref[rows:] = relay_ref[me ^ d]


def joined(near, relay):
    half, rows, count = near.shape
    return pl.pallas_call(
        join_kernel,
        out_shape=[jax.ShapeDtypeStruct((2 * rows, count), BF16)] * half,
        in_specs=[VMEM] * 2,
        out_specs=[VMEM] * half,
        compiler_params=params(4),
        cost_estimate=pl.CostEstimate(flops=JOIN_COST, bytes_accessed=MIB, transcendentals=0),
    )(near, relay)


def across(value, mask):
    devices = lax.axis_size("rng")
    return lax.ppermute(value, "rng", [(i, i ^ mask) for i in range(devices)])


def filter_table_kernel(
    local_pulses, flag_ref, after_ref, own_ref, out_ref, side_ref, cos_ref, sin_ref
):
    own_flag = flag_ref[0, lax.axis_index("sub"), 0]
    side_ref[...] = jnp.full(side_ref.shape, own_flag.astype(F32))
    rows, columns = own_ref.shape
    half, angles = rows // 2, rows
    base = cos_ref.shape[0]
    scale = 1.0 / math.sqrt(columns // 2)
    lane = lax.broadcasted_iota(jnp.int32, (8, columns), 1)
    slot = lane // (2 * local_pulses)
    second = lane // local_pulses % 2
    pulse = (slot * local_pulses + lane % local_pulses).astype(F32)
    lag = second.astype(F32) * 0.5
    per_angle = pulse * (1.0 / angles)
    row = lax.broadcasted_iota(jnp.int32, (8, columns), 0)
    step = cos_sin_pi(per_angle * (2 * base))
    for ref, side in ((out_ref, 1 - own_flag), (own_ref, own_flag)):
        first = side * half
        for i in range(base // 8):
            twice = (2 * (row + 8 * i + first) + 1 - angles).astype(F32)
            cosine, sine = cos_sin_pi(twice * per_angle - lag)
            cos_ref[8 * i : 8 * i + 8, :] = cosine * scale
            sin_ref[8 * i : 8 * i + 8, :] = sine * scale
        for j in range(half // base):
            for i in range(base // 16):
                pair = [], []
                for k in (2 * i, 2 * i + 1):
                    here = slice(8 * k, 8 * k + 8)
                    now = cos_ref[here, :], sin_ref[here, :]
                    pair[0].append(now[0])
                    pair[1].append(-now[1])
                    if j + 1 < half // base:
                        cos_ref[here, :], sin_ref[here, :] = rotated(now, step)
                begin = j * base + 16 * i
                ref[begin : begin + 16, :] = jnp.concatenate(pair[0]).astype(BF16)
                begin += half
                ref[begin : begin + 16, :] = jnp.concatenate(pair[1]).astype(BF16)


def filter_table(fore_flag, angles, local_pulses, earlier):
    side = 2 * local_pulses * lax.axis_size("rng")
    return pl.pallas_call(
        functools.partial(filter_table_kernel, local_pulses),
        out_shape=[jax.ShapeDtypeStruct((angles, side), BF16)] * 2 + [SIDE],
        in_specs=[SMEM, ANY],
        out_specs=[VMEM] * 3,
        scratch_shapes=[pltpu.VMEM((64, side), F32)] * 2,
        compiler_params=params(6),
        cost_estimate=pl.CostEstimate(flops=9_000_000, bytes_accessed=4 * MIB, transcendentals=0),
    )(fore_flag, earlier)


def merge_table_kernel(
    level, stride, flag_ref, offset_ref, shift_ref, range_ref, interp_ref, after_ref, centre_ref,
    rim_ref, turn_ref, matrix_ref, side_ref,
):
    group = lax.axis_index("sub")
    block = lax.axis_index("rng")
    bins = centre_ref.shape[-1]
    angles = turn_ref.shape[-2]
    total_bins = lax.axis_size("rng") * bins
    taps = range_ref.shape[1]
    band = (taps - bins) // 2
    rim = MAX_SHIFT + band
    kernel = range_ref[level]

    def moved(bin_id):
        tap = lax.broadcasted_iota(jnp.int32, (bin_id.shape[0], taps), 1)
        return dot(jnp.where(tap == bin_id, 1.0, 0.0).astype(BF16), kernel).astype(BF16)

    row = lax.broadcasted_iota(jnp.int32, (bins, 1), 0)
    upper = row + (bins - 2 * LANES)
    own_bin = jnp.where(row % LANES < LANES // 2, row, upper + LANES)
    own_bin = jnp.where(row >= LANES, jnp.where(row % LANES < LANES // 2, upper, row - LANES), own_bin)
    own_bin = jnp.where(row >= 2 * LANES, row - LANES, own_bin)
    own_flag = flag_ref[level, group, 0]
    side_ref[...] = jnp.full(side_ref.shape, own_flag.astype(F32))
    matrix_ref[0] = interp_ref[level, own_flag]
    matrix_ref[1] = interp_ref[level, 1 - own_flag]
    rim_row = lax.broadcasted_iota(jnp.int32, (2 * rim, 1), 0)
    rim_bin = jnp.where(rim_row < rim, rim_row - rim, rim_row - rim + bins)
    rim_ref[...] = jnp.zeros(rim_ref.shape, BF16)
    bin_id = block * bins + lax.broadcasted_iota(jnp.int32, (1, LANES), 1)
    reach = 1.0 + bin_id.astype(F32) * (1.0 / total_bins)
    rows = 64
    for child in range(2):
        member = group if child == 0 else group ^ stride
        lead = band - offset_ref[level, member, 0]
        centre_ref[child] = moved(own_bin + lead)
        ends = moved(rim_bin + lead)
        for part in range(2):
            for side in range(2):
                place = (2 * side + part) * rim
                rim_ref[child, part, place : place + rim, :] = ends[side * rim : (side + 1) * rim]

        rate = shift_ref[level, member]

        def turn_rows(i, carry):
            begin = pl.multiple_of(i * rows, rows)
            angle = begin + lax.broadcasted_iota(jnp.int32, (rows, LANES), 0)
            place = ((angle.astype(F32) + 0.5) * (1.0 / angles) - 0.5) * rate
            now = cos_sin_pi(place * reach)
            step = cos_sin_pi(place * (LANES / total_bins))
            for tile in range(bins // LANES):
                lanes = slice(tile * LANES, tile * LANES + LANES)
                turn_ref[child, 0, pl.ds(begin, rows), lanes] = now[0]
                turn_ref[child, 1, pl.ds(begin, rows), lanes] = now[1]
                now = rotated(now, step)
            return carry

        lax.fori_loop(0, angles // rows, turn_rows, 0)


def merge_tables(
    level, stride, fore_flag, band_offset, center_shift, range_kernel, angle_interp, earlier
):
    taps, bins = range_kernel.shape[1:]
    angles = angle_interp.shape[2]
    rim = MAX_SHIFT + (taps - bins) // 2
    return pl.pallas_call(
        functools.partial(merge_table_kernel, level, stride),
        out_shape=[
            jax.ShapeDtypeStruct((2, bins, bins), BF16),
            jax.ShapeDtypeStruct((2, 2, 4 * rim, bins), BF16),
            jax.ShapeDtypeStruct((2, 2, angles, bins), F32),
            jax.ShapeDtypeStruct((2, *angle_interp.shape[2:]), BF16),
            SIDE,
        ],
        in_specs=[SMEM] * 3 + [VMEM] * 2 + [ANY],
        out_specs=[VMEM] * 5,
        compiler_params=params(12),
        cost_estimate=pl.CostEstimate(
            flops=2_300_000_000, bytes_accessed=7 * MIB, transcendentals=0
        ),
    )(fore_flag, band_offset, center_shift, range_kernel, angle_interp, earlier)


def outer_kernel(pieces, side_ref, own_rows, out_rows, *refs):
    own_side = side_ref[:1, :]
    me = lax.axis_index("rng")
    own_ref, out_ref, *edge_refs = refs[pieces:-1]
    pulses_ref = refs[-1]
    rows = refs[0].shape[0] // 2
    for d, ref in enumerate(refs[:pieces]):
        for t in range(2):
            place = pl.multiple_of((me ^ (d + t * pieces)) * rows, rows)
            pulses_ref[pl.ds(place, rows), :] = ref[t * rows : (t + 1) * rows, :]
    images = dot(own_rows[...], pulses_ref[...]), dot(out_rows[...], pulses_ref[...])
    half = own_ref.shape[1]
    rim = LANES // 4
    lane = lax.broadcasted_iota(jnp.int32, (1, LANES), 1)
    edges = [0.0, 0.0]
    for part in range(2):
        own, out = (image[part * half : (part + 1) * half] for image in images)
        own_ref[part] = own.astype(BF16)
        out_ref[part] = out.astype(BF16)
        for side in range(2):
            value = jnp.where(own_side == side, own, out)
            group = 2 * part + side
            for end in range(2):
                turn = (group + end) * rim % LANES
                moved = pltpu.roll(value, turn, 1) if turn else value
                edges[end] = edges[end] + jnp.where(lane // rim == group, moved, 0.0)
    even = me % 2 == 0
    edge_refs[0][...] = jnp.where(even, edges[1], edges[0]).astype(BF16)
    edge_refs[1][...] = jnp.where(even, edges[0], edges[1]).astype(BF16)


def outer_image(own_side, own_rows, out_rows, pieces):
    angles, side = own_rows.shape
    image = jax.ShapeDtypeStruct((2, angles // 2, LANES), BF16)
    edge = jax.ShapeDtypeStruct((angles // 2, LANES), BF16)
    return pl.pallas_call(
        functools.partial(outer_kernel, len(pieces)),
        out_shape=[image, image, edge, edge],
        in_specs=[VMEM] * (3 + len(pieces)),
        out_specs=[VMEM] * 4,
        scratch_shapes=[pltpu.VMEM((side, LANES), BF16)],
        compiler_params=params(10),
        cost_estimate=pl.CostEstimate(
            flops=4 * angles * side * LANES, bytes_accessed=3 * MIB, transcendentals=0
        ),
    )(own_side, own_rows, out_rows, *pieces)


def inner_kernel(rows_ref, pulses_ref, image_ref):
    image = dot(rows_ref[...], pulses_ref[...])
    image_ref[...] = image.astype(BF16).reshape(image_ref.shape)


def inner_image(rows, pulses):
    angles, count = rows.shape[0], pulses.shape[1]
    return pl.pallas_call(
        inner_kernel,
        out_shape=jax.ShapeDtypeStruct((2, angles // 2, count), BF16),
        in_specs=[VMEM] * 2,
        out_specs=VMEM,
        compiler_params=params(8),
        cost_estimate=pl.CostEstimate(
            flops=2 * rows.size * count, bytes_accessed=3 * MIB, transcendentals=0
        ),
    )(rows, pulses)


def exchanged(value, begin):
    devices = lax.axis_size("rng")
    pairs = [(i, (i + 1) % devices) for i in range(begin, devices, 2)]
    return lax.ppermute(value, "rng", pairs + [(j, i) for i, j in pairs])


def rims_kernel(side_ref, first_ref, second_ref, own_ref, out_ref):
    own_side = side_ref[:1, :]
    rim = LANES // 4
    me, devices = lax.axis_index("rng"), lax.axis_size("rng")
    even = me % 2 == 0
    first, second = first_ref[...].astype(F32), second_ref[...].astype(F32)
    below = jnp.where(me == 0, 0.0, jnp.where(even, second, first))
    above = jnp.where(me == devices - 1, 0.0, jnp.where(even, first, second))
    group = lax.broadcasted_iota(jnp.int32, (1, LANES), 1) // rim
    packed = [0.0, 0.0]
    for end, value in enumerate((below, above)):
        for part in range(2):
            place = 2 * end + part
            for side in range(2):
                turn = (place - (2 * part + side)) * rim % LANES
                moved = pltpu.roll(value, turn, 1) if turn else value
                packed[side] = packed[side] + jnp.where(group == place, moved, 0.0)
    own_ref[...] = jnp.where(own_side == 0, packed[0], packed[1]).astype(BF16)
    out_ref[...] = jnp.where(own_side == 0, packed[1], packed[0]).astype(BF16)


def sorted_rims(own_side, first, second):
    return pl.pallas_call(
        rims_kernel,
        out_shape=[jax.ShapeDtypeStruct(first.shape, BF16)] * 2,
        in_specs=[VMEM] * 3,
        out_specs=[VMEM] * 2,
        compiler_params=params(4),
        cost_estimate=pl.CostEstimate(flops=1_000_000, bytes_accessed=MIB // 4, transcendentals=0),
    )(own_side, first, second)


def early_kernel(
    own_outer, own_inner, rims_ref, far_outer, far_rims, centre_ref, rim_ref, matrix_ref, turn_ref,
    merged_ref, partial_ref, value_ref,
):
    parts, half, count = own_outer.shape
    image = jnp.concatenate([own_outer[...], own_inner[...]], axis=2)
    value_ref[...] = dot(image.reshape(parts * half, image.shape[2]), centre_ref[0])
    rows = []
    for part in range(parts):
        value = value_ref[part * half : (part + 1) * half, :]
        rows.append((value + dot(rims_ref[...], rim_ref[0, part])).astype(BF16))
    merged_ref[0], merged_ref[1] = rotated(
        (dot(matrix_ref[0], rows[0]), dot(matrix_ref[0], rows[1])), (turn_ref[0, 0], turn_ref[0, 1])
    )
    for part in range(parts):
        value = dot(far_outer[part], centre_ref[1, :count, :])
        here = slice(part * half, (part + 1) * half)
        partial_ref[here, :] = value + dot(far_rims[...], rim_ref[1, part])


def late_kernel(
    far_inner, merged_ref, partial_ref, centre_ref, matrix_ref, turn_ref, out_ref, buffer, sems
):
    parts, half, count = far_inner.shape
    bins = centre_ref.shape[-1]
    inner = far_inner[...].reshape(parts * half, count)
    value = partial_ref[...] + dot(inner, centre_ref[1, bins - count :, :])
    rows = [value[part * half : (part + 1) * half].astype(BF16) for part in range(parts)]
    block = LANES
    copies = []
    for first in range(0, matrix_ref.shape[1], 2 * block):
        matrix = matrix_ref[1, first : first + 2 * block]
        terms = dot(matrix, rows[0]), dot(matrix, rows[1])
        for step in range(2):
            here = slice(first + step * block, first + (step + 1) * block)
            there = slice(step * block, (step + 1) * block)
            turned = rotated(
                (terms[0][there], terms[1][there]), (turn_ref[1, 0, here], turn_ref[1, 1, here])
            )
            for part in range(parts):
                buffer[part, here] = (merged_ref[part, here] + turned[part]).astype(buffer.dtype)
            copy = pltpu.make_async_copy(
                buffer.at[:, here], out_ref.at[:, here], sems.at[len(copies)]
            )
            copy.start()
            copies.append(copy)
    for copy in copies:
        copy.wait()


def merged_image(own, rims, far, far_rims, tables, dtype):
    centre, rim, turn, matrices, _ = tables
    angles, bins = turn.shape[-2:]
    cost = pl.CostEstimate(flops=4 * angles * bins * bins, bytes_accessed=8 * MIB, transcendentals=0)
    merged, partial = pl.pallas_call(
        early_kernel,
        out_shape=[
            jax.ShapeDtypeStruct((2, angles, bins), F32),
            jax.ShapeDtypeStruct((angles, bins), F32),
        ],
        in_specs=[VMEM] * 9,
        out_specs=[VMEM] * 2,
        scratch_shapes=[pltpu.VMEM((angles, bins), F32)],
        compiler_params=params(20),
        cost_estimate=cost,
    )(*own, rims, far[0], far_rims, centre, rim, matrices, turn)
    return pl.pallas_call(
        late_kernel,
        out_shape=jax.ShapeDtypeStruct((2, angles, bins), dtype),
        in_specs=[VMEM] * 6,
        out_specs=ANY,
        scratch_shapes=[
            pltpu.VMEM((2, angles, bins), dtype),
            pltpu.SemaphoreType.DMA((angles // LANES,)),
        ],
        compiler_params=params(20),
        cost_estimate=cost,
    )(far[1], merged, partial, centre, matrices, turn)


def after(value, *earlier):
    return lax.optimization_barrier((value, *earlier))[0]


def from_partner(value, stride):
    pairs = [(source, source ^ stride) for source in range(lax.axis_size("sub"))]
    return lax.ppermute(value, "sub", pairs)


def split_image(level, image, fore_flag, rim):
    angles, bins = image.shape[1:]
    half, step = angles // 2, LANES // 2
    own_flag = fore_flag[level, lax.axis_index("sub"), 0]
    sides = image.reshape(2, 2, half, bins)

    def pieces(side):
        rows = lax.dynamic_index_in_dim(sides, side, 1, keepdims=False)
        ends = [rows[..., :step], rows[..., -step:]]
        rest = [rows[..., -2 * step : -step], rows[..., step : -2 * step]]
        return jnp.concatenate(ends, axis=-1), jnp.concatenate(rest, axis=-1)

    def packed(edge):
        return edge.transpose(2, 0, 1, 3).reshape(half, 4 * rim)

    low, high = packed(sides[..., :rim]), packed(sides[..., -rim:])
    even = lax.axis_index("rng") % 2 == 0
    edges = jnp.where(even, high, low), jnp.where(even, low, high)
    return pieces(own_flag), pieces(1 - own_flag), edges


def on_device(echoes, fore_flag, band_offset, angle_interp, range_kernel, center_shift):
    devices = lax.axis_size("rng")
    half = devices // 2
    local_pulses = echoes.shape[1]
    bins = echoes.shape[2] // devices
    angles = angle_interp.shape[2]
    rim = MAX_SHIFT + (range_kernel.shape[1] - bins) // 2
    levels = range_kernel.shape[0]
    settings = (fore_flag, band_offset, center_shift, range_kernel, angle_interp)

    far_blocks, near_blocks, blocks = placed(
        echoes.reshape(2 * local_pulses, devices * bins), devices
    )
    relay = across(far_blocks, half)
    pulses = lax.all_to_all(blocks, "rng", split_axis=0, concat_axis=0, tiled=True)
    sends = joined(near_blocks, relay)
    pieces = [across(value, d) if d else value for d, value in enumerate(sends)]
    own_matrix, out_matrix, own_side = filter_table(fore_flag, angles, local_pulses, sends[0])
    tables = merge_tables(0, 1, *settings, own_matrix)
    pieces[0] = after(pieces[0], tables[0])
    own_outer, out_outer, *edges = outer_image(own_side, own_matrix, out_matrix, pieces)

    pulses = after(pulses, out_outer).reshape(2 * local_pulses * devices, bins - LANES)
    out_inner = inner_image(out_matrix, pulses)
    own_inner = inner_image(own_matrix, pulses)
    far = [from_partner(value, 1) for value in (out_outer, out_inner)]
    edges = [after(edge, out_inner, far[0]) for edge in edges]
    own = own_outer, own_inner
    for level in range(levels):
        stride = 2**level
        if level > 0:
            tables = merge_tables(level, stride, *settings, image)
            own, out, edges = split_image(level, image, fore_flag, rim)
            far = [from_partner(value, stride) for value in out]
        edges = exchanged(edges[0], 0), exchanged(edges[1], 1)
        rims, out_rims = sorted_rims(tables[-1], *edges)
        far_rims = from_partner(out_rims, stride)
        image = merged_image(own, rims, far, far_rims, tables, BF16 if level + 1 < levels else F32)
    return image


def solution(mesh):
    placed_as = (
        P(None, ("sub", "rng"), None),
        P(None, None, "rng"),
        P(None, None, "rng"),
        P(),
        P(),
        P(),
    )
    return jax.shard_map(
        on_device, mesh=mesh, in_specs=placed_as, out_specs=P(None, "sub", "rng"), check_vma=False
    )
```

profile of v0, /device:TPU:0, one launch (start us, length us, event | category | flops | bytes accessed | tf_op | source)
XLA Modules:
  0.0 67.1 jit_solution(10252534202091983044)
XLA Ops:
  0.0 1.2 %copy-done.4 = bf16[2,32,8192]{2,1,0:T(8,128)(2,1)S(1)} copy-done((bf16[2,32,8192]{2,1,0:T(8,128)(2,1)S(1)}, bf16[2,32,8192]{2,1,0:T(8,128)(2,1)}, u32[]{:S(2)}) %copy-start.4) | copy-done | bytes 1048600
  1.2 1.1 %shard_map.64 = (bf16[8,64,128]{2,1,0:T(8,128)(2,1)S(1)}, bf16[8,64,128]{2,1,0:T(8,128)(2,1)S(1)}, bf16[16,64,384]{2,1,0:T(8,128)(2,1)}) custom-call(bf16[64,8192]{1,0:T(8,128)(2,1)S(1)} %bitcast.4), custom_call_target="tpu_custom_call" | custom-call | bytes 2097152 | tf_op jit(solution)/shard_map/pallas_call | solution.py:81
  2.3 4.0 %collective-permute-start = (bf16[8,64,128]{2,1,0:T(8,128)(2,1)S(1)}, bf16[8,64,128]{2,1,0:T(8,128)(2,1)S(1)}, u32[]{:S(2)}, u32[]{:S(2)}) collective-permute-start(bf16[8,64,128]{2,1,0:T(8,128)(2,1)S(1)} %get-tuple-element.37), channel_id=1, source_target_pairs={{0,8},{1,9},{2,10},{3,11},{4,12},{5,13},{6,14},{7,15},{8,0},{9,1},... | collective-permute-start | bytes 393224 | tf_op jit(solution)/shard_map/ppermute | solution.py:113
  6.3 3.9 %all-to-all-start = ((bf16[16,64,384]{2,1,0:T(8,128)(2,1)}), bf16[16,64,384]{2,1,0:T(8,128)(2,1)S(1)}, u32[]{:S(2)}, u32[]{:S(2)}) async-start(bf16[16,64,384]{2,1,0:T(8,128)(2,1)} %get-tuple-element.40), calls=%async_computation | async-start | bytes 1572864 | tf_op jit(solution)/shard_map/all_to_all | solution.py:483
  10.2 2.4 %collective-permute-done.relay_ref = bf16[8,64,128]{2,1,0:T(8,128)(2,1)S(1)} collective-permute-done((bf16[8,64,128]{2,1,0:T(8,128)(2,1)S(1)}, bf16[8,64,128]{2,1,0:T(8,128)(2,1)S(1)}, u32[]{:S(2)}, u32[]{:S(2)}) %collective-permute-start) | collective-permute-done | bytes 131104 | tf_op jit(solution)/shard_map/ppermute | solution.py:113
  12.6 0.6 shard_map.65
  13.3 0.0 collective-permute-start.1
  13.3 1.5 %collective-permute-start.2 = (bf16[128,128]{1,0:T(8,128)(2,1)S(1)}, bf16[128,128]{1,0:T(8,128)(2,1)S(1)}, u32[]{:S(2)}, u32[]{:S(2)}) collective-permute-start(bf16[128,128]{1,0:T(8,128)(2,1)S(1)} %get-tuple-element.46), channel_id=1, source_target_pairs={{0,2},{1,3},{2,0},{3,1},{4,6},{5,7},{6,4},{7,5},{8,10},{9,11},{10,... | collective-permute-start | bytes 98312 | tf_op jit(solution)/shard_map/ppermute | solution.py:113
  14.8 0.0 copy-done.22
  14.8 0.1 copy.7.flag_ref
  14.9 0.0 copy-done.23
  14.9 0.1 copy.9.offset_ref
  15.0 0.3 collective-permute-start.3
  15.3 0.8 %collective-permute-start.4 = (bf16[128,128]{1,0:T(8,128)(2,1)}, bf16[128,128]{1,0:T(8,128)(2,1)S(1)}, u32[]{:S(2)}, u32[]{:S(2)}) collective-permute-start(bf16[128,128]{1,0:T(8,128)(2,1)} %get-tuple-element.48), channel_id=1, source_target_pairs={{0,4},{1,5},{2,6},{3,7},{4,0},{5,1},{6,2},{7,3},{8,12},{9,13},{10,... | collective-permute-start | bytes 98312 | tf_op jit(solution)/shard_map/ppermute | solution.py:113
  16.1 0.8 %collective-permute-start.5 = (bf16[128,128]{1,0:T(8,128)(2,1)S(1)}, bf16[128,128]{1,0:T(8,128)(2,1)S(1)}, u32[]{:S(2)}, u32[]{:S(2)}) collective-permute-start(bf16[128,128]{1,0:T(8,128)(2,1)S(1)} %get-tuple-element.49), channel_id=1, source_target_pairs={{0,5},{1,4},{2,7},{3,6},{4,1},{5,0},{6,3},{7,2},{8,13},{9,12},{10,... | collective-permute-start | bytes 98312 | tf_op jit(solution)/shard_map/ppermute | solution.py:113
  17.0 1.9 %shard_map.66 = (bf16[512,1024]{1,0:T(8,128)(2,1)S(1)}, bf16[512,1024]{1,0:T(8,128)(2,1)S(1)}, f32[8,128]{1,0:T(8,128)S(1)}) custom-call(s32[1,2,1]{2,1,0:T(2,128)S(1)} %copy.7.flag_ref, bf16[128,128]{1,0:T(8,128)(2,1)S(1)} %get-tuple-element.44.after_ref.refs_0_), custom_call_target="tpu_custom_call" | custom-call | flops 9000000 | bytes 4194304 | tf_op jit(solution)/shard_map/pallas_call | solution.py:158
  18.9 0.0 collective-permute-done.1.refs_1_
  18.9 0.0 copy-start.9
  18.9 0.6 copy-done.9
  19.5 1.7 %collective-permute-start.6 = (bf16[128,128]{1,0:T(8,128)(2,1)S(1)}, bf16[128,128]{1,0:T(8,128)(2,1)S(1)}, u32[]{:S(2)}, u32[]{:S(2)}) collective-permute-start(bf16[128,128]{1,0:T(8,128)(2,1)S(1)} %get-tuple-element.50), channel_id=1, source_target_pairs={{0,6},{1,7},{2,4},{3,5},{4,2},{5,3},{6,0},{7,1},{8,14},{9,15},{10,... | collective-permute-start | bytes 98312 | tf_op jit(solution)/shard_map/ppermute | solution.py:113
  21.2 0.0 collective-permute-done.2.refs_2_
  21.2 0.6 copy-done.11
  21.8 1.0 %collective-permute-start.7 = (bf16[128,128]{1,0:T(8,128)(2,1)S(1)}, bf16[128,128]{1,0:T(8,128)(2,1)S(1)}, u32[]{:S(2)}, u32[]{:S(2)}) collective-permute-start(bf16[128,128]{1,0:T(8,128)(2,1)S(1)} %get-tuple-element.51), channel_id=1, source_target_pairs={{0,7},{1,6},{2,5},{3,4},{4,3},{5,2},{6,1},{7,0},{8,15},{9,14},{10,... | collective-permute-start | bytes 98312 | tf_op jit(solution)/shard_map/ppermute | solution.py:113
  22.8 0.0 copy-done.7
  22.8 0.0 copy-done.21
  22.9 1.1 %copy-done.13 = bf16[1,544,512]{2,1,0:T(8,128)(2,1)S(1)} copy-done((bf16[1,544,512]{2,1,0:T(8,128)(2,1)S(1)}, bf16[1,544,512]{2,1,0:T(8,128)(2,1)}, u32[]{:S(2)}) %copy-start.13) | copy-done | bytes 557080
  23.9 1.0 %copy-done.14 = bf16[1,2,512,256]{3,2,1,0:T(8,128)(2,1)S(1)} copy-done((bf16[1,2,512,256]{3,2,1,0:T(8,128)(2,1)S(1)}, bf16[1,2,512,256]{3,2,1,0:T(8,128)(2,1)}, u32[]{:S(2)}) %copy-start.14) | copy-done | bytes 524312
  25.0 3.8 %shard_map.67 = (bf16[2,512,512]{2,1,0:T(8,128)(2,1)S(1)}, bf16[2,2,128,512]{3,2,1,0:T(8,128)(2,1)S(1)}, f32[2,2,512,512]{3,2,1,0:T(8,128)S(1)}, bf16[2,512,256]{2,1,0:T(8,128)(2,1)S(1)}, f32[8,128]{1,0:T(8,128)S(1)}) custom-call(s32[1,2,1]{2,1,0:T(2,128)S(1)} %copy.7.flag_ref, s32[1,2,1]{2,1,0:T(2,128)S(1)} %copy.9.offset_ref, f32[1,2]{1,0:T(1,128)S(1)} %copy-done.21, ...), custom_call_target="tpu_custom_call" | custom-call | flops 2300000000 | bytes 7340032 | tf_op jit(solution)/shard_map/pallas_call | solution.py:236
  28.7 0.0 copy-start
  28.8 2.0 %copy-done = f32[2,2,512,512]{3,2,1,0:T(8,128)} copy-done((f32[2,2,512,512]{3,2,1,0:T(8,128)}, f32[2,2,512,512]{3,2,1,0:T(8,128)S(1)}, u32[]{:S(2)}) %copy-start) | copy-done | bytes 4194328
  30.7 1.0 %copy-done.2 = bf16[2,512,512]{2,1,0:T(8,128)(2,1)} copy-done((bf16[2,512,512]{2,1,0:T(8,128)(2,1)}, bf16[2,512,512]{2,1,0:T(8,128)(2,1)S(1)}, u32[]{:S(2)}) %copy-start.2) | copy-done | bytes 1048600
  31.7 0.8 %copy-done.5 = bf16[2,2,128,512]{3,2,1,0:T(8,128)(2,1)} copy-done((bf16[2,2,128,512]{3,2,1,0:T(8,128)(2,1)}, bf16[2,2,128,512]{3,2,1,0:T(8,128)(2,1)S(1)}, u32[]{:S(2)}) %copy-start.5) | copy-done | bytes 524312
  32.5 0.0 collective-permute-done.3.refs_3_
  32.5 0.0 collective-permute-done.4.refs_4_
  32.5 0.0 collective-permute-done.5.refs_5_
  32.5 0.0 collective-permute-done.6.refs_6_
  32.5 0.0 collective-permute-done.7.refs_7_
  32.5 0.0 copy-done.8
  32.5 0.0 copy-done.10
  32.5 0.0 copy-done.12
  32.5 0.9 %shard_map.68 = (bf16[2,256,128]{2,1,0:T(8,128)(2,1)S(1)}, bf16[2,256,128]{2,1,0:T(8,128)(2,1)S(1)}, bf16[256,128]{1,0:T(8,128)(2,1)S(1)}, bf16[256,128]{1,0:T(8,128)(2,1)S(1)}) custom-call(f32[8,128]{1,0:T(8,128)S(1)} %get-tuple-element.41.side_ref, bf16[512,1024]{1,0:T(8,128)(2,1)S(1)} %get-tuple-element.42.after_ref.own_rows.rows_ref, ...), custom_call_target="tpu_custom_call" | custom-call | flops 268435456 | bytes 3145728 | tf_op jit(solution)/shard_map/pallas_call | solution.py:289
  33.4 0.6 copy-done.15
  34.1 0.6 copy-done.17
  34.7 0.6 copy-done.19
  35.3 0.0 all-to-all-done
  35.3 0.0 copy-start.1
  35.3 0.7 %shard_map.69 = bf16[2,256,384]{2,1,0:T(8,128)(2,1)S(1)} custom-call(bf16[512,1024]{1,0:T(8,128)(2,1)S(1)} %get-tuple-element.39.out_rows.rows_ref, bf16[1024,384]{1,0:T(8,128)(2,1)S(1)} %bitcast.2), custom_call_target="tpu_custom_call" | custom-call | flops 402653184 | bytes 3145728 | tf_op jit(solution)/shard_map/pallas_call | solution.py:309
  36.1 1.7 %collective-permute-start.8 = (bf16[2,256,384]{2,1,0:T(8,128)(2,1)S(1)}, bf16[2,256,384]{2,1,0:T(8,128)(2,1)S(1)}, u32[]{:S(2)}, u32[]{:S(2)}) collective-permute-start(bf16[2,256,384]{2,1,0:T(8,128)(2,1)S(1)} %shard_map.69), channel_id=1, source_target_pairs={{0,16},{16,0},{1,17},{17,1},{2,18},{18,2},{3,19},{19,3},{4,20},{20... | collective-permute-start | bytes 1179656 | tf_op jit(solution)/shard_map/ppermute | solution.py:445
  37.7 0.4 collective-permute-start.9
  38.2 12.1 %collective-permute-done.9.far_outer = bf16[2,256,128]{2,1,0:T(8,128)(2,1)S(1)} collective-permute-done((bf16[2,256,128]{2,1,0:T(8,128)(2,1)S(1)}, bf16[2,256,128]{2,1,0:T(8,128)(2,1)S(1)}, u32[]{:S(2)}, u32[]{:S(2)}) %collective-permute-start.9) | collective-permute-done | bytes 131104 | tf_op jit(solution)/shard_map/ppermute | solution.py:445
  50.2 0.0 collective-permute-start.10
  50.2 4.7 %collective-permute-start.11 = (bf16[256,128]{1,0:T(8,128)(2,1)S(1)}, bf16[256,128]{1,0:T(8,128)(2,1)S(1)}, u32[]{:S(2)}, u32[]{:S(2)}) collective-permute-start(bf16[256,128]{1,0:T(8,128)(2,1)S(1)} %copy-done.18), channel_id=1, source_target_pairs={{1,2},{3,4},{5,6},{7,8},{9,10},{11,12},{13,14},{15,0},{2,1},{4,3},... | collective-permute-start | bytes 196616 | tf_op jit(solution)/shard_map/ppermute | solution.py:324
  54.9 0.0 collective-permute-done.10.first_ref
  54.9 1.9 %collective-permute-done.11.second_ref = bf16[256,128]{1,0:T(8,128)(2,1)S(1)} collective-permute-done((bf16[256,128]{1,0:T(8,128)(2,1)S(1)}, bf16[256,128]{1,0:T(8,128)(2,1)S(1)}, u32[]{:S(2)}, u32[]{:S(2)}) %collective-permute-start.11) | collective-permute-done | bytes 65568 | tf_op jit(solution)/shard_map/ppermute | solution.py:324
  56.9 0.2 shard_map.71
  57.1 1.6 %collective-permute-start.12 = (bf16[256,128]{1,0:T(8,128)(2,1)S(1)}, bf16[256,128]{1,0:T(8,128)(2,1)S(1)}, u32[]{:S(2)}, u32[]{:S(2)}) collective-permute-start(bf16[256,128]{1,0:T(8,128)(2,1)S(1)} %get-tuple-element.61), channel_id=1, source_target_pairs={{0,16},{16,0},{1,17},{17,1},{2,18},{18,2},{3,19},{19,3},{4,20},{20... | collective-permute-start | bytes 196616 | tf_op jit(solution)/shard_map/ppermute | solution.py:445
  58.6 0.7 %shard_map.70.own_inner = bf16[2,256,384]{2,1,0:T(8,128)(2,1)S(1)} custom-call(bf16[512,1024]{1,0:T(8,128)(2,1)S(1)} %get-tuple-element.42.after_ref.own_rows.rows_ref, bf16[1024,384]{1,0:T(8,128)(2,1)S(1)} %bitcast.3), custom_call_target="tpu_custom_call" | custom-call | flops 402653184 | bytes 3145728 | tf_op jit(solution)/shard_map/pallas_call | solution.py:309
  59.4 2.0 %collective-permute-done.12.far_rims = bf16[256,128]{1,0:T(8,128)(2,1)S(1)} collective-permute-done((bf16[256,128]{1,0:T(8,128)(2,1)S(1)}, bf16[256,128]{1,0:T(8,128)(2,1)S(1)}, u32[]{:S(2)}, u32[]{:S(2)}) %collective-permute-start.12) | collective-permute-done | bytes 65568 | tf_op jit(solution)/shard_map/ppermute | solution.py:445
  61.4 0.0 copy-done.1
  61.4 1.2 %copy-done.3 = bf16[2,512,512]{2,1,0:T(8,128)(2,1)S(1)} copy-done((bf16[2,512,512]{2,1,0:T(8,128)(2,1)S(1)}, bf16[2,512,512]{2,1,0:T(8,128)(2,1)}, u32[]{:S(2)}) %copy-start.3) | copy-done | bytes 1048600
  62.6 1.0 %copy-done.6 = bf16[2,2,128,512]{3,2,1,0:T(8,128)(2,1)S(1)} copy-done((bf16[2,2,128,512]{3,2,1,0:T(8,128)(2,1)S(1)}, bf16[2,2,128,512]{3,2,1,0:T(8,128)(2,1)}, u32[]{:S(2)}) %copy-start.6) | copy-done | bytes 524312
  63.7 1.4 %shard_map.72 = (f32[2,512,512]{2,1,0:T(8,128)S(1)}, f32[512,512]{1,0:T(8,128)S(1)}) custom-call(bf16[2,256,128]{2,1,0:T(8,128)(2,1)S(1)} %get-tuple-element.54.own_outer, bf16[2,256,384]{2,1,0:T(8,128)(2,1)S(1)} %shard_map.70.own_inner, bf16[256,128]{1,0:T(8,128)(2,1)S(1)} %get-tuple-element.60.rims_ref, ...), custom_call_target="tpu_custom_call" | custom-call | flops 536870912 | bytes 8388608 | tf_op jit(solution)/shard_map/pallas_call | solution.py:413
  65.0 0.0 collective-permute-done.8.far_inner
  65.0 2.0 %shard_map.73 = f32[2,512,512]{2,1,0:T(8,128)} custom-call(bf16[2,256,384]{2,1,0:T(8,128)(2,1)S(1)} %collective-permute-done.8.far_inner, f32[2,512,512]{2,1,0:T(8,128)S(1)} %get-tuple-element.65.merged_ref, f32[512,512]{1,0:T(8,128)S(1)} %get-tuple-element.66.partial_ref, bf16[2,512,512]{2,1,0:T(8,128)(2,1)S(1)} %copy-done.3, ...), custom_call_target="tpu_custom_call" | custom-call | flops 536870912 | bytes 8388608 | tf_op jit(solution)/shard_map/pallas_call | solution.py:425
  (24 shorter events, 0.0 us)
Async XLA Ops:
  0.0 1.2 %copy-start.4 = (bf16[2,32,8192]{2,1,0:T(8,128)(2,1)S(1)}, bf16[2,32,8192]{2,1,0:T(8,128)(2,1)}, u32[]{:S(2)}) copy-start(bf16[2,32,8192]{2,1,0:T(8,128)(2,1)} %param.6) | copy-start | bytes 3145732
  2.3 10.3 %collective-permute-start = (bf16[8,64,128]{2,1,0:T(8,128)(2,1)S(1)}, bf16[8,64,128]{2,1,0:T(8,128)(2,1)S(1)}, u32[]{:S(2)}, u32[]{:S(2)}) collective-permute-start(bf16[8,64,128]{2,1,0:T(8,128)(2,1)S(1)} %get-tuple-element.37), channel_id=1, source_target_pairs={{0,8},{1,9},{2,10},{3,11},{4,12},{5,13},{6,14},{7,15},{8,0},{9,1},... | collective-permute-start | bytes 393224 | tf_op jit(solution)/shard_map/ppermute | solution.py:113
  6.3 29.0 %all-to-all-start = ((bf16[16,64,384]{2,1,0:T(8,128)(2,1)}), bf16[16,64,384]{2,1,0:T(8,128)(2,1)S(1)}, u32[]{:S(2)}, u32[]{:S(2)}) async-start(bf16[16,64,384]{2,1,0:T(8,128)(2,1)} %get-tuple-element.40), calls=%async_computation | async-start | bytes 1572864 | tf_op jit(solution)/shard_map/all_to_all | solution.py:483
  12.6 2.2 %copy-start.22 = (s32[1,2,1]{1,2,0:T(1,128)S(1)}, s32[1,2,1]{1,2,0:T(1,128)}, u32[]{:S(2)}) copy-start(s32[1,2,1]{1,2,0:T(1,128)} %param.7) | copy-start | bytes 28
  12.6 2.3 %copy-start.23 = (s32[1,2,1]{1,2,0:T(1,128)S(1)}, s32[1,2,1]{1,2,0:T(1,128)}, u32[]{:S(2)}) copy-start(s32[1,2,1]{1,2,0:T(1,128)} %param.8) | copy-start | bytes 28
  12.6 10.2 %copy-start.21 = (f32[1,2]{1,0:T(1,128)S(1)}, f32[1,2]{1,0:T(1,128)}, u32[]{:S(2)}) copy-start(f32[1,2]{1,0:T(1,128)} %shift_ref.1) | copy-start | bytes 28
  13.3 9.6 %copy-start.7 = (bf16[128,128]{1,0:T(8,128)(2,1)}, bf16[128,128]{1,0:T(8,128)(2,1)S(1)}, u32[]{:S(2)}) copy-start(bf16[128,128]{1,0:T(8,128)(2,1)S(1)} %get-tuple-element.44.after_ref.refs_0_) | copy-start | bytes 98308
  13.3 5.6 %collective-permute-start.1 = (bf16[128,128]{1,0:T(8,128)(2,1)S(1)}, bf16[128,128]{1,0:T(8,128)(2,1)S(1)}, u32[]{:S(2)}, u32[]{:S(2)}) collective-permute-start(bf16[128,128]{1,0:T(8,128)(2,1)S(1)} %get-tuple-element.45), channel_id=1, source_target_pairs={{0,1},{1,0},{2,3},{3,2},{4,5},{5,4},{6,7},{7,6},{8,9},{9,8},{10,11... | collective-permute-start | bytes 98312 | tf_op jit(solution)/shard_map/ppermute | solution.py:113
  13.3 7.9 %collective-permute-start.2 = (bf16[128,128]{1,0:T(8,128)(2,1)S(1)}, bf16[128,128]{1,0:T(8,128)(2,1)S(1)}, u32[]{:S(2)}, u32[]{:S(2)}) collective-permute-start(bf16[128,128]{1,0:T(8,128)(2,1)S(1)} %get-tuple-element.46), channel_id=1, source_target_pairs={{0,2},{1,3},{2,0},{3,1},{4,6},{5,7},{6,4},{7,5},{8,10},{9,11},{10,... | collective-permute-start | bytes 98312 | tf_op jit(solution)/shard_map/ppermute | solution.py:113
  15.0 17.5 %collective-permute-start.3 = (bf16[128,128]{1,0:T(8,128)(2,1)}, bf16[128,128]{1,0:T(8,128)(2,1)S(1)}, u32[]{:S(2)}, u32[]{:S(2)}) collective-permute-start(bf16[128,128]{1,0:T(8,128)(2,1)} %get-tuple-element.47), channel_id=1, source_target_pairs={{0,3},{1,2},{2,1},{3,0},{4,7},{5,6},{6,5},{7,4},{8,11},{9,10},{10,... | collective-permute-start | bytes 98312 | tf_op jit(solution)/shard_map/ppermute | solution.py:113
  15.3 17.2 %collective-permute-start.4 = (bf16[128,128]{1,0:T(8,128)(2,1)}, bf16[128,128]{1,0:T(8,128)(2,1)S(1)}, u32[]{:S(2)}, u32[]{:S(2)}) collective-permute-start(bf16[128,128]{1,0:T(8,128)(2,1)} %get-tuple-element.48), channel_id=1, source_target_pairs={{0,4},{1,5},{2,6},{3,7},{4,0},{5,1},{6,2},{7,3},{8,12},{9,13},{10,... | collective-permute-start | bytes 98312 | tf_op jit(solution)/shard_map/ppermute | solution.py:113
  16.1 16.4 %collective-permute-start.5 = (bf16[128,128]{1,0:T(8,128)(2,1)S(1)}, bf16[128,128]{1,0:T(8,128)(2,1)S(1)}, u32[]{:S(2)}, u32[]{:S(2)}) collective-permute-start(bf16[128,128]{1,0:T(8,128)(2,1)S(1)} %get-tuple-element.49), channel_id=1, source_target_pairs={{0,5},{1,4},{2,7},{3,6},{4,1},{5,0},{6,3},{7,2},{8,13},{9,12},{10,... | collective-permute-start | bytes 98312 | tf_op jit(solution)/shard_map/ppermute | solution.py:113
  18.9 0.6 copy-start.9
  19.5 13.0 %collective-permute-start.6 = (bf16[128,128]{1,0:T(8,128)(2,1)S(1)}, bf16[128,128]{1,0:T(8,128)(2,1)S(1)}, u32[]{:S(2)}, u32[]{:S(2)}) collective-permute-start(bf16[128,128]{1,0:T(8,128)(2,1)S(1)} %get-tuple-element.50), channel_id=1, source_target_pairs={{0,6},{1,7},{2,4},{3,5},{4,2},{5,3},{6,0},{7,1},{8,14},{9,15},{10,... | collective-permute-start | bytes 98312 | tf_op jit(solution)/shard_map/ppermute | solution.py:113
  21.2 0.6 copy-start.11
  21.8 10.7 %collective-permute-start.7 = (bf16[128,128]{1,0:T(8,128)(2,1)S(1)}, bf16[128,128]{1,0:T(8,128)(2,1)S(1)}, u32[]{:S(2)}, u32[]{:S(2)}) collective-permute-start(bf16[128,128]{1,0:T(8,128)(2,1)S(1)} %get-tuple-element.51), channel_id=1, source_target_pairs={{0,7},{1,6},{2,5},{3,4},{4,3},{5,2},{6,1},{7,0},{8,15},{9,14},{10,... | collective-permute-start | bytes 98312 | tf_op jit(solution)/shard_map/ppermute | solution.py:113
  22.9 1.1 %copy-start.13 = (bf16[1,544,512]{2,1,0:T(8,128)(2,1)S(1)}, bf16[1,544,512]{2,1,0:T(8,128)(2,1)}, u32[]{:S(2)}) copy-start(bf16[1,544,512]{2,1,0:T(8,128)(2,1)} %range_ref.1) | copy-start | bytes 1671172
  23.9 1.0 %copy-start.14 = (bf16[1,2,512,256]{3,2,1,0:T(8,128)(2,1)S(1)}, bf16[1,2,512,256]{3,2,1,0:T(8,128)(2,1)}, u32[]{:S(2)}) copy-start(bf16[1,2,512,256]{3,2,1,0:T(8,128)(2,1)} %interp_ref.1) | copy-start | bytes 1572868
  24.9 7.6 %copy-start.8 = (bf16[128,128]{1,0:T(8,128)(2,1)S(1)}, bf16[128,128]{1,0:T(8,128)(2,1)}, u32[]{:S(2)}) copy-start(bf16[128,128]{1,0:T(8,128)(2,1)} %copy-done.7) | copy-start | bytes 98308
  25.0 7.6 %copy-start.10 = (bf16[128,128]{1,0:T(8,128)(2,1)S(1)}, bf16[128,128]{1,0:T(8,128)(2,1)}, u32[]{:S(2)}) copy-start(bf16[128,128]{1,0:T(8,128)(2,1)} %copy-done.9) | copy-start | bytes 98308
  25.0 7.6 %copy-start.12 = (bf16[128,128]{1,0:T(8,128)(2,1)S(1)}, bf16[128,128]{1,0:T(8,128)(2,1)}, u32[]{:S(2)}) copy-start(bf16[128,128]{1,0:T(8,128)(2,1)} %copy-done.11) | copy-start | bytes 98308
  28.7 2.0 %copy-start = (f32[2,2,512,512]{3,2,1,0:T(8,128)}, f32[2,2,512,512]{3,2,1,0:T(8,128)S(1)}, u32[]{:S(2)}) copy-start(f32[2,2,512,512]{3,2,1,0:T(8,128)S(1)} %get-tuple-element.64.turn_ref) | copy-start | bytes 12582916
  30.7 1.0 %copy-start.2 = (bf16[2,512,512]{2,1,0:T(8,128)(2,1)}, bf16[2,512,512]{2,1,0:T(8,128)(2,1)S(1)}, u32[]{:S(2)}) copy-start(bf16[2,512,512]{2,1,0:T(8,128)(2,1)S(1)} %get-tuple-element.43.centre_ref) | copy-start | bytes 3145732
  31.7 0.8 %copy-start.5 = (bf16[2,2,128,512]{3,2,1,0:T(8,128)(2,1)}, bf16[2,2,128,512]{3,2,1,0:T(8,128)(2,1)S(1)}, u32[]{:S(2)}) copy-start(bf16[2,2,128,512]{3,2,1,0:T(8,128)(2,1)S(1)} %get-tuple-element.62.rim_ref) | copy-start | bytes 1572868
  33.4 0.6 copy-start.15
  34.1 0.6 copy-start.17
  34.7 0.6 copy-start.19
  35.3 2.4 %copy-start.16 = (bf16[2,256,128]{2,1,0:T(8,128)(2,1)S(1)}, bf16[2,256,128]{2,1,0:T(8,128)(2,1)}, u32[]{:S(2)}) copy-start(bf16[2,256,128]{2,1,0:T(8,128)(2,1)} %copy-done.15) | copy-start | bytes 393220
  35.3 14.9 %copy-start.20 = (bf16[256,128]{1,0:T(8,128)(2,1)S(1)}, bf16[256,128]{1,0:T(8,128)(2,1)}, u32[]{:S(2)}) copy-start(bf16[256,128]{1,0:T(8,128)(2,1)} %copy-done.19) | copy-start | bytes 196612
  35.3 14.9 %copy-start.18 = (bf16[256,128]{1,0:T(8,128)(2,1)S(1)}, bf16[256,128]{1,0:T(8,128)(2,1)}, u32[]{:S(2)}) copy-start(bf16[256,128]{1,0:T(8,128)(2,1)} %copy-done.17) | copy-start | bytes 196612
  35.3 26.1 %copy-start.1 = (f32[2,2,512,512]{3,2,1,0:T(8,128)S(1)}, f32[2,2,512,512]{3,2,1,0:T(8,128)}, u32[]{:S(2)}) copy-start(f32[2,2,512,512]{3,2,1,0:T(8,128)} %copy-done) | copy-start | bytes 12582916
  36.1 29.0 %collective-permute-start.8 = (bf16[2,256,384]{2,1,0:T(8,128)(2,1)S(1)}, bf16[2,256,384]{2,1,0:T(8,128)(2,1)S(1)}, u32[]{:S(2)}, u32[]{:S(2)}) collective-permute-start(bf16[2,256,384]{2,1,0:T(8,128)(2,1)S(1)} %shard_map.69), channel_id=1, source_target_pairs={{0,16},{16,0},{1,17},{17,1},{2,18},{18,2},{3,19},{19,3},{4,20},{20... | collective-permute-start | bytes 1179656 | tf_op jit(solution)/shard_map/ppermute | solution.py:445
  37.7 12.5 %collective-permute-start.9 = (bf16[2,256,128]{2,1,0:T(8,128)(2,1)S(1)}, bf16[2,256,128]{2,1,0:T(8,128)(2,1)S(1)}, u32[]{:S(2)}, u32[]{:S(2)}) collective-permute-start(bf16[2,256,128]{2,1,0:T(8,128)(2,1)S(1)} %copy-done.16), channel_id=1, source_target_pairs={{0,16},{16,0},{1,17},{17,1},{2,18},{18,2},{3,19},{19,3},{4,20},{20... | collective-permute-start | bytes 393224 | tf_op jit(solution)/shard_map/ppermute | solution.py:445
  50.2 4.7 %collective-permute-start.10 = (bf16[256,128]{1,0:T(8,128)(2,1)S(1)}, bf16[256,128]{1,0:T(8,128)(2,1)S(1)}, u32[]{:S(2)}, u32[]{:S(2)}) collective-permute-start(bf16[256,128]{1,0:T(8,128)(2,1)S(1)} %copy-done.20), channel_id=1, source_target_pairs={{0,1},{2,3},{4,5},{6,7},{8,9},{10,11},{12,13},{14,15},{1,0},{3,2},... | collective-permute-start | bytes 196616 | tf_op jit(solution)/shard_map/ppermute | solution.py:324
  50.2 6.6 %collective-permute-start.11 = (bf16[256,128]{1,0:T(8,128)(2,1)S(1)}, bf16[256,128]{1,0:T(8,128)(2,1)S(1)}, u32[]{:S(2)}, u32[]{:S(2)}) collective-permute-start(bf16[256,128]{1,0:T(8,128)(2,1)S(1)} %copy-done.18), channel_id=1, source_target_pairs={{1,2},{3,4},{5,6},{7,8},{9,10},{11,12},{13,14},{15,0},{2,1},{4,3},... | collective-permute-start | bytes 196616 | tf_op jit(solution)/shard_map/ppermute | solution.py:324
  57.1 4.3 %collective-permute-start.12 = (bf16[256,128]{1,0:T(8,128)(2,1)S(1)}, bf16[256,128]{1,0:T(8,128)(2,1)S(1)}, u32[]{:S(2)}, u32[]{:S(2)}) collective-permute-start(bf16[256,128]{1,0:T(8,128)(2,1)S(1)} %get-tuple-element.61), channel_id=1, source_target_pairs={{0,16},{16,0},{1,17},{17,1},{2,18},{18,2},{3,19},{19,3},{4,20},{20... | collective-permute-start | bytes 196616 | tf_op jit(solution)/shard_map/ppermute | solution.py:445
  61.4 1.2 %copy-start.3 = (bf16[2,512,512]{2,1,0:T(8,128)(2,1)S(1)}, bf16[2,512,512]{2,1,0:T(8,128)(2,1)}, u32[]{:S(2)}) copy-start(bf16[2,512,512]{2,1,0:T(8,128)(2,1)} %copy-done.2) | copy-start | bytes 3145732
  62.6 1.0 %copy-start.6 = (bf16[2,2,128,512]{3,2,1,0:T(8,128)(2,1)S(1)}, bf16[2,2,128,512]{3,2,1,0:T(8,128)(2,1)}, u32[]{:S(2)}) copy-start(bf16[2,2,128,512]{3,2,1,0:T(8,128)(2,1)} %copy-done.5) | copy-start | bytes 1572868
where the time goes:
time: 67.5 us; the launch traced here: 67.1 us
  starting transfers between devices  22.5 us (33%)
  waiting for transfers between devices  18.5 us (27%)
  Pallas kernels  13.2 us (20%)
  local copies, waits for them, and re-layouts  12.6 us (19%)
    ppermute x3, waiting for transfers between devices, from_partner(): return lax.ppermute(value, 'sub', pairs)  14.1 us
    unnamed x50, local copies, waits for them, and re-layouts  12.6 us
    ppermute x8, starting transfers between devices, across(): return lax.ppermute(value, 'rng', [(i, i ^ mask) for i in range(devices)])  10.3 us
    ppermute x2, starting transfers between devices, exchanged(): return lax.ppermute(value, 'rng', pairs + [(j, i) for i, j in pairs])  4.69 us
    all_to_all x1, starting transfers between devices, on_device(): lax.all_to_all(blocks, 'rng', split_axis=0, concat_axis=0, tiled=True)  3.88 us
    pallas_call x1, Pallas kernels, merge_tables(): pl.pallas_call(functools.partial(merge_table_kernel, level, stride), out_...  3.78 us
    ppermute x3, starting transfers between devices, from_partner(): return lax.ppermute(value, 'sub', pairs)  3.68 us
    ppermute x8, waiting for transfers between devices, across(): return lax.ppermute(value, 'rng', [(i, i ^ mask) for i in range(devices)])  2.43 us
  transfers between devices with their start and end apart: 14, of which 4 were waited for; matrix products, arithmetic and copies ran while one was open for 0% of the time, Pallas kernels for 14%

commit v1 on v0

--- a/solution.py
+++ b/solution.py
@@ -299,23 +299,25 @@
     )(own_side, own_rows, out_rows, *pieces)
 
 
-def inner_kernel(rows_ref, pulses_ref, image_ref):
+def inner_kernel(rows_ref, pulses_ref, outer_ref, image_ref):
     image = dot(rows_ref[...], pulses_ref[...])
-    image_ref[...] = image.astype(BF16).reshape(image_ref.shape)
-
-
-def inner_image(rows, pulses):
-    angles, count = rows.shape[0], pulses.shape[1]
+    parts, half, count = outer_ref.shape
+    image_ref[:, :, :count] = outer_ref[...]
+    image_ref[:, :, count:] = image.astype(BF16).reshape(parts, half, image.shape[1])
+
+
+def whole_image(rows, pulses, outer):
+    parts, half, count = outer.shape
     return pl.pallas_call(
         inner_kernel,
-        out_shape=jax.ShapeDtypeStruct((2, angles // 2, count), BF16),
-        in_specs=[VMEM] * 2,
+        out_shape=jax.ShapeDtypeStruct((parts, half, count + pulses.shape[1]), BF16),
+        in_specs=[VMEM] * 3,
         out_specs=VMEM,
         compiler_params=params(8),
         cost_estimate=pl.CostEstimate(
-            flops=2 * rows.size * count, bytes_accessed=3 * MIB, transcendentals=0
+            flops=2 * rows.size * pulses.shape[1], bytes_accessed=3 * MIB, transcendentals=0
         ),
-    )(rows, pulses)
+    )(rows, pulses, outer)
 
 
 def exchanged(value, begin):
@@ -356,34 +358,31 @@
     )(own_side, first, second)
 
 
+def resampled(image_ref, rims_ref, centre_ref, rim_ref, value_ref, child):
+    parts, half, bins = image_ref.shape
+    value_ref[...] = dot(image_ref[...].reshape(parts * half, bins), centre_ref[child])
+    rims = rims_ref[...]
+    return [
+        (value_ref[part * half : (part + 1) * half, :] + dot(rims, rim_ref[child, part])).astype(BF16)
+        for part in range(parts)
+    ]
+
+
 def early_kernel(
-    own_outer, own_inner, rims_ref, far_outer, far_rims, centre_ref, rim_ref, matrix_ref, turn_ref,
-    merged_ref, partial_ref, value_ref,
+    own_ref, rims_ref, centre_ref, rim_ref, matrix_ref, turn_ref, merged_ref, value_ref
 ):
-    parts, half, count = own_outer.shape
-    image = jnp.concatenate([own_outer[...], own_inner[...]], axis=2)
-    value_ref[...] = dot(image.reshape(parts * half, image.shape[2]), centre_ref[0])
-    rows = []
-    for part in range(parts):
-        value = value_ref[part * half : (part + 1) * half, :]
-        rows.append((value + dot(rims_ref[...], rim_ref[0, part])).astype(BF16))
+    rows = resampled(own_ref, rims_ref, centre_ref, rim_ref, value_ref, 0)
     merged_ref[0], merged_ref[1] = rotated(
         (dot(matrix_ref[0], rows[0]), dot(matrix_ref[0], rows[1])), (turn_ref[0, 0], turn_ref[0, 1])
     )
-    for part in range(parts):
-        value = dot(far_outer[part], centre_ref[1, :count, :])
-        here = slice(part * half, (part + 1) * half)
-        partial_ref[here, :] = value + dot(far_rims[...], rim_ref[1, part])
 
 
 def late_kernel(
-    far_inner, merged_ref, partial_ref, centre_ref, matrix_ref, turn_ref, out_ref, buffer, sems
+    far_ref, rims_ref, merged_ref, centre_ref, rim_ref, matrix_ref, turn_ref, out_ref, buffer,
+    value_ref, sems,
 ):
-    parts, half, count = far_inner.shape
-    bins = centre_ref.shape[-1]
-    inner = far_inner[...].reshape(parts * half, count)
-    value = partial_ref[...] + dot(inner, centre_ref[1, bins - count :, :])
-    rows = [value[part * half : (part + 1) * half].astype(BF16) for part in range(parts)]
+    rows = resampled(far_ref, rims_ref, centre_ref, rim_ref, value_ref, 1)
+    parts = len(rows)
     block = LANES
     copies = []
     for first in range(0, matrix_ref.shape[1], 2 * block):
@@ -410,30 +409,29 @@
     centre, rim, turn, matrices, _ = tables
     angles, bins = turn.shape[-2:]
     cost = pl.CostEstimate(flops=4 * angles * bins * bins, bytes_accessed=8 * MIB, transcendentals=0)
-    merged, partial = pl.pallas_call(
+    value = pltpu.VMEM((angles, bins), F32)
+    merged = pl.pallas_call(
         early_kernel,
-        out_shape=[
-            jax.ShapeDtypeStruct((2, angles, bins), F32),
-            jax.ShapeDtypeStruct((angles, bins), F32),
-        ],
-        in_specs=[VMEM] * 9,
-        out_specs=[VMEM] * 2,
-        scratch_shapes=[pltpu.VMEM((angles, bins), F32)],
-        compiler_params=params(20),
+        out_shape=jax.ShapeDtypeStruct((2, angles, bins), F32),
+        in_specs=[VMEM] * 6,
+        out_specs=VMEM,
+        scratch_shapes=[value],
+        compiler_params=params(16),
         cost_estimate=cost,
-    )(*own, rims, far[0], far_rims, centre, rim, matrices, turn)
+    )(own, rims, centre, rim, matrices, turn)
     return pl.pallas_call(
         late_kernel,
         out_shape=jax.ShapeDtypeStruct((2, angles, bins), dtype),
-        in_specs=[VMEM] * 6,
+        in_specs=[VMEM] * 7,
         out_specs=ANY,
         scratch_shapes=[
             pltpu.VMEM((2, angles, bins), dtype),
+            value,
             pltpu.SemaphoreType.DMA((angles // LANES,)),
         ],
-        compiler_params=params(20),
+        compiler_params=params(16),
         cost_estimate=cost,
-    )(far[1], merged, partial, centre, matrices, turn)
+    )(far, far_rims, merged, centre, rim, matrices, turn)
 
 
 def after(value, *earlier):
@@ -455,7 +453,7 @@
         rows = lax.dynamic_index_in_dim(sides, side, 1, keepdims=False)
         ends = [rows[..., :step], rows[..., -step:]]
         rest = [rows[..., -2 * step : -step], rows[..., step : -2 * step]]
-        return jnp.concatenate(ends, axis=-1), jnp.concatenate(rest, axis=-1)
+        return jnp.concatenate(ends + rest, axis=-1)
 
     def packed(edge):
         return edge.transpose(2, 0, 1, 3).reshape(half, 4 * rim)
@@ -484,24 +482,22 @@
     sends = joined(near_blocks, relay)
     pieces = [across(value, d) if d else value for d, value in enumerate(sends)]
     own_matrix, out_matrix, own_side = filter_table(fore_flag, angles, local_pulses, sends[0])
-    tables = merge_tables(0, 1, *settings, own_matrix)
-    pieces[0] = after(pieces[0], tables[0])
     own_outer, out_outer, *edges = outer_image(own_side, own_matrix, out_matrix, pieces)
 
     pulses = after(pulses, out_outer).reshape(2 * local_pulses * devices, bins - LANES)
-    out_inner = inner_image(out_matrix, pulses)
-    own_inner = inner_image(own_matrix, pulses)
-    far = [from_partner(value, 1) for value in (out_outer, out_inner)]
-    edges = [after(edge, out_inner, far[0]) for edge in edges]
-    own = own_outer, own_inner
+    out = whole_image(out_matrix, pulses, out_outer)
+    own = whole_image(own_matrix, pulses, own_outer)
+    edges = [after(edge, out) for edge in edges]
+    tables = merge_tables(0, 1, *settings, own)
     for level in range(levels):
         stride = 2**level
         if level > 0:
             tables = merge_tables(level, stride, *settings, image)
             own, out, edges = split_image(level, image, fore_flag, rim)
-            far = [from_partner(value, stride) for value in out]
+            own_side = tables[-1]
+        far = from_partner(out, stride)
         edges = exchanged(edges[0], 0), exchanged(edges[1], 1)
-        rims, out_rims = sorted_rims(tables[-1], *edges)
+        rims, out_rims = sorted_rims(own_side, *edges)
         far_rims = from_partner(out_rims, stride)
         image = merged_image(own, rims, far, far_rims, tables, BF16 if level + 1 < levels else F32)
     return image

time: 67.5 us -> 49.8 us (0.74)
  the two profiles are of different devices: /device:TPU:0 before, /device:TPU:16 now
where the time goes in v1:
time: 49.8 us; the launch traced here: 49.5 us
  starting transfers between devices  17.6 us (35%)
  waiting for transfers between devices  15.3 us (31%)
  Pallas kernels  13.6 us (27%)
  local copies, waits for them, and re-layouts  2.98 us (6%)
    ppermute x8, starting transfers between devices, across(): return lax.ppermute(value, 'rng', [(i, i ^ mask) for i in range(devices)])  8.49 us
    ppermute x8, waiting for transfers between devices, across(): return lax.ppermute(value, 'rng', [(i, i ^ mask) for i in range(devices)])  8.24 us
    all_to_all x1, starting transfers between devices, on_device(): lax.all_to_all(blocks, 'rng', split_axis=0, concat_axis=0, tiled=True)  6.72 us
    pallas_call x1, Pallas kernels, merge_tables(): pl.pallas_call(functools.partial(merge_table_kernel, level, stride), out_...  4.27 us
    ppermute x2, waiting for transfers between devices, exchanged(): return lax.ppermute(value, 'rng', pairs + [(j, i) for i, j in pairs])  4.09 us
    unnamed x18, local copies, waits for them, and re-layouts  2.98 us
    ppermute x2, waiting for transfers between devices, from_partner(): return lax.ppermute(value, 'sub', pairs)  2.97 us
    pallas_call x1, Pallas kernels, merged_image(): pl.pallas_call(late_kernel, out_shape=jax.ShapeDtypeStruct((2, angles, bi...  2.18 us
  transfers between devices with their start and end apart: 13, of which 5 were waited for; matrix products, arithmetic and copies ran while one was open for 0% of the time, Pallas kernels for 20%

profile of v1, /device:TPU:16, one launch (start us, length us, event | category | flops | bytes accessed | tf_op | source)
XLA Modules:
  0.0 49.5 jit_solution(10449876176244818946)
XLA Ops:
  0.0 0.0 copy-start
  0.0 1.2 %copy-done = bf16[2,32,8192]{2,1,0:T(8,128)(2,1)S(1)} copy-done((bf16[2,32,8192]{2,1,0:T(8,128)(2,1)S(1)}, bf16[2,32,8192]{2,1,0:T(8,128)(2,1)}, u32[]{:S(2)}) %copy-start) | copy-done | bytes 1048600
  1.2 1.0 %shard_map.64 = (bf16[8,64,128]{2,1,0:T(8,128)(2,1)S(1)}, bf16[8,64,128]{2,1,0:T(8,128)(2,1)S(1)}, bf16[16,64,384]{2,1,0:T(8,128)(2,1)}) custom-call(bf16[64,8192]{1,0:T(8,128)(2,1)S(1)} %bitcast.4), custom_call_target="tpu_custom_call" | custom-call | bytes 2097152 | tf_op jit(solution)/shard_map/pallas_call | solution.py:81
  2.3 0.0 collective-permute-start
  2.3 6.7 %all-to-all-start = ((bf16[16,64,384]{2,1,0:T(8,128)(2,1)}), bf16[16,64,384]{2,1,0:T(8,128)(2,1)S(1)}, u32[]{:S(2)}, u32[]{:S(2)}) async-start(bf16[16,64,384]{2,1,0:T(8,128)(2,1)} %get-tuple-element.36), calls=%async_computation | async-start | bytes 1572864 | tf_op jit(solution)/shard_map/all_to_all | solution.py:481
  9.0 0.0 collective-permute-done.relay_ref
  9.0 0.0 copy-start.6
  9.0 0.2 collective-permute-start.1
  9.2 1.5 %collective-permute-start.2 = (bf16[128,128]{1,0:T(8,128)(2,1)S(1)}, bf16[128,128]{1,0:T(8,128)(2,1)S(1)}, u32[]{:S(2)}, u32[]{:S(2)}) collective-permute-start(bf16[128,128]{1,0:T(8,128)(2,1)S(1)} %get-tuple-element.40), channel_id=1, source_target_pairs={{0,2},{1,3},{2,0},{3,1},{4,6},{5,7},{6,4},{7,5},{8,10},{9,11},{10,... | collective-permute-start | bytes 98312 | tf_op jit(solution)/shard_map/ppermute | solution.py:113
  10.7 0.2 collective-permute-start.3
  11.0 3.8 %collective-permute-start.4 = (bf16[128,128]{1,0:T(8,128)(2,1)S(1)}, bf16[128,128]{1,0:T(8,128)(2,1)S(1)}, u32[]{:S(2)}, u32[]{:S(2)}) collective-permute-start(bf16[128,128]{1,0:T(8,128)(2,1)S(1)} %get-tuple-element.42), channel_id=1, source_target_pairs={{0,4},{1,5},{2,6},{3,7},{4,0},{5,1},{6,2},{7,3},{8,12},{9,13},{10,... | collective-permute-start | bytes 98312 | tf_op jit(solution)/shard_map/ppermute | solution.py:113
  14.7 0.0 collective-permute-start.5
  14.7 0.0 collective-permute-done.1.refs_1_
  14.7 2.6 %collective-permute-start.6 = (bf16[128,128]{1,0:T(8,128)(2,1)S(1)}, bf16[128,128]{1,0:T(8,128)(2,1)S(1)}, u32[]{:S(2)}, u32[]{:S(2)}) collective-permute-start(bf16[128,128]{1,0:T(8,128)(2,1)S(1)} %get-tuple-element.44), channel_id=1, source_target_pairs={{0,6},{1,7},{2,4},{3,5},{4,2},{5,3},{6,0},{7,1},{8,14},{9,15},{10,... | collective-permute-start | bytes 98312 | tf_op jit(solution)/shard_map/ppermute | solution.py:113
  17.4 0.0 collective-permute-done.2.refs_2_
  17.4 0.2 collective-permute-start.7
  17.5 0.0 copy-done.6
  17.5 0.1 copy.7.flag_ref
  17.6 1.9 %shard_map.66 = (bf16[512,1024]{1,0:T(8,128)(2,1)S(1)}, bf16[512,1024]{1,0:T(8,128)(2,1)S(1)}, f32[8,128]{1,0:T(8,128)S(1)}) custom-call(s32[1,2,1]{2,1,0:T(2,128)S(1)} %copy.7.flag_ref, bf16[128,128]{1,0:T(8,128)(2,1)S(1)} %get-tuple-element.34.after_ref.refs_0_), custom_call_target="tpu_custom_call" | custom-call | flops 9000000 | bytes 4194304 | tf_op jit(solution)/shard_map/pallas_call | solution.py:158
  19.5 0.0 collective-permute-done.3.refs_3_
  19.5 6.0 %collective-permute-done.4.refs_4_ = bf16[128,128]{1,0:T(8,128)(2,1)S(1)} collective-permute-done((bf16[128,128]{1,0:T(8,128)(2,1)S(1)}, bf16[128,128]{1,0:T(8,128)(2,1)S(1)}, u32[]{:S(2)}, u32[]{:S(2)}) %collective-permute-start.4) | collective-permute-done | bytes 32800 | tf_op jit(solution)/shard_map/ppermute | solution.py:113
  25.6 0.0 collective-permute-done.5.refs_5_
  25.6 2.2 %collective-permute-done.6.refs_6_ = bf16[128,128]{1,0:T(8,128)(2,1)S(1)} collective-permute-done((bf16[128,128]{1,0:T(8,128)(2,1)S(1)}, bf16[128,128]{1,0:T(8,128)(2,1)S(1)}, u32[]{:S(2)}, u32[]{:S(2)}) %collective-permute-start.6) | collective-permute-done | bytes 32800 | tf_op jit(solution)/shard_map/ppermute | solution.py:113
  27.8 0.0 collective-permute-done.7.refs_7_
  27.8 0.0 copy-start.7
  27.8 1.5 %shard_map.67 = (bf16[2,256,128]{2,1,0:T(8,128)(2,1)S(1)}, bf16[2,256,128]{2,1,0:T(8,128)(2,1)S(1)}, bf16[256,128]{1,0:T(8,128)(2,1)}, bf16[256,128]{1,0:T(8,128)(2,1)}) custom-call(f32[8,128]{1,0:T(8,128)S(1)} %get-tuple-element.37.side_ref, bf16[512,1024]{1,0:T(8,128)(2,1)S(1)} %get-tuple-element.38.own_rows.rows_ref, ...), custom_call_target="tpu_custom_call" | custom-call | flops 268435456 | bytes 3145728 | tf_op jit(solution)/shard_map/pallas_call | solution.py:289
  29.3 0.0 copy-start.1
  29.3 0.6 %copy-done.1 = bf16[2,256,128]{2,1,0:T(8,128)(2,1)} copy-done((bf16[2,256,128]{2,1,0:T(8,128)(2,1)}, bf16[2,256,128]{2,1,0:T(8,128)(2,1)S(1)}, u32[]{:S(2)}) %copy-start.1) | copy-done | bytes 131096
  29.9 0.0 all-to-all-done
  30.0 0.0 copy-start.2
  30.0 0.9 %copy-done.2 = bf16[2,256,128]{2,1,0:T(8,128)(2,1)S(1)} copy-done((bf16[2,256,128]{2,1,0:T(8,128)(2,1)S(1)}, bf16[2,256,128]{2,1,0:T(8,128)(2,1)}, u32[]{:S(2)}) %copy-start.2) | copy-done | bytes 131096
  30.9 0.0 copy-start.5
  30.9 0.7 %shard_map.68 = bf16[2,256,512]{2,1,0:T(8,128)(2,1)S(1)} custom-call(bf16[512,1024]{1,0:T(8,128)(2,1)S(1)} %get-tuple-element.35.out_rows.rows_ref, bf16[1024,384]{1,0:T(8,128)(2,1)S(1)} %bitcast.2, bf16[2,256,128]{2,1,0:T(8,128)(2,1)S(1)} %copy-done.2), custom_call_target="tpu_custom_call" | custom-call | flops 402653184 | bytes 3145728 | tf_op jit(solution)/shard_map/pallas_call | solution.py:311
  31.6 1.6 %collective-permute-start.8 = (bf16[2,256,512]{2,1,0:T(8,128)(2,1)S(1)}, bf16[2,256,512]{2,1,0:T(8,128)(2,1)S(1)}, u32[]{:S(2)}, u32[]{:S(2)}) collective-permute-start(bf16[2,256,512]{2,1,0:T(8,128)(2,1)S(1)} %shard_map.68), channel_id=1, source_target_pairs={{0,16},{16,0},{1,17},{17,1},{2,18},{18,2},{3,19},{19,3},{4,20},{20... | collective-permute-start | bytes 1572872 | tf_op jit(solution)/shard_map/ppermute | solution.py:443
  33.2 0.2 collective-permute-start.9
  33.3 0.0 collective-permute-start.10
  33.3 0.0 copy-done.7
  33.3 0.1 copy.9.offset_ref
  33.4 0.0 copy-start.3
  33.4 0.0 copy-start.4
  33.4 0.7 %shard_map.70.after_ref.own_ref = bf16[2,256,512]{2,1,0:T(8,128)(2,1)S(1)} custom-call(bf16[512,1024]{1,0:T(8,128)(2,1)S(1)} %get-tuple-element.38.own_rows.rows_ref, bf16[1024,384]{1,0:T(8,128)(2,1)S(1)} %bitcast.3, bf16[2,256,128]{2,1,0:T(8,128)(2,1)S(1)} %get-tuple-element.53.outer_ref), custom_call_target="tpu_custom_call" | custom-call | flops 402653184 | bytes 3145728 | tf_op jit(solution)/shard_map/pallas_call | solution.py:311
  34.2 0.5 collective-permute-done.9.first_ref
  34.6 3.6 %collective-permute-done.10.second_ref = bf16[256,128]{1,0:T(8,128)(2,1)S(1)} collective-permute-done((bf16[256,128]{1,0:T(8,128)(2,1)}, bf16[256,128]{1,0:T(8,128)(2,1)S(1)}, u32[]{:S(2)}, u32[]{:S(2)}) %collective-permute-start.10) | collective-permute-done | bytes 65568 | tf_op jit(solution)/shard_map/ppermute | solution.py:326
  38.2 0.2 shard_map.69
  38.4 0.6 %collective-permute-start.11 = (bf16[256,128]{1,0:T(8,128)(2,1)S(1)}, bf16[256,128]{1,0:T(8,128)(2,1)S(1)}, u32[]{:S(2)}, u32[]{:S(2)}) collective-permute-start(bf16[256,128]{1,0:T(8,128)(2,1)S(1)} %get-tuple-element.52), channel_id=1, source_target_pairs={{0,16},{16,0},{1,17},{17,1},{2,18},{18,2},{3,19},{19,3},{4,20},{20... | collective-permute-start | bytes 196616 | tf_op jit(solution)/shard_map/ppermute | solution.py:443
  39.0 0.0 copy-done.5
  39.0 0.0 copy-done.3
  39.0 0.0 copy-done.4
  39.0 4.3 %shard_map.71 = (bf16[2,512,512]{2,1,0:T(8,128)(2,1)S(1)}, bf16[2,2,128,512]{3,2,1,0:T(8,128)(2,1)S(1)}, f32[2,2,512,512]{3,2,1,0:T(8,128)S(1)}, bf16[2,512,256]{2,1,0:T(8,128)(2,1)S(1)}, f32[8,128]{1,0:T(8,128)}) custom-call(s32[1,2,1]{2,1,0:T(2,128)S(1)} %copy.7.flag_ref, s32[1,2,1]{2,1,0:T(2,128)S(1)} %copy.9.offset_ref, f32[1,2]{1,0:T(1,128)S(1)} %copy-done.5, ...), custom_call_target="tpu_custom_call" | custom-call | flops 2300000000 | bytes 7340032 | tf_op jit(solution)/shard_map/pallas_call | solution.py:236
  43.3 1.1 %shard_map.72.merged_ref = f32[2,512,512]{2,1,0:T(8,128)S(1)} custom-call(bf16[2,256,512]{2,1,0:T(8,128)(2,1)S(1)} %shard_map.70.after_ref.own_ref, bf16[256,128]{1,0:T(8,128)(2,1)S(1)} %get-tuple-element.54.rims_ref, bf16[2,512,512]{2,1,0:T(8,128)(2,1)S(1)} %get-tuple-element.55.centre_ref, bf16[2,2,128,512]{3,2,1,0:T(8,128)(2,1)S(1)} %get-tuple-element.56.rim_ref, ...), custom_call_target="tpu_custom_call" | custom-call | flops 536870912 | bytes 8388608 | tf_op jit(solution)/shard_map/pallas_call | solution.py:413
  44.4 3.0 %collective-permute-done.11.rims_ref = bf16[256,128]{1,0:T(8,128)(2,1)S(1)} collective-permute-done((bf16[256,128]{1,0:T(8,128)(2,1)S(1)}, bf16[256,128]{1,0:T(8,128)(2,1)S(1)}, u32[]{:S(2)}, u32[]{:S(2)}) %collective-permute-start.11) | collective-permute-done | bytes 65568 | tf_op jit(solution)/shard_map/ppermute | solution.py:443
  47.3 0.0 collective-permute-done.8.far_ref
  47.3 2.2 %shard_map.73 = f32[2,512,512]{2,1,0:T(8,128)} custom-call(bf16[2,256,512]{2,1,0:T(8,128)(2,1)S(1)} %collective-permute-done.8.far_ref, bf16[256,128]{1,0:T(8,128)(2,1)S(1)} %collective-permute-done.11.rims_ref, f32[2,512,512]{2,1,0:T(8,128)S(1)} %shard_map.72.merged_ref, bf16[2,512,512]{2,1,0:T(8,128)(2,1)S(1)} %get-tuple-element.55.centre_ref, ...), custom_call_target="tpu_custom_call" | custom-call | flops 536870912 | bytes 8388608 | tf_op jit(solution)/shard_map/pallas_call | solution.py:422
  (1 shorter events, 0.0 us)
Async XLA Ops:
  0.0 1.2 %copy-start = (bf16[2,32,8192]{2,1,0:T(8,128)(2,1)S(1)}, bf16[2,32,8192]{2,1,0:T(8,128)(2,1)}, u32[]{:S(2)}) copy-start(bf16[2,32,8192]{2,1,0:T(8,128)(2,1)} %param.6) | copy-start | bytes 3145732
  2.3 6.7 %collective-permute-start = (bf16[8,64,128]{2,1,0:T(8,128)(2,1)S(1)}, bf16[8,64,128]{2,1,0:T(8,128)(2,1)S(1)}, u32[]{:S(2)}, u32[]{:S(2)}) collective-permute-start(bf16[8,64,128]{2,1,0:T(8,128)(2,1)S(1)} %get-tuple-element.33), channel_id=1, source_target_pairs={{0,8},{1,9},{2,10},{3,11},{4,12},{5,13},{6,14},{7,15},{8,0},{9,1},... | collective-permute-start | bytes 393224 | tf_op jit(solution)/shard_map/ppermute | solution.py:113
  2.3 27.7 %all-to-all-start = ((bf16[16,64,384]{2,1,0:T(8,128)(2,1)}), bf16[16,64,384]{2,1,0:T(8,128)(2,1)S(1)}, u32[]{:S(2)}, u32[]{:S(2)}) async-start(bf16[16,64,384]{2,1,0:T(8,128)(2,1)} %get-tuple-element.36), calls=%async_computation | async-start | bytes 1572864 | tf_op jit(solution)/shard_map/all_to_all | solution.py:481
  9.0 8.6 %copy-start.6 = (s32[1,2,1]{1,2,0:T(1,128)S(1)}, s32[1,2,1]{1,2,0:T(1,128)}, u32[]{:S(2)}) copy-start(s32[1,2,1]{1,2,0:T(1,128)} %param.7) | copy-start | bytes 28
  9.0 5.7 %collective-permute-start.1 = (bf16[128,128]{1,0:T(8,128)(2,1)S(1)}, bf16[128,128]{1,0:T(8,128)(2,1)S(1)}, u32[]{:S(2)}, u32[]{:S(2)}) collective-permute-start(bf16[128,128]{1,0:T(8,128)(2,1)S(1)} %get-tuple-element.39), channel_id=1, source_target_pairs={{0,1},{1,0},{2,3},{3,2},{4,5},{5,4},{6,7},{7,6},{8,9},{9,8},{10,11... | collective-permute-start | bytes 98312 | tf_op jit(solution)/shard_map/ppermute | solution.py:113
  9.2 8.1 %collective-permute-start.2 = (bf16[128,128]{1,0:T(8,128)(2,1)S(1)}, bf16[128,128]{1,0:T(8,128)(2,1)S(1)}, u32[]{:S(2)}, u32[]{:S(2)}) collective-permute-start(bf16[128,128]{1,0:T(8,128)(2,1)S(1)} %get-tuple-element.40), channel_id=1, source_target_pairs={{0,2},{1,3},{2,0},{3,1},{4,6},{5,7},{6,4},{7,5},{8,10},{9,11},{10,... | collective-permute-start | bytes 98312 | tf_op jit(solution)/shard_map/ppermute | solution.py:113
  10.7 8.8 %collective-permute-start.3 = (bf16[128,128]{1,0:T(8,128)(2,1)S(1)}, bf16[128,128]{1,0:T(8,128)(2,1)S(1)}, u32[]{:S(2)}, u32[]{:S(2)}) collective-permute-start(bf16[128,128]{1,0:T(8,128)(2,1)S(1)} %get-tuple-element.41), channel_id=1, source_target_pairs={{0,3},{1,2},{2,1},{3,0},{4,7},{5,6},{6,5},{7,4},{8,11},{9,10},{10,... | collective-permute-start | bytes 98312 | tf_op jit(solution)/shard_map/ppermute | solution.py:113
  11.0 14.6 %collective-permute-start.4 = (bf16[128,128]{1,0:T(8,128)(2,1)S(1)}, bf16[128,128]{1,0:T(8,128)(2,1)S(1)}, u32[]{:S(2)}, u32[]{:S(2)}) collective-permute-start(bf16[128,128]{1,0:T(8,128)(2,1)S(1)} %get-tuple-element.42), channel_id=1, source_target_pairs={{0,4},{1,5},{2,6},{3,7},{4,0},{5,1},{6,2},{7,3},{8,12},{9,13},{10,... | collective-permute-start | bytes 98312 | tf_op jit(solution)/shard_map/ppermute | solution.py:113
  14.7 10.9 %collective-permute-start.5 = (bf16[128,128]{1,0:T(8,128)(2,1)S(1)}, bf16[128,128]{1,0:T(8,128)(2,1)S(1)}, u32[]{:S(2)}, u32[]{:S(2)}) collective-permute-start(bf16[128,128]{1,0:T(8,128)(2,1)S(1)} %get-tuple-element.43), channel_id=1, source_target_pairs={{0,5},{1,4},{2,7},{3,6},{4,1},{5,0},{6,3},{7,2},{8,13},{9,12},{10,... | collective-permute-start | bytes 98312 | tf_op jit(solution)/shard_map/ppermute | solution.py:113
  14.7 13.0 %collective-permute-start.6 = (bf16[128,128]{1,0:T(8,128)(2,1)S(1)}, bf16[128,128]{1,0:T(8,128)(2,1)S(1)}, u32[]{:S(2)}, u32[]{:S(2)}) collective-permute-start(bf16[128,128]{1,0:T(8,128)(2,1)S(1)} %get-tuple-element.44), channel_id=1, source_target_pairs={{0,6},{1,7},{2,4},{3,5},{4,2},{5,3},{6,0},{7,1},{8,14},{9,15},{10,... | collective-permute-start | bytes 98312 | tf_op jit(solution)/shard_map/ppermute | solution.py:113
  17.4 10.4 %collective-permute-start.7 = (bf16[128,128]{1,0:T(8,128)(2,1)S(1)}, bf16[128,128]{1,0:T(8,128)(2,1)S(1)}, u32[]{:S(2)}, u32[]{:S(2)}) collective-permute-start(bf16[128,128]{1,0:T(8,128)(2,1)S(1)} %get-tuple-element.45), channel_id=1, source_target_pairs={{0,7},{1,6},{2,5},{3,4},{4,3},{5,2},{6,1},{7,0},{8,15},{9,14},{10,... | collective-permute-start | bytes 98312 | tf_op jit(solution)/shard_map/ppermute | solution.py:113
  27.8 5.6 %copy-start.7 = (s32[1,2,1]{1,2,0:T(1,128)S(1)}, s32[1,2,1]{1,2,0:T(1,128)}, u32[]{:S(2)}) copy-start(s32[1,2,1]{1,2,0:T(1,128)} %param.8) | copy-start | bytes 28
  29.3 0.6 %copy-start.1 = (bf16[2,256,128]{2,1,0:T(8,128)(2,1)}, bf16[2,256,128]{2,1,0:T(8,128)(2,1)S(1)}, u32[]{:S(2)}) copy-start(bf16[2,256,128]{2,1,0:T(8,128)(2,1)S(1)} %get-tuple-element.46.outer_ref) | copy-start | bytes 393220
  30.0 0.9 %copy-start.2 = (bf16[2,256,128]{2,1,0:T(8,128)(2,1)S(1)}, bf16[2,256,128]{2,1,0:T(8,128)(2,1)}, u32[]{:S(2)}) copy-start(bf16[2,256,128]{2,1,0:T(8,128)(2,1)} %copy-done.1) | copy-start | bytes 393220
  30.9 8.1 %copy-start.5 = (f32[1,2]{1,0:T(1,128)S(1)}, f32[1,2]{1,0:T(1,128)}, u32[]{:S(2)}) copy-start(f32[1,2]{1,0:T(1,128)} %shift_ref.1) | copy-start | bytes 28
  31.6 15.8 %collective-permute-start.8 = (bf16[2,256,512]{2,1,0:T(8,128)(2,1)S(1)}, bf16[2,256,512]{2,1,0:T(8,128)(2,1)S(1)}, u32[]{:S(2)}, u32[]{:S(2)}) collective-permute-start(bf16[2,256,512]{2,1,0:T(8,128)(2,1)S(1)} %shard_map.68), channel_id=1, source_target_pairs={{0,16},{16,0},{1,17},{17,1},{2,18},{18,2},{3,19},{19,3},{4,20},{20... | collective-permute-start | bytes 1572872 | tf_op jit(solution)/shard_map/ppermute | solution.py:443
  33.2 1.5 %collective-permute-start.9 = (bf16[256,128]{1,0:T(8,128)(2,1)}, bf16[256,128]{1,0:T(8,128)(2,1)S(1)}, u32[]{:S(2)}, u32[]{:S(2)}) collective-permute-start(bf16[256,128]{1,0:T(8,128)(2,1)} %get-tuple-element.49), channel_id=1, source_target_pairs={{0,1},{2,3},{4,5},{6,7},{8,9},{10,11},{12,13},{14,15},{1,0},{3,2},... | collective-permute-start | bytes 196616 | tf_op jit(solution)/shard_map/ppermute | solution.py:326
  33.3 4.9 %collective-permute-start.10 = (bf16[256,128]{1,0:T(8,128)(2,1)}, bf16[256,128]{1,0:T(8,128)(2,1)S(1)}, u32[]{:S(2)}, u32[]{:S(2)}) collective-permute-start(bf16[256,128]{1,0:T(8,128)(2,1)} %get-tuple-element.51), channel_id=1, source_target_pairs={{1,2},{3,4},{5,6},{7,8},{9,10},{11,12},{13,14},{15,0},{2,1},{4,3},... | collective-permute-start | bytes 196616 | tf_op jit(solution)/shard_map/ppermute | solution.py:326
  33.4 5.6 %copy-start.3 = (bf16[1,544,512]{2,1,0:T(8,128)(2,1)S(1)}, bf16[1,544,512]{2,1,0:T(8,128)(2,1)}, u32[]{:S(2)}) copy-start(bf16[1,544,512]{2,1,0:T(8,128)(2,1)} %range_ref.1) | copy-start | bytes 1671172
  33.4 5.6 %copy-start.4 = (bf16[1,2,512,256]{3,2,1,0:T(8,128)(2,1)S(1)}, bf16[1,2,512,256]{3,2,1,0:T(8,128)(2,1)}, u32[]{:S(2)}) copy-start(bf16[1,2,512,256]{3,2,1,0:T(8,128)(2,1)} %interp_ref.1) | copy-start | bytes 1572868
  38.4 8.9 %collective-permute-start.11 = (bf16[256,128]{1,0:T(8,128)(2,1)S(1)}, bf16[256,128]{1,0:T(8,128)(2,1)S(1)}, u32[]{:S(2)}, u32[]{:S(2)}) collective-permute-start(bf16[256,128]{1,0:T(8,128)(2,1)S(1)} %get-tuple-element.52), channel_id=1, source_target_pairs={{0,16},{16,0},{1,17},{17,1},{2,18},{18,2},{3,19},{19,3},{4,20},{20... | collective-permute-start | bytes 196616 | tf_op jit(solution)/shard_map/ppermute | solution.py:443

commit v2 on v1

--- a/solution.py
+++ b/solution.py
@@ -113,13 +113,12 @@
     return lax.ppermute(value, "rng", [(i, i ^ mask) for i in range(devices)])
 
 
-def filter_table_kernel(
-    local_pulses, flag_ref, after_ref, own_ref, out_ref, side_ref, cos_ref, sin_ref
-):
+def filter_table_kernel(local_pulses, flag_ref, after_ref, rows_ref, side_ref, cos_ref, sin_ref):
     own_flag = flag_ref[0, lax.axis_index("sub"), 0]
     side_ref[...] = jnp.full(side_ref.shape, own_flag.astype(F32))
-    rows, columns = own_ref.shape
-    half, angles = rows // 2, rows
+    angles, columns = rows_ref.shape
+    half = angles // 2
+    first = (1 - own_flag) * half
     base = cos_ref.shape[0]
     scale = 1.0 / math.sqrt(columns // 2)
     lane = lax.broadcasted_iota(jnp.int32, (8, columns), 1)
@@ -129,37 +128,35 @@
     lag = second.astype(F32) * 0.5
     per_angle = pulse * (1.0 / angles)
     row = lax.broadcasted_iota(jnp.int32, (8, columns), 0)
+    for i in range(base // 8):
+        twice = (2 * (row + 8 * i + first) + 1 - angles).astype(F32)
+        cosine, sine = cos_sin_pi(twice * per_angle - lag)
+        cos_ref[8 * i : 8 * i + 8, :] = cosine * scale
+        sin_ref[8 * i : 8 * i + 8, :] = sine * scale
     step = cos_sin_pi(per_angle * (2 * base))
-    for ref, side in ((out_ref, 1 - own_flag), (own_ref, own_flag)):
-        first = side * half
-        for i in range(base // 8):
-            twice = (2 * (row + 8 * i + first) + 1 - angles).astype(F32)
-            cosine, sine = cos_sin_pi(twice * per_angle - lag)
-            cos_ref[8 * i : 8 * i + 8, :] = cosine * scale
-            sin_ref[8 * i : 8 * i + 8, :] = sine * scale
-        for j in range(half // base):
-            for i in range(base // 16):
-                pair = [], []
-                for k in (2 * i, 2 * i + 1):
-                    here = slice(8 * k, 8 * k + 8)
-                    now = cos_ref[here, :], sin_ref[here, :]
-                    pair[0].append(now[0])
-                    pair[1].append(-now[1])
-                    if j + 1 < half // base:
-                        cos_ref[here, :], sin_ref[here, :] = rotated(now, step)
-                begin = j * base + 16 * i
-                ref[begin : begin + 16, :] = jnp.concatenate(pair[0]).astype(BF16)
-                begin += half
-                ref[begin : begin + 16, :] = jnp.concatenate(pair[1]).astype(BF16)
+    for j in range(half // base):
+        for i in range(base // 16):
+            pair = [], []
+            for k in (2 * i, 2 * i + 1):
+                here = slice(8 * k, 8 * k + 8)
+                now = cos_ref[here, :], sin_ref[here, :]
+                pair[0].append(now[0])
+                pair[1].append(-now[1])
+                if j + 1 < half // base:
+                    cos_ref[here, :], sin_ref[here, :] = rotated(now, step)
+            begin = j * base + 16 * i
+            rows_ref[begin : begin + 16, :] = jnp.concatenate(pair[0]).astype(BF16)
+            begin += half
+            rows_ref[begin : begin + 16, :] = jnp.concatenate(pair[1]).astype(BF16)
 
 
 def filter_table(fore_flag, angles, local_pulses, earlier):
     side = 2 * local_pulses * lax.axis_size("rng")
     return pl.pallas_call(
         functools.partial(filter_table_kernel, local_pulses),
-        out_shape=[jax.ShapeDtypeStruct((angles, side), BF16)] * 2 + [SIDE],
+        out_shape=[jax.ShapeDtypeStruct((angles, side), BF16), SIDE],
         in_specs=[SMEM, ANY],
-        out_specs=[VMEM] * 3,
+        out_specs=[VMEM] * 2,
         scratch_shapes=[pltpu.VMEM((64, side), F32)] * 2,
         compiler_params=params(6),
         cost_estimate=pl.CostEstimate(flops=9_000_000, bytes_accessed=4 * MIB, transcendentals=0),
@@ -168,7 +165,7 @@
 
 def merge_table_kernel(
     level, stride, flag_ref, offset_ref, shift_ref, range_ref, interp_ref, after_ref, centre_ref,
-    rim_ref, turn_ref, matrix_ref, side_ref,
+    rim_ref, turn_ref, matrix_ref, side_ref, kernel_ref, sems,
 ):
     group = lax.axis_index("sub")
     block = lax.axis_index("rng")
@@ -178,29 +175,54 @@
     taps = range_ref.shape[1]
     band = (taps - bins) // 2
     rim = MAX_SHIFT + band
-    kernel = range_ref[level]
+    own_flag = flag_ref[level, group, 0]
+    side_ref[...] = jnp.full(side_ref.shape, own_flag.astype(F32))
+    copies = [
+        pltpu.make_async_copy(source, target, sems.at[i])
+        for i, (source, target) in enumerate(
+            (
+                (range_ref.at[level], kernel_ref),
+                (interp_ref.at[level, own_flag], matrix_ref.at[0]),
+                (interp_ref.at[level, 1 - own_flag], matrix_ref.at[1]),
+            )
+        )
+    ]
+    for copy in copies:
+        copy.start()
 
     def moved(bin_id):
         tap = lax.broadcasted_iota(jnp.int32, (bin_id.shape[0], taps), 1)
-        return dot(jnp.where(tap == bin_id, 1.0, 0.0).astype(BF16), kernel).astype(BF16)
+        hot = jnp.where(tap == bin_id, 1.0, 0.0).astype(BF16)
+        return dot(hot, kernel_ref[...]).astype(BF16)
 
     row = lax.broadcasted_iota(jnp.int32, (bins, 1), 0)
     upper = row + (bins - 2 * LANES)
     own_bin = jnp.where(row % LANES < LANES // 2, row, upper + LANES)
     own_bin = jnp.where(row >= LANES, jnp.where(row % LANES < LANES // 2, upper, row - LANES), own_bin)
     own_bin = jnp.where(row >= 2 * LANES, row - LANES, own_bin)
-    own_flag = flag_ref[level, group, 0]
-    side_ref[...] = jnp.full(side_ref.shape, own_flag.astype(F32))
-    matrix_ref[0] = interp_ref[level, own_flag]
-    matrix_ref[1] = interp_ref[level, 1 - own_flag]
     rim_row = lax.broadcasted_iota(jnp.int32, (2 * rim, 1), 0)
     rim_bin = jnp.where(rim_row < rim, rim_row - rim, rim_row - rim + bins)
     rim_ref[...] = jnp.zeros(rim_ref.shape, BF16)
-    bin_id = block * bins + lax.broadcasted_iota(jnp.int32, (1, LANES), 1)
+    bin_id = block * bins + lax.broadcasted_iota(jnp.int32, (8, bins), 1)
     reach = 1.0 + bin_id.astype(F32) * (1.0 / total_bins)
-    rows = 64
-    for child in range(2):
-        member = group if child == 0 else group ^ stride
+    line = lax.broadcasted_iota(jnp.int32, (8, bins), 0)
+    base = 64
+    members = group, group ^ stride
+    for child, member in enumerate(members):
+        rate = shift_ref[level, member]
+        for first in range(0, base, 8):
+            angle = (first + line).astype(F32)
+            now = cos_sin_pi(rate * ((angle + 0.5) * (1.0 / angles) - 0.5) * reach)
+            turn_ref[child, 0, first : first + 8, :] = now[0]
+            turn_ref[child, 1, first : first + 8, :] = now[1]
+        step = cos_sin_pi(rate * (base / angles) * reach)
+        for first in range(base, angles, 8):
+            here, last = slice(first, first + 8), slice(first - base, first - base + 8)
+            now = rotated((turn_ref[child, 0, last, :], turn_ref[child, 1, last, :]), step)
+            turn_ref[child, 0, here, :], turn_ref[child, 1, here, :] = now
+    for copy in copies:
+        copy.wait()
+    for child, member in enumerate(members):
         lead = band - offset_ref[level, member, 0]
         centre_ref[child] = moved(own_bin + lead)
         ends = moved(rim_bin + lead)
@@ -208,23 +230,6 @@
             for side in range(2):
                 place = (2 * side + part) * rim
                 rim_ref[child, part, place : place + rim, :] = ends[side * rim : (side + 1) * rim]
-
-        rate = shift_ref[level, member]
-
-        def turn_rows(i, carry):
-            begin = pl.multiple_of(i * rows, rows)
-            angle = begin + lax.broadcasted_iota(jnp.int32, (rows, LANES), 0)
-            place = ((angle.astype(F32) + 0.5) * (1.0 / angles) - 0.5) * rate
-            now = cos_sin_pi(place * reach)
-            step = cos_sin_pi(place * (LANES / total_bins))
-            for tile in range(bins // LANES):
-                lanes = slice(tile * LANES, tile * LANES + LANES)
-                turn_ref[child, 0, pl.ds(begin, rows), lanes] = now[0]
-                turn_ref[child, 1, pl.ds(begin, rows), lanes] = now[1]
-                now = rotated(now, step)
-            return carry
-
-        lax.fori_loop(0, angles // rows, turn_rows, 0)
 
 
 def merge_tables(
@@ -242,8 +247,9 @@
             jax.ShapeDtypeStruct((2, *angle_interp.shape[2:]), BF16),
             SIDE,
         ],
-        in_specs=[SMEM] * 3 + [VMEM] * 2 + [ANY],
+        in_specs=[SMEM] * 3 + [ANY] * 3,
         out_specs=[VMEM] * 5,
+        scratch_shapes=[pltpu.VMEM((taps, bins), BF16), pltpu.SemaphoreType.DMA((3,))],
         compiler_params=params(12),
         cost_estimate=pl.CostEstimate(
             flops=2_300_000_000, bytes_accessed=7 * MIB, transcendentals=0
@@ -251,7 +257,13 @@
     )(fore_flag, band_offset, center_shift, range_kernel, angle_interp, earlier)
 
 
-def outer_kernel(pieces, side_ref, own_rows, out_rows, *refs):
+def alternating(pulses, local_pulses):
+    row = lax.broadcasted_iota(jnp.int32, (pulses.shape[0], 1), 0)
+    pulse = row // (2 * local_pulses) * local_pulses + row % local_pulses
+    return jnp.where(pulse % 2 == 1, -pulses.astype(F32), pulses.astype(F32)).astype(BF16)
+
+
+def outer_kernel(pieces, side_ref, rows_ref, *refs):
     own_side = side_ref[:1, :]
     me = lax.axis_index("rng")
     own_ref, out_ref, *edge_refs = refs[pieces:-1]
@@ -261,13 +273,15 @@
         for t in range(2):
             place = pl.multiple_of((me ^ (d + t * pieces)) * rows, rows)
             pulses_ref[pl.ds(place, rows), :] = ref[t * rows : (t + 1) * rows, :]
-    images = dot(own_rows[...], pulses_ref[...]), dot(out_rows[...], pulses_ref[...])
+    pulses = pulses_ref[...]
+    own_parts = dot(rows_ref[...], alternating(pulses, rows // 2))
+    out_parts = dot(rows_ref[...], pulses)
     half = own_ref.shape[1]
     rim = LANES // 4
     lane = lax.broadcasted_iota(jnp.int32, (1, LANES), 1)
     edges = [0.0, 0.0]
     for part in range(2):
-        own, out = (image[part * half : (part + 1) * half] for image in images)
+        own, out = (value[part * half : (part + 1) * half] for value in (own_parts, out_parts))
         own_ref[part] = own.astype(BF16)
         out_ref[part] = out.astype(BF16)
         for side in range(2):
@@ -282,42 +296,48 @@
     edge_refs[1][...] = jnp.where(even, edges[0], edges[1]).astype(BF16)
 
 
-def outer_image(own_side, own_rows, out_rows, pieces):
-    angles, side = own_rows.shape
+def outer_image(own_side, rows, pieces):
+    angles, side = rows.shape
     image = jax.ShapeDtypeStruct((2, angles // 2, LANES), BF16)
     edge = jax.ShapeDtypeStruct((angles // 2, LANES), BF16)
     return pl.pallas_call(
         functools.partial(outer_kernel, len(pieces)),
         out_shape=[image, image, edge, edge],
-        in_specs=[VMEM] * (3 + len(pieces)),
+        in_specs=[VMEM] * (2 + len(pieces)),
         out_specs=[VMEM] * 4,
         scratch_shapes=[pltpu.VMEM((side, LANES), BF16)],
         compiler_params=params(10),
         cost_estimate=pl.CostEstimate(
             flops=4 * angles * side * LANES, bytes_accessed=3 * MIB, transcendentals=0
         ),
-    )(own_side, own_rows, out_rows, *pieces)
-
-
-def inner_kernel(rows_ref, pulses_ref, outer_ref, image_ref):
+    )(own_side, rows, *pieces)
+
+
+def partner_rows_kernel(rows_ref, pulses_ref, image_ref):
     image = dot(rows_ref[...], pulses_ref[...])
+    image_ref[...] = image.astype(BF16).reshape(image_ref.shape)
+
+
+def own_rows_kernel(local_pulses, rows_ref, pulses_ref, outer_ref, image_ref):
+    image = dot(rows_ref[...], alternating(pulses_ref[...], local_pulses))
     parts, half, count = outer_ref.shape
     image_ref[:, :, :count] = outer_ref[...]
     image_ref[:, :, count:] = image.astype(BF16).reshape(parts, half, image.shape[1])
 
 
-def whole_image(rows, pulses, outer):
-    parts, half, count = outer.shape
-    return pl.pallas_call(
-        inner_kernel,
-        out_shape=jax.ShapeDtypeStruct((parts, half, count + pulses.shape[1]), BF16),
-        in_specs=[VMEM] * 3,
+def inner_image(kernel, angles, rows, pulses, outer=()):
+    count = pulses.shape[1]
+    whole = count + (outer[0].shape[2] if outer else 0)
+    return pl.pallas_call(
+        kernel,
+        out_shape=jax.ShapeDtypeStruct((2, angles // 2, whole), BF16),
+        in_specs=[VMEM] * (2 + len(outer)),
         out_specs=VMEM,
-        compiler_params=params(8),
+        compiler_params=params(10),
         cost_estimate=pl.CostEstimate(
-            flops=2 * rows.size * pulses.shape[1], bytes_accessed=3 * MIB, transcendentals=0
+            flops=2 * angles * rows.shape[1] * count, bytes_accessed=3 * MIB, transcendentals=0
         ),
-    )(rows, pulses, outer)
+    )(rows, pulses, *outer)
 
 
 def exchanged(value, begin):
@@ -358,9 +378,9 @@
     )(own_side, first, second)
 
 
-def resampled(image_ref, rims_ref, centre_ref, rim_ref, value_ref, child):
-    parts, half, bins = image_ref.shape
-    value_ref[...] = dot(image_ref[...].reshape(parts * half, bins), centre_ref[child])
+def resampled(image, rims_ref, centre_ref, rim_ref, value_ref, child):
+    parts, half, bins = image.shape
+    value_ref[...] = dot(image.reshape(parts * half, bins), centre_ref[child])
     rims = rims_ref[...]
     return [
         (value_ref[part * half : (part + 1) * half, :] + dot(rims, rim_ref[child, part])).astype(BF16)
@@ -371,17 +391,18 @@
 def early_kernel(
     own_ref, rims_ref, centre_ref, rim_ref, matrix_ref, turn_ref, merged_ref, value_ref
 ):
-    rows = resampled(own_ref, rims_ref, centre_ref, rim_ref, value_ref, 0)
+    rows = resampled(own_ref[...], rims_ref, centre_ref, rim_ref, value_ref, 0)
     merged_ref[0], merged_ref[1] = rotated(
         (dot(matrix_ref[0], rows[0]), dot(matrix_ref[0], rows[1])), (turn_ref[0, 0], turn_ref[0, 1])
     )
 
 
 def late_kernel(
-    far_ref, rims_ref, merged_ref, centre_ref, rim_ref, matrix_ref, turn_ref, out_ref, buffer,
-    value_ref, sems,
+    far_outer, far_inner, rims_ref, merged_ref, centre_ref, rim_ref, matrix_ref, turn_ref, out_ref,
+    buffer, value_ref, sems,
 ):
-    rows = resampled(far_ref, rims_ref, centre_ref, rim_ref, value_ref, 1)
+    image = jnp.concatenate([far_outer[...], far_inner[...]], axis=2)
+    rows = resampled(image, rims_ref, centre_ref, rim_ref, value_ref, 1)
     parts = len(rows)
     block = LANES
     copies = []
@@ -422,7 +443,7 @@
     return pl.pallas_call(
         late_kernel,
         out_shape=jax.ShapeDtypeStruct((2, angles, bins), dtype),
-        in_specs=[VMEM] * 7,
+        in_specs=[VMEM] * 8,
         out_specs=ANY,
         scratch_shapes=[
             pltpu.VMEM((2, angles, bins), dtype),
@@ -431,7 +452,7 @@
         ],
         compiler_params=params(16),
         cost_estimate=cost,
-    )(far, far_rims, merged, centre, rim, matrices, turn)
+    )(*far, far_rims, merged, centre, rim, matrices, turn)
 
 
 def after(value, *earlier):
@@ -481,24 +502,28 @@
     pulses = lax.all_to_all(blocks, "rng", split_axis=0, concat_axis=0, tiled=True)
     sends = joined(near_blocks, relay)
     pieces = [across(value, d) if d else value for d, value in enumerate(sends)]
-    own_matrix, out_matrix, own_side = filter_table(fore_flag, angles, local_pulses, sends[0])
-    own_outer, out_outer, *edges = outer_image(own_side, own_matrix, out_matrix, pieces)
+    matrix, own_side = filter_table(fore_flag, angles, local_pulses, sends[0])
+    own_outer, out_outer, *edges = outer_image(own_side, matrix, pieces)
+
+    def halos(side, edges, stride):
+        rims, out_rims = sorted_rims(side, exchanged(edges[0], 0), exchanged(edges[1], 1))
+        return rims, from_partner(out_rims, stride)
 
     pulses = after(pulses, out_outer).reshape(2 * local_pulses * devices, bins - LANES)
-    out = whole_image(out_matrix, pulses, out_outer)
-    own = whole_image(own_matrix, pulses, own_outer)
-    edges = [after(edge, out) for edge in edges]
+    out_inner = inner_image(partner_rows_kernel, angles, matrix, pulses)
+    far = [from_partner(value, 1) for value in (out_outer, out_inner)]
+    rims, far_rims = halos(own_side, [after(edge, out_inner) for edge in edges], 1)
+    pulses = after(pulses, far[0])
+    own_kernel = functools.partial(own_rows_kernel, local_pulses)
+    own = inner_image(own_kernel, angles, matrix, pulses, (own_outer,))
     tables = merge_tables(0, 1, *settings, own)
     for level in range(levels):
         stride = 2**level
         if level > 0:
             tables = merge_tables(level, stride, *settings, image)
             own, out, edges = split_image(level, image, fore_flag, rim)
-            own_side = tables[-1]
-        far = from_partner(out, stride)
-        edges = exchanged(edges[0], 0), exchanged(edges[1], 1)
-        rims, out_rims = sorted_rims(own_side, *edges)
-        far_rims = from_partner(out_rims, stride)
+            far = [from_partner(value, stride) for value in (out[..., :LANES], out[..., LANES:])]
+            rims, far_rims = halos(tables[-1], edges, stride)
         image = merged_image(own, rims, far, far_rims, tables, BF16 if level + 1 < levels else F32)
     return image
 

time: 49.8 us -> 47.7 us (0.958)
  Pallas kernels: 13.6 us -> 11.6 us
  starting transfers between devices: 17.6 us -> 18.9 us
  local copies, waits for them, and re-layouts: 2.98 us -> 2.08 us
  waiting for transfers between devices: 15.3 us -> 14.8 us
    ppermute x2, waiting for transfers between devices: 4.09 us -> 0.4 us  [exchanged(): return lax.ppermute(value, 'rng', pairs + [(j, i) for i, j in pairs])]
    ppermute x2 -> x3, waiting for transfers between devices: 2.97 us -> 5.46 us  [from_partner(): return lax.ppermute(value, 'sub', pairs)]
    ppermute x2 -> x3, starting transfers between devices: 2.16 us -> 3.68 us  [from_partner(): return lax.ppermute(value, 'sub', pairs)]
    pallas_call x1, Pallas kernels: 4.27 us -> 2.79 us  [merge_tables(): pl.pallas_call(functools.partial(merge_table_kernel, level, stride), out_...]
    unnamed x18 -> x14, local copies, waits for them, and re-layouts: 2.98 us -> 2.08 us
    ppermute x8, waiting for transfers between devices: 8.24 us -> 8.89 us  [across(): return lax.ppermute(value, 'rng', [(i, i ^ mask) for i in range(devices)])]
    pallas_call x1, Pallas kernels: 1.9 us -> 1.26 us  [filter_table(): pl.pallas_call(functools.partial(filter_table_kernel, local_pulses), out_...]
  transfers between devices with their start and end apart: 13 -> 14, of which waited for: 5 -> 5; matrix products, arithmetic and copies ran while one was open for 0% -> 2% of each run, Pallas kernels for 20% -> 18%
where the time goes in v2:
time: 47.7 us; the launch traced here: 47.4 us
  starting transfers between devices  18.9 us (40%)
  waiting for transfers between devices  14.8 us (31%)
  Pallas kernels  11.6 us (24%)
  local copies, waits for them, and re-layouts  2.08 us (4%)
    ppermute x8, waiting for transfers between devices, across(): return lax.ppermute(value, 'rng', [(i, i ^ mask) for i in range(devices)])  8.89 us
    ppermute x8, starting transfers between devices, across(): return lax.ppermute(value, 'rng', [(i, i ^ mask) for i in range(devices)])  8.49 us
    all_to_all x1, starting transfers between devices, on_device(): lax.all_to_all(blocks, 'rng', split_axis=0, concat_axis=0, tiled=True)  6.72 us
    ppermute x3, waiting for transfers between devices, from_partner(): return lax.ppermute(value, 'sub', pairs)  5.46 us
    ppermute x3, starting transfers between devices, from_partner(): return lax.ppermute(value, 'sub', pairs)  3.68 us
    pallas_call x1, Pallas kernels, merge_tables(): pl.pallas_call(functools.partial(merge_table_kernel, level, stride), out_...  2.79 us
    pallas_call x1, Pallas kernels, merged_image(): pl.pallas_call(late_kernel, out_shape=jax.ShapeDtypeStruct((2, angles, bi...  2.18 us
    unnamed x14, local copies, waits for them, and re-layouts  2.08 us
  transfers between devices with their start and end apart: 14, of which 5 were waited for; matrix products, arithmetic and copies ran while one was open for 2% of the time, Pallas kernels for 18%

profile of v2, /device:TPU:16, one launch (start us, length us, event | category | flops | bytes accessed | tf_op | source)
XLA Modules:
  0.0 47.4 jit_solution(12063142620269062313)
XLA Ops:
  0.0 0.0 copy-start
  0.0 1.2 %copy-done = bf16[2,32,8192]{2,1,0:T(8,128)(2,1)S(1)} copy-done((bf16[2,32,8192]{2,1,0:T(8,128)(2,1)S(1)}, bf16[2,32,8192]{2,1,0:T(8,128)(2,1)}, u32[]{:S(2)}) %copy-start) | copy-done | bytes 1048600
  1.2 1.0 %shard_map.64 = (bf16[8,64,128]{2,1,0:T(8,128)(2,1)S(1)}, bf16[8,64,128]{2,1,0:T(8,128)(2,1)S(1)}, bf16[16,64,384]{2,1,0:T(8,128)(2,1)}) custom-call(bf16[64,8192]{1,0:T(8,128)(2,1)S(1)} %bitcast.4), custom_call_target="tpu_custom_call" | custom-call | bytes 2097152 | tf_op jit(solution)/shard_map/pallas_call | solution.py:81
  2.3 0.0 collective-permute-start
  2.3 6.7 %all-to-all-start = ((bf16[16,64,384]{2,1,0:T(8,128)(2,1)}), bf16[16,64,384]{2,1,0:T(8,128)(2,1)S(1)}, u32[]{:S(2)}, u32[]{:S(2)}) async-start(bf16[16,64,384]{2,1,0:T(8,128)(2,1)} %get-tuple-element.45), calls=%async_computation | async-start | bytes 1572864 | tf_op jit(solution)/shard_map/all_to_all | solution.py:502
  9.0 0.0 collective-permute-done.relay_ref
  9.0 0.0 copy-start.5
  9.0 0.2 collective-permute-start.1
  9.2 1.5 %collective-permute-start.2 = (bf16[128,128]{1,0:T(8,128)(2,1)S(1)}, bf16[128,128]{1,0:T(8,128)(2,1)S(1)}, u32[]{:S(2)}, u32[]{:S(2)}) collective-permute-start(bf16[128,128]{1,0:T(8,128)(2,1)S(1)} %get-tuple-element.38), channel_id=1, source_target_pairs={{0,2},{1,3},{2,0},{3,1},{4,6},{5,7},{6,4},{7,5},{8,10},{9,11},{10,... | collective-permute-start | bytes 98312 | tf_op jit(solution)/shard_map/ppermute | solution.py:113
  10.7 0.2 collective-permute-start.3
  11.0 3.8 %collective-permute-start.4 = (bf16[128,128]{1,0:T(8,128)(2,1)S(1)}, bf16[128,128]{1,0:T(8,128)(2,1)S(1)}, u32[]{:S(2)}, u32[]{:S(2)}) collective-permute-start(bf16[128,128]{1,0:T(8,128)(2,1)S(1)} %get-tuple-element.40), channel_id=1, source_target_pairs={{0,4},{1,5},{2,6},{3,7},{4,0},{5,1},{6,2},{7,3},{8,12},{9,13},{10,... | collective-permute-start | bytes 98312 | tf_op jit(solution)/shard_map/ppermute | solution.py:113
  14.7 0.0 collective-permute-start.5
  14.7 0.0 collective-permute-done.1.refs_1_
  14.7 2.6 %collective-permute-start.6 = (bf16[128,128]{1,0:T(8,128)(2,1)S(1)}, bf16[128,128]{1,0:T(8,128)(2,1)S(1)}, u32[]{:S(2)}, u32[]{:S(2)}) collective-permute-start(bf16[128,128]{1,0:T(8,128)(2,1)S(1)} %get-tuple-element.42), channel_id=1, source_target_pairs={{0,6},{1,7},{2,4},{3,5},{4,2},{5,3},{6,0},{7,1},{8,14},{9,15},{10,... | collective-permute-start | bytes 98312 | tf_op jit(solution)/shard_map/ppermute | solution.py:113
  17.4 0.0 collective-permute-done.2.refs_2_
  17.4 0.2 collective-permute-start.7
  17.5 0.0 copy-done.5
  17.5 0.1 copy.7.flag_ref
  17.6 1.3 %shard_map.66 = (bf16[512,1024]{1,0:T(8,128)(2,1)S(1)}, f32[8,128]{1,0:T(8,128)S(1)}) custom-call(s32[1,2,1]{2,1,0:T(2,128)S(1)} %copy.7.flag_ref, bf16[128,128]{1,0:T(8,128)(2,1)S(1)} %get-tuple-element.34.after_ref.refs_0_), custom_call_target="tpu_custom_call" | custom-call | flops 9000000 | bytes 4194304 | tf_op jit(solution)/shard_map/pallas_call | solution.py:155
  18.9 0.0 collective-permute-done.3.refs_3_
  18.9 6.7 %collective-permute-done.4.refs_4_ = bf16[128,128]{1,0:T(8,128)(2,1)S(1)} collective-permute-done((bf16[128,128]{1,0:T(8,128)(2,1)S(1)}, bf16[128,128]{1,0:T(8,128)(2,1)S(1)}, u32[]{:S(2)}, u32[]{:S(2)}) %collective-permute-start.4) | collective-permute-done | bytes 32800 | tf_op jit(solution)/shard_map/ppermute | solution.py:113
  25.6 0.0 collective-permute-done.5.refs_5_
  25.6 2.2 %collective-permute-done.6.refs_6_ = bf16[128,128]{1,0:T(8,128)(2,1)S(1)} collective-permute-done((bf16[128,128]{1,0:T(8,128)(2,1)S(1)}, bf16[128,128]{1,0:T(8,128)(2,1)S(1)}, u32[]{:S(2)}, u32[]{:S(2)}) %collective-permute-start.6) | collective-permute-done | bytes 32800 | tf_op jit(solution)/shard_map/ppermute | solution.py:113
  27.8 0.0 collective-permute-done.7.refs_7_
  27.8 1.5 %shard_map.67 = (bf16[2,256,128]{2,1,0:T(8,128)(2,1)S(1)}, bf16[2,256,128]{2,1,0:T(8,128)(2,1)}, bf16[256,128]{1,0:T(8,128)(2,1)}, bf16[256,128]{1,0:T(8,128)(2,1)S(1)}) custom-call(f32[8,128]{1,0:T(8,128)S(1)} %get-tuple-element.35.side_ref, bf16[512,1024]{1,0:T(8,128)(2,1)S(1)} %get-tuple-element.36.rows_ref, ...), custom_call_target="tpu_custom_call" | custom-call | flops 268435456 | bytes 3145728 | tf_op jit(solution)/shard_map/pallas_call | solution.py:303
  29.3 0.0 copy-start.3
  29.3 1.5 %collective-permute-start.8 = (bf16[2,256,128]{2,1,0:T(8,128)(2,1)}, bf16[2,256,128]{2,1,0:T(8,128)(2,1)S(1)}, u32[]{:S(2)}, u32[]{:S(2)}) collective-permute-start(bf16[2,256,128]{2,1,0:T(8,128)(2,1)} %get-tuple-element.44), channel_id=1, source_target_pairs={{0,16},{16,0},{1,17},{17,1},{2,18},{18,2},{3,19},{19,3},{4,20},{20... | collective-permute-start | bytes 393224 | tf_op jit(solution)/shard_map/ppermute | solution.py:464
  30.8 0.0 all-to-all-done
  30.8 0.0 copy-start.2
  30.8 0.0 copy-start.4
  30.8 0.7 %shard_map.68 = bf16[2,256,384]{2,1,0:T(8,128)(2,1)S(1)} custom-call(bf16[512,1024]{1,0:T(8,128)(2,1)S(1)} %get-tuple-element.36.rows_ref, bf16[1024,384]{1,0:T(8,128)(2,1)S(1)} %bitcast.2), custom_call_target="tpu_custom_call" | custom-call | flops 402653184 | bytes 3145728 | tf_op jit(solution)/shard_map/pallas_call | solution.py:331
  31.6 0.6 %collective-permute-start.9 = (bf16[2,256,384]{2,1,0:T(8,128)(2,1)S(1)}, bf16[2,256,384]{2,1,0:T(8,128)(2,1)S(1)}, u32[]{:S(2)}, u32[]{:S(2)}) collective-permute-start(bf16[2,256,384]{2,1,0:T(8,128)(2,1)S(1)} %shard_map.68), channel_id=1, source_target_pairs={{0,16},{16,0},{1,17},{17,1},{2,18},{18,2},{3,19},{19,3},{4,20},{20... | collective-permute-start | bytes 1179656 | tf_op jit(solution)/shard_map/ppermute | solution.py:464
  32.1 0.0 copy-done.3
  32.1 0.0 collective-permute-start.10
  32.1 0.0 collective-permute-start.11
  32.2 0.7 %copy.9.offset_ref = s32[1,2,1]{2,1,0:T(2,128)S(1)} copy(s32[1,2,1]{1,2,0:T(1,128)} %param.8) | data formatting | bytes 16 | tf_op args[2]
  32.9 0.0 copy-start.1
  32.9 2.9 %collective-permute-done.8.far_outer = bf16[2,256,128]{2,1,0:T(8,128)(2,1)S(1)} collective-permute-done((bf16[2,256,128]{2,1,0:T(8,128)(2,1)}, bf16[2,256,128]{2,1,0:T(8,128)(2,1)S(1)}, u32[]{:S(2)}, u32[]{:S(2)}) %collective-permute-start.8) | collective-permute-done | bytes 131104 | tf_op jit(solution)/shard_map/ppermute | solution.py:464
  35.8 0.8 %shard_map.70.after_ref.own_ref = bf16[2,256,512]{2,1,0:T(8,128)(2,1)S(1)} custom-call(bf16[512,1024]{1,0:T(8,128)(2,1)S(1)} %get-tuple-element.36.rows_ref, bf16[1024,384]{1,0:T(8,128)(2,1)S(1)} %bitcast.3, bf16[2,256,128]{2,1,0:T(8,128)(2,1)S(1)} %get-tuple-element.53.outer_ref), custom_call_target="tpu_custom_call" | custom-call | flops 402653184 | bytes 3145728 | tf_op jit(solution)/shard_map/pallas_call | solution.py:331
  36.6 0.0 collective-permute-done.10.first_ref
  36.7 0.4 collective-permute-done.11.second_ref
  37.1 0.2 shard_map.69
  37.2 1.6 %collective-permute-start.12 = (bf16[256,128]{1,0:T(8,128)(2,1)S(1)}, bf16[256,128]{1,0:T(8,128)(2,1)S(1)}, u32[]{:S(2)}, u32[]{:S(2)}) collective-permute-start(bf16[256,128]{1,0:T(8,128)(2,1)S(1)} %get-tuple-element.51), channel_id=1, source_target_pairs={{0,16},{16,0},{1,17},{17,1},{2,18},{18,2},{3,19},{19,3},{4,20},{20... | collective-permute-start | bytes 196616 | tf_op jit(solution)/shard_map/ppermute | solution.py:464
  38.8 0.0 copy-done.2
  38.8 0.0 copy-done.4
  38.8 0.0 copy-done.1
  38.8 2.8 %shard_map.71 = (bf16[2,512,512]{2,1,0:T(8,128)(2,1)S(1)}, bf16[2,2,128,512]{3,2,1,0:T(8,128)(2,1)S(1)}, f32[2,2,512,512]{3,2,1,0:T(8,128)S(1)}, bf16[2,512,256]{2,1,0:T(8,128)(2,1)S(1)}, f32[8,128]{1,0:T(8,128)}) custom-call(s32[1,2,1]{2,1,0:T(2,128)S(1)} %copy.7.flag_ref, s32[1,2,1]{2,1,0:T(2,128)S(1)} %copy.9.offset_ref, f32[1,2]{1,0:T(1,128)S(1)} %copy-done.4, ...), custom_call_target="tpu_custom_call" | custom-call | flops 2300000000 | bytes 7340032 | tf_op jit(solution)/shard_map/pallas_call | solution.py:241
  41.6 1.1 %shard_map.72.merged_ref = f32[2,512,512]{2,1,0:T(8,128)S(1)} custom-call(bf16[2,256,512]{2,1,0:T(8,128)(2,1)S(1)} %shard_map.70.after_ref.own_ref, bf16[256,128]{1,0:T(8,128)(2,1)S(1)} %get-tuple-element.54.rims_ref, bf16[2,512,512]{2,1,0:T(8,128)(2,1)S(1)} %get-tuple-element.55.centre_ref, bf16[2,2,128,512]{3,2,1,0:T(8,128)(2,1)S(1)} %get-tuple-element.56.rim_ref, ...), custom_call_target="tpu_custom_call" | custom-call | flops 536870912 | bytes 8388608 | tf_op jit(solution)/shard_map/pallas_call | solution.py:434
  42.7 2.5 %collective-permute-done.12.rims_ref = bf16[256,128]{1,0:T(8,128)(2,1)S(1)} collective-permute-done((bf16[256,128]{1,0:T(8,128)(2,1)S(1)}, bf16[256,128]{1,0:T(8,128)(2,1)S(1)}, u32[]{:S(2)}, u32[]{:S(2)}) %collective-permute-start.12) | collective-permute-done | bytes 65568 | tf_op jit(solution)/shard_map/ppermute | solution.py:464
  45.2 0.0 collective-permute-done.9.far_inner
  45.2 2.2 %shard_map.73 = f32[2,512,512]{2,1,0:T(8,128)} custom-call(bf16[2,256,128]{2,1,0:T(8,128)(2,1)S(1)} %collective-permute-done.8.far_outer, bf16[2,256,384]{2,1,0:T(8,128)(2,1)S(1)} %collective-permute-done.9.far_inner, bf16[256,128]{1,0:T(8,128)(2,1)S(1)} %collective-permute-done.12.rims_ref, f32[2,512,512]{2,1,0:T(8,128)S(1)} %shard_map.72.merged_ref, ...), custom_call_target="tpu_custom_call" | custom-call | flops 536870912 | bytes 8388608 | tf_op jit(solution)/shard_map/pallas_call | solution.py:443
  (1 shorter events, 0.0 us)
Async XLA Ops:
  0.0 1.2 %copy-start = (bf16[2,32,8192]{2,1,0:T(8,128)(2,1)S(1)}, bf16[2,32,8192]{2,1,0:T(8,128)(2,1)}, u32[]{:S(2)}) copy-start(bf16[2,32,8192]{2,1,0:T(8,128)(2,1)} %param.6) | copy-start | bytes 3145732
  2.3 6.7 %collective-permute-start = (bf16[8,64,128]{2,1,0:T(8,128)(2,1)S(1)}, bf16[8,64,128]{2,1,0:T(8,128)(2,1)S(1)}, u32[]{:S(2)}, u32[]{:S(2)}) collective-permute-start(bf16[8,64,128]{2,1,0:T(8,128)(2,1)S(1)} %get-tuple-element.33), channel_id=1, source_target_pairs={{0,8},{1,9},{2,10},{3,11},{4,12},{5,13},{6,14},{7,15},{8,0},{9,1},... | collective-permute-start | bytes 393224 | tf_op jit(solution)/shard_map/ppermute | solution.py:113
  2.3 28.6 %all-to-all-start = ((bf16[16,64,384]{2,1,0:T(8,128)(2,1)}), bf16[16,64,384]{2,1,0:T(8,128)(2,1)S(1)}, u32[]{:S(2)}, u32[]{:S(2)}) async-start(bf16[16,64,384]{2,1,0:T(8,128)(2,1)} %get-tuple-element.45), calls=%async_computation | async-start | bytes 1572864 | tf_op jit(solution)/shard_map/all_to_all | solution.py:502
  9.0 8.6 %copy-start.5 = (s32[1,2,1]{1,2,0:T(1,128)S(1)}, s32[1,2,1]{1,2,0:T(1,128)}, u32[]{:S(2)}) copy-start(s32[1,2,1]{1,2,0:T(1,128)} %param.7) | copy-start | bytes 28
  9.0 5.7 %collective-permute-start.1 = (bf16[128,128]{1,0:T(8,128)(2,1)S(1)}, bf16[128,128]{1,0:T(8,128)(2,1)S(1)}, u32[]{:S(2)}, u32[]{:S(2)}) collective-permute-start(bf16[128,128]{1,0:T(8,128)(2,1)S(1)} %get-tuple-element.37), channel_id=1, source_target_pairs={{0,1},{1,0},{2,3},{3,2},{4,5},{5,4},{6,7},{7,6},{8,9},{9,8},{10,11... | collective-permute-start | bytes 98312 | tf_op jit(solution)/shard_map/ppermute | solution.py:113
  9.2 8.1 %collective-permute-start.2 = (bf16[128,128]{1,0:T(8,128)(2,1)S(1)}, bf16[128,128]{1,0:T(8,128)(2,1)S(1)}, u32[]{:S(2)}, u32[]{:S(2)}) collective-permute-start(bf16[128,128]{1,0:T(8,128)(2,1)S(1)} %get-tuple-element.38), channel_id=1, source_target_pairs={{0,2},{1,3},{2,0},{3,1},{4,6},{5,7},{6,4},{7,5},{8,10},{9,11},{10,... | collective-permute-start | bytes 98312 | tf_op jit(solution)/shard_map/ppermute | solution.py:113
  10.7 8.2 %collective-permute-start.3 = (bf16[128,128]{1,0:T(8,128)(2,1)S(1)}, bf16[128,128]{1,0:T(8,128)(2,1)S(1)}, u32[]{:S(2)}, u32[]{:S(2)}) collective-permute-start(bf16[128,128]{1,0:T(8,128)(2,1)S(1)} %get-tuple-element.39), channel_id=1, source_target_pairs={{0,3},{1,2},{2,1},{3,0},{4,7},{5,6},{6,5},{7,4},{8,11},{9,10},{10,... | collective-permute-start | bytes 98312 | tf_op jit(solution)/shard_map/ppermute | solution.py:113
  11.0 14.6 %collective-permute-start.4 = (bf16[128,128]{1,0:T(8,128)(2,1)S(1)}, bf16[128,128]{1,0:T(8,128)(2,1)S(1)}, u32[]{:S(2)}, u32[]{:S(2)}) collective-permute-start(bf16[128,128]{1,0:T(8,128)(2,1)S(1)} %get-tuple-element.40), channel_id=1, source_target_pairs={{0,4},{1,5},{2,6},{3,7},{4,0},{5,1},{6,2},{7,3},{8,12},{9,13},{10,... | collective-permute-start | bytes 98312 | tf_op jit(solution)/shard_map/ppermute | solution.py:113
  14.7 10.9 %collective-permute-start.5 = (bf16[128,128]{1,0:T(8,128)(2,1)S(1)}, bf16[128,128]{1,0:T(8,128)(2,1)S(1)}, u32[]{:S(2)}, u32[]{:S(2)}) collective-permute-start(bf16[128,128]{1,0:T(8,128)(2,1)S(1)} %get-tuple-element.41), channel_id=1, source_target_pairs={{0,5},{1,4},{2,7},{3,6},{4,1},{5,0},{6,3},{7,2},{8,13},{9,12},{10,... | collective-permute-start | bytes 98312 | tf_op jit(solution)/shard_map/ppermute | solution.py:113
  14.7 13.0 %collective-permute-start.6 = (bf16[128,128]{1,0:T(8,128)(2,1)S(1)}, bf16[128,128]{1,0:T(8,128)(2,1)S(1)}, u32[]{:S(2)}, u32[]{:S(2)}) collective-permute-start(bf16[128,128]{1,0:T(8,128)(2,1)S(1)} %get-tuple-element.42), channel_id=1, source_target_pairs={{0,6},{1,7},{2,4},{3,5},{4,2},{5,3},{6,0},{7,1},{8,14},{9,15},{10,... | collective-permute-start | bytes 98312 | tf_op jit(solution)/shard_map/ppermute | solution.py:113
  17.4 10.4 %collective-permute-start.7 = (bf16[128,128]{1,0:T(8,128)(2,1)S(1)}, bf16[128,128]{1,0:T(8,128)(2,1)S(1)}, u32[]{:S(2)}, u32[]{:S(2)}) collective-permute-start(bf16[128,128]{1,0:T(8,128)(2,1)S(1)} %get-tuple-element.43), channel_id=1, source_target_pairs={{0,7},{1,6},{2,5},{3,4},{4,3},{5,2},{6,1},{7,0},{8,15},{9,14},{10,... | collective-permute-start | bytes 98312 | tf_op jit(solution)/shard_map/ppermute | solution.py:113
  29.3 2.8 %copy-start.3 = (bf16[256,128]{1,0:T(8,128)(2,1)}, bf16[256,128]{1,0:T(8,128)(2,1)S(1)}, u32[]{:S(2)}) copy-start(bf16[256,128]{1,0:T(8,128)(2,1)S(1)} %get-tuple-element.50) | copy-start | bytes 196612
  29.3 6.5 %collective-permute-start.8 = (bf16[2,256,128]{2,1,0:T(8,128)(2,1)}, bf16[2,256,128]{2,1,0:T(8,128)(2,1)S(1)}, u32[]{:S(2)}, u32[]{:S(2)}) collective-permute-start(bf16[2,256,128]{2,1,0:T(8,128)(2,1)} %get-tuple-element.44), channel_id=1, source_target_pairs={{0,16},{16,0},{1,17},{17,1},{2,18},{18,2},{3,19},{19,3},{4,20},{20... | collective-permute-start | bytes 393224 | tf_op jit(solution)/shard_map/ppermute | solution.py:464
  30.8 8.0 %copy-start.2 = (bf16[1,2,512,256]{3,2,1,0:T(8,128)(2,1)S(1)}, bf16[1,2,512,256]{3,2,1,0:T(8,128)(2,1)}, u32[]{:S(2)}) copy-start(bf16[1,2,512,256]{3,2,1,0:T(8,128)(2,1)} %interp_ref.1) | copy-start | bytes 1572868
  30.8 8.0 %copy-start.4 = (f32[1,2]{1,0:T(1,128)S(1)}, f32[1,2]{1,0:T(1,128)}, u32[]{:S(2)}) copy-start(f32[1,2]{1,0:T(1,128)} %shift_ref.1) | copy-start | bytes 28
  31.6 13.7 %collective-permute-start.9 = (bf16[2,256,384]{2,1,0:T(8,128)(2,1)S(1)}, bf16[2,256,384]{2,1,0:T(8,128)(2,1)S(1)}, u32[]{:S(2)}, u32[]{:S(2)}) collective-permute-start(bf16[2,256,384]{2,1,0:T(8,128)(2,1)S(1)} %shard_map.68), channel_id=1, source_target_pairs={{0,16},{16,0},{1,17},{17,1},{2,18},{18,2},{3,19},{19,3},{4,20},{20... | collective-permute-start | bytes 1179656 | tf_op jit(solution)/shard_map/ppermute | solution.py:464
  32.1 4.5 %collective-permute-start.10 = (bf16[256,128]{1,0:T(8,128)(2,1)}, bf16[256,128]{1,0:T(8,128)(2,1)S(1)}, u32[]{:S(2)}, u32[]{:S(2)}) collective-permute-start(bf16[256,128]{1,0:T(8,128)(2,1)} %get-tuple-element.48), channel_id=1, source_target_pairs={{0,1},{2,3},{4,5},{6,7},{8,9},{10,11},{12,13},{14,15},{1,0},{3,2},... | collective-permute-start | bytes 196616 | tf_op jit(solution)/shard_map/ppermute | solution.py:346
  32.1 4.9 %collective-permute-start.11 = (bf16[256,128]{1,0:T(8,128)(2,1)}, bf16[256,128]{1,0:T(8,128)(2,1)S(1)}, u32[]{:S(2)}, u32[]{:S(2)}) collective-permute-start(bf16[256,128]{1,0:T(8,128)(2,1)} %copy-done.3), channel_id=1, source_target_pairs={{1,2},{3,4},{5,6},{7,8},{9,10},{11,12},{13,14},{15,0},{2,1},{4,3},... | collective-permute-start | bytes 196616 | tf_op jit(solution)/shard_map/ppermute | solution.py:346
  32.9 5.9 %copy-start.1 = (bf16[1,544,512]{2,1,0:T(8,128)(2,1)S(1)}, bf16[1,544,512]{2,1,0:T(8,128)(2,1)}, u32[]{:S(2)}) copy-start(bf16[1,544,512]{2,1,0:T(8,128)(2,1)} %range_ref.1) | copy-start | bytes 1671172
  37.2 8.0 %collective-permute-start.12 = (bf16[256,128]{1,0:T(8,128)(2,1)S(1)}, bf16[256,128]{1,0:T(8,128)(2,1)S(1)}, u32[]{:S(2)}, u32[]{:S(2)}) collective-permute-start(bf16[256,128]{1,0:T(8,128)(2,1)S(1)} %get-tuple-element.51), channel_id=1, source_target_pairs={{0,16},{16,0},{1,17},{17,1},{2,18},{18,2},{3,19},{19,3},{4,20},{20... | collective-permute-start | bytes 196616 | tf_op jit(solution)/shard_map/ppermute | solution.py:464

commit v3 on v2

--- a/solution.py
+++ b/solution.py
@@ -503,17 +503,16 @@
     sends = joined(near_blocks, relay)
     pieces = [across(value, d) if d else value for d, value in enumerate(sends)]
     matrix, own_side = filter_table(fore_flag, angles, local_pulses, sends[0])
-    own_outer, out_outer, *edges = outer_image(own_side, matrix, pieces)
-
     def halos(side, edges, stride):
         rims, out_rims = sorted_rims(side, exchanged(edges[0], 0), exchanged(edges[1], 1))
         return rims, from_partner(out_rims, stride)
 
-    pulses = after(pulses, out_outer).reshape(2 * local_pulses * devices, bins - LANES)
+    pulses = after(pulses, *pieces[1:]).reshape(2 * local_pulses * devices, bins - LANES)
     out_inner = inner_image(partner_rows_kernel, angles, matrix, pulses)
+    pieces[0] = after(pieces[0], out_inner)
+    own_outer, out_outer, *edges = outer_image(own_side, matrix, pieces)
     far = [from_partner(value, 1) for value in (out_outer, out_inner)]
-    rims, far_rims = halos(own_side, [after(edge, out_inner) for edge in edges], 1)
-    pulses = after(pulses, far[0])
+    rims, far_rims = halos(own_side, edges, 1)
     own_kernel = functools.partial(own_rows_kernel, local_pulses)
     own = inner_image(own_kernel, angles, matrix, pulses, (own_outer,))
     tables = merge_tables(0, 1, *settings, own)

time: 47.7 us -> 49.1 us (1.029)
  the two profiles are of different devices: /device:TPU:16 before, /device:TPU:0 now
where the time goes in v3:
time: 49.1 us; the launch traced here: 48.9 us
  starting transfers between devices  21.1 us (43%)
  waiting for transfers between devices  12.9 us (26%)
  Pallas kernels  11.6 us (24%)
  local copies, waits for them, and re-layouts  3.14 us (6%)
    ppermute x8, starting transfers between devices, across(): return lax.ppermute(value, 'rng', [(i, i ^ mask) for i in range(devices)])  9.66 us
    ppermute x8, waiting for transfers between devices, across(): return lax.ppermute(value, 'rng', [(i, i ^ mask) for i in range(devices)])  9.51 us
    ppermute x2, starting transfers between devices, exchanged(): return lax.ppermute(value, 'rng', pairs + [(j, i) for i, j in pairs])  4.68 us
    all_to_all x1, starting transfers between devices, on_device(): lax.all_to_all(blocks, 'rng', split_axis=0, concat_axis=0, tiled=True)  3.88 us
    unnamed x16, local copies, waits for them, and re-layouts  3.14 us
    ppermute x3, starting transfers between devices, from_partner(): return lax.ppermute(value, 'sub', pairs)  2.89 us
    pallas_call x1, Pallas kernels, merge_tables(): pl.pallas_call(functools.partial(merge_table_kernel, level, stride), out_...  2.79 us
    all_to_all x1, waiting for transfers between devices, on_device(): lax.all_to_all(blocks, 'rng', split_axis=0, concat_axis=0, tiled=True)  2.54 us
  transfers between devices with their start and end apart: 14, of which 8 were waited for; matrix products, arithmetic and copies ran while one was open for 0% of the time, Pallas kernels for 16%

profile of v3, /device:TPU:0, one launch (start us, length us, event | category | flops | bytes accessed | tf_op | source)
XLA Modules:
  0.0 48.9 jit_solution(8762008416161990002)
XLA Ops:
  0.0 0.0 copy-start
  0.0 1.2 %copy-done = bf16[2,32,8192]{2,1,0:T(8,128)(2,1)S(1)} copy-done((bf16[2,32,8192]{2,1,0:T(8,128)(2,1)S(1)}, bf16[2,32,8192]{2,1,0:T(8,128)(2,1)}, u32[]{:S(2)}) %copy-start) | copy-done | bytes 1048600
  1.2 1.0 %shard_map.64 = (bf16[8,64,128]{2,1,0:T(8,128)(2,1)S(1)}, bf16[8,64,128]{2,1,0:T(8,128)(2,1)S(1)}, bf16[16,64,384]{2,1,0:T(8,128)(2,1)}) custom-call(bf16[64,8192]{1,0:T(8,128)(2,1)S(1)} %bitcast.4), custom_call_target="tpu_custom_call" | custom-call | bytes 2097152 | tf_op jit(solution)/shard_map/pallas_call | solution.py:81
  2.3 4.0 %collective-permute-start = (bf16[8,64,128]{2,1,0:T(8,128)(2,1)S(1)}, bf16[8,64,128]{2,1,0:T(8,128)(2,1)S(1)}, u32[]{:S(2)}, u32[]{:S(2)}) collective-permute-start(bf16[8,64,128]{2,1,0:T(8,128)(2,1)S(1)} %get-tuple-element.31), channel_id=1, source_target_pairs={{0,8},{1,9},{2,10},{3,11},{4,12},{5,13},{6,14},{7,15},{8,0},{9,1},... | collective-permute-start | bytes 393224 | tf_op jit(solution)/shard_map/ppermute | solution.py:113
  6.3 3.9 %all-to-all-start = ((bf16[16,64,384]{2,1,0:T(8,128)(2,1)}), bf16[16,64,384]{2,1,0:T(8,128)(2,1)S(1)}, u32[]{:S(2)}, u32[]{:S(2)}) async-start(bf16[16,64,384]{2,1,0:T(8,128)(2,1)} %get-tuple-element.35), calls=%async_computation | async-start | bytes 1572864 | tf_op jit(solution)/shard_map/all_to_all | solution.py:502
  10.2 2.4 %collective-permute-done.relay_ref = bf16[8,64,128]{2,1,0:T(8,128)(2,1)S(1)} collective-permute-done((bf16[8,64,128]{2,1,0:T(8,128)(2,1)S(1)}, bf16[8,64,128]{2,1,0:T(8,128)(2,1)S(1)}, u32[]{:S(2)}, u32[]{:S(2)}) %collective-permute-start) | collective-permute-done | bytes 131104 | tf_op jit(solution)/shard_map/ppermute | solution.py:113
  12.6 0.0 copy-start.5
  12.6 0.0 copy-start.6
  12.6 0.1 collective-permute-start.1
  12.7 1.6 %collective-permute-start.2 = (bf16[128,128]{1,0:T(8,128)(2,1)S(1)}, bf16[128,128]{1,0:T(8,128)(2,1)S(1)}, u32[]{:S(2)}, u32[]{:S(2)}) collective-permute-start(bf16[128,128]{1,0:T(8,128)(2,1)S(1)} %get-tuple-element.37), channel_id=1, source_target_pairs={{0,2},{1,3},{2,0},{3,1},{4,6},{5,7},{6,4},{7,5},{8,10},{9,11},{10,... | collective-permute-start | bytes 98312 | tf_op jit(solution)/shard_map/ppermute | solution.py:113
  14.3 0.3 collective-permute-start.3
  14.6 0.8 %collective-permute-start.4 = (bf16[128,128]{1,0:T(8,128)(2,1)S(1)}, bf16[128,128]{1,0:T(8,128)(2,1)S(1)}, u32[]{:S(2)}, u32[]{:S(2)}) collective-permute-start(bf16[128,128]{1,0:T(8,128)(2,1)S(1)} %get-tuple-element.39), channel_id=1, source_target_pairs={{0,4},{1,5},{2,6},{3,7},{4,0},{5,1},{6,2},{7,3},{8,12},{9,13},{10,... | collective-permute-start | bytes 98312 | tf_op jit(solution)/shard_map/ppermute | solution.py:113
  15.4 0.9 %collective-permute-start.5 = (bf16[128,128]{1,0:T(8,128)(2,1)S(1)}, bf16[128,128]{1,0:T(8,128)(2,1)S(1)}, u32[]{:S(2)}, u32[]{:S(2)}) collective-permute-start(bf16[128,128]{1,0:T(8,128)(2,1)S(1)} %get-tuple-element.40), channel_id=1, source_target_pairs={{0,5},{1,4},{2,7},{3,6},{4,1},{5,0},{6,3},{7,2},{8,13},{9,12},{10,... | collective-permute-start | bytes 98312 | tf_op jit(solution)/shard_map/ppermute | solution.py:113
  16.3 0.0 collective-permute-done.1.refs_1_
  16.3 1.7 %collective-permute-start.6 = (bf16[128,128]{1,0:T(8,128)(2,1)S(1)}, bf16[128,128]{1,0:T(8,128)(2,1)S(1)}, u32[]{:S(2)}, u32[]{:S(2)}) collective-permute-start(bf16[128,128]{1,0:T(8,128)(2,1)S(1)} %get-tuple-element.41), channel_id=1, source_target_pairs={{0,6},{1,7},{2,4},{3,5},{4,2},{5,3},{6,0},{7,1},{8,14},{9,15},{10,... | collective-permute-start | bytes 98312 | tf_op jit(solution)/shard_map/ppermute | solution.py:113
  18.0 0.7 %collective-permute-done.2.refs_2_ = bf16[128,128]{1,0:T(8,128)(2,1)S(1)} collective-permute-done((bf16[128,128]{1,0:T(8,128)(2,1)S(1)}, bf16[128,128]{1,0:T(8,128)(2,1)S(1)}, u32[]{:S(2)}, u32[]{:S(2)}) %collective-permute-start.2) | collective-permute-done | bytes 32800 | tf_op jit(solution)/shard_map/ppermute | solution.py:113
  18.7 0.2 collective-permute-start.7
  19.0 0.0 copy-done.5
  19.0 0.1 copy.7.flag_ref
  19.1 1.3 %shard_map.66 = (bf16[512,1024]{1,0:T(8,128)(2,1)S(1)}, f32[8,128]{1,0:T(8,128)S(1)}) custom-call(s32[1,2,1]{2,1,0:T(2,128)S(1)} %copy.7.flag_ref, bf16[128,128]{1,0:T(8,128)(2,1)S(1)} %get-tuple-element.44.after_ref.refs_0_), custom_call_target="tpu_custom_call" | custom-call | flops 9000000 | bytes 4194304 | tf_op jit(solution)/shard_map/pallas_call | solution.py:155
  20.3 0.0 collective-permute-done.3.refs_3_
  20.3 4.7 %collective-permute-done.4.refs_4_ = bf16[128,128]{1,0:T(8,128)(2,1)S(1)} collective-permute-done((bf16[128,128]{1,0:T(8,128)(2,1)S(1)}, bf16[128,128]{1,0:T(8,128)(2,1)S(1)}, u32[]{:S(2)}, u32[]{:S(2)}) %collective-permute-start.4) | collective-permute-done | bytes 32800 | tf_op jit(solution)/shard_map/ppermute | solution.py:113
  25.0 0.5 %collective-permute-done.5.refs_5_ = bf16[128,128]{1,0:T(8,128)(2,1)S(1)} collective-permute-done((bf16[128,128]{1,0:T(8,128)(2,1)S(1)}, bf16[128,128]{1,0:T(8,128)(2,1)S(1)}, u32[]{:S(2)}, u32[]{:S(2)}) %collective-permute-start.5) | collective-permute-done | bytes 32800 | tf_op jit(solution)/shard_map/ppermute | solution.py:113
  25.5 0.7 %collective-permute-done.6.refs_6_ = bf16[128,128]{1,0:T(8,128)(2,1)S(1)} collective-permute-done((bf16[128,128]{1,0:T(8,128)(2,1)S(1)}, bf16[128,128]{1,0:T(8,128)(2,1)S(1)}, u32[]{:S(2)}, u32[]{:S(2)}) %collective-permute-start.6) | collective-permute-done | bytes 32800 | tf_op jit(solution)/shard_map/ppermute | solution.py:113
  26.2 0.5 %collective-permute-done.7.refs_7_ = bf16[128,128]{1,0:T(8,128)(2,1)S(1)} collective-permute-done((bf16[128,128]{1,0:T(8,128)(2,1)S(1)}, bf16[128,128]{1,0:T(8,128)(2,1)S(1)}, u32[]{:S(2)}, u32[]{:S(2)}) %collective-permute-start.7) | collective-permute-done | bytes 32800 | tf_op jit(solution)/shard_map/ppermute | solution.py:113
  26.7 2.5 %all-to-all-done = bf16[16,64,384]{2,1,0:T(8,128)(2,1)S(1)} async-done(((bf16[16,64,384]{2,1,0:T(8,128)(2,1)}), bf16[16,64,384]{2,1,0:T(8,128)(2,1)S(1)}, u32[]{:S(2)}, u32[]{:S(2)}) %all-to-all-start) | async-done | bytes 786464 | tf_op jit(solution)/shard_map/all_to_all | solution.py:502
  29.3 0.7 %shard_map.67 = bf16[2,256,384]{2,1,0:T(8,128)(2,1)S(1)} custom-call(bf16[512,1024]{1,0:T(8,128)(2,1)S(1)} %get-tuple-element.34.rows_ref, bf16[1024,384]{1,0:T(8,128)(2,1)S(1)} %bitcast.2), custom_call_target="tpu_custom_call" | custom-call | flops 402653184 | bytes 3145728 | tf_op jit(solution)/shard_map/pallas_call | solution.py:331
  30.0 0.0 copy-start.2
  30.0 0.0 copy-start.4
  30.0 1.6 %collective-permute-start.9 = (bf16[2,256,384]{2,1,0:T(8,128)(2,1)S(1)}, bf16[2,256,384]{2,1,0:T(8,128)(2,1)S(1)}, u32[]{:S(2)}, u32[]{:S(2)}) collective-permute-start(bf16[2,256,384]{2,1,0:T(8,128)(2,1)S(1)} %shard_map.67), channel_id=1, source_target_pairs={{0,16},{16,0},{1,17},{17,1},{2,18},{18,2},{3,19},{19,3},{4,20},{20... | collective-permute-start | bytes 1179656 | tf_op jit(solution)/shard_map/ppermute | solution.py:464
  31.6 1.6 %shard_map.68 = (bf16[2,256,128]{2,1,0:T(8,128)(2,1)S(1)}, bf16[2,256,128]{2,1,0:T(8,128)(2,1)S(1)}, bf16[256,128]{1,0:T(8,128)(2,1)}, bf16[256,128]{1,0:T(8,128)(2,1)}) custom-call(f32[8,128]{1,0:T(8,128)S(1)} %get-tuple-element.33.side_ref, bf16[512,1024]{1,0:T(8,128)(2,1)S(1)} %get-tuple-element.34.rows_ref, ...), custom_call_target="tpu_custom_call" | custom-call | flops 268435456 | bytes 3145728 | tf_op jit(solution)/shard_map/pallas_call | solution.py:303
  33.2 0.0 copy-start.3
  33.2 0.7 %copy-done.3 = bf16[2,256,128]{2,1,0:T(8,128)(2,1)} copy-done((bf16[2,256,128]{2,1,0:T(8,128)(2,1)}, bf16[2,256,128]{2,1,0:T(8,128)(2,1)S(1)}, u32[]{:S(2)}) %copy-start.3) | copy-done | bytes 131096
  33.8 0.0 collective-permute-start.10
  33.8 4.7 %collective-permute-start.11 = (bf16[256,128]{1,0:T(8,128)(2,1)}, bf16[256,128]{1,0:T(8,128)(2,1)S(1)}, u32[]{:S(2)}, u32[]{:S(2)}) collective-permute-start(bf16[256,128]{1,0:T(8,128)(2,1)} %get-tuple-element.47), channel_id=1, source_target_pairs={{1,2},{3,4},{5,6},{7,8},{9,10},{11,12},{13,14},{15,0},{2,1},{4,3},... | collective-permute-start | bytes 196616 | tf_op jit(solution)/shard_map/ppermute | solution.py:346
  38.5 0.0 copy-done.6
  38.5 0.1 copy.9.offset_ref
  38.6 0.5 %collective-permute-start.8 = (bf16[2,256,128]{2,1,0:T(8,128)(2,1)}, bf16[2,256,128]{2,1,0:T(8,128)(2,1)S(1)}, u32[]{:S(2)}, u32[]{:S(2)}) collective-permute-start(bf16[2,256,128]{2,1,0:T(8,128)(2,1)} %copy-done.3), channel_id=1, source_target_pairs={{0,16},{16,0},{1,17},{17,1},{2,18},{18,2},{3,19},{19,3},{4,20},{20... | collective-permute-start | bytes 393224 | tf_op jit(solution)/shard_map/ppermute | solution.py:464
  39.1 0.8 %shard_map.70.after_ref.own_ref = bf16[2,256,512]{2,1,0:T(8,128)(2,1)S(1)} custom-call(bf16[512,1024]{1,0:T(8,128)(2,1)S(1)} %get-tuple-element.34.rows_ref, bf16[1024,384]{1,0:T(8,128)(2,1)S(1)} %bitcast.3, bf16[2,256,128]{2,1,0:T(8,128)(2,1)S(1)} %get-tuple-element.49.outer_ref), custom_call_target="tpu_custom_call" | custom-call | flops 402653184 | bytes 3145728 | tf_op jit(solution)/shard_map/pallas_call | solution.py:331
  39.9 0.0 collective-permute-done.10.first_ref
  39.9 0.8 %collective-permute-done.11.second_ref = bf16[256,128]{1,0:T(8,128)(2,1)S(1)} collective-permute-done((bf16[256,128]{1,0:T(8,128)(2,1)}, bf16[256,128]{1,0:T(8,128)(2,1)S(1)}, u32[]{:S(2)}, u32[]{:S(2)}) %collective-permute-start.11) | collective-permute-done | bytes 65568 | tf_op jit(solution)/shard_map/ppermute | solution.py:346
  40.7 0.2 shard_map.69
  40.9 0.8 %collective-permute-start.12 = (bf16[256,128]{1,0:T(8,128)(2,1)S(1)}, bf16[256,128]{1,0:T(8,128)(2,1)S(1)}, u32[]{:S(2)}, u32[]{:S(2)}) collective-permute-start(bf16[256,128]{1,0:T(8,128)(2,1)S(1)} %get-tuple-element.48), channel_id=1, source_target_pairs={{0,16},{16,0},{1,17},{17,1},{2,18},{18,2},{3,19},{19,3},{4,20},{20... | collective-permute-start | bytes 196616 | tf_op jit(solution)/shard_map/ppermute | solution.py:464
  41.7 0.0 copy-done.2
  41.7 0.0 copy-done.4
  41.7 0.0 copy-start.1
  41.7 1.1 %copy-done.1 = bf16[1,544,512]{2,1,0:T(8,128)(2,1)S(1)} copy-done((bf16[1,544,512]{2,1,0:T(8,128)(2,1)S(1)}, bf16[1,544,512]{2,1,0:T(8,128)(2,1)}, u32[]{:S(2)}) %copy-start.1) | copy-done | bytes 557080
  42.7 2.8 %shard_map.71 = (bf16[2,512,512]{2,1,0:T(8,128)(2,1)S(1)}, bf16[2,2,128,512]{3,2,1,0:T(8,128)(2,1)S(1)}, f32[2,2,512,512]{3,2,1,0:T(8,128)S(1)}, bf16[2,512,256]{2,1,0:T(8,128)(2,1)S(1)}, f32[8,128]{1,0:T(8,128)}) custom-call(s32[1,2,1]{2,1,0:T(2,128)S(1)} %copy.7.flag_ref, s32[1,2,1]{2,1,0:T(2,128)S(1)} %copy.9.offset_ref, f32[1,2]{1,0:T(1,128)S(1)} %copy-done.4, ...), custom_call_target="tpu_custom_call" | custom-call | flops 2300000000 | bytes 7340032 | tf_op jit(solution)/shard_map/pallas_call | solution.py:241
  45.6 1.1 %shard_map.72.merged_ref = f32[2,512,512]{2,1,0:T(8,128)S(1)} custom-call(bf16[2,256,512]{2,1,0:T(8,128)(2,1)S(1)} %shard_map.70.after_ref.own_ref, bf16[256,128]{1,0:T(8,128)(2,1)S(1)} %get-tuple-element.50.rims_ref, bf16[2,512,512]{2,1,0:T(8,128)(2,1)S(1)} %get-tuple-element.51.centre_ref, bf16[2,2,128,512]{3,2,1,0:T(8,128)(2,1)S(1)} %get-tuple-element.52.rim_ref, ...), custom_call_target="tpu_custom_call" | custom-call | flops 536870912 | bytes 8388608 | tf_op jit(solution)/shard_map/pallas_call | solution.py:434
  46.6 0.0 collective-permute-done.8.far_outer
  46.7 0.0 collective-permute-done.12.rims_ref
  46.7 0.0 collective-permute-done.9.far_inner
  46.7 2.2 %shard_map.73 = f32[2,512,512]{2,1,0:T(8,128)} custom-call(bf16[2,256,128]{2,1,0:T(8,128)(2,1)S(1)} %collective-permute-done.8.far_outer, bf16[2,256,384]{2,1,0:T(8,128)(2,1)S(1)} %collective-permute-done.9.far_inner, bf16[256,128]{1,0:T(8,128)(2,1)S(1)} %collective-permute-done.12.rims_ref, f32[2,512,512]{2,1,0:T(8,128)S(1)} %shard_map.72.merged_ref, ...), custom_call_target="tpu_custom_call" | custom-call | flops 536870912 | bytes 8388608 | tf_op jit(solution)/shard_map/pallas_call | solution.py:443
  (1 shorter events, 0.0 us)
Async XLA Ops:
  0.0 1.2 %copy-start = (bf16[2,32,8192]{2,1,0:T(8,128)(2,1)S(1)}, bf16[2,32,8192]{2,1,0:T(8,128)(2,1)}, u32[]{:S(2)}) copy-start(bf16[2,32,8192]{2,1,0:T(8,128)(2,1)} %param.6) | copy-start | bytes 3145732
  2.3 10.3 %collective-permute-start = (bf16[8,64,128]{2,1,0:T(8,128)(2,1)S(1)}, bf16[8,64,128]{2,1,0:T(8,128)(2,1)S(1)}, u32[]{:S(2)}, u32[]{:S(2)}) collective-permute-start(bf16[8,64,128]{2,1,0:T(8,128)(2,1)S(1)} %get-tuple-element.31), channel_id=1, source_target_pairs={{0,8},{1,9},{2,10},{3,11},{4,12},{5,13},{6,14},{7,15},{8,0},{9,1},... | collective-permute-start | bytes 393224 | tf_op jit(solution)/shard_map/ppermute | solution.py:113
  6.3 23.0 %all-to-all-start = ((bf16[16,64,384]{2,1,0:T(8,128)(2,1)}), bf16[16,64,384]{2,1,0:T(8,128)(2,1)S(1)}, u32[]{:S(2)}, u32[]{:S(2)}) async-start(bf16[16,64,384]{2,1,0:T(8,128)(2,1)} %get-tuple-element.35), calls=%async_computation | async-start | bytes 1572864 | tf_op jit(solution)/shard_map/all_to_all | solution.py:502
  12.6 6.4 %copy-start.5 = (s32[1,2,1]{1,2,0:T(1,128)S(1)}, s32[1,2,1]{1,2,0:T(1,128)}, u32[]{:S(2)}) copy-start(s32[1,2,1]{1,2,0:T(1,128)} %param.7) | copy-start | bytes 28
  12.6 25.9 %copy-start.6 = (s32[1,2,1]{1,2,0:T(1,128)S(1)}, s32[1,2,1]{1,2,0:T(1,128)}, u32[]{:S(2)}) copy-start(s32[1,2,1]{1,2,0:T(1,128)} %param.8) | copy-start | bytes 28
  12.6 3.6 %collective-permute-start.1 = (bf16[128,128]{1,0:T(8,128)(2,1)S(1)}, bf16[128,128]{1,0:T(8,128)(2,1)S(1)}, u32[]{:S(2)}, u32[]{:S(2)}) collective-permute-start(bf16[128,128]{1,0:T(8,128)(2,1)S(1)} %get-tuple-element.36), channel_id=1, source_target_pairs={{0,1},{1,0},{2,3},{3,2},{4,5},{5,4},{6,7},{7,6},{8,9},{9,8},{10,11... | collective-permute-start | bytes 98312 | tf_op jit(solution)/shard_map/ppermute | solution.py:113
  12.7 6.0 %collective-permute-start.2 = (bf16[128,128]{1,0:T(8,128)(2,1)S(1)}, bf16[128,128]{1,0:T(8,128)(2,1)S(1)}, u32[]{:S(2)}, u32[]{:S(2)}) collective-permute-start(bf16[128,128]{1,0:T(8,128)(2,1)S(1)} %get-tuple-element.37), channel_id=1, source_target_pairs={{0,2},{1,3},{2,0},{3,1},{4,6},{5,7},{6,4},{7,5},{8,10},{9,11},{10,... | collective-permute-start | bytes 98312 | tf_op jit(solution)/shard_map/ppermute | solution.py:113
  14.3 6.0 %collective-permute-start.3 = (bf16[128,128]{1,0:T(8,128)(2,1)S(1)}, bf16[128,128]{1,0:T(8,128)(2,1)S(1)}, u32[]{:S(2)}, u32[]{:S(2)}) collective-permute-start(bf16[128,128]{1,0:T(8,128)(2,1)S(1)} %get-tuple-element.38), channel_id=1, source_target_pairs={{0,3},{1,2},{2,1},{3,0},{4,7},{5,6},{6,5},{7,4},{8,11},{9,10},{10,... | collective-permute-start | bytes 98312 | tf_op jit(solution)/shard_map/ppermute | solution.py:113
  14.6 10.4 %collective-permute-start.4 = (bf16[128,128]{1,0:T(8,128)(2,1)S(1)}, bf16[128,128]{1,0:T(8,128)(2,1)S(1)}, u32[]{:S(2)}, u32[]{:S(2)}) collective-permute-start(bf16[128,128]{1,0:T(8,128)(2,1)S(1)} %get-tuple-element.39), channel_id=1, source_target_pairs={{0,4},{1,5},{2,6},{3,7},{4,0},{5,1},{6,2},{7,3},{8,12},{9,13},{10,... | collective-permute-start | bytes 98312 | tf_op jit(solution)/shard_map/ppermute | solution.py:113
  15.4 10.1 %collective-permute-start.5 = (bf16[128,128]{1,0:T(8,128)(2,1)S(1)}, bf16[128,128]{1,0:T(8,128)(2,1)S(1)}, u32[]{:S(2)}, u32[]{:S(2)}) collective-permute-start(bf16[128,128]{1,0:T(8,128)(2,1)S(1)} %get-tuple-element.40), channel_id=1, source_target_pairs={{0,5},{1,4},{2,7},{3,6},{4,1},{5,0},{6,3},{7,2},{8,13},{9,12},{10,... | collective-permute-start | bytes 98312 | tf_op jit(solution)/shard_map/ppermute | solution.py:113
  16.3 9.9 %collective-permute-start.6 = (bf16[128,128]{1,0:T(8,128)(2,1)S(1)}, bf16[128,128]{1,0:T(8,128)(2,1)S(1)}, u32[]{:S(2)}, u32[]{:S(2)}) collective-permute-start(bf16[128,128]{1,0:T(8,128)(2,1)S(1)} %get-tuple-element.41), channel_id=1, source_target_pairs={{0,6},{1,7},{2,4},{3,5},{4,2},{5,3},{6,0},{7,1},{8,14},{9,15},{10,... | collective-permute-start | bytes 98312 | tf_op jit(solution)/shard_map/ppermute | solution.py:113
  18.7 8.0 %collective-permute-start.7 = (bf16[128,128]{1,0:T(8,128)(2,1)S(1)}, bf16[128,128]{1,0:T(8,128)(2,1)S(1)}, u32[]{:S(2)}, u32[]{:S(2)}) collective-permute-start(bf16[128,128]{1,0:T(8,128)(2,1)S(1)} %get-tuple-element.42), channel_id=1, source_target_pairs={{0,7},{1,6},{2,5},{3,4},{4,3},{5,2},{6,1},{7,0},{8,15},{9,14},{10,... | collective-permute-start | bytes 98312 | tf_op jit(solution)/shard_map/ppermute | solution.py:113
  30.0 11.7 %copy-start.2 = (bf16[1,2,512,256]{3,2,1,0:T(8,128)(2,1)S(1)}, bf16[1,2,512,256]{3,2,1,0:T(8,128)(2,1)}, u32[]{:S(2)}) copy-start(bf16[1,2,512,256]{3,2,1,0:T(8,128)(2,1)} %interp_ref.1) | copy-start | bytes 1572868
  30.0 11.7 %copy-start.4 = (f32[1,2]{1,0:T(1,128)S(1)}, f32[1,2]{1,0:T(1,128)}, u32[]{:S(2)}) copy-start(f32[1,2]{1,0:T(1,128)} %shift_ref.1) | copy-start | bytes 28
  30.0 16.7 %collective-permute-start.9 = (bf16[2,256,384]{2,1,0:T(8,128)(2,1)S(1)}, bf16[2,256,384]{2,1,0:T(8,128)(2,1)S(1)}, u32[]{:S(2)}, u32[]{:S(2)}) collective-permute-start(bf16[2,256,384]{2,1,0:T(8,128)(2,1)S(1)} %shard_map.67), channel_id=1, source_target_pairs={{0,16},{16,0},{1,17},{17,1},{2,18},{18,2},{3,19},{19,3},{4,20},{20... | collective-permute-start | bytes 1179656 | tf_op jit(solution)/shard_map/ppermute | solution.py:464
  33.2 0.7 %copy-start.3 = (bf16[2,256,128]{2,1,0:T(8,128)(2,1)}, bf16[2,256,128]{2,1,0:T(8,128)(2,1)S(1)}, u32[]{:S(2)}) copy-start(bf16[2,256,128]{2,1,0:T(8,128)(2,1)S(1)} %get-tuple-element.45) | copy-start | bytes 393220
  33.8 6.1 %collective-permute-start.10 = (bf16[256,128]{1,0:T(8,128)(2,1)}, bf16[256,128]{1,0:T(8,128)(2,1)S(1)}, u32[]{:S(2)}, u32[]{:S(2)}) collective-permute-start(bf16[256,128]{1,0:T(8,128)(2,1)} %get-tuple-element.46), channel_id=1, source_target_pairs={{0,1},{2,3},{4,5},{6,7},{8,9},{10,11},{12,13},{14,15},{1,0},{3,2},... | collective-permute-start | bytes 196616 | tf_op jit(solution)/shard_map/ppermute | solution.py:346
  33.8 6.9 %collective-permute-start.11 = (bf16[256,128]{1,0:T(8,128)(2,1)}, bf16[256,128]{1,0:T(8,128)(2,1)S(1)}, u32[]{:S(2)}, u32[]{:S(2)}) collective-permute-start(bf16[256,128]{1,0:T(8,128)(2,1)} %get-tuple-element.47), channel_id=1, source_target_pairs={{1,2},{3,4},{5,6},{7,8},{9,10},{11,12},{13,14},{15,0},{2,1},{4,3},... | collective-permute-start | bytes 196616 | tf_op jit(solution)/shard_map/ppermute | solution.py:346
  38.6 8.1 %collective-permute-start.8 = (bf16[2,256,128]{2,1,0:T(8,128)(2,1)}, bf16[2,256,128]{2,1,0:T(8,128)(2,1)S(1)}, u32[]{:S(2)}, u32[]{:S(2)}) collective-permute-start(bf16[2,256,128]{2,1,0:T(8,128)(2,1)} %copy-done.3), channel_id=1, source_target_pairs={{0,16},{16,0},{1,17},{17,1},{2,18},{18,2},{3,19},{19,3},{4,20},{20... | collective-permute-start | bytes 393224 | tf_op jit(solution)/shard_map/ppermute | solution.py:464
  40.9 5.8 %collective-permute-start.12 = (bf16[256,128]{1,0:T(8,128)(2,1)S(1)}, bf16[256,128]{1,0:T(8,128)(2,1)S(1)}, u32[]{:S(2)}, u32[]{:S(2)}) collective-permute-start(bf16[256,128]{1,0:T(8,128)(2,1)S(1)} %get-tuple-element.48), channel_id=1, source_target_pairs={{0,16},{16,0},{1,17},{17,1},{2,18},{18,2},{3,19},{19,3},{4,20},{20... | collective-permute-start | bytes 196616 | tf_op jit(solution)/shard_map/ppermute | solution.py:464
  41.7 1.1 %copy-start.1 = (bf16[1,544,512]{2,1,0:T(8,128)(2,1)S(1)}, bf16[1,544,512]{2,1,0:T(8,128)(2,1)}, u32[]{:S(2)}) copy-start(bf16[1,544,512]{2,1,0:T(8,128)(2,1)} %range_ref.1) | copy-start | bytes 1671172

commit v4 on v3

--- a/solution.py
+++ b/solution.py
@@ -512,10 +512,11 @@
     pieces[0] = after(pieces[0], out_inner)
     own_outer, out_outer, *edges = outer_image(own_side, matrix, pieces)
     far = [from_partner(value, 1) for value in (out_outer, out_inner)]
-    rims, far_rims = halos(own_side, edges, 1)
     own_kernel = functools.partial(own_rows_kernel, local_pulses)
     own = inner_image(own_kernel, angles, matrix, pulses, (own_outer,))
     tables = merge_tables(0, 1, *settings, own)
+    edges[1] = after(edges[1], tables[0])
+    rims, far_rims = halos(own_side, edges, 1)
     for level in range(levels):
         stride = 2**level
         if level > 0:

time: 49.1 us -> 49.9 us (1.016)
  waiting for transfers between devices: 12.9 us -> 16.1 us
  local copies, waits for them, and re-layouts: 3.14 us -> 1.43 us
  Pallas kernels: 11.6 us -> 10.9 us
    ppermute x3, waiting for transfers between devices: 0.01 us -> 2.68 us  [from_partner(): return lax.ppermute(value, 'sub', pairs)]
    unnamed x16 -> x14, local copies, waits for them, and re-layouts: 3.14 us -> 1.43 us
    pallas_call x1, Pallas kernels: 1.57 us -> 0.92 us  [outer_image(): pl.pallas_call(functools.partial(outer_kernel, len(pieces)), out_shape=[i...]
    ppermute x2, waiting for transfers between devices: 0.81 us -> 1.45 us  [exchanged(): return lax.ppermute(value, 'rng', pairs + [(j, i) for i, j in pairs])]
  transfers between devices with their start and end apart: 14 -> 14, of which waited for: 8 -> 10; matrix products, arithmetic and copies ran while one was open for 0% -> 0% of each run, Pallas kernels for 16% -> 14%
where the time goes in v4:
time: 49.9 us; the launch traced here: 49.6 us
  starting transfers between devices  21 us (42%)
  waiting for transfers between devices  16.1 us (32%)
  Pallas kernels  10.9 us (22%)
  local copies, waits for them, and re-layouts  1.43 us (3%)
    ppermute x8, starting transfers between devices, across(): return lax.ppermute(value, 'rng', [(i, i ^ mask) for i in range(devices)])  9.65 us
    ppermute x8, waiting for transfers between devices, across(): return lax.ppermute(value, 'rng', [(i, i ^ mask) for i in range(devices)])  9.43 us
    ppermute x2, starting transfers between devices, exchanged(): return lax.ppermute(value, 'rng', pairs + [(j, i) for i, j in pairs])  4.8 us
    all_to_all x1, starting transfers between devices, on_device(): lax.all_to_all(blocks, 'rng', split_axis=0, concat_axis=0, tiled=True)  3.88 us
    pallas_call x1, Pallas kernels, merge_tables(): pl.pallas_call(functools.partial(merge_table_kernel, level, stride), out_...  2.8 us
    ppermute x3, waiting for transfers between devices, from_partner(): return lax.ppermute(value, 'sub', pairs)  2.68 us
    ppermute x3, starting transfers between devices, from_partner(): return lax.ppermute(value, 'sub', pairs)  2.65 us
    all_to_all x1, waiting for transfers between devices, on_device(): lax.all_to_all(blocks, 'rng', split_axis=0, concat_axis=0, tiled=True)  2.54 us
  transfers between devices with their start and end apart: 14, of which 10 were waited for; matrix products, arithmetic and copies ran while one was open for 0% of the time, Pallas kernels for 14%

profile of v4, /device:TPU:0, one launch (start us, length us, event | category | flops | bytes accessed | tf_op | source)
XLA Modules:
  0.0 49.6 jit_solution(7023898644585059520)
XLA Ops:
  0.0 0.0 copy-start
  0.0 1.2 %copy-done = bf16[2,32,8192]{2,1,0:T(8,128)(2,1)S(1)} copy-done((bf16[2,32,8192]{2,1,0:T(8,128)(2,1)S(1)}, bf16[2,32,8192]{2,1,0:T(8,128)(2,1)}, u32[]{:S(2)}) %copy-start) | copy-done | bytes 1048600
  1.2 1.0 %shard_map.64 = (bf16[8,64,128]{2,1,0:T(8,128)(2,1)S(1)}, bf16[8,64,128]{2,1,0:T(8,128)(2,1)S(1)}, bf16[16,64,384]{2,1,0:T(8,128)(2,1)}) custom-call(bf16[64,8192]{1,0:T(8,128)(2,1)S(1)} %bitcast.4), custom_call_target="tpu_custom_call" | custom-call | bytes 2097152 | tf_op jit(solution)/shard_map/pallas_call | solution.py:81
  2.3 4.0 %collective-permute-start = (bf16[8,64,128]{2,1,0:T(8,128)(2,1)S(1)}, bf16[8,64,128]{2,1,0:T(8,128)(2,1)S(1)}, u32[]{:S(2)}, u32[]{:S(2)}) collective-permute-start(bf16[8,64,128]{2,1,0:T(8,128)(2,1)S(1)} %get-tuple-element.32), channel_id=1, source_target_pairs={{0,8},{1,9},{2,10},{3,11},{4,12},{5,13},{6,14},{7,15},{8,0},{9,1},... | collective-permute-start | bytes 393224 | tf_op jit(solution)/shard_map/ppermute | solution.py:113
  6.3 3.9 %all-to-all-start = ((bf16[16,64,384]{2,1,0:T(8,128)(2,1)}), bf16[16,64,384]{2,1,0:T(8,128)(2,1)S(1)}, u32[]{:S(2)}, u32[]{:S(2)}) async-start(bf16[16,64,384]{2,1,0:T(8,128)(2,1)} %get-tuple-element.36), calls=%async_computation | async-start | bytes 1572864 | tf_op jit(solution)/shard_map/all_to_all | solution.py:502
  10.2 2.4 %collective-permute-done.relay_ref = bf16[8,64,128]{2,1,0:T(8,128)(2,1)S(1)} collective-permute-done((bf16[8,64,128]{2,1,0:T(8,128)(2,1)S(1)}, bf16[8,64,128]{2,1,0:T(8,128)(2,1)S(1)}, u32[]{:S(2)}, u32[]{:S(2)}) %collective-permute-start) | collective-permute-done | bytes 131104 | tf_op jit(solution)/shard_map/ppermute | solution.py:113
  12.6 0.0 copy-start.4
  12.6 0.0 copy-start.5
  12.6 0.1 collective-permute-start.1
  12.7 1.6 %collective-permute-start.2 = (bf16[128,128]{1,0:T(8,128)(2,1)S(1)}, bf16[128,128]{1,0:T(8,128)(2,1)S(1)}, u32[]{:S(2)}, u32[]{:S(2)}) collective-permute-start(bf16[128,128]{1,0:T(8,128)(2,1)S(1)} %get-tuple-element.38), channel_id=1, source_target_pairs={{0,2},{1,3},{2,0},{3,1},{4,6},{5,7},{6,4},{7,5},{8,10},{9,11},{10,... | collective-permute-start | bytes 98312 | tf_op jit(solution)/shard_map/ppermute | solution.py:113
  14.3 0.3 collective-permute-start.3
  14.6 0.8 %collective-permute-start.4 = (bf16[128,128]{1,0:T(8,128)(2,1)S(1)}, bf16[128,128]{1,0:T(8,128)(2,1)S(1)}, u32[]{:S(2)}, u32[]{:S(2)}) collective-permute-start(bf16[128,128]{1,0:T(8,128)(2,1)S(1)} %get-tuple-element.40), channel_id=1, source_target_pairs={{0,4},{1,5},{2,6},{3,7},{4,0},{5,1},{6,2},{7,3},{8,12},{9,13},{10,... | collective-permute-start | bytes 98312 | tf_op jit(solution)/shard_map/ppermute | solution.py:113
  15.4 0.9 %collective-permute-start.5 = (bf16[128,128]{1,0:T(8,128)(2,1)S(1)}, bf16[128,128]{1,0:T(8,128)(2,1)S(1)}, u32[]{:S(2)}, u32[]{:S(2)}) collective-permute-start(bf16[128,128]{1,0:T(8,128)(2,1)S(1)} %get-tuple-element.41), channel_id=1, source_target_pairs={{0,5},{1,4},{2,7},{3,6},{4,1},{5,0},{6,3},{7,2},{8,13},{9,12},{10,... | collective-permute-start | bytes 98312 | tf_op jit(solution)/shard_map/ppermute | solution.py:113
  16.3 0.0 collective-permute-done.1.refs_1_
  16.3 1.7 %collective-permute-start.6 = (bf16[128,128]{1,0:T(8,128)(2,1)S(1)}, bf16[128,128]{1,0:T(8,128)(2,1)S(1)}, u32[]{:S(2)}, u32[]{:S(2)}) collective-permute-start(bf16[128,128]{1,0:T(8,128)(2,1)S(1)} %get-tuple-element.42), channel_id=1, source_target_pairs={{0,6},{1,7},{2,4},{3,5},{4,2},{5,3},{6,0},{7,1},{8,14},{9,15},{10,... | collective-permute-start | bytes 98312 | tf_op jit(solution)/shard_map/ppermute | solution.py:113
  18.0 0.7 %collective-permute-done.2.refs_2_ = bf16[128,128]{1,0:T(8,128)(2,1)S(1)} collective-permute-done((bf16[128,128]{1,0:T(8,128)(2,1)S(1)}, bf16[128,128]{1,0:T(8,128)(2,1)S(1)}, u32[]{:S(2)}, u32[]{:S(2)}) %collective-permute-start.2) | collective-permute-done | bytes 32800 | tf_op jit(solution)/shard_map/ppermute | solution.py:113
  18.7 0.2 collective-permute-start.7
  19.0 0.0 copy-done.4
  19.0 0.1 copy.7.flag_ref
  19.1 0.0 copy-done.5
  19.1 0.1 copy.9.offset_ref
  19.1 1.3 %shard_map.66 = (bf16[512,1024]{1,0:T(8,128)(2,1)S(1)}, f32[8,128]{1,0:T(8,128)S(1)}) custom-call(s32[1,2,1]{2,1,0:T(2,128)S(1)} %copy.7.flag_ref, bf16[128,128]{1,0:T(8,128)(2,1)S(1)} %get-tuple-element.45.after_ref.refs_0_), custom_call_target="tpu_custom_call" | custom-call | flops 9000000 | bytes 4194304 | tf_op jit(solution)/shard_map/pallas_call | solution.py:155
  20.4 0.0 collective-permute-done.3.refs_3_
  20.4 4.6 %collective-permute-done.4.refs_4_ = bf16[128,128]{1,0:T(8,128)(2,1)S(1)} collective-permute-done((bf16[128,128]{1,0:T(8,128)(2,1)S(1)}, bf16[128,128]{1,0:T(8,128)(2,1)S(1)}, u32[]{:S(2)}, u32[]{:S(2)}) %collective-permute-start.4) | collective-permute-done | bytes 32800 | tf_op jit(solution)/shard_map/ppermute | solution.py:113
  25.0 0.5 collective-permute-done.5.refs_5_
  25.5 0.7 %collective-permute-done.6.refs_6_ = bf16[128,128]{1,0:T(8,128)(2,1)S(1)} collective-permute-done((bf16[128,128]{1,0:T(8,128)(2,1)S(1)}, bf16[128,128]{1,0:T(8,128)(2,1)S(1)}, u32[]{:S(2)}, u32[]{:S(2)}) %collective-permute-start.6) | collective-permute-done | bytes 32800 | tf_op jit(solution)/shard_map/ppermute | solution.py:113
  26.2 0.5 %collective-permute-done.7.refs_7_ = bf16[128,128]{1,0:T(8,128)(2,1)S(1)} collective-permute-done((bf16[128,128]{1,0:T(8,128)(2,1)S(1)}, bf16[128,128]{1,0:T(8,128)(2,1)S(1)}, u32[]{:S(2)}, u32[]{:S(2)}) %collective-permute-start.7) | collective-permute-done | bytes 32800 | tf_op jit(solution)/shard_map/ppermute | solution.py:113
  26.7 2.5 %all-to-all-done = bf16[16,64,384]{2,1,0:T(8,128)(2,1)S(1)} async-done(((bf16[16,64,384]{2,1,0:T(8,128)(2,1)}), bf16[16,64,384]{2,1,0:T(8,128)(2,1)S(1)}, u32[]{:S(2)}, u32[]{:S(2)}) %all-to-all-start) | async-done | bytes 786464 | tf_op jit(solution)/shard_map/all_to_all | solution.py:502
  29.3 0.7 %shard_map.67 = bf16[2,256,384]{2,1,0:T(8,128)(2,1)S(1)} custom-call(bf16[512,1024]{1,0:T(8,128)(2,1)S(1)} %get-tuple-element.35.rows_ref, bf16[1024,384]{1,0:T(8,128)(2,1)S(1)} %bitcast.2), custom_call_target="tpu_custom_call" | custom-call | flops 402653184 | bytes 3145728 | tf_op jit(solution)/shard_map/pallas_call | solution.py:331
  30.0 0.0 copy-start.1
  30.0 0.0 copy-start.2
  30.0 0.0 copy-start.3
  30.0 1.6 %collective-permute-start.9 = (bf16[2,256,384]{2,1,0:T(8,128)(2,1)S(1)}, bf16[2,256,384]{2,1,0:T(8,128)(2,1)S(1)}, u32[]{:S(2)}, u32[]{:S(2)}) collective-permute-start(bf16[2,256,384]{2,1,0:T(8,128)(2,1)S(1)} %shard_map.67), channel_id=1, source_target_pairs={{0,16},{16,0},{1,17},{17,1},{2,18},{18,2},{3,19},{19,3},{4,20},{20... | collective-permute-start | bytes 1179656 | tf_op jit(solution)/shard_map/ppermute | solution.py:464
  31.6 0.9 %shard_map.68 = (bf16[2,256,128]{2,1,0:T(8,128)(2,1)S(1)}, bf16[2,256,128]{2,1,0:T(8,128)(2,1)S(1)}, bf16[256,128]{1,0:T(8,128)(2,1)S(1)}, bf16[256,128]{1,0:T(8,128)(2,1)S(1)}) custom-call(f32[8,128]{1,0:T(8,128)S(1)} %get-tuple-element.34.side_ref, bf16[512,1024]{1,0:T(8,128)(2,1)S(1)} %get-tuple-element.35.rows_ref, ...), custom_call_target="tpu_custom_call" | custom-call | flops 268435456 | bytes 3145728 | tf_op jit(solution)/shard_map/pallas_call | solution.py:303
  32.5 0.1 collective-permute-start.10
  32.6 0.8 %shard_map.69.after_ref.own_ref = bf16[2,256,512]{2,1,0:T(8,128)(2,1)S(1)} custom-call(bf16[512,1024]{1,0:T(8,128)(2,1)S(1)} %get-tuple-element.35.rows_ref, bf16[1024,384]{1,0:T(8,128)(2,1)S(1)} %bitcast.3, bf16[2,256,128]{2,1,0:T(8,128)(2,1)S(1)} %get-tuple-element.49.outer_ref), custom_call_target="tpu_custom_call" | custom-call | flops 402653184 | bytes 3145728 | tf_op jit(solution)/shard_map/pallas_call | solution.py:331
  33.4 0.0 copy-done.1
  33.4 0.0 copy-done.2
  33.4 0.0 copy-done.3
  33.4 2.8 %shard_map.70 = (bf16[2,512,512]{2,1,0:T(8,128)(2,1)S(1)}, bf16[2,2,128,512]{3,2,1,0:T(8,128)(2,1)S(1)}, f32[2,2,512,512]{3,2,1,0:T(8,128)S(1)}, bf16[2,512,256]{2,1,0:T(8,128)(2,1)S(1)}, f32[8,128]{1,0:T(8,128)}) custom-call(s32[1,2,1]{2,1,0:T(2,128)S(1)} %copy.7.flag_ref, s32[1,2,1]{2,1,0:T(2,128)S(1)} %copy.9.offset_ref, f32[1,2]{1,0:T(1,128)S(1)} %copy-done.3, ...), custom_call_target="tpu_custom_call" | custom-call | flops 2300000000 | bytes 7340032 | tf_op jit(solution)/shard_map/pallas_call | solution.py:241
  36.2 4.7 %collective-permute-start.11 = (bf16[256,128]{1,0:T(8,128)(2,1)S(1)}, bf16[256,128]{1,0:T(8,128)(2,1)S(1)}, u32[]{:S(2)}, u32[]{:S(2)}) collective-permute-start(bf16[256,128]{1,0:T(8,128)(2,1)S(1)} %get-tuple-element.51), channel_id=1, source_target_pairs={{1,2},{3,4},{5,6},{7,8},{9,10},{11,12},{13,14},{15,0},{2,1},{4,3},... | collective-permute-start | bytes 196616 | tf_op jit(solution)/shard_map/ppermute | solution.py:346
  41.0 0.5 %collective-permute-start.8 = (bf16[2,256,128]{2,1,0:T(8,128)(2,1)S(1)}, bf16[2,256,128]{2,1,0:T(8,128)(2,1)S(1)}, u32[]{:S(2)}, u32[]{:S(2)}) collective-permute-start(bf16[2,256,128]{2,1,0:T(8,128)(2,1)S(1)} %get-tuple-element.46), channel_id=1, source_target_pairs={{0,16},{16,0},{1,17},{17,1},{2,18},{18,2},{3,19},{19,3},{4,20},{20... | collective-permute-start | bytes 393224 | tf_op jit(solution)/shard_map/ppermute | solution.py:464
  41.5 0.0 collective-permute-done.10.first_ref
  41.5 1.4 %collective-permute-done.11.second_ref = bf16[256,128]{1,0:T(8,128)(2,1)S(1)} collective-permute-done((bf16[256,128]{1,0:T(8,128)(2,1)S(1)}, bf16[256,128]{1,0:T(8,128)(2,1)S(1)}, u32[]{:S(2)}, u32[]{:S(2)}) %collective-permute-start.11) | collective-permute-done | bytes 65568 | tf_op jit(solution)/shard_map/ppermute | solution.py:346
  42.9 0.2 shard_map.71
  43.1 0.6 %collective-permute-start.12 = (bf16[256,128]{1,0:T(8,128)(2,1)S(1)}, bf16[256,128]{1,0:T(8,128)(2,1)S(1)}, u32[]{:S(2)}, u32[]{:S(2)}) collective-permute-start(bf16[256,128]{1,0:T(8,128)(2,1)S(1)} %get-tuple-element.52), channel_id=1, source_target_pairs={{0,16},{16,0},{1,17},{17,1},{2,18},{18,2},{3,19},{19,3},{4,20},{20... | collective-permute-start | bytes 196616 | tf_op jit(solution)/shard_map/ppermute | solution.py:464
  43.7 1.1 %shard_map.72.merged_ref = f32[2,512,512]{2,1,0:T(8,128)S(1)} custom-call(bf16[2,256,512]{2,1,0:T(8,128)(2,1)S(1)} %shard_map.69.after_ref.own_ref, bf16[256,128]{1,0:T(8,128)(2,1)S(1)} %get-tuple-element.53.rims_ref, bf16[2,512,512]{2,1,0:T(8,128)(2,1)S(1)} %get-tuple-element.50.centre_ref, bf16[2,2,128,512]{3,2,1,0:T(8,128)(2,1)S(1)} %get-tuple-element.54.rim_ref, ...), custom_call_target="tpu_custom_call" | custom-call | flops 536870912 | bytes 8388608 | tf_op jit(solution)/shard_map/pallas_call | solution.py:434
  44.8 1.2 %collective-permute-done.8.far_outer = bf16[2,256,128]{2,1,0:T(8,128)(2,1)S(1)} collective-permute-done((bf16[2,256,128]{2,1,0:T(8,128)(2,1)S(1)}, bf16[2,256,128]{2,1,0:T(8,128)(2,1)S(1)}, u32[]{:S(2)}, u32[]{:S(2)}) %collective-permute-start.8) | collective-permute-done | bytes 131104 | tf_op jit(solution)/shard_map/ppermute | solution.py:464
  45.9 1.5 %collective-permute-done.12.rims_ref = bf16[256,128]{1,0:T(8,128)(2,1)S(1)} collective-permute-done((bf16[256,128]{1,0:T(8,128)(2,1)S(1)}, bf16[256,128]{1,0:T(8,128)(2,1)S(1)}, u32[]{:S(2)}, u32[]{:S(2)}) %collective-permute-start.12) | collective-permute-done | bytes 65568 | tf_op jit(solution)/shard_map/ppermute | solution.py:464
  47.4 0.0 collective-permute-done.9.far_inner
  47.4 2.2 %shard_map.73 = f32[2,512,512]{2,1,0:T(8,128)} custom-call(bf16[2,256,128]{2,1,0:T(8,128)(2,1)S(1)} %collective-permute-done.8.far_outer, bf16[2,256,384]{2,1,0:T(8,128)(2,1)S(1)} %collective-permute-done.9.far_inner, bf16[256,128]{1,0:T(8,128)(2,1)S(1)} %collective-permute-done.12.rims_ref, f32[2,512,512]{2,1,0:T(8,128)S(1)} %shard_map.72.merged_ref, ...), custom_call_target="tpu_custom_call" | custom-call | flops 536870912 | bytes 8388608 | tf_op jit(solution)/shard_map/pallas_call | solution.py:443
  (1 shorter events, 0.0 us)
Async XLA Ops:
  0.0 1.2 %copy-start = (bf16[2,32,8192]{2,1,0:T(8,128)(2,1)S(1)}, bf16[2,32,8192]{2,1,0:T(8,128)(2,1)}, u32[]{:S(2)}) copy-start(bf16[2,32,8192]{2,1,0:T(8,128)(2,1)} %param.6) | copy-start | bytes 3145732
  2.3 10.3 %collective-permute-start = (bf16[8,64,128]{2,1,0:T(8,128)(2,1)S(1)}, bf16[8,64,128]{2,1,0:T(8,128)(2,1)S(1)}, u32[]{:S(2)}, u32[]{:S(2)}) collective-permute-start(bf16[8,64,128]{2,1,0:T(8,128)(2,1)S(1)} %get-tuple-element.32), channel_id=1, source_target_pairs={{0,8},{1,9},{2,10},{3,11},{4,12},{5,13},{6,14},{7,15},{8,0},{9,1},... | collective-permute-start | bytes 393224 | tf_op jit(solution)/shard_map/ppermute | solution.py:113
  6.3 23.0 %all-to-all-start = ((bf16[16,64,384]{2,1,0:T(8,128)(2,1)}), bf16[16,64,384]{2,1,0:T(8,128)(2,1)S(1)}, u32[]{:S(2)}, u32[]{:S(2)}) async-start(bf16[16,64,384]{2,1,0:T(8,128)(2,1)} %get-tuple-element.36), calls=%async_computation | async-start | bytes 1572864 | tf_op jit(solution)/shard_map/all_to_all | solution.py:502
  12.6 6.4 %copy-start.4 = (s32[1,2,1]{1,2,0:T(1,128)S(1)}, s32[1,2,1]{1,2,0:T(1,128)}, u32[]{:S(2)}) copy-start(s32[1,2,1]{1,2,0:T(1,128)} %param.7) | copy-start | bytes 28
  12.6 6.5 %copy-start.5 = (s32[1,2,1]{1,2,0:T(1,128)S(1)}, s32[1,2,1]{1,2,0:T(1,128)}, u32[]{:S(2)}) copy-start(s32[1,2,1]{1,2,0:T(1,128)} %param.8) | copy-start | bytes 28
  12.6 3.6 %collective-permute-start.1 = (bf16[128,128]{1,0:T(8,128)(2,1)S(1)}, bf16[128,128]{1,0:T(8,128)(2,1)S(1)}, u32[]{:S(2)}, u32[]{:S(2)}) collective-permute-start(bf16[128,128]{1,0:T(8,128)(2,1)S(1)} %get-tuple-element.37), channel_id=1, source_target_pairs={{0,1},{1,0},{2,3},{3,2},{4,5},{5,4},{6,7},{7,6},{8,9},{9,8},{10,11... | collective-permute-start | bytes 98312 | tf_op jit(solution)/shard_map/ppermute | solution.py:113
  12.7 6.0 %collective-permute-start.2 = (bf16[128,128]{1,0:T(8,128)(2,1)S(1)}, bf16[128,128]{1,0:T(8,128)(2,1)S(1)}, u32[]{:S(2)}, u32[]{:S(2)}) collective-permute-start(bf16[128,128]{1,0:T(8,128)(2,1)S(1)} %get-tuple-element.38), channel_id=1, source_target_pairs={{0,2},{1,3},{2,0},{3,1},{4,6},{5,7},{6,4},{7,5},{8,10},{9,11},{10,... | collective-permute-start | bytes 98312 | tf_op jit(solution)/shard_map/ppermute | solution.py:113
  14.3 6.1 %collective-permute-start.3 = (bf16[128,128]{1,0:T(8,128)(2,1)S(1)}, bf16[128,128]{1,0:T(8,128)(2,1)S(1)}, u32[]{:S(2)}, u32[]{:S(2)}) collective-permute-start(bf16[128,128]{1,0:T(8,128)(2,1)S(1)} %get-tuple-element.39), channel_id=1, source_target_pairs={{0,3},{1,2},{2,1},{3,0},{4,7},{5,6},{6,5},{7,4},{8,11},{9,10},{10,... | collective-permute-start | bytes 98312 | tf_op jit(solution)/shard_map/ppermute | solution.py:113
  14.6 10.5 %collective-permute-start.4 = (bf16[128,128]{1,0:T(8,128)(2,1)S(1)}, bf16[128,128]{1,0:T(8,128)(2,1)S(1)}, u32[]{:S(2)}, u32[]{:S(2)}) collective-permute-start(bf16[128,128]{1,0:T(8,128)(2,1)S(1)} %get-tuple-element.40), channel_id=1, source_target_pairs={{0,4},{1,5},{2,6},{3,7},{4,0},{5,1},{6,2},{7,3},{8,12},{9,13},{10,... | collective-permute-start | bytes 98312 | tf_op jit(solution)/shard_map/ppermute | solution.py:113
  15.4 10.1 %collective-permute-start.5 = (bf16[128,128]{1,0:T(8,128)(2,1)S(1)}, bf16[128,128]{1,0:T(8,128)(2,1)S(1)}, u32[]{:S(2)}, u32[]{:S(2)}) collective-permute-start(bf16[128,128]{1,0:T(8,128)(2,1)S(1)} %get-tuple-element.41), channel_id=1, source_target_pairs={{0,5},{1,4},{2,7},{3,6},{4,1},{5,0},{6,3},{7,2},{8,13},{9,12},{10,... | collective-permute-start | bytes 98312 | tf_op jit(solution)/shard_map/ppermute | solution.py:113
  16.3 10.0 %collective-permute-start.6 = (bf16[128,128]{1,0:T(8,128)(2,1)S(1)}, bf16[128,128]{1,0:T(8,128)(2,1)S(1)}, u32[]{:S(2)}, u32[]{:S(2)}) collective-permute-start(bf16[128,128]{1,0:T(8,128)(2,1)S(1)} %get-tuple-element.42), channel_id=1, source_target_pairs={{0,6},{1,7},{2,4},{3,5},{4,2},{5,3},{6,0},{7,1},{8,14},{9,15},{10,... | collective-permute-start | bytes 98312 | tf_op jit(solution)/shard_map/ppermute | solution.py:113
  18.7 8.0 %collective-permute-start.7 = (bf16[128,128]{1,0:T(8,128)(2,1)S(1)}, bf16[128,128]{1,0:T(8,128)(2,1)S(1)}, u32[]{:S(2)}, u32[]{:S(2)}) collective-permute-start(bf16[128,128]{1,0:T(8,128)(2,1)S(1)} %get-tuple-element.43), channel_id=1, source_target_pairs={{0,7},{1,6},{2,5},{3,4},{4,3},{5,2},{6,1},{7,0},{8,15},{9,14},{10,... | collective-permute-start | bytes 98312 | tf_op jit(solution)/shard_map/ppermute | solution.py:113
  30.0 3.4 %copy-start.1 = (bf16[1,544,512]{2,1,0:T(8,128)(2,1)S(1)}, bf16[1,544,512]{2,1,0:T(8,128)(2,1)}, u32[]{:S(2)}) copy-start(bf16[1,544,512]{2,1,0:T(8,128)(2,1)} %range_ref.1) | copy-start | bytes 1671172
  30.0 3.4 %copy-start.2 = (bf16[1,2,512,256]{3,2,1,0:T(8,128)(2,1)S(1)}, bf16[1,2,512,256]{3,2,1,0:T(8,128)(2,1)}, u32[]{:S(2)}) copy-start(bf16[1,2,512,256]{3,2,1,0:T(8,128)(2,1)} %interp_ref.1) | copy-start | bytes 1572868
  30.0 3.4 %copy-start.3 = (f32[1,2]{1,0:T(1,128)S(1)}, f32[1,2]{1,0:T(1,128)}, u32[]{:S(2)}) copy-start(f32[1,2]{1,0:T(1,128)} %shift_ref.1) | copy-start | bytes 28
  30.0 17.4 %collective-permute-start.9 = (bf16[2,256,384]{2,1,0:T(8,128)(2,1)S(1)}, bf16[2,256,384]{2,1,0:T(8,128)(2,1)S(1)}, u32[]{:S(2)}, u32[]{:S(2)}) collective-permute-start(bf16[2,256,384]{2,1,0:T(8,128)(2,1)S(1)} %shard_map.67), channel_id=1, source_target_pairs={{0,16},{16,0},{1,17},{17,1},{2,18},{18,2},{3,19},{19,3},{4,20},{20... | collective-permute-start | bytes 1179656 | tf_op jit(solution)/shard_map/ppermute | solution.py:464
  32.5 9.0 %collective-permute-start.10 = (bf16[256,128]{1,0:T(8,128)(2,1)S(1)}, bf16[256,128]{1,0:T(8,128)(2,1)S(1)}, u32[]{:S(2)}, u32[]{:S(2)}) collective-permute-start(bf16[256,128]{1,0:T(8,128)(2,1)S(1)} %get-tuple-element.47), channel_id=1, source_target_pairs={{0,1},{2,3},{4,5},{6,7},{8,9},{10,11},{12,13},{14,15},{1,0},{3,2},... | collective-permute-start | bytes 196616 | tf_op jit(solution)/shard_map/ppermute | solution.py:346
  36.2 6.7 %collective-permute-start.11 = (bf16[256,128]{1,0:T(8,128)(2,1)S(1)}, bf16[256,128]{1,0:T(8,128)(2,1)S(1)}, u32[]{:S(2)}, u32[]{:S(2)}) collective-permute-start(bf16[256,128]{1,0:T(8,128)(2,1)S(1)} %get-tuple-element.51), channel_id=1, source_target_pairs={{1,2},{3,4},{5,6},{7,8},{9,10},{11,12},{13,14},{15,0},{2,1},{4,3},... | collective-permute-start | bytes 196616 | tf_op jit(solution)/shard_map/ppermute | solution.py:346
  41.0 5.0 %collective-permute-start.8 = (bf16[2,256,128]{2,1,0:T(8,128)(2,1)S(1)}, bf16[2,256,128]{2,1,0:T(8,128)(2,1)S(1)}, u32[]{:S(2)}, u32[]{:S(2)}) collective-permute-start(bf16[2,256,128]{2,1,0:T(8,128)(2,1)S(1)} %get-tuple-element.46), channel_id=1, source_target_pairs={{0,16},{16,0},{1,17},{17,1},{2,18},{18,2},{3,19},{19,3},{4,20},{20... | collective-permute-start | bytes 393224 | tf_op jit(solution)/shard_map/ppermute | solution.py:464
  43.1 4.3 %collective-permute-start.12 = (bf16[256,128]{1,0:T(8,128)(2,1)S(1)}, bf16[256,128]{1,0:T(8,128)(2,1)S(1)}, u32[]{:S(2)}, u32[]{:S(2)}) collective-permute-start(bf16[256,128]{1,0:T(8,128)(2,1)S(1)} %get-tuple-element.52), channel_id=1, source_target_pairs={{0,16},{16,0},{1,17},{17,1},{2,18},{18,2},{3,19},{19,3},{4,20},{20... | collective-permute-start | bytes 196616 | tf_op jit(solution)/shard_map/ppermute | solution.py:464

commit v5 on v3

--- a/solution.py
+++ b/solution.py
@@ -342,8 +342,9 @@
 
 def exchanged(value, begin):
     devices = lax.axis_size("rng")
-    pairs = [(i, (i + 1) % devices) for i in range(begin, devices, 2)]
-    return lax.ppermute(value, "rng", pairs + [(j, i) for i, j in pairs])
+    pairs = [(i, i + 1) for i in range(begin, devices - 1, 2)]
+    ends = [(i, i) for i in range(devices) if all(i not in pair for pair in pairs)]
+    return lax.ppermute(value, "rng", pairs + [(j, i) for i, j in pairs] + ends)
 
 
 def rims_kernel(side_ref, first_ref, second_ref, own_ref, out_ref):
@@ -503,26 +504,26 @@
     sends = joined(near_blocks, relay)
     pieces = [across(value, d) if d else value for d, value in enumerate(sends)]
     matrix, own_side = filter_table(fore_flag, angles, local_pulses, sends[0])
-    def halos(side, edges, stride):
-        rims, out_rims = sorted_rims(side, exchanged(edges[0], 0), exchanged(edges[1], 1))
-        return rims, from_partner(out_rims, stride)
-
     pulses = after(pulses, *pieces[1:]).reshape(2 * local_pulses * devices, bins - LANES)
     out_inner = inner_image(partner_rows_kernel, angles, matrix, pulses)
     pieces[0] = after(pieces[0], out_inner)
     own_outer, out_outer, *edges = outer_image(own_side, matrix, pieces)
     far = [from_partner(value, 1) for value in (out_outer, out_inner)]
-    rims, far_rims = halos(own_side, edges, 1)
+    edges = exchanged(edges[0], 0), exchanged(edges[1], 1)
     own_kernel = functools.partial(own_rows_kernel, local_pulses)
     own = inner_image(own_kernel, angles, matrix, pulses, (own_outer,))
     tables = merge_tables(0, 1, *settings, own)
+    edges = after(edges[0], tables[0]), edges[1]
     for level in range(levels):
         stride = 2**level
         if level > 0:
             tables = merge_tables(level, stride, *settings, image)
             own, out, edges = split_image(level, image, fore_flag, rim)
             far = [from_partner(value, stride) for value in (out[..., :LANES], out[..., LANES:])]
-            rims, far_rims = halos(tables[-1], edges, stride)
+            edges = exchanged(edges[0], 0), exchanged(edges[1], 1)
+            own_side = tables[-1]
+        rims, out_rims = sorted_rims(own_side, *edges)
+        far_rims = from_partner(out_rims, stride)
         image = merged_image(own, rims, far, far_rims, tables, BF16 if level + 1 < levels else F32)
     return image
 

time: 49.1 us -> 47.8 us (0.974)
  the two profiles are of different devices: /device:TPU:0 before, /device:TPU:16 now
where the time goes in v5:
time: 47.8 us; the launch traced here: 47.3 us
  starting transfers between devices  21.3 us (45%)
  waiting for transfers between devices  13.4 us (28%)
  Pallas kernels  11 us (23%)
  local copies, waits for them, and re-layouts  1.44 us (3%)
    ppermute x8, waiting for transfers between devices, across(): return lax.ppermute(value, 'rng', [(i, i ^ mask) for i in range(devices)])  8.89 us
    ppermute x8, starting transfers between devices, across(): return lax.ppermute(value, 'rng', [(i, i ^ mask) for i in range(devices)])  8.48 us
    all_to_all x1, starting transfers between devices, on_device(): lax.all_to_all(blocks, 'rng', split_axis=0, concat_axis=0, tiled=True)  6.72 us
    ppermute x3, starting transfers between devices, from_partner(): return lax.ppermute(value, 'sub', pairs)  3.73 us
    ppermute x3, waiting for transfers between devices, from_partner(): return lax.ppermute(value, 'sub', pairs)  3.04 us
    pallas_call x1, Pallas kernels, merge_tables(): pl.pallas_call(functools.partial(merge_table_kernel, level, stride), out_...  2.8 us
    ppermute x2, starting transfers between devices, exchanged(): return lax.ppermute(value, 'rng', pairs + [(j, i) for i, j in pairs] + ends)  2.41 us
    pallas_call x1, Pallas kernels, merged_image(): pl.pallas_call(late_kernel, out_shape=jax.ShapeDtypeStruct((2, angles, bi...  2.18 us
  transfers between devices with their start and end apart: 14, of which 5 were waited for; matrix products, arithmetic and copies ran while one was open for 0% of the time, Pallas kernels for 15%

profile of v5, /device:TPU:16, one launch (start us, length us, event | category | flops | bytes accessed | tf_op | source)
XLA Modules:
  0.0 47.3 jit_solution(8410931267464680098)
XLA Ops:
  0.0 0.0 copy-start
  0.0 1.2 %copy-done = bf16[2,32,8192]{2,1,0:T(8,128)(2,1)S(1)} copy-done((bf16[2,32,8192]{2,1,0:T(8,128)(2,1)S(1)}, bf16[2,32,8192]{2,1,0:T(8,128)(2,1)}, u32[]{:S(2)}) %copy-start) | copy-done | bytes 1048600
  1.2 1.0 %shard_map.64 = (bf16[8,64,128]{2,1,0:T(8,128)(2,1)S(1)}, bf16[8,64,128]{2,1,0:T(8,128)(2,1)S(1)}, bf16[16,64,384]{2,1,0:T(8,128)(2,1)}) custom-call(bf16[64,8192]{1,0:T(8,128)(2,1)S(1)} %bitcast.4), custom_call_target="tpu_custom_call" | custom-call | bytes 2097152 | tf_op jit(solution)/shard_map/pallas_call | solution.py:81
  2.3 0.0 collective-permute-start
  2.3 6.7 %all-to-all-start = ((bf16[16,64,384]{2,1,0:T(8,128)(2,1)}), bf16[16,64,384]{2,1,0:T(8,128)(2,1)S(1)}, u32[]{:S(2)}, u32[]{:S(2)}) async-start(bf16[16,64,384]{2,1,0:T(8,128)(2,1)} %get-tuple-element.36), calls=%async_computation | async-start | bytes 1572864 | tf_op jit(solution)/shard_map/all_to_all | solution.py:503
  9.0 0.0 collective-permute-done.relay_ref
  9.0 0.0 copy-start.4
  9.0 0.0 copy-start.5
  9.0 0.2 collective-permute-start.1
  9.3 1.5 %collective-permute-start.2 = (bf16[128,128]{1,0:T(8,128)(2,1)S(1)}, bf16[128,128]{1,0:T(8,128)(2,1)S(1)}, u32[]{:S(2)}, u32[]{:S(2)}) collective-permute-start(bf16[128,128]{1,0:T(8,128)(2,1)S(1)} %get-tuple-element.38), channel_id=1, source_target_pairs={{0,2},{1,3},{2,0},{3,1},{4,6},{5,7},{6,4},{7,5},{8,10},{9,11},{10,... | collective-permute-start | bytes 98312 | tf_op jit(solution)/shard_map/ppermute | solution.py:113
  10.7 0.2 collective-permute-start.3
  11.0 3.8 %collective-permute-start.4 = (bf16[128,128]{1,0:T(8,128)(2,1)S(1)}, bf16[128,128]{1,0:T(8,128)(2,1)S(1)}, u32[]{:S(2)}, u32[]{:S(2)}) collective-permute-start(bf16[128,128]{1,0:T(8,128)(2,1)S(1)} %get-tuple-element.40), channel_id=1, source_target_pairs={{0,4},{1,5},{2,6},{3,7},{4,0},{5,1},{6,2},{7,3},{8,12},{9,13},{10,... | collective-permute-start | bytes 98312 | tf_op jit(solution)/shard_map/ppermute | solution.py:113
  14.7 0.0 collective-permute-start.5
  14.7 0.0 collective-permute-done.1.refs_1_
  14.8 2.6 %collective-permute-start.6 = (bf16[128,128]{1,0:T(8,128)(2,1)S(1)}, bf16[128,128]{1,0:T(8,128)(2,1)S(1)}, u32[]{:S(2)}, u32[]{:S(2)}) collective-permute-start(bf16[128,128]{1,0:T(8,128)(2,1)S(1)} %get-tuple-element.42), channel_id=1, source_target_pairs={{0,6},{1,7},{2,4},{3,5},{4,2},{5,3},{6,0},{7,1},{8,14},{9,15},{10,... | collective-permute-start | bytes 98312 | tf_op jit(solution)/shard_map/ppermute | solution.py:113
  17.4 0.0 collective-permute-done.2.refs_2_
  17.4 0.2 collective-permute-start.7
  17.5 0.0 copy-done.4
  17.5 0.1 copy.7.flag_ref
  17.6 1.3 %shard_map.66 = (bf16[512,1024]{1,0:T(8,128)(2,1)S(1)}, f32[8,128]{1,0:T(8,128)S(1)}) custom-call(s32[1,2,1]{2,1,0:T(2,128)S(1)} %copy.7.flag_ref, bf16[128,128]{1,0:T(8,128)(2,1)S(1)} %get-tuple-element.45.after_ref.refs_0_), custom_call_target="tpu_custom_call" | custom-call | flops 9000000 | bytes 4194304 | tf_op jit(solution)/shard_map/pallas_call | solution.py:155
  18.9 0.0 collective-permute-done.3.refs_3_
  18.9 6.7 %collective-permute-done.4.refs_4_ = bf16[128,128]{1,0:T(8,128)(2,1)S(1)} collective-permute-done((bf16[128,128]{1,0:T(8,128)(2,1)S(1)}, bf16[128,128]{1,0:T(8,128)(2,1)S(1)}, u32[]{:S(2)}, u32[]{:S(2)}) %collective-permute-start.4) | collective-permute-done | bytes 32800 | tf_op jit(solution)/shard_map/ppermute | solution.py:113
  25.6 0.0 collective-permute-done.5.refs_5_
  25.6 2.2 %collective-permute-done.6.refs_6_ = bf16[128,128]{1,0:T(8,128)(2,1)S(1)} collective-permute-done((bf16[128,128]{1,0:T(8,128)(2,1)S(1)}, bf16[128,128]{1,0:T(8,128)(2,1)S(1)}, u32[]{:S(2)}, u32[]{:S(2)}) %collective-permute-start.6) | collective-permute-done | bytes 32800 | tf_op jit(solution)/shard_map/ppermute | solution.py:113
  27.8 0.0 collective-permute-done.7.refs_7_
  27.8 1.4 %all-to-all-done = bf16[16,64,384]{2,1,0:T(8,128)(2,1)S(1)} async-done(((bf16[16,64,384]{2,1,0:T(8,128)(2,1)}), bf16[16,64,384]{2,1,0:T(8,128)(2,1)S(1)}, u32[]{:S(2)}, u32[]{:S(2)}) %all-to-all-start) | async-done | bytes 786464 | tf_op jit(solution)/shard_map/all_to_all | solution.py:503
  29.2 0.7 %shard_map.67 = bf16[2,256,384]{2,1,0:T(8,128)(2,1)S(1)} custom-call(bf16[512,1024]{1,0:T(8,128)(2,1)S(1)} %get-tuple-element.35.rows_ref, bf16[1024,384]{1,0:T(8,128)(2,1)S(1)} %bitcast.2), custom_call_target="tpu_custom_call" | custom-call | flops 402653184 | bytes 3145728 | tf_op jit(solution)/shard_map/pallas_call | solution.py:331
  29.9 0.0 copy-start.1
  29.9 0.0 copy-start.3
  29.9 1.6 %collective-permute-start.9 = (bf16[2,256,384]{2,1,0:T(8,128)(2,1)S(1)}, bf16[2,256,384]{2,1,0:T(8,128)(2,1)S(1)}, u32[]{:S(2)}, u32[]{:S(2)}) collective-permute-start(bf16[2,256,384]{2,1,0:T(8,128)(2,1)S(1)} %shard_map.67), channel_id=1, source_target_pairs={{0,16},{16,0},{1,17},{17,1},{2,18},{18,2},{3,19},{19,3},{4,20},{20... | collective-permute-start | bytes 1179656 | tf_op jit(solution)/shard_map/ppermute | solution.py:465
  31.5 0.0 copy-done.5
  31.5 0.1 copy.9.offset_ref
  31.6 0.0 copy-start.2
  31.6 0.9 %shard_map.68 = (bf16[2,256,128]{2,1,0:T(8,128)(2,1)S(1)}, bf16[2,256,128]{2,1,0:T(8,128)(2,1)S(1)}, bf16[256,128]{1,0:T(8,128)(2,1)S(1)}, bf16[256,128]{1,0:T(8,128)(2,1)S(1)}) custom-call(f32[8,128]{1,0:T(8,128)S(1)} %get-tuple-element.34.side_ref, bf16[512,1024]{1,0:T(8,128)(2,1)S(1)} %get-tuple-element.35.rows_ref, ...), custom_call_target="tpu_custom_call" | custom-call | flops 268435456 | bytes 3145728 | tf_op jit(solution)/shard_map/pallas_call | solution.py:303
  32.5 0.1 collective-permute-start.10
  32.6 2.3 %collective-permute-start.11 = (bf16[256,128]{1,0:T(8,128)(2,1)S(1)}, bf16[256,128]{1,0:T(8,128)(2,1)S(1)}, u32[]{:S(2)}, u32[]{:S(2)}) collective-permute-start(bf16[256,128]{1,0:T(8,128)(2,1)S(1)} %get-tuple-element.51), channel_id=1, source_target_pairs={{1,2},{3,4},{5,6},{7,8},{9,10},{11,12},{13,14},{2,1},{4,3},{6,5},{... | collective-permute-start | bytes 196616 | tf_op jit(solution)/shard_map/ppermute | solution.py:347
  35.0 0.6 %collective-permute-start.8 = (bf16[2,256,128]{2,1,0:T(8,128)(2,1)S(1)}, bf16[2,256,128]{2,1,0:T(8,128)(2,1)S(1)}, u32[]{:S(2)}, u32[]{:S(2)}) collective-permute-start(bf16[2,256,128]{2,1,0:T(8,128)(2,1)S(1)} %get-tuple-element.46), channel_id=1, source_target_pairs={{0,16},{16,0},{1,17},{17,1},{2,18},{18,2},{3,19},{19,3},{4,20},{20... | collective-permute-start | bytes 393224 | tf_op jit(solution)/shard_map/ppermute | solution.py:465
  35.5 0.8 %shard_map.69.after_ref.own_ref = bf16[2,256,512]{2,1,0:T(8,128)(2,1)S(1)} custom-call(bf16[512,1024]{1,0:T(8,128)(2,1)S(1)} %get-tuple-element.35.rows_ref, bf16[1024,384]{1,0:T(8,128)(2,1)S(1)} %bitcast.3, bf16[2,256,128]{2,1,0:T(8,128)(2,1)S(1)} %get-tuple-element.48.outer_ref), custom_call_target="tpu_custom_call" | custom-call | flops 402653184 | bytes 3145728 | tf_op jit(solution)/shard_map/pallas_call | solution.py:331
  36.3 0.0 copy-done.1
  36.3 0.0 copy-done.3
  36.3 0.0 copy-done.2
  36.4 2.8 %shard_map.70 = (bf16[2,512,512]{2,1,0:T(8,128)(2,1)S(1)}, bf16[2,2,128,512]{3,2,1,0:T(8,128)(2,1)S(1)}, f32[2,2,512,512]{3,2,1,0:T(8,128)S(1)}, bf16[2,512,256]{2,1,0:T(8,128)(2,1)S(1)}, f32[8,128]{1,0:T(8,128)}) custom-call(s32[1,2,1]{2,1,0:T(2,128)S(1)} %copy.7.flag_ref, s32[1,2,1]{2,1,0:T(2,128)S(1)} %copy.9.offset_ref, f32[1,2]{1,0:T(1,128)S(1)} %copy-done.3, ...), custom_call_target="tpu_custom_call" | custom-call | flops 2300000000 | bytes 7340032 | tf_op jit(solution)/shard_map/pallas_call | solution.py:241
  39.2 0.0 collective-permute-done.10.first_ref
  39.2 0.0 collective-permute-done.11.second_ref
  39.2 0.2 shard_map.71
  39.4 1.6 %collective-permute-start.12 = (bf16[256,128]{1,0:T(8,128)(2,1)S(1)}, bf16[256,128]{1,0:T(8,128)(2,1)S(1)}, u32[]{:S(2)}, u32[]{:S(2)}) collective-permute-start(bf16[256,128]{1,0:T(8,128)(2,1)S(1)} %get-tuple-element.52), channel_id=1, source_target_pairs={{0,16},{16,0},{1,17},{17,1},{2,18},{18,2},{3,19},{19,3},{4,20},{20... | collective-permute-start | bytes 196616 | tf_op jit(solution)/shard_map/ppermute | solution.py:465
  40.9 1.1 %shard_map.72.merged_ref = f32[2,512,512]{2,1,0:T(8,128)S(1)} custom-call(bf16[2,256,512]{2,1,0:T(8,128)(2,1)S(1)} %shard_map.69.after_ref.own_ref, bf16[256,128]{1,0:T(8,128)(2,1)S(1)} %get-tuple-element.53.rims_ref, bf16[2,512,512]{2,1,0:T(8,128)(2,1)S(1)} %get-tuple-element.49.centre_ref, bf16[2,2,128,512]{3,2,1,0:T(8,128)(2,1)S(1)} %get-tuple-element.54.rim_ref, ...), custom_call_target="tpu_custom_call" | custom-call | flops 536870912 | bytes 8388608 | tf_op jit(solution)/shard_map/pallas_call | solution.py:435
  42.0 2.3 %collective-permute-done.8.far_outer = bf16[2,256,128]{2,1,0:T(8,128)(2,1)S(1)} collective-permute-done((bf16[2,256,128]{2,1,0:T(8,128)(2,1)S(1)}, bf16[2,256,128]{2,1,0:T(8,128)(2,1)S(1)}, u32[]{:S(2)}, u32[]{:S(2)}) %collective-permute-start.8) | collective-permute-done | bytes 131104 | tf_op jit(solution)/shard_map/ppermute | solution.py:465
  44.4 0.7 %collective-permute-done.12.rims_ref = bf16[256,128]{1,0:T(8,128)(2,1)S(1)} collective-permute-done((bf16[256,128]{1,0:T(8,128)(2,1)S(1)}, bf16[256,128]{1,0:T(8,128)(2,1)S(1)}, u32[]{:S(2)}, u32[]{:S(2)}) %collective-permute-start.12) | collective-permute-done | bytes 65568 | tf_op jit(solution)/shard_map/ppermute | solution.py:465
  45.1 0.0 collective-permute-done.9.far_inner
  45.1 2.2 %shard_map.73 = f32[2,512,512]{2,1,0:T(8,128)} custom-call(bf16[2,256,128]{2,1,0:T(8,128)(2,1)S(1)} %collective-permute-done.8.far_outer, bf16[2,256,384]{2,1,0:T(8,128)(2,1)S(1)} %collective-permute-done.9.far_inner, bf16[256,128]{1,0:T(8,128)(2,1)S(1)} %collective-permute-done.12.rims_ref, f32[2,512,512]{2,1,0:T(8,128)S(1)} %shard_map.72.merged_ref, ...), custom_call_target="tpu_custom_call" | custom-call | flops 536870912 | bytes 8388608 | tf_op jit(solution)/shard_map/pallas_call | solution.py:444
  (1 shorter events, 0.0 us)
Async XLA Ops:
  0.0 1.2 %copy-start = (bf16[2,32,8192]{2,1,0:T(8,128)(2,1)S(1)}, bf16[2,32,8192]{2,1,0:T(8,128)(2,1)}, u32[]{:S(2)}) copy-start(bf16[2,32,8192]{2,1,0:T(8,128)(2,1)} %param.6) | copy-start | bytes 3145732
  2.3 6.7 %collective-permute-start = (bf16[8,64,128]{2,1,0:T(8,128)(2,1)S(1)}, bf16[8,64,128]{2,1,0:T(8,128)(2,1)S(1)}, u32[]{:S(2)}, u32[]{:S(2)}) collective-permute-start(bf16[8,64,128]{2,1,0:T(8,128)(2,1)S(1)} %get-tuple-element.32), channel_id=1, source_target_pairs={{0,8},{1,9},{2,10},{3,11},{4,12},{5,13},{6,14},{7,15},{8,0},{9,1},... | collective-permute-start | bytes 393224 | tf_op jit(solution)/shard_map/ppermute | solution.py:113
  2.3 26.9 %all-to-all-start = ((bf16[16,64,384]{2,1,0:T(8,128)(2,1)}), bf16[16,64,384]{2,1,0:T(8,128)(2,1)S(1)}, u32[]{:S(2)}, u32[]{:S(2)}) async-start(bf16[16,64,384]{2,1,0:T(8,128)(2,1)} %get-tuple-element.36), calls=%async_computation | async-start | bytes 1572864 | tf_op jit(solution)/shard_map/all_to_all | solution.py:503
  9.0 8.6 %copy-start.4 = (s32[1,2,1]{1,2,0:T(1,128)S(1)}, s32[1,2,1]{1,2,0:T(1,128)}, u32[]{:S(2)}) copy-start(s32[1,2,1]{1,2,0:T(1,128)} %param.7) | copy-start | bytes 28
  9.0 22.5 %copy-start.5 = (s32[1,2,1]{1,2,0:T(1,128)S(1)}, s32[1,2,1]{1,2,0:T(1,128)}, u32[]{:S(2)}) copy-start(s32[1,2,1]{1,2,0:T(1,128)} %param.8) | copy-start | bytes 28
  9.0 5.7 %collective-permute-start.1 = (bf16[128,128]{1,0:T(8,128)(2,1)S(1)}, bf16[128,128]{1,0:T(8,128)(2,1)S(1)}, u32[]{:S(2)}, u32[]{:S(2)}) collective-permute-start(bf16[128,128]{1,0:T(8,128)(2,1)S(1)} %get-tuple-element.37), channel_id=1, source_target_pairs={{0,1},{1,0},{2,3},{3,2},{4,5},{5,4},{6,7},{7,6},{8,9},{9,8},{10,11... | collective-permute-start | bytes 98312 | tf_op jit(solution)/shard_map/ppermute | solution.py:113
  9.3 8.1 %collective-permute-start.2 = (bf16[128,128]{1,0:T(8,128)(2,1)S(1)}, bf16[128,128]{1,0:T(8,128)(2,1)S(1)}, u32[]{:S(2)}, u32[]{:S(2)}) collective-permute-start(bf16[128,128]{1,0:T(8,128)(2,1)S(1)} %get-tuple-element.38), channel_id=1, source_target_pairs={{0,2},{1,3},{2,0},{3,1},{4,6},{5,7},{6,4},{7,5},{8,10},{9,11},{10,... | collective-permute-start | bytes 98312 | tf_op jit(solution)/shard_map/ppermute | solution.py:113
  10.7 8.2 %collective-permute-start.3 = (bf16[128,128]{1,0:T(8,128)(2,1)S(1)}, bf16[128,128]{1,0:T(8,128)(2,1)S(1)}, u32[]{:S(2)}, u32[]{:S(2)}) collective-permute-start(bf16[128,128]{1,0:T(8,128)(2,1)S(1)} %get-tuple-element.39), channel_id=1, source_target_pairs={{0,3},{1,2},{2,1},{3,0},{4,7},{5,6},{6,5},{7,4},{8,11},{9,10},{10,... | collective-permute-start | bytes 98312 | tf_op jit(solution)/shard_map/ppermute | solution.py:113
  11.0 14.6 %collective-permute-start.4 = (bf16[128,128]{1,0:T(8,128)(2,1)S(1)}, bf16[128,128]{1,0:T(8,128)(2,1)S(1)}, u32[]{:S(2)}, u32[]{:S(2)}) collective-permute-start(bf16[128,128]{1,0:T(8,128)(2,1)S(1)} %get-tuple-element.40), channel_id=1, source_target_pairs={{0,4},{1,5},{2,6},{3,7},{4,0},{5,1},{6,2},{7,3},{8,12},{9,13},{10,... | collective-permute-start | bytes 98312 | tf_op jit(solution)/shard_map/ppermute | solution.py:113
  14.7 10.8 %collective-permute-start.5 = (bf16[128,128]{1,0:T(8,128)(2,1)S(1)}, bf16[128,128]{1,0:T(8,128)(2,1)S(1)}, u32[]{:S(2)}, u32[]{:S(2)}) collective-permute-start(bf16[128,128]{1,0:T(8,128)(2,1)S(1)} %get-tuple-element.41), channel_id=1, source_target_pairs={{0,5},{1,4},{2,7},{3,6},{4,1},{5,0},{6,3},{7,2},{8,13},{9,12},{10,... | collective-permute-start | bytes 98312 | tf_op jit(solution)/shard_map/ppermute | solution.py:113
  14.8 13.0 %collective-permute-start.6 = (bf16[128,128]{1,0:T(8,128)(2,1)S(1)}, bf16[128,128]{1,0:T(8,128)(2,1)S(1)}, u32[]{:S(2)}, u32[]{:S(2)}) collective-permute-start(bf16[128,128]{1,0:T(8,128)(2,1)S(1)} %get-tuple-element.42), channel_id=1, source_target_pairs={{0,6},{1,7},{2,4},{3,5},{4,2},{5,3},{6,0},{7,1},{8,14},{9,15},{10,... | collective-permute-start | bytes 98312 | tf_op jit(solution)/shard_map/ppermute | solution.py:113
  17.4 10.4 %collective-permute-start.7 = (bf16[128,128]{1,0:T(8,128)(2,1)S(1)}, bf16[128,128]{1,0:T(8,128)(2,1)S(1)}, u32[]{:S(2)}, u32[]{:S(2)}) collective-permute-start(bf16[128,128]{1,0:T(8,128)(2,1)S(1)} %get-tuple-element.43), channel_id=1, source_target_pairs={{0,7},{1,6},{2,5},{3,4},{4,3},{5,2},{6,1},{7,0},{8,15},{9,14},{10,... | collective-permute-start | bytes 98312 | tf_op jit(solution)/shard_map/ppermute | solution.py:113
  29.9 6.4 %copy-start.1 = (bf16[1,544,512]{2,1,0:T(8,128)(2,1)S(1)}, bf16[1,544,512]{2,1,0:T(8,128)(2,1)}, u32[]{:S(2)}) copy-start(bf16[1,544,512]{2,1,0:T(8,128)(2,1)} %range_ref.1) | copy-start | bytes 1671172
  29.9 6.4 %copy-start.3 = (f32[1,2]{1,0:T(1,128)S(1)}, f32[1,2]{1,0:T(1,128)}, u32[]{:S(2)}) copy-start(f32[1,2]{1,0:T(1,128)} %shift_ref.1) | copy-start | bytes 28
  29.9 15.2 %collective-permute-start.9 = (bf16[2,256,384]{2,1,0:T(8,128)(2,1)S(1)}, bf16[2,256,384]{2,1,0:T(8,128)(2,1)S(1)}, u32[]{:S(2)}, u32[]{:S(2)}) collective-permute-start(bf16[2,256,384]{2,1,0:T(8,128)(2,1)S(1)} %shard_map.67), channel_id=1, source_target_pairs={{0,16},{16,0},{1,17},{17,1},{2,18},{18,2},{3,19},{19,3},{4,20},{20... | collective-permute-start | bytes 1179656 | tf_op jit(solution)/shard_map/ppermute | solution.py:465
  31.6 4.8 %copy-start.2 = (bf16[1,2,512,256]{3,2,1,0:T(8,128)(2,1)S(1)}, bf16[1,2,512,256]{3,2,1,0:T(8,128)(2,1)}, u32[]{:S(2)}) copy-start(bf16[1,2,512,256]{3,2,1,0:T(8,128)(2,1)} %interp_ref.1) | copy-start | bytes 1572868
  32.5 6.6 %collective-permute-start.10 = (bf16[256,128]{1,0:T(8,128)(2,1)S(1)}, bf16[256,128]{1,0:T(8,128)(2,1)S(1)}, u32[]{:S(2)}, u32[]{:S(2)}) collective-permute-start(bf16[256,128]{1,0:T(8,128)(2,1)S(1)} %get-tuple-element.47), channel_id=1, source_target_pairs={{0,1},{2,3},{4,5},{6,7},{8,9},{10,11},{12,13},{14,15},{1,0},{3,2},... | collective-permute-start | bytes 196616 | tf_op jit(solution)/shard_map/ppermute | solution.py:347
  32.6 6.6 %collective-permute-start.11 = (bf16[256,128]{1,0:T(8,128)(2,1)S(1)}, bf16[256,128]{1,0:T(8,128)(2,1)S(1)}, u32[]{:S(2)}, u32[]{:S(2)}) collective-permute-start(bf16[256,128]{1,0:T(8,128)(2,1)S(1)} %get-tuple-element.51), channel_id=1, source_target_pairs={{1,2},{3,4},{5,6},{7,8},{9,10},{11,12},{13,14},{2,1},{4,3},{6,5},{... | collective-permute-start | bytes 196616 | tf_op jit(solution)/shard_map/ppermute | solution.py:347
  35.0 9.4 %collective-permute-start.8 = (bf16[2,256,128]{2,1,0:T(8,128)(2,1)S(1)}, bf16[2,256,128]{2,1,0:T(8,128)(2,1)S(1)}, u32[]{:S(2)}, u32[]{:S(2)}) collective-permute-start(bf16[2,256,128]{2,1,0:T(8,128)(2,1)S(1)} %get-tuple-element.46), channel_id=1, source_target_pairs={{0,16},{16,0},{1,17},{17,1},{2,18},{18,2},{3,19},{19,3},{4,20},{20... | collective-permute-start | bytes 393224 | tf_op jit(solution)/shard_map/ppermute | solution.py:465
  39.4 5.7 %collective-permute-start.12 = (bf16[256,128]{1,0:T(8,128)(2,1)S(1)}, bf16[256,128]{1,0:T(8,128)(2,1)S(1)}, u32[]{:S(2)}, u32[]{:S(2)}) collective-permute-start(bf16[256,128]{1,0:T(8,128)(2,1)S(1)} %get-tuple-element.52), channel_id=1, source_target_pairs={{0,16},{16,0},{1,17},{17,1},{2,18},{18,2},{3,19},{19,3},{4,20},{20... | collective-permute-start | bytes 196616 | tf_op jit(solution)/shard_map/ppermute | solution.py:465

commit v6 on v5

--- a/solution.py
+++ b/solution.py
@@ -398,33 +398,70 @@
     )
 
 
-def late_kernel(
-    far_outer, far_inner, rims_ref, merged_ref, centre_ref, rim_ref, matrix_ref, turn_ref, out_ref,
-    buffer, value_ref, sems,
-):
-    image = jnp.concatenate([far_outer[...], far_inner[...]], axis=2)
-    rows = resampled(image, rims_ref, centre_ref, rim_ref, value_ref, 1)
-    parts = len(rows)
-    block = LANES
+def ends_of(value):
+    count = value.shape[-1]
+    return jnp.concatenate([value[..., :LANES], value[..., count - LANES :]], axis=-1)
+
+
+def finish(values, lanes, merged_ref, matrix_ref, turn_ref, out_ref, buffer, sems):
+    rows = [value.astype(BF16) for value in values]
     copies = []
-    for first in range(0, matrix_ref.shape[1], 2 * block):
-        matrix = matrix_ref[1, first : first + 2 * block]
+    block = 2 * LANES
+    for first in range(0, matrix_ref.shape[1], block):
+        here = slice(first, first + block)
+        matrix = matrix_ref[1, here]
         terms = dot(matrix, rows[0]), dot(matrix, rows[1])
-        for step in range(2):
-            here = slice(first + step * block, first + (step + 1) * block)
-            there = slice(step * block, (step + 1) * block)
+        at = 0
+        for begin, end in lanes:
+            there = slice(at, at + end - begin)
             turned = rotated(
-                (terms[0][there], terms[1][there]), (turn_ref[1, 0, here], turn_ref[1, 1, here])
+                (terms[0][:, there], terms[1][:, there]),
+                (turn_ref[1, 0, here, begin:end], turn_ref[1, 1, here, begin:end]),
             )
-            for part in range(parts):
-                buffer[part, here] = (merged_ref[part, here] + turned[part]).astype(buffer.dtype)
+            for part in range(2):
+                total = merged_ref[part, here, begin:end] + turned[part]
+                buffer[part, here, there] = total.astype(buffer.dtype)
             copy = pltpu.make_async_copy(
-                buffer.at[:, here], out_ref.at[:, here], sems.at[len(copies)]
+                buffer.at[:, here, there],
+                out_ref.at[:, here, pl.ds(begin, end - begin)],
+                sems.at[len(copies)],
             )
             copy.start()
             copies.append(copy)
+            at += end - begin
     for copy in copies:
         copy.wait()
+
+
+def middle_kernel(
+    far_inner, merged_ref, centre_ref, matrix_ref, turn_ref, out_ref, partial_ref, buffer, sems
+):
+    parts, half, count = far_inner.shape
+    bins = centre_ref.shape[2]
+    inner = far_inner[...].reshape(parts * half, count)
+    value = dot(inner, centre_ref[1, bins - count :, LANES : bins - LANES])
+    values = [value[part * half : (part + 1) * half] for part in range(parts)]
+    finish(
+        values, [(LANES, bins - LANES)], merged_ref, matrix_ref, turn_ref, out_ref, buffer, sems
+    )
+    partial_ref[...] = dot(inner, ends_of(centre_ref[1, bins - count :, :]))
+
+
+def end_kernel(
+    far_outer, partial_ref, rims_ref, merged_ref, centre_ref, rim_ref, matrix_ref, turn_ref,
+    begun_ref, out_ref, buffer, sems,
+):
+    parts, half, count = far_outer.shape
+    bins = centre_ref.shape[2]
+    centre = ends_of(centre_ref[1, :count, :])
+    values = [
+        partial_ref[part * half : (part + 1) * half, :]
+        + dot(far_outer[part], centre)
+        + dot(rims_ref[...], ends_of(rim_ref[1, part]))
+        for part in range(parts)
+    ]
+    lanes = [(0, LANES), (bins - LANES, bins)]
+    finish(values, lanes, merged_ref, matrix_ref, turn_ref, out_ref, buffer, sems)
 
 
 def merged_image(own, rims, far, far_rims, tables, dtype):
@@ -441,19 +478,33 @@
         compiler_params=params(16),
         cost_estimate=cost,
     )(own, rims, centre, rim, matrices, turn)
-    return pl.pallas_call(
-        late_kernel,
-        out_shape=jax.ShapeDtypeStruct((2, angles, bins), dtype),
-        in_specs=[VMEM] * 8,
-        out_specs=ANY,
+    image = jax.ShapeDtypeStruct((2, angles, bins), dtype)
+    middle, ends = bins - 2 * LANES, 2 * LANES
+    begun, partial = pl.pallas_call(
+        middle_kernel,
+        out_shape=[image, jax.ShapeDtypeStruct((angles, ends), F32)],
+        in_specs=[VMEM] * 5,
+        out_specs=[ANY, VMEM],
         scratch_shapes=[
-            pltpu.VMEM((2, angles, bins), dtype),
-            value,
+            pltpu.VMEM((2, angles, middle), dtype),
             pltpu.SemaphoreType.DMA((angles // LANES,)),
         ],
         compiler_params=params(16),
         cost_estimate=cost,
-    )(*far, far_rims, merged, centre, rim, matrices, turn)
+    )(far[1], merged, centre, matrices, turn)
+    return pl.pallas_call(
+        end_kernel,
+        out_shape=image,
+        in_specs=[VMEM] * 8 + [ANY],
+        out_specs=ANY,
+        scratch_shapes=[
+            pltpu.VMEM((2, angles, ends), dtype),
+            pltpu.SemaphoreType.DMA((angles // LANES,)),
+        ],
+        input_output_aliases={8: 0},
+        compiler_params=params(16),
+        cost_estimate=cost,
+    )(far[0], partial, far_rims, merged, centre, rim, matrices, turn, begun)
 
 
 def after(value, *earlier):

time: 47.8 us -> 47.3 us (0.990)
  waiting for transfers between devices: 13.4 us -> 11.3 us
  Pallas kernels: 11 us -> 12.4 us
    ppermute x3, waiting for transfers between devices: 3.04 us -> 1.03 us  [from_partner(): return lax.ppermute(value, 'sub', pairs)]
    pallas_call x1 -> x2, Pallas kernels: 2.18 us -> 3.63 us  [the longest x1 2 us: merged_image(): pl.pallas_call(middle_kernel, out_shape=[image, jax.ShapeDtypeStruct((ang...]
  transfers between devices with their start and end apart: 14 -> 14, of which waited for: 5 -> 5; matrix products, arithmetic and copies ran while one was open for 0% -> 0% of each run, Pallas kernels for 15% -> 19%
where the time goes in v6:
time: 47.3 us; the launch traced here: 46.7 us
  starting transfers between devices  21.3 us (45%)
  Pallas kernels  12.4 us (26%)
  waiting for transfers between devices  11.3 us (24%)
  local copies, waits for them, and re-layouts  1.44 us (3%)
    ppermute x8, waiting for transfers between devices, across(): return lax.ppermute(value, 'rng', [(i, i ^ mask) for i in range(devices)])  8.89 us
    ppermute x8, starting transfers between devices, across(): return lax.ppermute(value, 'rng', [(i, i ^ mask) for i in range(devices)])  8.48 us
    all_to_all x1, starting transfers between devices, on_device(): lax.all_to_all(blocks, 'rng', split_axis=0, concat_axis=0, tiled=True)  6.72 us
    ppermute x3, starting transfers between devices, from_partner(): return lax.ppermute(value, 'sub', pairs)  3.73 us
    pallas_call x1, Pallas kernels, merge_tables(): pl.pallas_call(functools.partial(merge_table_kernel, level, stride), out_...  2.8 us
    ppermute x2, starting transfers between devices, exchanged(): return lax.ppermute(value, 'rng', pairs + [(j, i) for i, j in pairs] + ends)  2.41 us
    pallas_call x1, Pallas kernels, merged_image(): pl.pallas_call(middle_kernel, out_shape=[image, jax.ShapeDtypeStruct((ang...  2 us
    pallas_call x1, Pallas kernels, merged_image(): pl.pallas_call(end_kernel, out_shape=image, in_specs=[VMEM] * 8 + [ANY],...  1.63 us
  transfers between devices with their start and end apart: 14, of which 5 were waited for; matrix products, arithmetic and copies ran while one was open for 0% of the time, Pallas kernels for 19%

profile of v6, /device:TPU:16, one launch (start us, length us, event | category | flops | bytes accessed | tf_op | source)
XLA Modules:
  0.0 46.7 jit_solution(10983411000327639898)
XLA Ops:
  0.0 0.0 copy-start
  0.0 1.2 %copy-done = bf16[2,32,8192]{2,1,0:T(8,128)(2,1)S(1)} copy-done((bf16[2,32,8192]{2,1,0:T(8,128)(2,1)S(1)}, bf16[2,32,8192]{2,1,0:T(8,128)(2,1)}, u32[]{:S(2)}) %copy-start) | copy-done | bytes 1048600
  1.2 1.0 %shard_map.64 = (bf16[8,64,128]{2,1,0:T(8,128)(2,1)S(1)}, bf16[8,64,128]{2,1,0:T(8,128)(2,1)S(1)}, bf16[16,64,384]{2,1,0:T(8,128)(2,1)}) custom-call(bf16[64,8192]{1,0:T(8,128)(2,1)S(1)} %bitcast.4), custom_call_target="tpu_custom_call" | custom-call | bytes 2097152 | tf_op jit(solution)/shard_map/pallas_call | solution.py:81
  2.3 0.0 collective-permute-start
  2.3 6.7 %all-to-all-start = ((bf16[16,64,384]{2,1,0:T(8,128)(2,1)}), bf16[16,64,384]{2,1,0:T(8,128)(2,1)S(1)}, u32[]{:S(2)}, u32[]{:S(2)}) async-start(bf16[16,64,384]{2,1,0:T(8,128)(2,1)} %get-tuple-element.38), calls=%async_computation | async-start | bytes 1572864 | tf_op jit(solution)/shard_map/all_to_all | solution.py:554
  9.0 0.0 collective-permute-done.relay_ref
  9.0 0.0 copy-start.4
  9.0 0.0 copy-start.5
  9.0 0.2 collective-permute-start.1
  9.3 1.5 %collective-permute-start.2 = (bf16[128,128]{1,0:T(8,128)(2,1)S(1)}, bf16[128,128]{1,0:T(8,128)(2,1)S(1)}, u32[]{:S(2)}, u32[]{:S(2)}) collective-permute-start(bf16[128,128]{1,0:T(8,128)(2,1)S(1)} %get-tuple-element.40), channel_id=1, source_target_pairs={{0,2},{1,3},{2,0},{3,1},{4,6},{5,7},{6,4},{7,5},{8,10},{9,11},{10,... | collective-permute-start | bytes 98312 | tf_op jit(solution)/shard_map/ppermute | solution.py:113
  10.7 0.2 collective-permute-start.3
  11.0 3.8 %collective-permute-start.4 = (bf16[128,128]{1,0:T(8,128)(2,1)S(1)}, bf16[128,128]{1,0:T(8,128)(2,1)S(1)}, u32[]{:S(2)}, u32[]{:S(2)}) collective-permute-start(bf16[128,128]{1,0:T(8,128)(2,1)S(1)} %get-tuple-element.42), channel_id=1, source_target_pairs={{0,4},{1,5},{2,6},{3,7},{4,0},{5,1},{6,2},{7,3},{8,12},{9,13},{10,... | collective-permute-start | bytes 98312 | tf_op jit(solution)/shard_map/ppermute | solution.py:113
  14.7 0.0 collective-permute-start.5
  14.7 0.0 collective-permute-done.1.refs_1_
  14.8 2.6 %collective-permute-start.6 = (bf16[128,128]{1,0:T(8,128)(2,1)S(1)}, bf16[128,128]{1,0:T(8,128)(2,1)S(1)}, u32[]{:S(2)}, u32[]{:S(2)}) collective-permute-start(bf16[128,128]{1,0:T(8,128)(2,1)S(1)} %get-tuple-element.44), channel_id=1, source_target_pairs={{0,6},{1,7},{2,4},{3,5},{4,2},{5,3},{6,0},{7,1},{8,14},{9,15},{10,... | collective-permute-start | bytes 98312 | tf_op jit(solution)/shard_map/ppermute | solution.py:113
  17.4 0.0 collective-permute-done.2.refs_2_
  17.4 0.2 collective-permute-start.7
  17.5 0.0 copy-done.4
  17.5 0.1 copy.8.flag_ref
  17.6 1.3 %shard_map.66 = (bf16[512,1024]{1,0:T(8,128)(2,1)S(1)}, f32[8,128]{1,0:T(8,128)S(1)}) custom-call(s32[1,2,1]{2,1,0:T(2,128)S(1)} %copy.8.flag_ref, bf16[128,128]{1,0:T(8,128)(2,1)S(1)} %get-tuple-element.47.after_ref.refs_0_), custom_call_target="tpu_custom_call" | custom-call | flops 9000000 | bytes 4194304 | tf_op jit(solution)/shard_map/pallas_call | solution.py:155
  18.9 0.0 collective-permute-done.3.refs_3_
  18.9 6.7 %collective-permute-done.4.refs_4_ = bf16[128,128]{1,0:T(8,128)(2,1)S(1)} collective-permute-done((bf16[128,128]{1,0:T(8,128)(2,1)S(1)}, bf16[128,128]{1,0:T(8,128)(2,1)S(1)}, u32[]{:S(2)}, u32[]{:S(2)}) %collective-permute-start.4) | collective-permute-done | bytes 32800 | tf_op jit(solution)/shard_map/ppermute | solution.py:113
  25.6 0.0 collective-permute-done.5.refs_5_
  25.6 2.2 %collective-permute-done.6.refs_6_ = bf16[128,128]{1,0:T(8,128)(2,1)S(1)} collective-permute-done((bf16[128,128]{1,0:T(8,128)(2,1)S(1)}, bf16[128,128]{1,0:T(8,128)(2,1)S(1)}, u32[]{:S(2)}, u32[]{:S(2)}) %collective-permute-start.6) | collective-permute-done | bytes 32800 | tf_op jit(solution)/shard_map/ppermute | solution.py:113
  27.8 0.0 collective-permute-done.7.refs_7_
  27.8 1.4 %all-to-all-done = bf16[16,64,384]{2,1,0:T(8,128)(2,1)S(1)} async-done(((bf16[16,64,384]{2,1,0:T(8,128)(2,1)}), bf16[16,64,384]{2,1,0:T(8,128)(2,1)S(1)}, u32[]{:S(2)}, u32[]{:S(2)}) %all-to-all-start) | async-done | bytes 786464 | tf_op jit(solution)/shard_map/all_to_all | solution.py:554
  29.2 0.7 %shard_map.67 = bf16[2,256,384]{2,1,0:T(8,128)(2,1)S(1)} custom-call(bf16[512,1024]{1,0:T(8,128)(2,1)S(1)} %get-tuple-element.37.rows_ref, bf16[1024,384]{1,0:T(8,128)(2,1)S(1)} %bitcast.2), custom_call_target="tpu_custom_call" | custom-call | flops 402653184 | bytes 3145728 | tf_op jit(solution)/shard_map/pallas_call | solution.py:331
  29.9 0.0 copy-start.1
  29.9 0.0 copy-start.3
  29.9 1.6 %collective-permute-start.9 = (bf16[2,256,384]{2,1,0:T(8,128)(2,1)S(1)}, bf16[2,256,384]{2,1,0:T(8,128)(2,1)S(1)}, u32[]{:S(2)}, u32[]{:S(2)}) collective-permute-start(bf16[2,256,384]{2,1,0:T(8,128)(2,1)S(1)} %shard_map.67), channel_id=1, source_target_pairs={{0,16},{16,0},{1,17},{17,1},{2,18},{18,2},{3,19},{19,3},{4,20},{20... | collective-permute-start | bytes 1179656 | tf_op jit(solution)/shard_map/ppermute | solution.py:516
  31.5 0.0 copy-done.5
  31.5 0.1 copy.10.offset_ref
  31.6 0.0 copy-start.2
  31.6 0.9 %shard_map.68 = (bf16[2,256,128]{2,1,0:T(8,128)(2,1)S(1)}, bf16[2,256,128]{2,1,0:T(8,128)(2,1)S(1)}, bf16[256,128]{1,0:T(8,128)(2,1)S(1)}, bf16[256,128]{1,0:T(8,128)(2,1)S(1)}) custom-call(f32[8,128]{1,0:T(8,128)S(1)} %get-tuple-element.36.side_ref, bf16[512,1024]{1,0:T(8,128)(2,1)S(1)} %get-tuple-element.37.rows_ref, ...), custom_call_target="tpu_custom_call" | custom-call | flops 268435456 | bytes 3145728 | tf_op jit(solution)/shard_map/pallas_call | solution.py:303
  32.5 0.1 collective-permute-start.10
  32.6 2.3 %collective-permute-start.11 = (bf16[256,128]{1,0:T(8,128)(2,1)S(1)}, bf16[256,128]{1,0:T(8,128)(2,1)S(1)}, u32[]{:S(2)}, u32[]{:S(2)}) collective-permute-start(bf16[256,128]{1,0:T(8,128)(2,1)S(1)} %get-tuple-element.53), channel_id=1, source_target_pairs={{1,2},{3,4},{5,6},{7,8},{9,10},{11,12},{13,14},{2,1},{4,3},{6,5},{... | collective-permute-start | bytes 196616 | tf_op jit(solution)/shard_map/ppermute | solution.py:347
  35.0 0.6 %collective-permute-start.8 = (bf16[2,256,128]{2,1,0:T(8,128)(2,1)S(1)}, bf16[2,256,128]{2,1,0:T(8,128)(2,1)S(1)}, u32[]{:S(2)}, u32[]{:S(2)}) collective-permute-start(bf16[2,256,128]{2,1,0:T(8,128)(2,1)S(1)} %get-tuple-element.48), channel_id=1, source_target_pairs={{0,16},{16,0},{1,17},{17,1},{2,18},{18,2},{3,19},{19,3},{4,20},{20... | collective-permute-start | bytes 393224 | tf_op jit(solution)/shard_map/ppermute | solution.py:516
  35.5 0.8 %shard_map.69.after_ref.own_ref = bf16[2,256,512]{2,1,0:T(8,128)(2,1)S(1)} custom-call(bf16[512,1024]{1,0:T(8,128)(2,1)S(1)} %get-tuple-element.37.rows_ref, bf16[1024,384]{1,0:T(8,128)(2,1)S(1)} %bitcast.3, bf16[2,256,128]{2,1,0:T(8,128)(2,1)S(1)} %get-tuple-element.49.outer_ref), custom_call_target="tpu_custom_call" | custom-call | flops 402653184 | bytes 3145728 | tf_op jit(solution)/shard_map/pallas_call | solution.py:331
  36.3 0.0 copy-done.1
  36.3 0.0 copy-done.3
  36.3 0.0 copy-done.2
  36.4 2.8 %shard_map.70 = (bf16[2,512,512]{2,1,0:T(8,128)(2,1)S(1)}, bf16[2,2,128,512]{3,2,1,0:T(8,128)(2,1)S(1)}, f32[2,2,512,512]{3,2,1,0:T(8,128)S(1)}, bf16[2,512,256]{2,1,0:T(8,128)(2,1)S(1)}, f32[8,128]{1,0:T(8,128)}) custom-call(s32[1,2,1]{2,1,0:T(2,128)S(1)} %copy.8.flag_ref, s32[1,2,1]{2,1,0:T(2,128)S(1)} %copy.10.offset_ref, f32[1,2]{1,0:T(1,128)S(1)} %copy-done.3, ...), custom_call_target="tpu_custom_call" | custom-call | flops 2300000000 | bytes 7340032 | tf_op jit(solution)/shard_map/pallas_call | solution.py:241
  39.2 0.0 collective-permute-done.10.first_ref
  39.2 0.0 collective-permute-done.11.second_ref
  39.2 0.2 shard_map.71
  39.4 1.6 %collective-permute-start.12 = (bf16[256,128]{1,0:T(8,128)(2,1)S(1)}, bf16[256,128]{1,0:T(8,128)(2,1)S(1)}, u32[]{:S(2)}, u32[]{:S(2)}) collective-permute-start(bf16[256,128]{1,0:T(8,128)(2,1)S(1)} %get-tuple-element.59), channel_id=1, source_target_pairs={{0,16},{16,0},{1,17},{17,1},{2,18},{18,2},{3,19},{19,3},{4,20},{20... | collective-permute-start | bytes 196616 | tf_op jit(solution)/shard_map/ppermute | solution.py:516
  40.9 1.1 %shard_map.72.merged_ref = f32[2,512,512]{2,1,0:T(8,128)S(1)} custom-call(bf16[2,256,512]{2,1,0:T(8,128)(2,1)S(1)} %shard_map.69.after_ref.own_ref, bf16[256,128]{1,0:T(8,128)(2,1)S(1)} %get-tuple-element.54.rims_ref, bf16[2,512,512]{2,1,0:T(8,128)(2,1)S(1)} %get-tuple-element.51.centre_ref, bf16[2,2,128,512]{3,2,1,0:T(8,128)(2,1)S(1)} %get-tuple-element.55.rim_ref, ...), custom_call_target="tpu_custom_call" | custom-call | flops 536870912 | bytes 8388608 | tf_op jit(solution)/shard_map/pallas_call | solution.py:472
  42.0 0.0 collective-permute-done.9.far_inner
  42.0 2.0 %shard_map.73 = (f32[2,512,512]{2,1,0:T(8,128)}, f32[512,256]{1,0:T(8,128)S(1)}) custom-call(bf16[2,256,384]{2,1,0:T(8,128)(2,1)S(1)} %collective-permute-done.9.far_inner, f32[2,512,512]{2,1,0:T(8,128)S(1)} %shard_map.72.merged_ref, bf16[2,512,512]{2,1,0:T(8,128)(2,1)S(1)} %get-tuple-element.51.centre_ref, ...), custom_call_target="tpu_custom_call" | custom-call | flops 536870912 | bytes 8388608 | tf_op jit(solution)/shard_map/pallas_call | solution.py:483
  44.0 0.3 collective-permute-done.8.far_outer
  44.4 0.7 %collective-permute-done.12.rims_ref = bf16[256,128]{1,0:T(8,128)(2,1)S(1)} collective-permute-done((bf16[256,128]{1,0:T(8,128)(2,1)S(1)}, bf16[256,128]{1,0:T(8,128)(2,1)S(1)}, u32[]{:S(2)}, u32[]{:S(2)}) %collective-permute-start.12) | collective-permute-done | bytes 65568 | tf_op jit(solution)/shard_map/ppermute | solution.py:516
  45.1 1.6 %shard_map.74 = f32[2,512,512]{2,1,0:T(8,128)} custom-call(bf16[2,256,128]{2,1,0:T(8,128)(2,1)S(1)} %collective-permute-done.8.far_outer, f32[512,256]{1,0:T(8,128)S(1)} %get-tuple-element.58.partial_ref, bf16[256,128]{1,0:T(8,128)(2,1)S(1)} %collective-permute-done.12.rims_ref, ...), custom_call_target="tpu_custom_call", output_to_operand_aliasing={{}: (8, {})} | custom-call | flops 536870912 | bytes 8388608 | tf_op jit(solution)/shard_map/pallas_call | solution.py:495
  (1 shorter events, 0.0 us)
Async XLA Ops:
  0.0 1.2 %copy-start = (bf16[2,32,8192]{2,1,0:T(8,128)(2,1)S(1)}, bf16[2,32,8192]{2,1,0:T(8,128)(2,1)}, u32[]{:S(2)}) copy-start(bf16[2,32,8192]{2,1,0:T(8,128)(2,1)} %param.6) | copy-start | bytes 3145732
  2.3 6.7 %collective-permute-start = (bf16[8,64,128]{2,1,0:T(8,128)(2,1)S(1)}, bf16[8,64,128]{2,1,0:T(8,128)(2,1)S(1)}, u32[]{:S(2)}, u32[]{:S(2)}) collective-permute-start(bf16[8,64,128]{2,1,0:T(8,128)(2,1)S(1)} %get-tuple-element.34), channel_id=1, source_target_pairs={{0,8},{1,9},{2,10},{3,11},{4,12},{5,13},{6,14},{7,15},{8,0},{9,1},... | collective-permute-start | bytes 393224 | tf_op jit(solution)/shard_map/ppermute | solution.py:113
  2.3 26.9 %all-to-all-start = ((bf16[16,64,384]{2,1,0:T(8,128)(2,1)}), bf16[16,64,384]{2,1,0:T(8,128)(2,1)S(1)}, u32[]{:S(2)}, u32[]{:S(2)}) async-start(bf16[16,64,384]{2,1,0:T(8,128)(2,1)} %get-tuple-element.38), calls=%async_computation | async-start | bytes 1572864 | tf_op jit(solution)/shard_map/all_to_all | solution.py:554
  9.0 8.6 %copy-start.4 = (s32[1,2,1]{1,2,0:T(1,128)S(1)}, s32[1,2,1]{1,2,0:T(1,128)}, u32[]{:S(2)}) copy-start(s32[1,2,1]{1,2,0:T(1,128)} %param.7) | copy-start | bytes 28
  9.0 22.5 %copy-start.5 = (s32[1,2,1]{1,2,0:T(1,128)S(1)}, s32[1,2,1]{1,2,0:T(1,128)}, u32[]{:S(2)}) copy-start(s32[1,2,1]{1,2,0:T(1,128)} %param.8) | copy-start | bytes 28
  9.0 5.7 %collective-permute-start.1 = (bf16[128,128]{1,0:T(8,128)(2,1)S(1)}, bf16[128,128]{1,0:T(8,128)(2,1)S(1)}, u32[]{:S(2)}, u32[]{:S(2)}) collective-permute-start(bf16[128,128]{1,0:T(8,128)(2,1)S(1)} %get-tuple-element.39), channel_id=1, source_target_pairs={{0,1},{1,0},{2,3},{3,2},{4,5},{5,4},{6,7},{7,6},{8,9},{9,8},{10,11... | collective-permute-start | bytes 98312 | tf_op jit(solution)/shard_map/ppermute | solution.py:113
  9.3 8.1 %collective-permute-start.2 = (bf16[128,128]{1,0:T(8,128)(2,1)S(1)}, bf16[128,128]{1,0:T(8,128)(2,1)S(1)}, u32[]{:S(2)}, u32[]{:S(2)}) collective-permute-start(bf16[128,128]{1,0:T(8,128)(2,1)S(1)} %get-tuple-element.40), channel_id=1, source_target_pairs={{0,2},{1,3},{2,0},{3,1},{4,6},{5,7},{6,4},{7,5},{8,10},{9,11},{10,... | collective-permute-start | bytes 98312 | tf_op jit(solution)/shard_map/ppermute | solution.py:113
  10.7 8.2 %collective-permute-start.3 = (bf16[128,128]{1,0:T(8,128)(2,1)S(1)}, bf16[128,128]{1,0:T(8,128)(2,1)S(1)}, u32[]{:S(2)}, u32[]{:S(2)}) collective-permute-start(bf16[128,128]{1,0:T(8,128)(2,1)S(1)} %get-tuple-element.41), channel_id=1, source_target_pairs={{0,3},{1,2},{2,1},{3,0},{4,7},{5,6},{6,5},{7,4},{8,11},{9,10},{10,... | collective-permute-start | bytes 98312 | tf_op jit(solution)/shard_map/ppermute | solution.py:113
  11.0 14.6 %collective-permute-start.4 = (bf16[128,128]{1,0:T(8,128)(2,1)S(1)}, bf16[128,128]{1,0:T(8,128)(2,1)S(1)}, u32[]{:S(2)}, u32[]{:S(2)}) collective-permute-start(bf16[128,128]{1,0:T(8,128)(2,1)S(1)} %get-tuple-element.42), channel_id=1, source_target_pairs={{0,4},{1,5},{2,6},{3,7},{4,0},{5,1},{6,2},{7,3},{8,12},{9,13},{10,... | collective-permute-start | bytes 98312 | tf_op jit(solution)/shard_map/ppermute | solution.py:113
  14.7 10.8 %collective-permute-start.5 = (bf16[128,128]{1,0:T(8,128)(2,1)S(1)}, bf16[128,128]{1,0:T(8,128)(2,1)S(1)}, u32[]{:S(2)}, u32[]{:S(2)}) collective-permute-start(bf16[128,128]{1,0:T(8,128)(2,1)S(1)} %get-tuple-element.43), channel_id=1, source_target_pairs={{0,5},{1,4},{2,7},{3,6},{4,1},{5,0},{6,3},{7,2},{8,13},{9,12},{10,... | collective-permute-start | bytes 98312 | tf_op jit(solution)/shard_map/ppermute | solution.py:113
  14.8 13.0 %collective-permute-start.6 = (bf16[128,128]{1,0:T(8,128)(2,1)S(1)}, bf16[128,128]{1,0:T(8,128)(2,1)S(1)}, u32[]{:S(2)}, u32[]{:S(2)}) collective-permute-start(bf16[128,128]{1,0:T(8,128)(2,1)S(1)} %get-tuple-element.44), channel_id=1, source_target_pairs={{0,6},{1,7},{2,4},{3,5},{4,2},{5,3},{6,0},{7,1},{8,14},{9,15},{10,... | collective-permute-start | bytes 98312 | tf_op jit(solution)/shard_map/ppermute | solution.py:113
  17.4 10.4 %collective-permute-start.7 = (bf16[128,128]{1,0:T(8,128)(2,1)S(1)}, bf16[128,128]{1,0:T(8,128)(2,1)S(1)}, u32[]{:S(2)}, u32[]{:S(2)}) collective-permute-start(bf16[128,128]{1,0:T(8,128)(2,1)S(1)} %get-tuple-element.45), channel_id=1, source_target_pairs={{0,7},{1,6},{2,5},{3,4},{4,3},{5,2},{6,1},{7,0},{8,15},{9,14},{10,... | collective-permute-start | bytes 98312 | tf_op jit(solution)/shard_map/ppermute | solution.py:113
  29.9 6.4 %copy-start.1 = (bf16[1,544,512]{2,1,0:T(8,128)(2,1)S(1)}, bf16[1,544,512]{2,1,0:T(8,128)(2,1)}, u32[]{:S(2)}) copy-start(bf16[1,544,512]{2,1,0:T(8,128)(2,1)} %range_ref.1) | copy-start | bytes 1671172
  29.9 6.4 %copy-start.3 = (f32[1,2]{1,0:T(1,128)S(1)}, f32[1,2]{1,0:T(1,128)}, u32[]{:S(2)}) copy-start(f32[1,2]{1,0:T(1,128)} %shift_ref.1) | copy-start | bytes 28
  29.9 12.1 %collective-permute-start.9 = (bf16[2,256,384]{2,1,0:T(8,128)(2,1)S(1)}, bf16[2,256,384]{2,1,0:T(8,128)(2,1)S(1)}, u32[]{:S(2)}, u32[]{:S(2)}) collective-permute-start(bf16[2,256,384]{2,1,0:T(8,128)(2,1)S(1)} %shard_map.67), channel_id=1, source_target_pairs={{0,16},{16,0},{1,17},{17,1},{2,18},{18,2},{3,19},{19,3},{4,20},{20... | collective-permute-start | bytes 1179656 | tf_op jit(solution)/shard_map/ppermute | solution.py:516
  31.6 4.8 %copy-start.2 = (bf16[1,2,512,256]{3,2,1,0:T(8,128)(2,1)S(1)}, bf16[1,2,512,256]{3,2,1,0:T(8,128)(2,1)}, u32[]{:S(2)}) copy-start(bf16[1,2,512,256]{3,2,1,0:T(8,128)(2,1)} %interp_ref.1) | copy-start | bytes 1572868
  32.5 6.6 %collective-permute-start.10 = (bf16[256,128]{1,0:T(8,128)(2,1)S(1)}, bf16[256,128]{1,0:T(8,128)(2,1)S(1)}, u32[]{:S(2)}, u32[]{:S(2)}) collective-permute-start(bf16[256,128]{1,0:T(8,128)(2,1)S(1)} %get-tuple-element.50), channel_id=1, source_target_pairs={{0,1},{2,3},{4,5},{6,7},{8,9},{10,11},{12,13},{14,15},{1,0},{3,2},... | collective-permute-start | bytes 196616 | tf_op jit(solution)/shard_map/ppermute | solution.py:347
  32.6 6.6 %collective-permute-start.11 = (bf16[256,128]{1,0:T(8,128)(2,1)S(1)}, bf16[256,128]{1,0:T(8,128)(2,1)S(1)}, u32[]{:S(2)}, u32[]{:S(2)}) collective-permute-start(bf16[256,128]{1,0:T(8,128)(2,1)S(1)} %get-tuple-element.53), channel_id=1, source_target_pairs={{1,2},{3,4},{5,6},{7,8},{9,10},{11,12},{13,14},{2,1},{4,3},{6,5},{... | collective-permute-start | bytes 196616 | tf_op jit(solution)/shard_map/ppermute | solution.py:347
  35.0 9.4 %collective-permute-start.8 = (bf16[2,256,128]{2,1,0:T(8,128)(2,1)S(1)}, bf16[2,256,128]{2,1,0:T(8,128)(2,1)S(1)}, u32[]{:S(2)}, u32[]{:S(2)}) collective-permute-start(bf16[2,256,128]{2,1,0:T(8,128)(2,1)S(1)} %get-tuple-element.48), channel_id=1, source_target_pairs={{0,16},{16,0},{1,17},{17,1},{2,18},{18,2},{3,19},{19,3},{4,20},{20... | collective-permute-start | bytes 393224 | tf_op jit(solution)/shard_map/ppermute | solution.py:516
  39.4 5.7 %collective-permute-start.12 = (bf16[256,128]{1,0:T(8,128)(2,1)S(1)}, bf16[256,128]{1,0:T(8,128)(2,1)S(1)}, u32[]{:S(2)}, u32[]{:S(2)}) collective-permute-start(bf16[256,128]{1,0:T(8,128)(2,1)S(1)} %get-tuple-element.59), channel_id=1, source_target_pairs={{0,16},{16,0},{1,17},{17,1},{2,18},{18,2},{3,19},{19,3},{4,20},{20... | collective-permute-start | bytes 196616 | tf_op jit(solution)/shard_map/ppermute | solution.py:516

commit v7 on v6

--- a/solution.py
+++ b/solution.py
@@ -266,24 +266,29 @@
 def outer_kernel(pieces, side_ref, rows_ref, *refs):
     own_side = side_ref[:1, :]
     me = lax.axis_index("rng")
-    own_ref, out_ref, *edge_refs = refs[pieces:-1]
-    pulses_ref = refs[-1]
+    own_ref, *sent_refs = refs[pieces : pieces + 4]
+    pulses_ref, *held_refs, sems = refs[pieces + 4 :]
+    copies = [
+        pltpu.make_async_copy(held, sent, sems.at[i])
+        for i, (held, sent) in enumerate(zip(held_refs, sent_refs))
+    ]
     rows = refs[0].shape[0] // 2
     for d, ref in enumerate(refs[:pieces]):
         for t in range(2):
             place = pl.multiple_of((me ^ (d + t * pieces)) * rows, rows)
             pulses_ref[pl.ds(place, rows), :] = ref[t * rows : (t + 1) * rows, :]
     pulses = pulses_ref[...]
+    half = own_ref.shape[1]
+    out_parts = dot(rows_ref[...], pulses)
+    for part in range(2):
+        held_refs[0][part] = out_parts[part * half : (part + 1) * half].astype(BF16)
+    copies[0].start()
     own_parts = dot(rows_ref[...], alternating(pulses, rows // 2))
-    out_parts = dot(rows_ref[...], pulses)
-    half = own_ref.shape[1]
     rim = LANES // 4
     lane = lax.broadcasted_iota(jnp.int32, (1, LANES), 1)
     edges = [0.0, 0.0]
     for part in range(2):
         own, out = (value[part * half : (part + 1) * half] for value in (own_parts, out_parts))
-        own_ref[part] = own.astype(BF16)
-        out_ref[part] = out.astype(BF16)
         for side in range(2):
             value = jnp.where(own_side == side, own, out)
             group = 2 * part + side
@@ -292,8 +297,14 @@
                 moved = pltpu.roll(value, turn, 1) if turn else value
                 edges[end] = edges[end] + jnp.where(lane // rim == group, moved, 0.0)
     even = me % 2 == 0
-    edge_refs[0][...] = jnp.where(even, edges[1], edges[0]).astype(BF16)
-    edge_refs[1][...] = jnp.where(even, edges[0], edges[1]).astype(BF16)
+    held_refs[1][...] = jnp.where(even, edges[1], edges[0]).astype(BF16)
+    held_refs[2][...] = jnp.where(even, edges[0], edges[1]).astype(BF16)
+    copies[1].start()
+    copies[2].start()
+    for part in range(2):
+        own_ref[part] = own_parts[part * half : (part + 1) * half].astype(BF16)
+    for copy in copies:
+        copy.wait()
 
 
 def outer_image(own_side, rows, pieces):
@@ -304,8 +315,12 @@
         functools.partial(outer_kernel, len(pieces)),
         out_shape=[image, image, edge, edge],
         in_specs=[VMEM] * (2 + len(pieces)),
-        out_specs=[VMEM] * 4,
-        scratch_shapes=[pltpu.VMEM((side, LANES), BF16)],
+        out_specs=[VMEM] + [ANY] * 3,
+        scratch_shapes=[
+            pltpu.VMEM((side, LANES), BF16),
+            *(pltpu.VMEM(value.shape, BF16) for value in (image, edge, edge)),
+            pltpu.SemaphoreType.DMA((3,)),
+        ],
         compiler_params=params(10),
         cost_estimate=pl.CostEstimate(
             flops=4 * angles * side * LANES, bytes_accessed=3 * MIB, transcendentals=0
@@ -555,12 +570,13 @@
     sends = joined(near_blocks, relay)
     pieces = [across(value, d) if d else value for d, value in enumerate(sends)]
     matrix, own_side = filter_table(fore_flag, angles, local_pulses, sends[0])
-    pulses = after(pulses, *pieces[1:]).reshape(2 * local_pulses * devices, bins - LANES)
+    own_outer, out_outer, *edges = outer_image(own_side, matrix, pieces)
+    pulses = after(pulses, out_outer).reshape(2 * local_pulses * devices, bins - LANES)
     out_inner = inner_image(partner_rows_kernel, angles, matrix, pulses)
-    pieces[0] = after(pieces[0], out_inner)
-    own_outer, out_outer, *edges = outer_image(own_side, matrix, pieces)
     far = [from_partner(value, 1) for value in (out_outer, out_inner)]
+    edges = [after(edge, out_inner) for edge in edges]
     edges = exchanged(edges[0], 0), exchanged(edges[1], 1)
+    pulses = after(pulses, far[0])
     own_kernel = functools.partial(own_rows_kernel, local_pulses)
     own = inner_image(own_kernel, angles, matrix, pulses, (own_outer,))
     tables = merge_tables(0, 1, *settings, own)

time: 47.3 us -> 50.3 us (1.063)
  waiting for transfers between devices: 11.3 us -> 13.5 us
  local copies, waits for them, and re-layouts: 1.44 us -> 2.06 us
  Pallas kernels: 12.4 us -> 13 us
    ppermute x3, waiting for transfers between devices: 1.03 us -> 3.6 us  [from_partner(): return lax.ppermute(value, 'sub', pairs)]
    all_to_all x1, waiting for transfers between devices: 1.4 us -> 0.01 us  [on_device(): lax.all_to_all(blocks, 'rng', split_axis=0, concat_axis=0, tiled=True)]
    ppermute x2, waiting for transfers between devices: 0.02 us -> 1 us  [exchanged(): return lax.ppermute(value, 'rng', pairs + [(j, i) for i, j in pairs] + ends)]
    unnamed x14 -> x16, local copies, waits for them, and re-layouts: 1.44 us -> 2.06 us
    pallas_call x1, Pallas kernels: 0.92 us -> 1.46 us  [outer_image(): pl.pallas_call(functools.partial(outer_kernel, len(pieces)), out_shape=[i...]
  transfers between devices with their start and end apart: 14 -> 14, of which waited for: 5 -> 4; matrix products, arithmetic and copies ran while one was open for 0% -> 0% of each run, Pallas kernels for 19% -> 21%
where the time goes in v7:
time: 50.3 us; the launch traced here: 49.5 us
  starting transfers between devices  20.8 us (41%)
  waiting for transfers between devices  13.5 us (27%)
  Pallas kernels  13 us (26%)
  local copies, waits for them, and re-layouts  2.06 us (4%)
    ppermute x8, waiting for transfers between devices, across(): return lax.ppermute(value, 'rng', [(i, i ^ mask) for i in range(devices)])  8.89 us
    ppermute x8, starting transfers between devices, across(): return lax.ppermute(value, 'rng', [(i, i ^ mask) for i in range(devices)])  8.48 us
    all_to_all x1, starting transfers between devices, on_device(): lax.all_to_all(blocks, 'rng', split_axis=0, concat_axis=0, tiled=True)  6.72 us
    ppermute x3, starting transfers between devices, from_partner(): return lax.ppermute(value, 'sub', pairs)  3.68 us
    ppermute x3, waiting for transfers between devices, from_partner(): return lax.ppermute(value, 'sub', pairs)  3.6 us
    pallas_call x1, Pallas kernels, merge_tables(): pl.pallas_call(functools.partial(merge_table_kernel, level, stride), out_...  2.8 us
    unnamed x16, local copies, waits for them, and re-layouts  2.06 us
    pallas_call x1, Pallas kernels, merged_image(): pl.pallas_call(middle_kernel, out_shape=[image, jax.ShapeDtypeStruct((ang...  1.99 us
  transfers between devices with their start and end apart: 14, of which 4 were waited for; matrix products, arithmetic and copies ran while one was open for 0% of the time, Pallas kernels for 21%

profile of v7, /device:TPU:16, one launch (start us, length us, event | category | flops | bytes accessed | tf_op | source)
XLA Modules:
  0.0 49.5 jit_solution(16825094199026174549)
XLA Ops:
  0.0 0.0 copy-start
  0.0 1.2 %copy-done = bf16[2,32,8192]{2,1,0:T(8,128)(2,1)S(1)} copy-done((bf16[2,32,8192]{2,1,0:T(8,128)(2,1)S(1)}, bf16[2,32,8192]{2,1,0:T(8,128)(2,1)}, u32[]{:S(2)}) %copy-start) | copy-done | bytes 1048600
  1.2 1.0 %shard_map.64 = (bf16[8,64,128]{2,1,0:T(8,128)(2,1)S(1)}, bf16[8,64,128]{2,1,0:T(8,128)(2,1)S(1)}, bf16[16,64,384]{2,1,0:T(8,128)(2,1)}) custom-call(bf16[64,8192]{1,0:T(8,128)(2,1)S(1)} %bitcast.4), custom_call_target="tpu_custom_call" | custom-call | bytes 2097152 | tf_op jit(solution)/shard_map/pallas_call | solution.py:81
  2.3 0.0 collective-permute-start
  2.3 6.7 %all-to-all-start = ((bf16[16,64,384]{2,1,0:T(8,128)(2,1)}), bf16[16,64,384]{2,1,0:T(8,128)(2,1)S(1)}, u32[]{:S(2)}, u32[]{:S(2)}) async-start(bf16[16,64,384]{2,1,0:T(8,128)(2,1)} %get-tuple-element.48), calls=%async_computation | async-start | bytes 1572864 | tf_op jit(solution)/shard_map/all_to_all | solution.py:569
  9.0 0.0 collective-permute-done.relay_ref
  9.0 0.0 copy-start.5
  9.0 0.0 copy-start.6
  9.0 0.2 collective-permute-start.1
  9.3 1.5 %collective-permute-start.2 = (bf16[128,128]{1,0:T(8,128)(2,1)S(1)}, bf16[128,128]{1,0:T(8,128)(2,1)S(1)}, u32[]{:S(2)}, u32[]{:S(2)}) collective-permute-start(bf16[128,128]{1,0:T(8,128)(2,1)S(1)} %get-tuple-element.41), channel_id=1, source_target_pairs={{0,2},{1,3},{2,0},{3,1},{4,6},{5,7},{6,4},{7,5},{8,10},{9,11},{10,... | collective-permute-start | bytes 98312 | tf_op jit(solution)/shard_map/ppermute | solution.py:113
  10.7 0.2 collective-permute-start.3
  11.0 3.8 %collective-permute-start.4 = (bf16[128,128]{1,0:T(8,128)(2,1)S(1)}, bf16[128,128]{1,0:T(8,128)(2,1)S(1)}, u32[]{:S(2)}, u32[]{:S(2)}) collective-permute-start(bf16[128,128]{1,0:T(8,128)(2,1)S(1)} %get-tuple-element.43), channel_id=1, source_target_pairs={{0,4},{1,5},{2,6},{3,7},{4,0},{5,1},{6,2},{7,3},{8,12},{9,13},{10,... | collective-permute-start | bytes 98312 | tf_op jit(solution)/shard_map/ppermute | solution.py:113
  14.7 0.0 collective-permute-start.5
  14.7 0.0 collective-permute-done.1.refs_1_
  14.8 2.6 %collective-permute-start.6 = (bf16[128,128]{1,0:T(8,128)(2,1)S(1)}, bf16[128,128]{1,0:T(8,128)(2,1)S(1)}, u32[]{:S(2)}, u32[]{:S(2)}) collective-permute-start(bf16[128,128]{1,0:T(8,128)(2,1)S(1)} %get-tuple-element.45), channel_id=1, source_target_pairs={{0,6},{1,7},{2,4},{3,5},{4,2},{5,3},{6,0},{7,1},{8,14},{9,15},{10,... | collective-permute-start | bytes 98312 | tf_op jit(solution)/shard_map/ppermute | solution.py:113
  17.4 0.0 collective-permute-done.2.refs_2_
  17.4 0.2 collective-permute-start.7
  17.5 0.0 copy-done.5
  17.5 0.1 copy.8.flag_ref
  17.6 1.3 %shard_map.66 = (bf16[512,1024]{1,0:T(8,128)(2,1)S(1)}, f32[8,128]{1,0:T(8,128)S(1)}) custom-call(s32[1,2,1]{2,1,0:T(2,128)S(1)} %copy.8.flag_ref, bf16[128,128]{1,0:T(8,128)(2,1)S(1)} %get-tuple-element.37.after_ref.refs_0_), custom_call_target="tpu_custom_call" | custom-call | flops 9000000 | bytes 4194304 | tf_op jit(solution)/shard_map/pallas_call | solution.py:155
  18.9 0.0 collective-permute-done.3.refs_3_
  18.9 6.7 %collective-permute-done.4.refs_4_ = bf16[128,128]{1,0:T(8,128)(2,1)S(1)} collective-permute-done((bf16[128,128]{1,0:T(8,128)(2,1)S(1)}, bf16[128,128]{1,0:T(8,128)(2,1)S(1)}, u32[]{:S(2)}, u32[]{:S(2)}) %collective-permute-start.4) | collective-permute-done | bytes 32800 | tf_op jit(solution)/shard_map/ppermute | solution.py:113
  25.6 0.0 collective-permute-done.5.refs_5_
  25.6 2.2 %collective-permute-done.6.refs_6_ = bf16[128,128]{1,0:T(8,128)(2,1)S(1)} collective-permute-done((bf16[128,128]{1,0:T(8,128)(2,1)S(1)}, bf16[128,128]{1,0:T(8,128)(2,1)S(1)}, u32[]{:S(2)}, u32[]{:S(2)}) %collective-permute-start.6) | collective-permute-done | bytes 32800 | tf_op jit(solution)/shard_map/ppermute | solution.py:113
  27.8 0.0 collective-permute-done.7.refs_7_
  27.8 1.5 %shard_map.67 = (bf16[2,256,128]{2,1,0:T(8,128)(2,1)S(1)}, bf16[2,256,128]{2,1,0:T(8,128)(2,1)}, bf16[256,128]{1,0:T(8,128)(2,1)S(1)}, bf16[256,128]{1,0:T(8,128)(2,1)S(1)}) custom-call(f32[8,128]{1,0:T(8,128)S(1)} %get-tuple-element.38.side_ref, bf16[512,1024]{1,0:T(8,128)(2,1)S(1)} %get-tuple-element.39.rows_ref, ...), custom_call_target="tpu_custom_call" | custom-call | flops 268435456 | bytes 3145728 | tf_op jit(solution)/shard_map/pallas_call | solution.py:314
  29.2 0.0 copy-start.3
  29.3 0.6 %copy-done.3 = bf16[256,128]{1,0:T(8,128)(2,1)} copy-done((bf16[256,128]{1,0:T(8,128)(2,1)}, bf16[256,128]{1,0:T(8,128)(2,1)S(1)}, u32[]{:S(2)}) %copy-start.3) | copy-done | bytes 65560
  29.9 1.5 %collective-permute-start.8 = (bf16[2,256,128]{2,1,0:T(8,128)(2,1)}, bf16[2,256,128]{2,1,0:T(8,128)(2,1)S(1)}, u32[]{:S(2)}, u32[]{:S(2)}) collective-permute-start(bf16[2,256,128]{2,1,0:T(8,128)(2,1)} %get-tuple-element.47), channel_id=1, source_target_pairs={{0,16},{16,0},{1,17},{17,1},{2,18},{18,2},{3,19},{19,3},{4,20},{20... | collective-permute-start | bytes 393224 | tf_op jit(solution)/shard_map/ppermute | solution.py:531
  31.4 0.0 all-to-all-done
  31.4 0.0 copy-start.1
  31.4 0.0 copy-start.4
  31.4 0.7 %shard_map.68 = bf16[2,256,384]{2,1,0:T(8,128)(2,1)S(1)} custom-call(bf16[512,1024]{1,0:T(8,128)(2,1)S(1)} %get-tuple-element.39.rows_ref, bf16[1024,384]{1,0:T(8,128)(2,1)S(1)} %bitcast.2), custom_call_target="tpu_custom_call" | custom-call | flops 402653184 | bytes 3145728 | tf_op jit(solution)/shard_map/pallas_call | solution.py:346
  32.1 0.6 %collective-permute-start.9 = (bf16[2,256,384]{2,1,0:T(8,128)(2,1)S(1)}, bf16[2,256,384]{2,1,0:T(8,128)(2,1)S(1)}, u32[]{:S(2)}, u32[]{:S(2)}) collective-permute-start(bf16[2,256,384]{2,1,0:T(8,128)(2,1)S(1)} %shard_map.68), channel_id=1, source_target_pairs={{0,16},{16,0},{1,17},{17,1},{2,18},{18,2},{3,19},{19,3},{4,20},{20... | collective-permute-start | bytes 1179656 | tf_op jit(solution)/shard_map/ppermute | solution.py:531
  32.7 0.0 copy-done.6
  32.7 0.1 copy.10.offset_ref
  32.8 0.0 copy-start.2
  32.8 3.6 %collective-permute-done.8.far_outer = bf16[2,256,128]{2,1,0:T(8,128)(2,1)S(1)} collective-permute-done((bf16[2,256,128]{2,1,0:T(8,128)(2,1)}, bf16[2,256,128]{2,1,0:T(8,128)(2,1)S(1)}, u32[]{:S(2)}, u32[]{:S(2)}) %collective-permute-start.8) | collective-permute-done | bytes 131104 | tf_op jit(solution)/shard_map/ppermute | solution.py:531
  36.4 0.0 collective-permute-start.10
  36.4 1.9 %collective-permute-start.11 = (bf16[256,128]{1,0:T(8,128)(2,1)S(1)}, bf16[256,128]{1,0:T(8,128)(2,1)S(1)}, u32[]{:S(2)}, u32[]{:S(2)}) collective-permute-start(bf16[256,128]{1,0:T(8,128)(2,1)S(1)} %get-tuple-element.57), channel_id=1, source_target_pairs={{1,2},{3,4},{5,6},{7,8},{9,10},{11,12},{13,14},{2,1},{4,3},{6,5},{... | collective-permute-start | bytes 196616 | tf_op jit(solution)/shard_map/ppermute | solution.py:362
  38.3 0.8 %shard_map.69.after_ref.own_ref = bf16[2,256,512]{2,1,0:T(8,128)(2,1)S(1)} custom-call(bf16[512,1024]{1,0:T(8,128)(2,1)S(1)} %get-tuple-element.39.rows_ref, bf16[1024,384]{1,0:T(8,128)(2,1)S(1)} %bitcast.3, bf16[2,256,128]{2,1,0:T(8,128)(2,1)S(1)} %get-tuple-element.51.outer_ref), custom_call_target="tpu_custom_call" | custom-call | flops 402653184 | bytes 3145728 | tf_op jit(solution)/shard_map/pallas_call | solution.py:346
  39.1 0.0 copy-done.1
  39.1 0.0 copy-done.4
  39.1 0.0 copy-done.2
  39.2 2.8 %shard_map.70 = (bf16[2,512,512]{2,1,0:T(8,128)(2,1)S(1)}, bf16[2,2,128,512]{3,2,1,0:T(8,128)(2,1)S(1)}, f32[2,2,512,512]{3,2,1,0:T(8,128)S(1)}, bf16[2,512,256]{2,1,0:T(8,128)(2,1)S(1)}, f32[8,128]{1,0:T(8,128)}) custom-call(s32[1,2,1]{2,1,0:T(2,128)S(1)} %copy.8.flag_ref, s32[1,2,1]{2,1,0:T(2,128)S(1)} %copy.10.offset_ref, f32[1,2]{1,0:T(1,128)S(1)} %copy-done.4, ...), custom_call_target="tpu_custom_call" | custom-call | flops 2300000000 | bytes 7340032 | tf_op jit(solution)/shard_map/pallas_call | solution.py:241
  42.0 0.0 collective-permute-done.10.first_ref
  42.0 1.0 %collective-permute-done.11.second_ref = bf16[256,128]{1,0:T(8,128)(2,1)S(1)} collective-permute-done((bf16[256,128]{1,0:T(8,128)(2,1)S(1)}, bf16[256,128]{1,0:T(8,128)(2,1)S(1)}, u32[]{:S(2)}, u32[]{:S(2)}) %collective-permute-start.11) | collective-permute-done | bytes 65568 | tf_op jit(solution)/shard_map/ppermute | solution.py:362
  43.0 0.2 shard_map.71
  43.1 1.6 %collective-permute-start.12 = (bf16[256,128]{1,0:T(8,128)(2,1)S(1)}, bf16[256,128]{1,0:T(8,128)(2,1)S(1)}, u32[]{:S(2)}, u32[]{:S(2)}) collective-permute-start(bf16[256,128]{1,0:T(8,128)(2,1)S(1)} %get-tuple-element.63), channel_id=1, source_target_pairs={{0,16},{16,0},{1,17},{17,1},{2,18},{18,2},{3,19},{19,3},{4,20},{20... | collective-permute-start | bytes 196616 | tf_op jit(solution)/shard_map/ppermute | solution.py:531
  44.7 1.1 %shard_map.72.merged_ref = f32[2,512,512]{2,1,0:T(8,128)S(1)} custom-call(bf16[2,256,512]{2,1,0:T(8,128)(2,1)S(1)} %shard_map.69.after_ref.own_ref, bf16[256,128]{1,0:T(8,128)(2,1)S(1)} %get-tuple-element.58.rims_ref, bf16[2,512,512]{2,1,0:T(8,128)(2,1)S(1)} %get-tuple-element.54.centre_ref, bf16[2,2,128,512]{3,2,1,0:T(8,128)(2,1)S(1)} %get-tuple-element.59.rim_ref, ...), custom_call_target="tpu_custom_call" | custom-call | flops 536870912 | bytes 8388608 | tf_op jit(solution)/shard_map/pallas_call | solution.py:487
  45.8 0.0 collective-permute-done.9.far_inner
  45.8 2.0 %shard_map.73 = (f32[2,512,512]{2,1,0:T(8,128)}, f32[512,256]{1,0:T(8,128)S(1)}) custom-call(bf16[2,256,384]{2,1,0:T(8,128)(2,1)S(1)} %collective-permute-done.9.far_inner, f32[2,512,512]{2,1,0:T(8,128)S(1)} %shard_map.72.merged_ref, bf16[2,512,512]{2,1,0:T(8,128)(2,1)S(1)} %get-tuple-element.54.centre_ref, ...), custom_call_target="tpu_custom_call" | custom-call | flops 536870912 | bytes 8388608 | tf_op jit(solution)/shard_map/pallas_call | solution.py:498
  47.8 0.0 collective-permute-done.12.rims_ref
  47.8 1.6 %shard_map.74 = f32[2,512,512]{2,1,0:T(8,128)} custom-call(bf16[2,256,128]{2,1,0:T(8,128)(2,1)S(1)} %collective-permute-done.8.far_outer, f32[512,256]{1,0:T(8,128)S(1)} %get-tuple-element.62.partial_ref, bf16[256,128]{1,0:T(8,128)(2,1)S(1)} %collective-permute-done.12.rims_ref, ...), custom_call_target="tpu_custom_call", output_to_operand_aliasing={{}: (8, {})} | custom-call | flops 536870912 | bytes 8388608 | tf_op jit(solution)/shard_map/pallas_call | solution.py:510
  (1 shorter events, 0.0 us)
Async XLA Ops:
  0.0 1.2 %copy-start = (bf16[2,32,8192]{2,1,0:T(8,128)(2,1)S(1)}, bf16[2,32,8192]{2,1,0:T(8,128)(2,1)}, u32[]{:S(2)}) copy-start(bf16[2,32,8192]{2,1,0:T(8,128)(2,1)} %param.6) | copy-start | bytes 3145732
  2.3 6.7 %collective-permute-start = (bf16[8,64,128]{2,1,0:T(8,128)(2,1)S(1)}, bf16[8,64,128]{2,1,0:T(8,128)(2,1)S(1)}, u32[]{:S(2)}, u32[]{:S(2)}) collective-permute-start(bf16[8,64,128]{2,1,0:T(8,128)(2,1)S(1)} %get-tuple-element.36), channel_id=1, source_target_pairs={{0,8},{1,9},{2,10},{3,11},{4,12},{5,13},{6,14},{7,15},{8,0},{9,1},... | collective-permute-start | bytes 393224 | tf_op jit(solution)/shard_map/ppermute | solution.py:113
  2.3 29.1 %all-to-all-start = ((bf16[16,64,384]{2,1,0:T(8,128)(2,1)}), bf16[16,64,384]{2,1,0:T(8,128)(2,1)S(1)}, u32[]{:S(2)}, u32[]{:S(2)}) async-start(bf16[16,64,384]{2,1,0:T(8,128)(2,1)} %get-tuple-element.48), calls=%async_computation | async-start | bytes 1572864 | tf_op jit(solution)/shard_map/all_to_all | solution.py:569
  9.0 8.6 %copy-start.5 = (s32[1,2,1]{1,2,0:T(1,128)S(1)}, s32[1,2,1]{1,2,0:T(1,128)}, u32[]{:S(2)}) copy-start(s32[1,2,1]{1,2,0:T(1,128)} %param.7) | copy-start | bytes 28
  9.0 23.7 %copy-start.6 = (s32[1,2,1]{1,2,0:T(1,128)S(1)}, s32[1,2,1]{1,2,0:T(1,128)}, u32[]{:S(2)}) copy-start(s32[1,2,1]{1,2,0:T(1,128)} %param.8) | copy-start | bytes 28
  9.0 5.7 %collective-permute-start.1 = (bf16[128,128]{1,0:T(8,128)(2,1)S(1)}, bf16[128,128]{1,0:T(8,128)(2,1)S(1)}, u32[]{:S(2)}, u32[]{:S(2)}) collective-permute-start(bf16[128,128]{1,0:T(8,128)(2,1)S(1)} %get-tuple-element.40), channel_id=1, source_target_pairs={{0,1},{1,0},{2,3},{3,2},{4,5},{5,4},{6,7},{7,6},{8,9},{9,8},{10,11... | collective-permute-start | bytes 98312 | tf_op jit(solution)/shard_map/ppermute | solution.py:113
  9.3 8.1 %collective-permute-start.2 = (bf16[128,128]{1,0:T(8,128)(2,1)S(1)}, bf16[128,128]{1,0:T(8,128)(2,1)S(1)}, u32[]{:S(2)}, u32[]{:S(2)}) collective-permute-start(bf16[128,128]{1,0:T(8,128)(2,1)S(1)} %get-tuple-element.41), channel_id=1, source_target_pairs={{0,2},{1,3},{2,0},{3,1},{4,6},{5,7},{6,4},{7,5},{8,10},{9,11},{10,... | collective-permute-start | bytes 98312 | tf_op jit(solution)/shard_map/ppermute | solution.py:113
  10.7 8.2 %collective-permute-start.3 = (bf16[128,128]{1,0:T(8,128)(2,1)S(1)}, bf16[128,128]{1,0:T(8,128)(2,1)S(1)}, u32[]{:S(2)}, u32[]{:S(2)}) collective-permute-start(bf16[128,128]{1,0:T(8,128)(2,1)S(1)} %get-tuple-element.42), channel_id=1, source_target_pairs={{0,3},{1,2},{2,1},{3,0},{4,7},{5,6},{6,5},{7,4},{8,11},{9,10},{10,... | collective-permute-start | bytes 98312 | tf_op jit(solution)/shard_map/ppermute | solution.py:113
  11.0 14.6 %collective-permute-start.4 = (bf16[128,128]{1,0:T(8,128)(2,1)S(1)}, bf16[128,128]{1,0:T(8,128)(2,1)S(1)}, u32[]{:S(2)}, u32[]{:S(2)}) collective-permute-start(bf16[128,128]{1,0:T(8,128)(2,1)S(1)} %get-tuple-element.43), channel_id=1, source_target_pairs={{0,4},{1,5},{2,6},{3,7},{4,0},{5,1},{6,2},{7,3},{8,12},{9,13},{10,... | collective-permute-start | bytes 98312 | tf_op jit(solution)/shard_map/ppermute | solution.py:113
  14.7 10.8 %collective-permute-start.5 = (bf16[128,128]{1,0:T(8,128)(2,1)S(1)}, bf16[128,128]{1,0:T(8,128)(2,1)S(1)}, u32[]{:S(2)}, u32[]{:S(2)}) collective-permute-start(bf16[128,128]{1,0:T(8,128)(2,1)S(1)} %get-tuple-element.44), channel_id=1, source_target_pairs={{0,5},{1,4},{2,7},{3,6},{4,1},{5,0},{6,3},{7,2},{8,13},{9,12},{10,... | collective-permute-start | bytes 98312 | tf_op jit(solution)/shard_map/ppermute | solution.py:113
  14.8 13.0 %collective-permute-start.6 = (bf16[128,128]{1,0:T(8,128)(2,1)S(1)}, bf16[128,128]{1,0:T(8,128)(2,1)S(1)}, u32[]{:S(2)}, u32[]{:S(2)}) collective-permute-start(bf16[128,128]{1,0:T(8,128)(2,1)S(1)} %get-tuple-element.45), channel_id=1, source_target_pairs={{0,6},{1,7},{2,4},{3,5},{4,2},{5,3},{6,0},{7,1},{8,14},{9,15},{10,... | collective-permute-start | bytes 98312 | tf_op jit(solution)/shard_map/ppermute | solution.py:113
  17.4 10.4 %collective-permute-start.7 = (bf16[128,128]{1,0:T(8,128)(2,1)S(1)}, bf16[128,128]{1,0:T(8,128)(2,1)S(1)}, u32[]{:S(2)}, u32[]{:S(2)}) collective-permute-start(bf16[128,128]{1,0:T(8,128)(2,1)S(1)} %get-tuple-element.46), channel_id=1, source_target_pairs={{0,7},{1,6},{2,5},{3,4},{4,3},{5,2},{6,1},{7,0},{8,15},{9,14},{10,... | collective-permute-start | bytes 98312 | tf_op jit(solution)/shard_map/ppermute | solution.py:113
  29.2 0.6 %copy-start.3 = (bf16[256,128]{1,0:T(8,128)(2,1)}, bf16[256,128]{1,0:T(8,128)(2,1)S(1)}, u32[]{:S(2)}) copy-start(bf16[256,128]{1,0:T(8,128)(2,1)S(1)} %get-tuple-element.53) | copy-start | bytes 196612
  29.9 6.5 %collective-permute-start.8 = (bf16[2,256,128]{2,1,0:T(8,128)(2,1)}, bf16[2,256,128]{2,1,0:T(8,128)(2,1)S(1)}, u32[]{:S(2)}, u32[]{:S(2)}) collective-permute-start(bf16[2,256,128]{2,1,0:T(8,128)(2,1)} %get-tuple-element.47), channel_id=1, source_target_pairs={{0,16},{16,0},{1,17},{17,1},{2,18},{18,2},{3,19},{19,3},{4,20},{20... | collective-permute-start | bytes 393224 | tf_op jit(solution)/shard_map/ppermute | solution.py:531
  31.4 7.7 %copy-start.1 = (bf16[1,544,512]{2,1,0:T(8,128)(2,1)S(1)}, bf16[1,544,512]{2,1,0:T(8,128)(2,1)}, u32[]{:S(2)}) copy-start(bf16[1,544,512]{2,1,0:T(8,128)(2,1)} %range_ref.1) | copy-start | bytes 1671172
  31.4 7.7 %copy-start.4 = (f32[1,2]{1,0:T(1,128)S(1)}, f32[1,2]{1,0:T(1,128)}, u32[]{:S(2)}) copy-start(f32[1,2]{1,0:T(1,128)} %shift_ref.1) | copy-start | bytes 28
  32.1 13.7 %collective-permute-start.9 = (bf16[2,256,384]{2,1,0:T(8,128)(2,1)S(1)}, bf16[2,256,384]{2,1,0:T(8,128)(2,1)S(1)}, u32[]{:S(2)}, u32[]{:S(2)}) collective-permute-start(bf16[2,256,384]{2,1,0:T(8,128)(2,1)S(1)} %shard_map.68), channel_id=1, source_target_pairs={{0,16},{16,0},{1,17},{17,1},{2,18},{18,2},{3,19},{19,3},{4,20},{20... | collective-permute-start | bytes 1179656 | tf_op jit(solution)/shard_map/ppermute | solution.py:531
  32.8 6.4 %copy-start.2 = (bf16[1,2,512,256]{3,2,1,0:T(8,128)(2,1)S(1)}, bf16[1,2,512,256]{3,2,1,0:T(8,128)(2,1)}, u32[]{:S(2)}) copy-start(bf16[1,2,512,256]{3,2,1,0:T(8,128)(2,1)} %interp_ref.1) | copy-start | bytes 1572868
  36.4 5.6 %collective-permute-start.10 = (bf16[256,128]{1,0:T(8,128)(2,1)}, bf16[256,128]{1,0:T(8,128)(2,1)S(1)}, u32[]{:S(2)}, u32[]{:S(2)}) collective-permute-start(bf16[256,128]{1,0:T(8,128)(2,1)} %copy-done.3), channel_id=1, source_target_pairs={{0,1},{2,3},{4,5},{6,7},{8,9},{10,11},{12,13},{14,15},{1,0},{3,2},... | collective-permute-start | bytes 196616 | tf_op jit(solution)/shard_map/ppermute | solution.py:362
  36.4 6.6 %collective-permute-start.11 = (bf16[256,128]{1,0:T(8,128)(2,1)S(1)}, bf16[256,128]{1,0:T(8,128)(2,1)S(1)}, u32[]{:S(2)}, u32[]{:S(2)}) collective-permute-start(bf16[256,128]{1,0:T(8,128)(2,1)S(1)} %get-tuple-element.57), channel_id=1, source_target_pairs={{1,2},{3,4},{5,6},{7,8},{9,10},{11,12},{13,14},{2,1},{4,3},{6,5},{... | collective-permute-start | bytes 196616 | tf_op jit(solution)/shard_map/ppermute | solution.py:362
  43.1 4.7 %collective-permute-start.12 = (bf16[256,128]{1,0:T(8,128)(2,1)S(1)}, bf16[256,128]{1,0:T(8,128)(2,1)S(1)}, u32[]{:S(2)}, u32[]{:S(2)}) collective-permute-start(bf16[256,128]{1,0:T(8,128)(2,1)S(1)} %get-tuple-element.63), channel_id=1, source_target_pairs={{0,16},{16,0},{1,17},{17,1},{2,18},{18,2},{3,19},{19,3},{4,20},{20... | collective-permute-start | bytes 196616 | tf_op jit(solution)/shard_map/ppermute | solution.py:531

commit v8 on v6

--- a/solution.py
+++ b/solution.py
@@ -555,26 +555,27 @@
     sends = joined(near_blocks, relay)
     pieces = [across(value, d) if d else value for d, value in enumerate(sends)]
     matrix, own_side = filter_table(fore_flag, angles, local_pulses, sends[0])
-    pulses = after(pulses, *pieces[1:]).reshape(2 * local_pulses * devices, bins - LANES)
+    own_outer, out_outer, *edges = outer_image(own_side, matrix, pieces)
+
+    def halos(side, edges, stride):
+        rims, out_rims = sorted_rims(side, exchanged(edges[0], 0), exchanged(edges[1], 1))
+        return rims, from_partner(out_rims, stride)
+
+    pulses = after(pulses, out_outer).reshape(2 * local_pulses * devices, bins - LANES)
     out_inner = inner_image(partner_rows_kernel, angles, matrix, pulses)
-    pieces[0] = after(pieces[0], out_inner)
-    own_outer, out_outer, *edges = outer_image(own_side, matrix, pieces)
     far = [from_partner(value, 1) for value in (out_outer, out_inner)]
-    edges = exchanged(edges[0], 0), exchanged(edges[1], 1)
+    rims, far_rims = halos(own_side, [after(edge, out_inner) for edge in edges], 1)
+    pulses = after(pulses, far[0])
     own_kernel = functools.partial(own_rows_kernel, local_pulses)
     own = inner_image(own_kernel, angles, matrix, pulses, (own_outer,))
     tables = merge_tables(0, 1, *settings, own)
-    edges = after(edges[0], tables[0]), edges[1]
     for level in range(levels):
         stride = 2**level
         if level > 0:
             tables = merge_tables(level, stride, *settings, image)
             own, out, edges = split_image(level, image, fore_flag, rim)
             far = [from_partner(value, stride) for value in (out[..., :LANES], out[..., LANES:])]
-            edges = exchanged(edges[0], 0), exchanged(edges[1], 1)
-            own_side = tables[-1]
-        rims, out_rims = sorted_rims(own_side, *edges)
-        far_rims = from_partner(out_rims, stride)
+            rims, far_rims = halos(tables[-1], edges, stride)
         image = merged_image(own, rims, far, far_rims, tables, BF16 if level + 1 < levels else F32)
     return image
 

time: 47.3 us -> 50.3 us (1.063)
  waiting for transfers between devices: 11.3 us -> 13.5 us
  local copies, waits for them, and re-layouts: 1.44 us -> 2.06 us
  Pallas kernels: 12.4 us -> 13 us
    ppermute x3, waiting for transfers between devices: 1.03 us -> 3.6 us  [from_partner(): return lax.ppermute(value, 'sub', pairs)]
    all_to_all x1, waiting for transfers between devices: 1.4 us -> 0.01 us  [on_device(): lax.all_to_all(blocks, 'rng', split_axis=0, concat_axis=0, tiled=True)]
    ppermute x2, waiting for transfers between devices: 0.02 us -> 1 us  [exchanged(): return lax.ppermute(value, 'rng', pairs + [(j, i) for i, j in pairs] + ends)]
    unnamed x14 -> x16, local copies, waits for them, and re-layouts: 1.44 us -> 2.06 us
    pallas_call x1, Pallas kernels: 0.92 us -> 1.46 us  [outer_image(): pl.pallas_call(functools.partial(outer_kernel, len(pieces)), out_shape=[i...]
  transfers between devices with their start and end apart: 14 -> 14, of which waited for: 5 -> 4; matrix products, arithmetic and copies ran while one was open for 0% -> 0% of each run, Pallas kernels for 19% -> 21%
where the time goes in v8:
time: 50.3 us; the launch traced here: 49.5 us
  starting transfers between devices  20.8 us (41%)
  waiting for transfers between devices  13.5 us (27%)
  Pallas kernels  13 us (26%)
  local copies, waits for them, and re-layouts  2.06 us (4%)
    ppermute x8, waiting for transfers between devices, across(): return lax.ppermute(value, 'rng', [(i, i ^ mask) for i in range(devices)])  8.89 us
    ppermute x8, starting transfers between devices, across(): return lax.ppermute(value, 'rng', [(i, i ^ mask) for i in range(devices)])  8.48 us
    all_to_all x1, starting transfers between devices, on_device(): lax.all_to_all(blocks, 'rng', split_axis=0, concat_axis=0, tiled=True)  6.72 us
    ppermute x3, starting transfers between devices, from_partner(): return lax.ppermute(value, 'sub', pairs)  3.67 us
    ppermute x3, waiting for transfers between devices, from_partner(): return lax.ppermute(value, 'sub', pairs)  3.6 us
    pallas_call x1, Pallas kernels, merge_tables(): pl.pallas_call(functools.partial(merge_table_kernel, level, stride), out_...  2.79 us
    unnamed x16, local copies, waits for them, and re-layouts  2.06 us
    pallas_call x1, Pallas kernels, merged_image(): pl.pallas_call(middle_kernel, out_shape=[image, jax.ShapeDtypeStruct((ang...  2 us
  transfers between devices with their start and end apart: 14, of which 4 were waited for; matrix products, arithmetic and copies ran while one was open for 0% of the time, Pallas kernels for 21%

profile of v8, /device:TPU:16, one launch (start us, length us, event | category | flops | bytes accessed | tf_op | source)
XLA Modules:
  0.0 49.5 jit_solution(9427464469261246364)
XLA Ops:
  0.0 0.0 copy-start
  0.0 1.2 %copy-done = bf16[2,32,8192]{2,1,0:T(8,128)(2,1)S(1)} copy-done((bf16[2,32,8192]{2,1,0:T(8,128)(2,1)S(1)}, bf16[2,32,8192]{2,1,0:T(8,128)(2,1)}, u32[]{:S(2)}) %copy-start) | copy-done | bytes 1048600
  1.2 1.0 %shard_map.64 = (bf16[8,64,128]{2,1,0:T(8,128)(2,1)S(1)}, bf16[8,64,128]{2,1,0:T(8,128)(2,1)S(1)}, bf16[16,64,384]{2,1,0:T(8,128)(2,1)}) custom-call(bf16[64,8192]{1,0:T(8,128)(2,1)S(1)} %bitcast.4), custom_call_target="tpu_custom_call" | custom-call | bytes 2097152 | tf_op jit(solution)/shard_map/pallas_call | solution.py:81
  2.3 0.0 collective-permute-start
  2.3 6.7 %all-to-all-start = ((bf16[16,64,384]{2,1,0:T(8,128)(2,1)}), bf16[16,64,384]{2,1,0:T(8,128)(2,1)S(1)}, u32[]{:S(2)}, u32[]{:S(2)}) async-start(bf16[16,64,384]{2,1,0:T(8,128)(2,1)} %get-tuple-element.47), calls=%async_computation | async-start | bytes 1572864 | tf_op jit(solution)/shard_map/all_to_all | solution.py:554
  9.0 0.0 collective-permute-done.relay_ref
  9.0 0.0 copy-start.5
  9.0 0.0 copy-start.6
  9.0 0.2 collective-permute-start.1
  9.3 1.5 %collective-permute-start.2 = (bf16[128,128]{1,0:T(8,128)(2,1)S(1)}, bf16[128,128]{1,0:T(8,128)(2,1)S(1)}, u32[]{:S(2)}, u32[]{:S(2)}) collective-permute-start(bf16[128,128]{1,0:T(8,128)(2,1)S(1)} %get-tuple-element.40), channel_id=1, source_target_pairs={{0,2},{1,3},{2,0},{3,1},{4,6},{5,7},{6,4},{7,5},{8,10},{9,11},{10,... | collective-permute-start | bytes 98312 | tf_op jit(solution)/shard_map/ppermute | solution.py:113
  10.7 0.2 collective-permute-start.3
  11.0 3.8 %collective-permute-start.4 = (bf16[128,128]{1,0:T(8,128)(2,1)S(1)}, bf16[128,128]{1,0:T(8,128)(2,1)S(1)}, u32[]{:S(2)}, u32[]{:S(2)}) collective-permute-start(bf16[128,128]{1,0:T(8,128)(2,1)S(1)} %get-tuple-element.42), channel_id=1, source_target_pairs={{0,4},{1,5},{2,6},{3,7},{4,0},{5,1},{6,2},{7,3},{8,12},{9,13},{10,... | collective-permute-start | bytes 98312 | tf_op jit(solution)/shard_map/ppermute | solution.py:113
  14.7 0.0 collective-permute-start.5
  14.7 0.0 collective-permute-done.1.refs_1_
  14.8 2.6 %collective-permute-start.6 = (bf16[128,128]{1,0:T(8,128)(2,1)S(1)}, bf16[128,128]{1,0:T(8,128)(2,1)S(1)}, u32[]{:S(2)}, u32[]{:S(2)}) collective-permute-start(bf16[128,128]{1,0:T(8,128)(2,1)S(1)} %get-tuple-element.44), channel_id=1, source_target_pairs={{0,6},{1,7},{2,4},{3,5},{4,2},{5,3},{6,0},{7,1},{8,14},{9,15},{10,... | collective-permute-start | bytes 98312 | tf_op jit(solution)/shard_map/ppermute | solution.py:113
  17.4 0.0 collective-permute-done.2.refs_2_
  17.4 0.2 collective-permute-start.7
  17.5 0.0 copy-done.5
  17.5 0.1 copy.8.flag_ref
  17.6 1.3 %shard_map.66 = (bf16[512,1024]{1,0:T(8,128)(2,1)S(1)}, f32[8,128]{1,0:T(8,128)S(1)}) custom-call(s32[1,2,1]{2,1,0:T(2,128)S(1)} %copy.8.flag_ref, bf16[128,128]{1,0:T(8,128)(2,1)S(1)} %get-tuple-element.36.after_ref.refs_0_), custom_call_target="tpu_custom_call" | custom-call | flops 9000000 | bytes 4194304 | tf_op jit(solution)/shard_map/pallas_call | solution.py:155
  18.9 0.0 collective-permute-done.3.refs_3_
  18.9 6.7 %collective-permute-done.4.refs_4_ = bf16[128,128]{1,0:T(8,128)(2,1)S(1)} collective-permute-done((bf16[128,128]{1,0:T(8,128)(2,1)S(1)}, bf16[128,128]{1,0:T(8,128)(2,1)S(1)}, u32[]{:S(2)}, u32[]{:S(2)}) %collective-permute-start.4) | collective-permute-done | bytes 32800 | tf_op jit(solution)/shard_map/ppermute | solution.py:113
  25.6 0.0 collective-permute-done.5.refs_5_
  25.6 2.2 %collective-permute-done.6.refs_6_ = bf16[128,128]{1,0:T(8,128)(2,1)S(1)} collective-permute-done((bf16[128,128]{1,0:T(8,128)(2,1)S(1)}, bf16[128,128]{1,0:T(8,128)(2,1)S(1)}, u32[]{:S(2)}, u32[]{:S(2)}) %collective-permute-start.6) | collective-permute-done | bytes 32800 | tf_op jit(solution)/shard_map/ppermute | solution.py:113
  27.8 0.0 collective-permute-done.7.refs_7_
  27.8 1.5 %shard_map.67 = (bf16[2,256,128]{2,1,0:T(8,128)(2,1)S(1)}, bf16[2,256,128]{2,1,0:T(8,128)(2,1)}, bf16[256,128]{1,0:T(8,128)(2,1)S(1)}, bf16[256,128]{1,0:T(8,128)(2,1)S(1)}) custom-call(f32[8,128]{1,0:T(8,128)S(1)} %get-tuple-element.37.side_ref, bf16[512,1024]{1,0:T(8,128)(2,1)S(1)} %get-tuple-element.38.rows_ref, ...), custom_call_target="tpu_custom_call" | custom-call | flops 268435456 | bytes 3145728 | tf_op jit(solution)/shard_map/pallas_call | solution.py:303
  29.2 0.0 copy-start.3
  29.2 0.6 %copy-done.3 = bf16[256,128]{1,0:T(8,128)(2,1)} copy-done((bf16[256,128]{1,0:T(8,128)(2,1)}, bf16[256,128]{1,0:T(8,128)(2,1)S(1)}, u32[]{:S(2)}) %copy-start.3) | copy-done | bytes 65560
  29.9 1.5 %collective-permute-start.8 = (bf16[2,256,128]{2,1,0:T(8,128)(2,1)}, bf16[2,256,128]{2,1,0:T(8,128)(2,1)S(1)}, u32[]{:S(2)}, u32[]{:S(2)}) collective-permute-start(bf16[2,256,128]{2,1,0:T(8,128)(2,1)} %get-tuple-element.46), channel_id=1, source_target_pairs={{0,16},{16,0},{1,17},{17,1},{2,18},{18,2},{3,19},{19,3},{4,20},{20... | collective-permute-start | bytes 393224 | tf_op jit(solution)/shard_map/ppermute | solution.py:516
  31.4 0.0 all-to-all-done
  31.4 0.0 copy-start.1
  31.4 0.0 copy-start.4
  31.4 0.7 %shard_map.68 = bf16[2,256,384]{2,1,0:T(8,128)(2,1)S(1)} custom-call(bf16[512,1024]{1,0:T(8,128)(2,1)S(1)} %get-tuple-element.38.rows_ref, bf16[1024,384]{1,0:T(8,128)(2,1)S(1)} %bitcast.2), custom_call_target="tpu_custom_call" | custom-call | flops 402653184 | bytes 3145728 | tf_op jit(solution)/shard_map/pallas_call | solution.py:331
  32.1 0.6 %collective-permute-start.9 = (bf16[2,256,384]{2,1,0:T(8,128)(2,1)S(1)}, bf16[2,256,384]{2,1,0:T(8,128)(2,1)S(1)}, u32[]{:S(2)}, u32[]{:S(2)}) collective-permute-start(bf16[2,256,384]{2,1,0:T(8,128)(2,1)S(1)} %shard_map.68), channel_id=1, source_target_pairs={{0,16},{16,0},{1,17},{17,1},{2,18},{18,2},{3,19},{19,3},{4,20},{20... | collective-permute-start | bytes 1179656 | tf_op jit(solution)/shard_map/ppermute | solution.py:516
  32.7 0.0 copy-done.6
  32.7 0.1 copy.10.offset_ref
  32.8 0.0 copy-start.2
  32.8 3.6 %collective-permute-done.8.far_outer = bf16[2,256,128]{2,1,0:T(8,128)(2,1)S(1)} collective-permute-done((bf16[2,256,128]{2,1,0:T(8,128)(2,1)}, bf16[2,256,128]{2,1,0:T(8,128)(2,1)S(1)}, u32[]{:S(2)}, u32[]{:S(2)}) %collective-permute-start.8) | collective-permute-done | bytes 131104 | tf_op jit(solution)/shard_map/ppermute | solution.py:516
  36.4 0.0 collective-permute-start.10
  36.4 1.9 %collective-permute-start.11 = (bf16[256,128]{1,0:T(8,128)(2,1)S(1)}, bf16[256,128]{1,0:T(8,128)(2,1)S(1)}, u32[]{:S(2)}, u32[]{:S(2)}) collective-permute-start(bf16[256,128]{1,0:T(8,128)(2,1)S(1)} %get-tuple-element.54), channel_id=1, source_target_pairs={{1,2},{3,4},{5,6},{7,8},{9,10},{11,12},{13,14},{2,1},{4,3},{6,5},{... | collective-permute-start | bytes 196616 | tf_op jit(solution)/shard_map/ppermute | solution.py:347
  38.3 0.8 %shard_map.69.after_ref.own_ref = bf16[2,256,512]{2,1,0:T(8,128)(2,1)S(1)} custom-call(bf16[512,1024]{1,0:T(8,128)(2,1)S(1)} %get-tuple-element.38.rows_ref, bf16[1024,384]{1,0:T(8,128)(2,1)S(1)} %bitcast.3, bf16[2,256,128]{2,1,0:T(8,128)(2,1)S(1)} %get-tuple-element.50.outer_ref), custom_call_target="tpu_custom_call" | custom-call | flops 402653184 | bytes 3145728 | tf_op jit(solution)/shard_map/pallas_call | solution.py:331
  39.1 0.0 copy-done.1
  39.1 0.0 copy-done.4
  39.1 0.0 copy-done.2
  39.1 2.8 %shard_map.71 = (bf16[2,512,512]{2,1,0:T(8,128)(2,1)S(1)}, bf16[2,2,128,512]{3,2,1,0:T(8,128)(2,1)S(1)}, f32[2,2,512,512]{3,2,1,0:T(8,128)S(1)}, bf16[2,512,256]{2,1,0:T(8,128)(2,1)S(1)}, f32[8,128]{1,0:T(8,128)}) custom-call(s32[1,2,1]{2,1,0:T(2,128)S(1)} %copy.8.flag_ref, s32[1,2,1]{2,1,0:T(2,128)S(1)} %copy.10.offset_ref, f32[1,2]{1,0:T(1,128)S(1)} %copy-done.4, ...), custom_call_target="tpu_custom_call" | custom-call | flops 2300000000 | bytes 7340032 | tf_op jit(solution)/shard_map/pallas_call | solution.py:241
  41.9 0.0 collective-permute-done.10.first_ref
  42.0 1.0 %collective-permute-done.11.second_ref = bf16[256,128]{1,0:T(8,128)(2,1)S(1)} collective-permute-done((bf16[256,128]{1,0:T(8,128)(2,1)S(1)}, bf16[256,128]{1,0:T(8,128)(2,1)S(1)}, u32[]{:S(2)}, u32[]{:S(2)}) %collective-permute-start.11) | collective-permute-done | bytes 65568 | tf_op jit(solution)/shard_map/ppermute | solution.py:347
  43.0 0.2 shard_map.70
  43.1 1.6 %collective-permute-start.12 = (bf16[256,128]{1,0:T(8,128)(2,1)S(1)}, bf16[256,128]{1,0:T(8,128)(2,1)S(1)}, u32[]{:S(2)}, u32[]{:S(2)}) collective-permute-start(bf16[256,128]{1,0:T(8,128)(2,1)S(1)} %get-tuple-element.61), channel_id=1, source_target_pairs={{0,16},{16,0},{1,17},{17,1},{2,18},{18,2},{3,19},{19,3},{4,20},{20... | collective-permute-start | bytes 196616 | tf_op jit(solution)/shard_map/ppermute | solution.py:516
  44.7 1.1 %shard_map.72.merged_ref = f32[2,512,512]{2,1,0:T(8,128)S(1)} custom-call(bf16[2,256,512]{2,1,0:T(8,128)(2,1)S(1)} %shard_map.69.after_ref.own_ref, bf16[256,128]{1,0:T(8,128)(2,1)S(1)} %get-tuple-element.55.rims_ref, bf16[2,512,512]{2,1,0:T(8,128)(2,1)S(1)} %get-tuple-element.56.centre_ref, bf16[2,2,128,512]{3,2,1,0:T(8,128)(2,1)S(1)} %get-tuple-element.57.rim_ref, ...), custom_call_target="tpu_custom_call" | custom-call | flops 536870912 | bytes 8388608 | tf_op jit(solution)/shard_map/pallas_call | solution.py:472
  45.8 0.0 collective-permute-done.9.far_inner
  45.8 2.0 %shard_map.73 = (f32[2,512,512]{2,1,0:T(8,128)}, f32[512,256]{1,0:T(8,128)S(1)}) custom-call(bf16[2,256,384]{2,1,0:T(8,128)(2,1)S(1)} %collective-permute-done.9.far_inner, f32[2,512,512]{2,1,0:T(8,128)S(1)} %shard_map.72.merged_ref, bf16[2,512,512]{2,1,0:T(8,128)(2,1)S(1)} %get-tuple-element.56.centre_ref, ...), custom_call_target="tpu_custom_call" | custom-call | flops 536870912 | bytes 8388608 | tf_op jit(solution)/shard_map/pallas_call | solution.py:483
  47.8 0.0 collective-permute-done.12.rims_ref
  47.8 1.6 %shard_map.74 = f32[2,512,512]{2,1,0:T(8,128)} custom-call(bf16[2,256,128]{2,1,0:T(8,128)(2,1)S(1)} %collective-permute-done.8.far_outer, f32[512,256]{1,0:T(8,128)S(1)} %get-tuple-element.60.partial_ref, bf16[256,128]{1,0:T(8,128)(2,1)S(1)} %collective-permute-done.12.rims_ref, ...), custom_call_target="tpu_custom_call", output_to_operand_aliasing={{}: (8, {})} | custom-call | flops 536870912 | bytes 8388608 | tf_op jit(solution)/shard_map/pallas_call | solution.py:495
  (1 shorter events, 0.0 us)
Async XLA Ops:
  0.0 1.2 %copy-start = (bf16[2,32,8192]{2,1,0:T(8,128)(2,1)S(1)}, bf16[2,32,8192]{2,1,0:T(8,128)(2,1)}, u32[]{:S(2)}) copy-start(bf16[2,32,8192]{2,1,0:T(8,128)(2,1)} %param.6) | copy-start | bytes 3145732
  2.3 6.7 %collective-permute-start = (bf16[8,64,128]{2,1,0:T(8,128)(2,1)S(1)}, bf16[8,64,128]{2,1,0:T(8,128)(2,1)S(1)}, u32[]{:S(2)}, u32[]{:S(2)}) collective-permute-start(bf16[8,64,128]{2,1,0:T(8,128)(2,1)S(1)} %get-tuple-element.35), channel_id=1, source_target_pairs={{0,8},{1,9},{2,10},{3,11},{4,12},{5,13},{6,14},{7,15},{8,0},{9,1},... | collective-permute-start | bytes 393224 | tf_op jit(solution)/shard_map/ppermute | solution.py:113
  2.3 29.1 %all-to-all-start = ((bf16[16,64,384]{2,1,0:T(8,128)(2,1)}), bf16[16,64,384]{2,1,0:T(8,128)(2,1)S(1)}, u32[]{:S(2)}, u32[]{:S(2)}) async-start(bf16[16,64,384]{2,1,0:T(8,128)(2,1)} %get-tuple-element.47), calls=%async_computation | async-start | bytes 1572864 | tf_op jit(solution)/shard_map/all_to_all | solution.py:554
  9.0 8.6 %copy-start.5 = (s32[1,2,1]{1,2,0:T(1,128)S(1)}, s32[1,2,1]{1,2,0:T(1,128)}, u32[]{:S(2)}) copy-start(s32[1,2,1]{1,2,0:T(1,128)} %param.7) | copy-start | bytes 28
  9.0 23.7 %copy-start.6 = (s32[1,2,1]{1,2,0:T(1,128)S(1)}, s32[1,2,1]{1,2,0:T(1,128)}, u32[]{:S(2)}) copy-start(s32[1,2,1]{1,2,0:T(1,128)} %param.8) | copy-start | bytes 28
  9.0 5.7 %collective-permute-start.1 = (bf16[128,128]{1,0:T(8,128)(2,1)S(1)}, bf16[128,128]{1,0:T(8,128)(2,1)S(1)}, u32[]{:S(2)}, u32[]{:S(2)}) collective-permute-start(bf16[128,128]{1,0:T(8,128)(2,1)S(1)} %get-tuple-element.39), channel_id=1, source_target_pairs={{0,1},{1,0},{2,3},{3,2},{4,5},{5,4},{6,7},{7,6},{8,9},{9,8},{10,11... | collective-permute-start | bytes 98312 | tf_op jit(solution)/shard_map/ppermute | solution.py:113
  9.3 8.1 %collective-permute-start.2 = (bf16[128,128]{1,0:T(8,128)(2,1)S(1)}, bf16[128,128]{1,0:T(8,128)(2,1)S(1)}, u32[]{:S(2)}, u32[]{:S(2)}) collective-permute-start(bf16[128,128]{1,0:T(8,128)(2,1)S(1)} %get-tuple-element.40), channel_id=1, source_target_pairs={{0,2},{1,3},{2,0},{3,1},{4,6},{5,7},{6,4},{7,5},{8,10},{9,11},{10,... | collective-permute-start | bytes 98312 | tf_op jit(solution)/shard_map/ppermute | solution.py:113
  10.7 8.2 %collective-permute-start.3 = (bf16[128,128]{1,0:T(8,128)(2,1)S(1)}, bf16[128,128]{1,0:T(8,128)(2,1)S(1)}, u32[]{:S(2)}, u32[]{:S(2)}) collective-permute-start(bf16[128,128]{1,0:T(8,128)(2,1)S(1)} %get-tuple-element.41), channel_id=1, source_target_pairs={{0,3},{1,2},{2,1},{3,0},{4,7},{5,6},{6,5},{7,4},{8,11},{9,10},{10,... | collective-permute-start | bytes 98312 | tf_op jit(solution)/shard_map/ppermute | solution.py:113
  11.0 14.6 %collective-permute-start.4 = (bf16[128,128]{1,0:T(8,128)(2,1)S(1)}, bf16[128,128]{1,0:T(8,128)(2,1)S(1)}, u32[]{:S(2)}, u32[]{:S(2)}) collective-permute-start(bf16[128,128]{1,0:T(8,128)(2,1)S(1)} %get-tuple-element.42), channel_id=1, source_target_pairs={{0,4},{1,5},{2,6},{3,7},{4,0},{5,1},{6,2},{7,3},{8,12},{9,13},{10,... | collective-permute-start | bytes 98312 | tf_op jit(solution)/shard_map/ppermute | solution.py:113
  14.7 10.8 %collective-permute-start.5 = (bf16[128,128]{1,0:T(8,128)(2,1)S(1)}, bf16[128,128]{1,0:T(8,128)(2,1)S(1)}, u32[]{:S(2)}, u32[]{:S(2)}) collective-permute-start(bf16[128,128]{1,0:T(8,128)(2,1)S(1)} %get-tuple-element.43), channel_id=1, source_target_pairs={{0,5},{1,4},{2,7},{3,6},{4,1},{5,0},{6,3},{7,2},{8,13},{9,12},{10,... | collective-permute-start | bytes 98312 | tf_op jit(solution)/shard_map/ppermute | solution.py:113
  14.8 13.0 %collective-permute-start.6 = (bf16[128,128]{1,0:T(8,128)(2,1)S(1)}, bf16[128,128]{1,0:T(8,128)(2,1)S(1)}, u32[]{:S(2)}, u32[]{:S(2)}) collective-permute-start(bf16[128,128]{1,0:T(8,128)(2,1)S(1)} %get-tuple-element.44), channel_id=1, source_target_pairs={{0,6},{1,7},{2,4},{3,5},{4,2},{5,3},{6,0},{7,1},{8,14},{9,15},{10,... | collective-permute-start | bytes 98312 | tf_op jit(solution)/shard_map/ppermute | solution.py:113
  17.4 10.4 %collective-permute-start.7 = (bf16[128,128]{1,0:T(8,128)(2,1)S(1)}, bf16[128,128]{1,0:T(8,128)(2,1)S(1)}, u32[]{:S(2)}, u32[]{:S(2)}) collective-permute-start(bf16[128,128]{1,0:T(8,128)(2,1)S(1)} %get-tuple-element.45), channel_id=1, source_target_pairs={{0,7},{1,6},{2,5},{3,4},{4,3},{5,2},{6,1},{7,0},{8,15},{9,14},{10,... | collective-permute-start | bytes 98312 | tf_op jit(solution)/shard_map/ppermute | solution.py:113
  29.2 0.6 %copy-start.3 = (bf16[256,128]{1,0:T(8,128)(2,1)}, bf16[256,128]{1,0:T(8,128)(2,1)S(1)}, u32[]{:S(2)}) copy-start(bf16[256,128]{1,0:T(8,128)(2,1)S(1)} %get-tuple-element.52) | copy-start | bytes 196612
  29.9 6.5 %collective-permute-start.8 = (bf16[2,256,128]{2,1,0:T(8,128)(2,1)}, bf16[2,256,128]{2,1,0:T(8,128)(2,1)S(1)}, u32[]{:S(2)}, u32[]{:S(2)}) collective-permute-start(bf16[2,256,128]{2,1,0:T(8,128)(2,1)} %get-tuple-element.46), channel_id=1, source_target_pairs={{0,16},{16,0},{1,17},{17,1},{2,18},{18,2},{3,19},{19,3},{4,20},{20... | collective-permute-start | bytes 393224 | tf_op jit(solution)/shard_map/ppermute | solution.py:516
  31.4 7.7 %copy-start.1 = (bf16[1,544,512]{2,1,0:T(8,128)(2,1)S(1)}, bf16[1,544,512]{2,1,0:T(8,128)(2,1)}, u32[]{:S(2)}) copy-start(bf16[1,544,512]{2,1,0:T(8,128)(2,1)} %range_ref.1) | copy-start | bytes 1671172
  31.4 7.7 %copy-start.4 = (f32[1,2]{1,0:T(1,128)S(1)}, f32[1,2]{1,0:T(1,128)}, u32[]{:S(2)}) copy-start(f32[1,2]{1,0:T(1,128)} %shift_ref.1) | copy-start | bytes 28
  32.1 13.7 %collective-permute-start.9 = (bf16[2,256,384]{2,1,0:T(8,128)(2,1)S(1)}, bf16[2,256,384]{2,1,0:T(8,128)(2,1)S(1)}, u32[]{:S(2)}, u32[]{:S(2)}) collective-permute-start(bf16[2,256,384]{2,1,0:T(8,128)(2,1)S(1)} %shard_map.68), channel_id=1, source_target_pairs={{0,16},{16,0},{1,17},{17,1},{2,18},{18,2},{3,19},{19,3},{4,20},{20... | collective-permute-start | bytes 1179656 | tf_op jit(solution)/shard_map/ppermute | solution.py:516
  32.8 6.4 %copy-start.2 = (bf16[1,2,512,256]{3,2,1,0:T(8,128)(2,1)S(1)}, bf16[1,2,512,256]{3,2,1,0:T(8,128)(2,1)}, u32[]{:S(2)}) copy-start(bf16[1,2,512,256]{3,2,1,0:T(8,128)(2,1)} %interp_ref.1) | copy-start | bytes 1572868
  36.4 5.6 %collective-permute-start.10 = (bf16[256,128]{1,0:T(8,128)(2,1)}, bf16[256,128]{1,0:T(8,128)(2,1)S(1)}, u32[]{:S(2)}, u32[]{:S(2)}) collective-permute-start(bf16[256,128]{1,0:T(8,128)(2,1)} %copy-done.3), channel_id=1, source_target_pairs={{0,1},{2,3},{4,5},{6,7},{8,9},{10,11},{12,13},{14,15},{1,0},{3,2},... | collective-permute-start | bytes 196616 | tf_op jit(solution)/shard_map/ppermute | solution.py:347
  36.4 6.6 %collective-permute-start.11 = (bf16[256,128]{1,0:T(8,128)(2,1)S(1)}, bf16[256,128]{1,0:T(8,128)(2,1)S(1)}, u32[]{:S(2)}, u32[]{:S(2)}) collective-permute-start(bf16[256,128]{1,0:T(8,128)(2,1)S(1)} %get-tuple-element.54), channel_id=1, source_target_pairs={{1,2},{3,4},{5,6},{7,8},{9,10},{11,12},{13,14},{2,1},{4,3},{6,5},{... | collective-permute-start | bytes 196616 | tf_op jit(solution)/shard_map/ppermute | solution.py:347
  43.1 4.7 %collective-permute-start.12 = (bf16[256,128]{1,0:T(8,128)(2,1)S(1)}, bf16[256,128]{1,0:T(8,128)(2,1)S(1)}, u32[]{:S(2)}, u32[]{:S(2)}) collective-permute-start(bf16[256,128]{1,0:T(8,128)(2,1)S(1)} %get-tuple-element.61), channel_id=1, source_target_pairs={{0,16},{16,0},{1,17},{17,1},{2,18},{18,2},{3,19},{19,3},{4,20},{20... | collective-permute-start | bytes 196616 | tf_op jit(solution)/shard_map/ppermute | solution.py:516

commit v9 on v6

--- a/solution.py
+++ b/solution.py
@@ -116,8 +116,8 @@
 def filter_table_kernel(local_pulses, flag_ref, after_ref, rows_ref, side_ref, cos_ref, sin_ref):
     own_flag = flag_ref[0, lax.axis_index("sub"), 0]
     side_ref[...] = jnp.full(side_ref.shape, own_flag.astype(F32))
-    angles, columns = rows_ref.shape
-    half = angles // 2
+    half, columns = rows_ref.shape
+    angles = 2 * half
     first = (1 - own_flag) * half
     base = cos_ref.shape[0]
     scale = 1.0 / math.sqrt(columns // 2)
@@ -136,25 +136,22 @@
     step = cos_sin_pi(per_angle * (2 * base))
     for j in range(half // base):
         for i in range(base // 16):
-            pair = [], []
+            pair = []
             for k in (2 * i, 2 * i + 1):
                 here = slice(8 * k, 8 * k + 8)
                 now = cos_ref[here, :], sin_ref[here, :]
-                pair[0].append(now[0])
-                pair[1].append(-now[1])
+                pair.append(now[0])
                 if j + 1 < half // base:
                     cos_ref[here, :], sin_ref[here, :] = rotated(now, step)
             begin = j * base + 16 * i
-            rows_ref[begin : begin + 16, :] = jnp.concatenate(pair[0]).astype(BF16)
-            begin += half
-            rows_ref[begin : begin + 16, :] = jnp.concatenate(pair[1]).astype(BF16)
+            rows_ref[begin : begin + 16, :] = jnp.concatenate(pair).astype(BF16)
 
 
 def filter_table(fore_flag, angles, local_pulses, earlier):
     side = 2 * local_pulses * lax.axis_size("rng")
     return pl.pallas_call(
         functools.partial(filter_table_kernel, local_pulses),
-        out_shape=[jax.ShapeDtypeStruct((angles, side), BF16), SIDE],
+        out_shape=[jax.ShapeDtypeStruct((angles // 2, side), BF16), SIDE],
         in_specs=[SMEM, ANY],
         out_specs=[VMEM] * 2,
         scratch_shapes=[pltpu.VMEM((64, side), F32)] * 2,
@@ -260,7 +257,15 @@
 def alternating(pulses, local_pulses):
     row = lax.broadcasted_iota(jnp.int32, (pulses.shape[0], 1), 0)
     pulse = row // (2 * local_pulses) * local_pulses + row % local_pulses
-    return jnp.where(pulse % 2 == 1, -pulses.astype(F32), pulses.astype(F32)).astype(BF16)
+    return jnp.where(pulse % 2 == 1, -pulses, pulses)
+
+
+def both_parts(pulses, local_pulses):
+    count = pulses.shape[0]
+    second = lax.broadcasted_iota(jnp.int32, (count, 1), 0) // local_pulses % 2 == 1
+    ahead, behind = pltpu.roll(pulses, count - local_pulses, 0), pltpu.roll(pulses, local_pulses, 0)
+    turned = jnp.where(second, -behind, ahead)
+    return jnp.concatenate([pulses, turned], axis=1).astype(BF16)
 
 
 def outer_kernel(pieces, side_ref, rows_ref, *refs):
@@ -274,14 +279,17 @@
             place = pl.multiple_of((me ^ (d + t * pieces)) * rows, rows)
             pulses_ref[pl.ds(place, rows), :] = ref[t * rows : (t + 1) * rows, :]
     pulses = pulses_ref[...]
-    own_parts = dot(rows_ref[...], alternating(pulses, rows // 2))
-    out_parts = dot(rows_ref[...], pulses)
+    pulses = pulses.astype(F32)
+    images = [
+        dot(rows_ref[...], both_parts(value, rows // 2))
+        for value in (alternating(pulses, rows // 2), pulses)
+    ]
     half = own_ref.shape[1]
     rim = LANES // 4
     lane = lax.broadcasted_iota(jnp.int32, (1, LANES), 1)
     edges = [0.0, 0.0]
     for part in range(2):
-        own, out = (value[part * half : (part + 1) * half] for value in (own_parts, out_parts))
+        own, out = (image[:, part * LANES : (part + 1) * LANES] for image in images)
         own_ref[part] = own.astype(BF16)
         out_ref[part] = out.astype(BF16)
         for side in range(2):
@@ -297,7 +305,8 @@
 
 
 def outer_image(own_side, rows, pieces):
-    angles, side = rows.shape
+    half, side = rows.shape
+    angles = 2 * half
     image = jax.ShapeDtypeStruct((2, angles // 2, LANES), BF16)
     edge = jax.ShapeDtypeStruct((angles // 2, LANES), BF16)
     return pl.pallas_call(
@@ -313,16 +322,21 @@
     )(own_side, rows, *pieces)
 
 
-def partner_rows_kernel(rows_ref, pulses_ref, image_ref):
-    image = dot(rows_ref[...], pulses_ref[...])
-    image_ref[...] = image.astype(BF16).reshape(image_ref.shape)
+def partner_rows_kernel(local_pulses, rows_ref, pulses_ref, image_ref):
+    count = pulses_ref.shape[1]
+    image = dot(rows_ref[...], both_parts(pulses_ref[...].astype(F32), local_pulses))
+    for part in range(2):
+        image_ref[part] = image[:, part * count : (part + 1) * count].astype(BF16)
 
 
 def own_rows_kernel(local_pulses, rows_ref, pulses_ref, outer_ref, image_ref):
-    image = dot(rows_ref[...], alternating(pulses_ref[...], local_pulses))
-    parts, half, count = outer_ref.shape
+    inner = pulses_ref.shape[1]
+    pulses = alternating(pulses_ref[...].astype(F32), local_pulses)
+    image = dot(rows_ref[...], both_parts(pulses, local_pulses))
+    count = outer_ref.shape[2]
     image_ref[:, :, :count] = outer_ref[...]
-    image_ref[:, :, count:] = image.astype(BF16).reshape(parts, half, image.shape[1])
+    for part in range(2):
+        image_ref[part, :, count:] = image[:, part * inner : (part + 1) * inner].astype(BF16)
 
 
 def inner_image(kernel, angles, rows, pulses, outer=()):
@@ -555,16 +569,19 @@
     sends = joined(near_blocks, relay)
     pieces = [across(value, d) if d else value for d, value in enumerate(sends)]
     matrix, own_side = filter_table(fore_flag, angles, local_pulses, sends[0])
-    pulses = after(pulses, *pieces[1:]).reshape(2 * local_pulses * devices, bins - LANES)
-    out_inner = inner_image(partner_rows_kernel, angles, matrix, pulses)
-    pieces[0] = after(pieces[0], out_inner)
     own_outer, out_outer, *edges = outer_image(own_side, matrix, pieces)
+
+    pulses = after(pulses, out_outer).reshape(2 * local_pulses * devices, bins - LANES)
+    out_kernel = functools.partial(partner_rows_kernel, local_pulses)
+    out_inner = inner_image(out_kernel, angles, matrix, pulses)
     far = [from_partner(value, 1) for value in (out_outer, out_inner)]
+    edges = [after(edge, out_inner) for edge in edges]
     edges = exchanged(edges[0], 0), exchanged(edges[1], 1)
+    pulses = after(pulses, far[0], *edges)
     own_kernel = functools.partial(own_rows_kernel, local_pulses)
     own = inner_image(own_kernel, angles, matrix, pulses, (own_outer,))
-    tables = merge_tables(0, 1, *settings, own)
-    edges = after(edges[0], tables[0]), edges[1]
+    rims, out_rims = sorted_rims(own_side, *edges)
+    tables = merge_tables(0, 1, *settings, after(out_rims, own))
     for level in range(levels):
         stride = 2**level
         if level > 0:
@@ -572,8 +589,7 @@
             own, out, edges = split_image(level, image, fore_flag, rim)
             far = [from_partner(value, stride) for value in (out[..., :LANES], out[..., LANES:])]
             edges = exchanged(edges[0], 0), exchanged(edges[1], 1)
-            own_side = tables[-1]
-        rims, out_rims = sorted_rims(own_side, *edges)
+            rims, out_rims = sorted_rims(tables[-1], *edges)
         far_rims = from_partner(out_rims, stride)
         image = merged_image(own, rims, far, far_rims, tables, BF16 if level + 1 < levels else F32)
     return image

time: 47.3 us -> 48.9 us (1.034)
  waiting for transfers between devices: 11.3 us -> 13.1 us
    ppermute x2, waiting for transfers between devices: 0.02 us -> 2.96 us  [exchanged(): return lax.ppermute(value, 'rng', pairs + [(j, i) for i, j in pairs] + ends)]
    all_to_all x1, waiting for transfers between devices: 1.4 us -> 0.01 us  [on_device(): lax.all_to_all(blocks, 'rng', split_axis=0, concat_axis=0, tiled=True)]
  transfers between devices with their start and end apart: 14 -> 14, of which waited for: 5 -> 4; matrix products, arithmetic and copies ran while one was open for 0% -> 0% of each run, Pallas kernels for 19% -> 20%
where the time goes in v9:
time: 48.9 us; the launch traced here: 48.2 us
  starting transfers between devices  21.3 us (44%)
  waiting for transfers between devices  13.1 us (27%)
  Pallas kernels  12.2 us (25%)
  local copies, waits for them, and re-layouts  1.44 us (3%)
    ppermute x8, waiting for transfers between devices, across(): return lax.ppermute(value, 'rng', [(i, i ^ mask) for i in range(devices)])  8.98 us
    ppermute x8, starting transfers between devices, across(): return lax.ppermute(value, 'rng', [(i, i ^ mask) for i in range(devices)])  8.48 us
    all_to_all x1, starting transfers between devices, on_device(): lax.all_to_all(blocks, 'rng', split_axis=0, concat_axis=0, tiled=True)  6.72 us
    ppermute x3, starting transfers between devices, from_partner(): return lax.ppermute(value, 'sub', pairs)  3.74 us
    ppermute x2, waiting for transfers between devices, exchanged(): return lax.ppermute(value, 'rng', pairs + [(j, i) for i, j in pairs] + ends)  2.96 us
    pallas_call x1, Pallas kernels, merge_tables(): pl.pallas_call(functools.partial(merge_table_kernel, level, stride), out_...  2.8 us
    ppermute x2, starting transfers between devices, exchanged(): return lax.ppermute(value, 'rng', pairs + [(j, i) for i, j in pairs] + ends)  2.34 us
    pallas_call x1, Pallas kernels, merged_image(): pl.pallas_call(middle_kernel, out_shape=[image, jax.ShapeDtypeStruct((ang...  1.99 us
  transfers between devices with their start and end apart: 14, of which 4 were waited for; matrix products, arithmetic and copies ran while one was open for 0% of the time, Pallas kernels for 20%

profile of v9, /device:TPU:16, one launch (start us, length us, event | category | flops | bytes accessed | tf_op | source)
XLA Modules:
  0.0 48.2 jit_solution(13798056795866589617)
XLA Ops:
  0.0 0.0 copy-start
  0.0 1.2 %copy-done = bf16[2,32,8192]{2,1,0:T(8,128)(2,1)S(1)} copy-done((bf16[2,32,8192]{2,1,0:T(8,128)(2,1)S(1)}, bf16[2,32,8192]{2,1,0:T(8,128)(2,1)}, u32[]{:S(2)}) %copy-start) | copy-done | bytes 1048600
  1.2 1.0 %shard_map.64 = (bf16[8,64,128]{2,1,0:T(8,128)(2,1)S(1)}, bf16[8,64,128]{2,1,0:T(8,128)(2,1)S(1)}, bf16[16,64,384]{2,1,0:T(8,128)(2,1)}) custom-call(bf16[64,8192]{1,0:T(8,128)(2,1)S(1)} %bitcast.4), custom_call_target="tpu_custom_call" | custom-call | bytes 2097152 | tf_op jit(solution)/shard_map/pallas_call | solution.py:81
  2.3 0.0 collective-permute-start
  2.3 6.7 %all-to-all-start = ((bf16[16,64,384]{2,1,0:T(8,128)(2,1)}), bf16[16,64,384]{2,1,0:T(8,128)(2,1)S(1)}, u32[]{:S(2)}, u32[]{:S(2)}) async-start(bf16[16,64,384]{2,1,0:T(8,128)(2,1)} %get-tuple-element.48), calls=%async_computation | async-start | bytes 1572864 | tf_op jit(solution)/shard_map/all_to_all | solution.py:568
  9.0 0.0 collective-permute-done.relay_ref
  9.0 0.0 copy-start.4
  9.0 0.0 copy-start.5
  9.0 0.2 collective-permute-start.1
  9.3 1.5 %collective-permute-start.2 = (bf16[128,128]{1,0:T(8,128)(2,1)S(1)}, bf16[128,128]{1,0:T(8,128)(2,1)S(1)}, u32[]{:S(2)}, u32[]{:S(2)}) collective-permute-start(bf16[128,128]{1,0:T(8,128)(2,1)S(1)} %get-tuple-element.41), channel_id=1, source_target_pairs={{0,2},{1,3},{2,0},{3,1},{4,6},{5,7},{6,4},{7,5},{8,10},{9,11},{10,... | collective-permute-start | bytes 98312 | tf_op jit(solution)/shard_map/ppermute | solution.py:113
  10.7 0.2 collective-permute-start.3
  11.0 3.8 %collective-permute-start.4 = (bf16[128,128]{1,0:T(8,128)(2,1)S(1)}, bf16[128,128]{1,0:T(8,128)(2,1)S(1)}, u32[]{:S(2)}, u32[]{:S(2)}) collective-permute-start(bf16[128,128]{1,0:T(8,128)(2,1)S(1)} %get-tuple-element.43), channel_id=1, source_target_pairs={{0,4},{1,5},{2,6},{3,7},{4,0},{5,1},{6,2},{7,3},{8,12},{9,13},{10,... | collective-permute-start | bytes 98312 | tf_op jit(solution)/shard_map/ppermute | solution.py:113
  14.7 0.0 collective-permute-start.5
  14.7 0.0 collective-permute-done.1.refs_1_
  14.8 2.6 %collective-permute-start.6 = (bf16[128,128]{1,0:T(8,128)(2,1)S(1)}, bf16[128,128]{1,0:T(8,128)(2,1)S(1)}, u32[]{:S(2)}, u32[]{:S(2)}) collective-permute-start(bf16[128,128]{1,0:T(8,128)(2,1)S(1)} %get-tuple-element.45), channel_id=1, source_target_pairs={{0,6},{1,7},{2,4},{3,5},{4,2},{5,3},{6,0},{7,1},{8,14},{9,15},{10,... | collective-permute-start | bytes 98312 | tf_op jit(solution)/shard_map/ppermute | solution.py:113
  17.4 0.0 collective-permute-done.2.refs_2_
  17.4 0.2 collective-permute-start.7
  17.5 0.0 copy-done.4
  17.5 0.1 copy.8.flag_ref
  17.6 1.2 %shard_map.66 = (bf16[256,1024]{1,0:T(8,128)(2,1)S(1)}, f32[8,128]{1,0:T(8,128)S(1)}) custom-call(s32[1,2,1]{2,1,0:T(2,128)S(1)} %copy.8.flag_ref, bf16[128,128]{1,0:T(8,128)(2,1)S(1)} %get-tuple-element.37.after_ref.refs_0_), custom_call_target="tpu_custom_call" | custom-call | flops 9000000 | bytes 4194304 | tf_op jit(solution)/shard_map/pallas_call | solution.py:152
  18.8 0.0 collective-permute-done.3.refs_3_
  18.8 6.8 %collective-permute-done.4.refs_4_ = bf16[128,128]{1,0:T(8,128)(2,1)S(1)} collective-permute-done((bf16[128,128]{1,0:T(8,128)(2,1)S(1)}, bf16[128,128]{1,0:T(8,128)(2,1)S(1)}, u32[]{:S(2)}, u32[]{:S(2)}) %collective-permute-start.4) | collective-permute-done | bytes 32800 | tf_op jit(solution)/shard_map/ppermute | solution.py:113
  25.6 0.0 collective-permute-done.5.refs_5_
  25.6 2.2 %collective-permute-done.6.refs_6_ = bf16[128,128]{1,0:T(8,128)(2,1)S(1)} collective-permute-done((bf16[128,128]{1,0:T(8,128)(2,1)S(1)}, bf16[128,128]{1,0:T(8,128)(2,1)S(1)}, u32[]{:S(2)}, u32[]{:S(2)}) %collective-permute-start.6) | collective-permute-done | bytes 32800 | tf_op jit(solution)/shard_map/ppermute | solution.py:113
  27.8 0.0 collective-permute-done.7.refs_7_
  27.8 0.8 %shard_map.67 = (bf16[2,256,128]{2,1,0:T(8,128)(2,1)S(1)}, bf16[2,256,128]{2,1,0:T(8,128)(2,1)S(1)}, bf16[256,128]{1,0:T(8,128)(2,1)S(1)}, bf16[256,128]{1,0:T(8,128)(2,1)S(1)}) custom-call(f32[8,128]{1,0:T(8,128)S(1)} %get-tuple-element.38.side_ref, bf16[256,1024]{1,0:T(8,128)(2,1)S(1)} %get-tuple-element.39.rows_ref, ...), custom_call_target="tpu_custom_call" | custom-call | flops 268435456 | bytes 3145728 | tf_op jit(solution)/shard_map/pallas_call | solution.py:312
  28.6 0.0 copy-start.1
  28.6 0.0 copy-start.3
  28.6 1.6 %collective-permute-start.8 = (bf16[2,256,128]{2,1,0:T(8,128)(2,1)S(1)}, bf16[2,256,128]{2,1,0:T(8,128)(2,1)S(1)}, u32[]{:S(2)}, u32[]{:S(2)}) collective-permute-start(bf16[2,256,128]{2,1,0:T(8,128)(2,1)S(1)} %get-tuple-element.47), channel_id=1, source_target_pairs={{0,16},{16,0},{1,17},{17,1},{2,18},{18,2},{3,19},{19,3},{4,20},{20... | collective-permute-start | bytes 393224 | tf_op jit(solution)/shard_map/ppermute | solution.py:530
  30.2 0.0 all-to-all-done
  30.2 0.6 %shard_map.68 = bf16[2,256,384]{2,1,0:T(8,128)(2,1)S(1)} custom-call(bf16[256,1024]{1,0:T(8,128)(2,1)S(1)} %get-tuple-element.39.rows_ref, bf16[1024,384]{1,0:T(8,128)(2,1)S(1)} %bitcast.2), custom_call_target="tpu_custom_call" | custom-call | flops 402653184 | bytes 3145728 | tf_op jit(solution)/shard_map/pallas_call | solution.py:345
  30.8 0.6 %collective-permute-start.9 = (bf16[2,256,384]{2,1,0:T(8,128)(2,1)S(1)}, bf16[2,256,384]{2,1,0:T(8,128)(2,1)S(1)}, u32[]{:S(2)}, u32[]{:S(2)}) collective-permute-start(bf16[2,256,384]{2,1,0:T(8,128)(2,1)S(1)} %shard_map.68), channel_id=1, source_target_pairs={{0,16},{16,0},{1,17},{17,1},{2,18},{18,2},{3,19},{19,3},{4,20},{20... | collective-permute-start | bytes 1179656 | tf_op jit(solution)/shard_map/ppermute | solution.py:530
  31.4 0.0 collective-permute-start.10
  31.4 2.3 %collective-permute-start.11 = (bf16[256,128]{1,0:T(8,128)(2,1)S(1)}, bf16[256,128]{1,0:T(8,128)(2,1)S(1)}, u32[]{:S(2)}, u32[]{:S(2)}) collective-permute-start(bf16[256,128]{1,0:T(8,128)(2,1)S(1)} %get-tuple-element.53), channel_id=1, source_target_pairs={{1,2},{3,4},{5,6},{7,8},{9,10},{11,12},{13,14},{2,1},{4,3},{6,5},{... | collective-permute-start | bytes 196616 | tf_op jit(solution)/shard_map/ppermute | solution.py:361
  33.7 0.0 copy-done.5
  33.7 0.1 copy.10.offset_ref
  33.8 0.0 copy-start.2
  33.8 1.2 %collective-permute-done.8.far_outer = bf16[2,256,128]{2,1,0:T(8,128)(2,1)S(1)} collective-permute-done((bf16[2,256,128]{2,1,0:T(8,128)(2,1)S(1)}, bf16[2,256,128]{2,1,0:T(8,128)(2,1)S(1)}, u32[]{:S(2)}, u32[]{:S(2)}) %collective-permute-start.8) | collective-permute-done | bytes 131104 | tf_op jit(solution)/shard_map/ppermute | solution.py:530
  35.0 0.0 collective-permute-done.10.first_ref
  35.0 3.0 %collective-permute-done.11.second_ref = bf16[256,128]{1,0:T(8,128)(2,1)S(1)} collective-permute-done((bf16[256,128]{1,0:T(8,128)(2,1)S(1)}, bf16[256,128]{1,0:T(8,128)(2,1)S(1)}, u32[]{:S(2)}, u32[]{:S(2)}) %collective-permute-start.11) | collective-permute-done | bytes 65568 | tf_op jit(solution)/shard_map/ppermute | solution.py:361
  37.9 0.2 shard_map.70
  38.1 1.6 %collective-permute-start.12 = (bf16[256,128]{1,0:T(8,128)(2,1)S(1)}, bf16[256,128]{1,0:T(8,128)(2,1)S(1)}, u32[]{:S(2)}, u32[]{:S(2)}) collective-permute-start(bf16[256,128]{1,0:T(8,128)(2,1)S(1)} %get-tuple-element.58.after_ref), channel_id=1, source_target_pairs={{0,16},{16,0},{1,17},{17,1},{2,18},{18,2},{3,19},{19,3},{4,20},{20... | collective-permute-start | bytes 196616 | tf_op jit(solution)/shard_map/ppermute | solution.py:530
  39.7 0.9 %shard_map.69.own_ref = bf16[2,256,512]{2,1,0:T(8,128)(2,1)S(1)} custom-call(bf16[256,1024]{1,0:T(8,128)(2,1)S(1)} %get-tuple-element.39.rows_ref, bf16[1024,384]{1,0:T(8,128)(2,1)S(1)} %bitcast.3, bf16[2,256,128]{2,1,0:T(8,128)(2,1)S(1)} %get-tuple-element.55.outer_ref), custom_call_target="tpu_custom_call" | custom-call | flops 402653184 | bytes 3145728 | tf_op jit(solution)/shard_map/pallas_call | solution.py:345
  40.6 0.0 copy-done.1
  40.7 0.0 copy-done.3
  40.7 0.0 copy-done.2
  40.7 2.8 %shard_map.71 = (bf16[2,512,512]{2,1,0:T(8,128)(2,1)S(1)}, bf16[2,2,128,512]{3,2,1,0:T(8,128)(2,1)S(1)}, f32[2,2,512,512]{3,2,1,0:T(8,128)S(1)}, bf16[2,512,256]{2,1,0:T(8,128)(2,1)S(1)}, f32[8,128]{1,0:T(8,128)}) custom-call(s32[1,2,1]{2,1,0:T(2,128)S(1)} %copy.8.flag_ref, s32[1,2,1]{2,1,0:T(2,128)S(1)} %copy.10.offset_ref, f32[1,2]{1,0:T(1,128)S(1)} %copy-done.3, ...), custom_call_target="tpu_custom_call" | custom-call | flops 2300000000 | bytes 7340032 | tf_op jit(solution)/shard_map/pallas_call | solution.py:238
  43.5 1.1 %shard_map.72.merged_ref = f32[2,512,512]{2,1,0:T(8,128)S(1)} custom-call(bf16[2,256,512]{2,1,0:T(8,128)(2,1)S(1)} %shard_map.69.own_ref, bf16[256,128]{1,0:T(8,128)(2,1)S(1)} %get-tuple-element.56.rims_ref, bf16[2,512,512]{2,1,0:T(8,128)(2,1)S(1)} %get-tuple-element.59.centre_ref, bf16[2,2,128,512]{3,2,1,0:T(8,128)(2,1)S(1)} %get-tuple-element.60.rim_ref, ...), custom_call_target="tpu_custom_call" | custom-call | flops 536870912 | bytes 8388608 | tf_op jit(solution)/shard_map/pallas_call | solution.py:486
  44.6 0.0 collective-permute-done.9.far_inner
  44.6 2.0 %shard_map.73 = (f32[2,512,512]{2,1,0:T(8,128)}, f32[512,256]{1,0:T(8,128)S(1)}) custom-call(bf16[2,256,384]{2,1,0:T(8,128)(2,1)S(1)} %collective-permute-done.9.far_inner, f32[2,512,512]{2,1,0:T(8,128)S(1)} %shard_map.72.merged_ref, bf16[2,512,512]{2,1,0:T(8,128)(2,1)S(1)} %get-tuple-element.59.centre_ref, ...), custom_call_target="tpu_custom_call" | custom-call | flops 536870912 | bytes 8388608 | tf_op jit(solution)/shard_map/pallas_call | solution.py:497
  46.6 0.0 collective-permute-done.12.rims_ref
  46.6 1.6 %shard_map.74 = f32[2,512,512]{2,1,0:T(8,128)} custom-call(bf16[2,256,128]{2,1,0:T(8,128)(2,1)S(1)} %collective-permute-done.8.far_outer, f32[512,256]{1,0:T(8,128)S(1)} %get-tuple-element.63.partial_ref, bf16[256,128]{1,0:T(8,128)(2,1)S(1)} %collective-permute-done.12.rims_ref, ...), custom_call_target="tpu_custom_call", output_to_operand_aliasing={{}: (8, {})} | custom-call | flops 536870912 | bytes 8388608 | tf_op jit(solution)/shard_map/pallas_call | solution.py:509
  (1 shorter events, 0.0 us)
Async XLA Ops:
  0.0 1.2 %copy-start = (bf16[2,32,8192]{2,1,0:T(8,128)(2,1)S(1)}, bf16[2,32,8192]{2,1,0:T(8,128)(2,1)}, u32[]{:S(2)}) copy-start(bf16[2,32,8192]{2,1,0:T(8,128)(2,1)} %param.6) | copy-start | bytes 3145732
  2.3 6.7 %collective-permute-start = (bf16[8,64,128]{2,1,0:T(8,128)(2,1)S(1)}, bf16[8,64,128]{2,1,0:T(8,128)(2,1)S(1)}, u32[]{:S(2)}, u32[]{:S(2)}) collective-permute-start(bf16[8,64,128]{2,1,0:T(8,128)(2,1)S(1)} %get-tuple-element.36), channel_id=1, source_target_pairs={{0,8},{1,9},{2,10},{3,11},{4,12},{5,13},{6,14},{7,15},{8,0},{9,1},... | collective-permute-start | bytes 393224 | tf_op jit(solution)/shard_map/ppermute | solution.py:113
  2.3 28.0 %all-to-all-start = ((bf16[16,64,384]{2,1,0:T(8,128)(2,1)}), bf16[16,64,384]{2,1,0:T(8,128)(2,1)S(1)}, u32[]{:S(2)}, u32[]{:S(2)}) async-start(bf16[16,64,384]{2,1,0:T(8,128)(2,1)} %get-tuple-element.48), calls=%async_computation | async-start | bytes 1572864 | tf_op jit(solution)/shard_map/all_to_all | solution.py:568
  9.0 8.6 %copy-start.4 = (s32[1,2,1]{1,2,0:T(1,128)S(1)}, s32[1,2,1]{1,2,0:T(1,128)}, u32[]{:S(2)}) copy-start(s32[1,2,1]{1,2,0:T(1,128)} %param.7) | copy-start | bytes 28
  9.0 24.7 %copy-start.5 = (s32[1,2,1]{1,2,0:T(1,128)S(1)}, s32[1,2,1]{1,2,0:T(1,128)}, u32[]{:S(2)}) copy-start(s32[1,2,1]{1,2,0:T(1,128)} %param.8) | copy-start | bytes 28
  9.0 5.7 %collective-permute-start.1 = (bf16[128,128]{1,0:T(8,128)(2,1)S(1)}, bf16[128,128]{1,0:T(8,128)(2,1)S(1)}, u32[]{:S(2)}, u32[]{:S(2)}) collective-permute-start(bf16[128,128]{1,0:T(8,128)(2,1)S(1)} %get-tuple-element.40), channel_id=1, source_target_pairs={{0,1},{1,0},{2,3},{3,2},{4,5},{5,4},{6,7},{7,6},{8,9},{9,8},{10,11... | collective-permute-start | bytes 98312 | tf_op jit(solution)/shard_map/ppermute | solution.py:113
  9.3 8.1 %collective-permute-start.2 = (bf16[128,128]{1,0:T(8,128)(2,1)S(1)}, bf16[128,128]{1,0:T(8,128)(2,1)S(1)}, u32[]{:S(2)}, u32[]{:S(2)}) collective-permute-start(bf16[128,128]{1,0:T(8,128)(2,1)S(1)} %get-tuple-element.41), channel_id=1, source_target_pairs={{0,2},{1,3},{2,0},{3,1},{4,6},{5,7},{6,4},{7,5},{8,10},{9,11},{10,... | collective-permute-start | bytes 98312 | tf_op jit(solution)/shard_map/ppermute | solution.py:113
  10.7 8.1 %collective-permute-start.3 = (bf16[128,128]{1,0:T(8,128)(2,1)S(1)}, bf16[128,128]{1,0:T(8,128)(2,1)S(1)}, u32[]{:S(2)}, u32[]{:S(2)}) collective-permute-start(bf16[128,128]{1,0:T(8,128)(2,1)S(1)} %get-tuple-element.42), channel_id=1, source_target_pairs={{0,3},{1,2},{2,1},{3,0},{4,7},{5,6},{6,5},{7,4},{8,11},{9,10},{10,... | collective-permute-start | bytes 98312 | tf_op jit(solution)/shard_map/ppermute | solution.py:113
  11.0 14.6 %collective-permute-start.4 = (bf16[128,128]{1,0:T(8,128)(2,1)S(1)}, bf16[128,128]{1,0:T(8,128)(2,1)S(1)}, u32[]{:S(2)}, u32[]{:S(2)}) collective-permute-start(bf16[128,128]{1,0:T(8,128)(2,1)S(1)} %get-tuple-element.43), channel_id=1, source_target_pairs={{0,4},{1,5},{2,6},{3,7},{4,0},{5,1},{6,2},{7,3},{8,12},{9,13},{10,... | collective-permute-start | bytes 98312 | tf_op jit(solution)/shard_map/ppermute | solution.py:113
  14.7 10.8 %collective-permute-start.5 = (bf16[128,128]{1,0:T(8,128)(2,1)S(1)}, bf16[128,128]{1,0:T(8,128)(2,1)S(1)}, u32[]{:S(2)}, u32[]{:S(2)}) collective-permute-start(bf16[128,128]{1,0:T(8,128)(2,1)S(1)} %get-tuple-element.44), channel_id=1, source_target_pairs={{0,5},{1,4},{2,7},{3,6},{4,1},{5,0},{6,3},{7,2},{8,13},{9,12},{10,... | collective-permute-start | bytes 98312 | tf_op jit(solution)/shard_map/ppermute | solution.py:113
  14.8 13.0 %collective-permute-start.6 = (bf16[128,128]{1,0:T(8,128)(2,1)S(1)}, bf16[128,128]{1,0:T(8,128)(2,1)S(1)}, u32[]{:S(2)}, u32[]{:S(2)}) collective-permute-start(bf16[128,128]{1,0:T(8,128)(2,1)S(1)} %get-tuple-element.45), channel_id=1, source_target_pairs={{0,6},{1,7},{2,4},{3,5},{4,2},{5,3},{6,0},{7,1},{8,14},{9,15},{10,... | collective-permute-start | bytes 98312 | tf_op jit(solution)/shard_map/ppermute | solution.py:113
  17.4 10.4 %collective-permute-start.7 = (bf16[128,128]{1,0:T(8,128)(2,1)S(1)}, bf16[128,128]{1,0:T(8,128)(2,1)S(1)}, u32[]{:S(2)}, u32[]{:S(2)}) collective-permute-start(bf16[128,128]{1,0:T(8,128)(2,1)S(1)} %get-tuple-element.46), channel_id=1, source_target_pairs={{0,7},{1,6},{2,5},{3,4},{4,3},{5,2},{6,1},{7,0},{8,15},{9,14},{10,... | collective-permute-start | bytes 98312 | tf_op jit(solution)/shard_map/ppermute | solution.py:113
  28.6 12.0 %copy-start.1 = (bf16[1,544,512]{2,1,0:T(8,128)(2,1)S(1)}, bf16[1,544,512]{2,1,0:T(8,128)(2,1)}, u32[]{:S(2)}) copy-start(bf16[1,544,512]{2,1,0:T(8,128)(2,1)} %range_ref.1) | copy-start | bytes 1671172
  28.6 12.0 %copy-start.3 = (f32[1,2]{1,0:T(1,128)S(1)}, f32[1,2]{1,0:T(1,128)}, u32[]{:S(2)}) copy-start(f32[1,2]{1,0:T(1,128)} %shift_ref.1) | copy-start | bytes 28
  28.6 6.4 %collective-permute-start.8 = (bf16[2,256,128]{2,1,0:T(8,128)(2,1)S(1)}, bf16[2,256,128]{2,1,0:T(8,128)(2,1)S(1)}, u32[]{:S(2)}, u32[]{:S(2)}) collective-permute-start(bf16[2,256,128]{2,1,0:T(8,128)(2,1)S(1)} %get-tuple-element.47), channel_id=1, source_target_pairs={{0,16},{16,0},{1,17},{17,1},{2,18},{18,2},{3,19},{19,3},{4,20},{20... | collective-permute-start | bytes 393224 | tf_op jit(solution)/shard_map/ppermute | solution.py:530
  30.8 13.8 %collective-permute-start.9 = (bf16[2,256,384]{2,1,0:T(8,128)(2,1)S(1)}, bf16[2,256,384]{2,1,0:T(8,128)(2,1)S(1)}, u32[]{:S(2)}, u32[]{:S(2)}) collective-permute-start(bf16[2,256,384]{2,1,0:T(8,128)(2,1)S(1)} %shard_map.68), channel_id=1, source_target_pairs={{0,16},{16,0},{1,17},{17,1},{2,18},{18,2},{3,19},{19,3},{4,20},{20... | collective-permute-start | bytes 1179656 | tf_op jit(solution)/shard_map/ppermute | solution.py:530
  31.4 3.6 %collective-permute-start.10 = (bf16[256,128]{1,0:T(8,128)(2,1)S(1)}, bf16[256,128]{1,0:T(8,128)(2,1)S(1)}, u32[]{:S(2)}, u32[]{:S(2)}) collective-permute-start(bf16[256,128]{1,0:T(8,128)(2,1)S(1)} %get-tuple-element.51), channel_id=1, source_target_pairs={{0,1},{2,3},{4,5},{6,7},{8,9},{10,11},{12,13},{14,15},{1,0},{3,2},... | collective-permute-start | bytes 196616 | tf_op jit(solution)/shard_map/ppermute | solution.py:361
  31.4 6.6 %collective-permute-start.11 = (bf16[256,128]{1,0:T(8,128)(2,1)S(1)}, bf16[256,128]{1,0:T(8,128)(2,1)S(1)}, u32[]{:S(2)}, u32[]{:S(2)}) collective-permute-start(bf16[256,128]{1,0:T(8,128)(2,1)S(1)} %get-tuple-element.53), channel_id=1, source_target_pairs={{1,2},{3,4},{5,6},{7,8},{9,10},{11,12},{13,14},{2,1},{4,3},{6,5},{... | collective-permute-start | bytes 196616 | tf_op jit(solution)/shard_map/ppermute | solution.py:361
  33.8 6.9 %copy-start.2 = (bf16[1,2,512,256]{3,2,1,0:T(8,128)(2,1)S(1)}, bf16[1,2,512,256]{3,2,1,0:T(8,128)(2,1)}, u32[]{:S(2)}) copy-start(bf16[1,2,512,256]{3,2,1,0:T(8,128)(2,1)} %interp_ref.1) | copy-start | bytes 1572868
  38.1 8.5 %collective-permute-start.12 = (bf16[256,128]{1,0:T(8,128)(2,1)S(1)}, bf16[256,128]{1,0:T(8,128)(2,1)S(1)}, u32[]{:S(2)}, u32[]{:S(2)}) collective-permute-start(bf16[256,128]{1,0:T(8,128)(2,1)S(1)} %get-tuple-element.58.after_ref), channel_id=1, source_target_pairs={{0,16},{16,0},{1,17},{17,1},{2,18},{18,2},{3,19},{19,3},{4,20},{20... | collective-permute-start | bytes 196616 | tf_op jit(solution)/shard_map/ppermute | solution.py:530

commit v10 on v9

--- a/solution.py
+++ b/solution.py
@@ -577,11 +577,11 @@
     far = [from_partner(value, 1) for value in (out_outer, out_inner)]
     edges = [after(edge, out_inner) for edge in edges]
     edges = exchanged(edges[0], 0), exchanged(edges[1], 1)
-    pulses = after(pulses, far[0], *edges)
+    pulses = after(pulses, far[0])
     own_kernel = functools.partial(own_rows_kernel, local_pulses)
     own = inner_image(own_kernel, angles, matrix, pulses, (own_outer,))
-    rims, out_rims = sorted_rims(own_side, *edges)
-    tables = merge_tables(0, 1, *settings, after(out_rims, own))
+    tables = merge_tables(0, 1, *settings, after(own_side, far[0]))
+    rims, out_rims = sorted_rims(own_side, after(edges[0], tables[0]), edges[1])
     for level in range(levels):
         stride = 2**level
         if level > 0:

time: 48.9 us -> 50.4 us (1.031)
  Pallas kernels: 12.2 us -> 12.9 us
  local copies, waits for them, and re-layouts: 1.44 us -> 2.07 us
    ppermute x3, waiting for transfers between devices: 1.17 us -> 3.73 us  [from_partner(): return lax.ppermute(value, 'sub', pairs)]
    ppermute x2, waiting for transfers between devices: 2.96 us -> 0.87 us  [exchanged(): return lax.ppermute(value, 'rng', pairs + [(j, i) for i, j in pairs] + ends)]
    pallas_call x1, Pallas kernels: 0.81 us -> 1.45 us  [outer_image(): pl.pallas_call(functools.partial(outer_kernel, len(pieces)), out_shape=[i...]
    unnamed x14 -> x16, local copies, waits for them, and re-layouts: 1.44 us -> 2.07 us
  transfers between devices with their start and end apart: 14 -> 14, of which waited for: 4 -> 4; matrix products, arithmetic and copies ran while one was open for 0% -> 0% of each run, Pallas kernels for 20% -> 21%
where the time goes in v10:
time: 50.4 us; the launch traced here: 49.5 us
  starting transfers between devices  20.8 us (41%)
  waiting for transfers between devices  13.6 us (27%)
  Pallas kernels  12.9 us (26%)
  local copies, waits for them, and re-layouts  2.07 us (4%)
    ppermute x8, waiting for transfers between devices, across(): return lax.ppermute(value, 'rng', [(i, i ^ mask) for i in range(devices)])  8.96 us
    ppermute x8, starting transfers between devices, across(): return lax.ppermute(value, 'rng', [(i, i ^ mask) for i in range(devices)])  8.46 us
    all_to_all x1, starting transfers between devices, on_device(): lax.all_to_all(blocks, 'rng', split_axis=0, concat_axis=0, tiled=True)  6.72 us
    ppermute x3, waiting for transfers between devices, from_partner(): return lax.ppermute(value, 'sub', pairs)  3.73 us
    ppermute x3, starting transfers between devices, from_partner(): return lax.ppermute(value, 'sub', pairs)  3.67 us
    pallas_call x1, Pallas kernels, merge_tables(): pl.pallas_call(functools.partial(merge_table_kernel, level, stride), out_...  2.8 us
    unnamed x16, local copies, waits for them, and re-layouts  2.07 us
    pallas_call x1, Pallas kernels, merged_image(): pl.pallas_call(middle_kernel, out_shape=[image, jax.ShapeDtypeStruct((ang...  2 us
  transfers between devices with their start and end apart: 14, of which 4 were waited for; matrix products, arithmetic and copies ran while one was open for 0% of the time, Pallas kernels for 21%

profile of v10, /device:TPU:16, one launch (start us, length us, event | category | flops | bytes accessed | tf_op | source)
XLA Modules:
  0.0 49.5 jit_solution(15376474829778280669)
XLA Ops:
  0.0 0.0 copy-start
  0.0 1.2 %copy-done = bf16[2,32,8192]{2,1,0:T(8,128)(2,1)S(1)} copy-done((bf16[2,32,8192]{2,1,0:T(8,128)(2,1)S(1)}, bf16[2,32,8192]{2,1,0:T(8,128)(2,1)}, u32[]{:S(2)}) %copy-start) | copy-done | bytes 1048600
  1.2 1.0 %shard_map.64 = (bf16[8,64,128]{2,1,0:T(8,128)(2,1)S(1)}, bf16[8,64,128]{2,1,0:T(8,128)(2,1)S(1)}, bf16[16,64,384]{2,1,0:T(8,128)(2,1)}) custom-call(bf16[64,8192]{1,0:T(8,128)(2,1)S(1)} %bitcast.4), custom_call_target="tpu_custom_call" | custom-call | bytes 2097152 | tf_op jit(solution)/shard_map/pallas_call | solution.py:81
  2.3 0.0 collective-permute-start
  2.3 6.7 %all-to-all-start = ((bf16[16,64,384]{2,1,0:T(8,128)(2,1)}), bf16[16,64,384]{2,1,0:T(8,128)(2,1)S(1)}, u32[]{:S(2)}, u32[]{:S(2)}) async-start(bf16[16,64,384]{2,1,0:T(8,128)(2,1)} %get-tuple-element.49), calls=%async_computation | async-start | bytes 1572864 | tf_op jit(solution)/shard_map/all_to_all | solution.py:568
  9.0 0.0 collective-permute-done.relay_ref
  9.0 0.0 copy-start.5
  9.0 0.0 copy-start.6
  9.0 0.0 copy-start.1
  9.1 0.0 copy-start.2
  9.1 0.0 copy-start.4
  9.1 0.2 collective-permute-start.1
  9.3 1.5 %collective-permute-start.2 = (bf16[128,128]{1,0:T(8,128)(2,1)S(1)}, bf16[128,128]{1,0:T(8,128)(2,1)S(1)}, u32[]{:S(2)}, u32[]{:S(2)}) collective-permute-start(bf16[128,128]{1,0:T(8,128)(2,1)S(1)} %get-tuple-element.42), channel_id=1, source_target_pairs={{0,2},{1,3},{2,0},{3,1},{4,6},{5,7},{6,4},{7,5},{8,10},{9,11},{10,... | collective-permute-start | bytes 98312 | tf_op jit(solution)/shard_map/ppermute | solution.py:113
  10.8 0.2 collective-permute-start.3
  11.0 3.8 %collective-permute-start.4 = (bf16[128,128]{1,0:T(8,128)(2,1)S(1)}, bf16[128,128]{1,0:T(8,128)(2,1)S(1)}, u32[]{:S(2)}, u32[]{:S(2)}) collective-permute-start(bf16[128,128]{1,0:T(8,128)(2,1)S(1)} %get-tuple-element.44), channel_id=1, source_target_pairs={{0,4},{1,5},{2,6},{3,7},{4,0},{5,1},{6,2},{7,3},{8,12},{9,13},{10,... | collective-permute-start | bytes 98312 | tf_op jit(solution)/shard_map/ppermute | solution.py:113
  14.8 0.0 collective-permute-start.5
  14.8 0.0 collective-permute-done.1.refs_1_
  14.8 2.6 %collective-permute-start.6 = (bf16[128,128]{1,0:T(8,128)(2,1)S(1)}, bf16[128,128]{1,0:T(8,128)(2,1)S(1)}, u32[]{:S(2)}, u32[]{:S(2)}) collective-permute-start(bf16[128,128]{1,0:T(8,128)(2,1)S(1)} %get-tuple-element.46), channel_id=1, source_target_pairs={{0,6},{1,7},{2,4},{3,5},{4,2},{5,3},{6,0},{7,1},{8,14},{9,15},{10,... | collective-permute-start | bytes 98312 | tf_op jit(solution)/shard_map/ppermute | solution.py:113
  17.4 0.0 collective-permute-done.2.refs_2_
  17.4 0.1 collective-permute-start.7
  17.5 0.0 copy-done.5
  17.5 0.1 copy.8.flag_ref
  17.6 1.2 %shard_map.66 = (bf16[256,1024]{1,0:T(8,128)(2,1)S(1)}, f32[8,128]{1,0:T(8,128)S(1)}) custom-call(s32[1,2,1]{2,1,0:T(2,128)S(1)} %copy.8.flag_ref, bf16[128,128]{1,0:T(8,128)(2,1)S(1)} %get-tuple-element.38.after_ref.refs_0_), custom_call_target="tpu_custom_call" | custom-call | flops 9000000 | bytes 4194304 | tf_op jit(solution)/shard_map/pallas_call | solution.py:152
  18.8 0.0 collective-permute-done.3.refs_3_
  18.8 6.8 %collective-permute-done.4.refs_4_ = bf16[128,128]{1,0:T(8,128)(2,1)S(1)} collective-permute-done((bf16[128,128]{1,0:T(8,128)(2,1)S(1)}, bf16[128,128]{1,0:T(8,128)(2,1)S(1)}, u32[]{:S(2)}, u32[]{:S(2)}) %collective-permute-start.4) | collective-permute-done | bytes 32800 | tf_op jit(solution)/shard_map/ppermute | solution.py:113
  25.6 0.0 collective-permute-done.5.refs_5_
  25.6 2.2 %collective-permute-done.6.refs_6_ = bf16[128,128]{1,0:T(8,128)(2,1)S(1)} collective-permute-done((bf16[128,128]{1,0:T(8,128)(2,1)S(1)}, bf16[128,128]{1,0:T(8,128)(2,1)S(1)}, u32[]{:S(2)}, u32[]{:S(2)}) %collective-permute-start.6) | collective-permute-done | bytes 32800 | tf_op jit(solution)/shard_map/ppermute | solution.py:113
  27.8 0.0 collective-permute-done.7.refs_7_
  27.8 1.4 %shard_map.67 = (bf16[2,256,128]{2,1,0:T(8,128)(2,1)S(1)}, bf16[2,256,128]{2,1,0:T(8,128)(2,1)}, bf16[256,128]{1,0:T(8,128)(2,1)S(1)}, bf16[256,128]{1,0:T(8,128)(2,1)S(1)}) custom-call(f32[8,128]{1,0:T(8,128)S(1)} %get-tuple-element.55.side_ref.after_ref, bf16[256,1024]{1,0:T(8,128)(2,1)S(1)} %get-tuple-element.40.rows_ref, ...), custom_call_target="tpu_custom_call" | custom-call | flops 268435456 | bytes 3145728 | tf_op jit(solution)/shard_map/pallas_call | solution.py:312
  29.2 0.0 copy-start.3
  29.2 0.6 %copy-done.3 = bf16[256,128]{1,0:T(8,128)(2,1)} copy-done((bf16[256,128]{1,0:T(8,128)(2,1)}, bf16[256,128]{1,0:T(8,128)(2,1)S(1)}, u32[]{:S(2)}) %copy-start.3) | copy-done | bytes 65560
  29.9 1.5 %collective-permute-start.8 = (bf16[2,256,128]{2,1,0:T(8,128)(2,1)}, bf16[2,256,128]{2,1,0:T(8,128)(2,1)S(1)}, u32[]{:S(2)}, u32[]{:S(2)}) collective-permute-start(bf16[2,256,128]{2,1,0:T(8,128)(2,1)} %get-tuple-element.48), channel_id=1, source_target_pairs={{0,16},{16,0},{1,17},{17,1},{2,18},{18,2},{3,19},{19,3},{4,20},{20... | collective-permute-start | bytes 393224 | tf_op jit(solution)/shard_map/ppermute | solution.py:530
  31.4 0.0 all-to-all-done
  31.4 0.6 %shard_map.68 = bf16[2,256,384]{2,1,0:T(8,128)(2,1)S(1)} custom-call(bf16[256,1024]{1,0:T(8,128)(2,1)S(1)} %get-tuple-element.40.rows_ref, bf16[1024,384]{1,0:T(8,128)(2,1)S(1)} %bitcast.2), custom_call_target="tpu_custom_call" | custom-call | flops 402653184 | bytes 3145728 | tf_op jit(solution)/shard_map/pallas_call | solution.py:345
  32.0 0.6 %collective-permute-start.9 = (bf16[2,256,384]{2,1,0:T(8,128)(2,1)S(1)}, bf16[2,256,384]{2,1,0:T(8,128)(2,1)S(1)}, u32[]{:S(2)}, u32[]{:S(2)}) collective-permute-start(bf16[2,256,384]{2,1,0:T(8,128)(2,1)S(1)} %shard_map.68), channel_id=1, source_target_pairs={{0,16},{16,0},{1,17},{17,1},{2,18},{18,2},{3,19},{19,3},{4,20},{20... | collective-permute-start | bytes 1179656 | tf_op jit(solution)/shard_map/ppermute | solution.py:530
  32.5 0.0 copy-done.6
  32.5 0.1 copy.10.offset_ref
  32.6 3.7 %collective-permute-done.8.far_outer = bf16[2,256,128]{2,1,0:T(8,128)(2,1)S(1)} collective-permute-done((bf16[2,256,128]{2,1,0:T(8,128)(2,1)}, bf16[2,256,128]{2,1,0:T(8,128)(2,1)S(1)}, u32[]{:S(2)}, u32[]{:S(2)}) %collective-permute-start.8) | collective-permute-done | bytes 131104 | tf_op jit(solution)/shard_map/ppermute | solution.py:530
  36.4 0.0 collective-permute-start.10
  36.4 1.9 %collective-permute-start.11 = (bf16[256,128]{1,0:T(8,128)(2,1)S(1)}, bf16[256,128]{1,0:T(8,128)(2,1)S(1)}, u32[]{:S(2)}, u32[]{:S(2)}) collective-permute-start(bf16[256,128]{1,0:T(8,128)(2,1)S(1)} %get-tuple-element.59), channel_id=1, source_target_pairs={{1,2},{3,4},{5,6},{7,8},{9,10},{11,12},{13,14},{2,1},{4,3},{6,5},{... | collective-permute-start | bytes 196616 | tf_op jit(solution)/shard_map/ppermute | solution.py:361
  38.3 0.0 copy-done.1
  38.3 0.0 copy-done.2
  38.3 0.0 copy-done.4
  38.3 2.8 %shard_map.70 = (bf16[2,512,512]{2,1,0:T(8,128)(2,1)S(1)}, bf16[2,2,128,512]{3,2,1,0:T(8,128)(2,1)S(1)}, f32[2,2,512,512]{3,2,1,0:T(8,128)S(1)}, bf16[2,512,256]{2,1,0:T(8,128)(2,1)S(1)}, f32[8,128]{1,0:T(8,128)}) custom-call(s32[1,2,1]{2,1,0:T(2,128)S(1)} %copy.8.flag_ref, s32[1,2,1]{2,1,0:T(2,128)S(1)} %copy.10.offset_ref, f32[1,2]{1,0:T(1,128)S(1)} %copy-done.4, ...), custom_call_target="tpu_custom_call" | custom-call | flops 2300000000 | bytes 7340032 | tf_op jit(solution)/shard_map/pallas_call | solution.py:238
  41.1 0.9 %shard_map.69.own_ref = bf16[2,256,512]{2,1,0:T(8,128)(2,1)S(1)} custom-call(bf16[256,1024]{1,0:T(8,128)(2,1)S(1)} %get-tuple-element.40.rows_ref, bf16[1024,384]{1,0:T(8,128)(2,1)S(1)} %bitcast.3, bf16[2,256,128]{2,1,0:T(8,128)(2,1)S(1)} %get-tuple-element.52.outer_ref), custom_call_target="tpu_custom_call" | custom-call | flops 402653184 | bytes 3145728 | tf_op jit(solution)/shard_map/pallas_call | solution.py:345
  42.1 0.0 collective-permute-done.10.first_ref
  42.1 0.9 %collective-permute-done.11.second_ref = bf16[256,128]{1,0:T(8,128)(2,1)S(1)} collective-permute-done((bf16[256,128]{1,0:T(8,128)(2,1)S(1)}, bf16[256,128]{1,0:T(8,128)(2,1)S(1)}, u32[]{:S(2)}, u32[]{:S(2)}) %collective-permute-start.11) | collective-permute-done | bytes 65568 | tf_op jit(solution)/shard_map/ppermute | solution.py:361
  42.9 0.2 shard_map.71
  43.1 1.6 %collective-permute-start.12 = (bf16[256,128]{1,0:T(8,128)(2,1)S(1)}, bf16[256,128]{1,0:T(8,128)(2,1)S(1)}, u32[]{:S(2)}, u32[]{:S(2)}) collective-permute-start(bf16[256,128]{1,0:T(8,128)(2,1)S(1)} %get-tuple-element.65), channel_id=1, source_target_pairs={{0,16},{16,0},{1,17},{17,1},{2,18},{18,2},{3,19},{19,3},{4,20},{20... | collective-permute-start | bytes 196616 | tf_op jit(solution)/shard_map/ppermute | solution.py:530
  44.7 1.1 %shard_map.72.merged_ref = f32[2,512,512]{2,1,0:T(8,128)S(1)} custom-call(bf16[2,256,512]{2,1,0:T(8,128)(2,1)S(1)} %shard_map.69.own_ref, bf16[256,128]{1,0:T(8,128)(2,1)S(1)} %get-tuple-element.60.rims_ref, bf16[2,512,512]{2,1,0:T(8,128)(2,1)S(1)} %get-tuple-element.56.centre_ref, bf16[2,2,128,512]{3,2,1,0:T(8,128)(2,1)S(1)} %get-tuple-element.61.rim_ref, ...), custom_call_target="tpu_custom_call" | custom-call | flops 536870912 | bytes 8388608 | tf_op jit(solution)/shard_map/pallas_call | solution.py:486
  45.8 0.0 collective-permute-done.9.far_inner
  45.8 2.0 %shard_map.73 = (f32[2,512,512]{2,1,0:T(8,128)}, f32[512,256]{1,0:T(8,128)S(1)}) custom-call(bf16[2,256,384]{2,1,0:T(8,128)(2,1)S(1)} %collective-permute-done.9.far_inner, f32[2,512,512]{2,1,0:T(8,128)S(1)} %shard_map.72.merged_ref, bf16[2,512,512]{2,1,0:T(8,128)(2,1)S(1)} %get-tuple-element.56.centre_ref, ...), custom_call_target="tpu_custom_call" | custom-call | flops 536870912 | bytes 8388608 | tf_op jit(solution)/shard_map/pallas_call | solution.py:497
  47.8 0.0 collective-permute-done.12.rims_ref
  47.8 1.6 %shard_map.74 = f32[2,512,512]{2,1,0:T(8,128)} custom-call(bf16[2,256,128]{2,1,0:T(8,128)(2,1)S(1)} %collective-permute-done.8.far_outer, f32[512,256]{1,0:T(8,128)S(1)} %get-tuple-element.64.partial_ref, bf16[256,128]{1,0:T(8,128)(2,1)S(1)} %collective-permute-done.12.rims_ref, ...), custom_call_target="tpu_custom_call", output_to_operand_aliasing={{}: (8, {})} | custom-call | flops 536870912 | bytes 8388608 | tf_op jit(solution)/shard_map/pallas_call | solution.py:509
  (1 shorter events, 0.0 us)
Async XLA Ops:
  0.0 1.2 %copy-start = (bf16[2,32,8192]{2,1,0:T(8,128)(2,1)S(1)}, bf16[2,32,8192]{2,1,0:T(8,128)(2,1)}, u32[]{:S(2)}) copy-start(bf16[2,32,8192]{2,1,0:T(8,128)(2,1)} %param.6) | copy-start | bytes 3145732
  2.3 6.7 %collective-permute-start = (bf16[8,64,128]{2,1,0:T(8,128)(2,1)S(1)}, bf16[8,64,128]{2,1,0:T(8,128)(2,1)S(1)}, u32[]{:S(2)}, u32[]{:S(2)}) collective-permute-start(bf16[8,64,128]{2,1,0:T(8,128)(2,1)S(1)} %get-tuple-element.37), channel_id=1, source_target_pairs={{0,8},{1,9},{2,10},{3,11},{4,12},{5,13},{6,14},{7,15},{8,0},{9,1},... | collective-permute-start | bytes 393224 | tf_op jit(solution)/shard_map/ppermute | solution.py:113
  2.3 29.1 %all-to-all-start = ((bf16[16,64,384]{2,1,0:T(8,128)(2,1)}), bf16[16,64,384]{2,1,0:T(8,128)(2,1)S(1)}, u32[]{:S(2)}, u32[]{:S(2)}) async-start(bf16[16,64,384]{2,1,0:T(8,128)(2,1)} %get-tuple-element.49), calls=%async_computation | async-start | bytes 1572864 | tf_op jit(solution)/shard_map/all_to_all | solution.py:568
  9.0 8.6 %copy-start.5 = (s32[1,2,1]{1,2,0:T(1,128)S(1)}, s32[1,2,1]{1,2,0:T(1,128)}, u32[]{:S(2)}) copy-start(s32[1,2,1]{1,2,0:T(1,128)} %param.7) | copy-start | bytes 28
  9.0 23.5 %copy-start.6 = (s32[1,2,1]{1,2,0:T(1,128)S(1)}, s32[1,2,1]{1,2,0:T(1,128)}, u32[]{:S(2)}) copy-start(s32[1,2,1]{1,2,0:T(1,128)} %param.8) | copy-start | bytes 28
  9.0 29.2 %copy-start.1 = (bf16[1,544,512]{2,1,0:T(8,128)(2,1)S(1)}, bf16[1,544,512]{2,1,0:T(8,128)(2,1)}, u32[]{:S(2)}) copy-start(bf16[1,544,512]{2,1,0:T(8,128)(2,1)} %range_ref.1) | copy-start | bytes 1671172
  9.1 29.2 %copy-start.2 = (bf16[1,2,512,256]{3,2,1,0:T(8,128)(2,1)S(1)}, bf16[1,2,512,256]{3,2,1,0:T(8,128)(2,1)}, u32[]{:S(2)}) copy-start(bf16[1,2,512,256]{3,2,1,0:T(8,128)(2,1)} %interp_ref.1) | copy-start | bytes 1572868
  9.1 29.2 %copy-start.4 = (f32[1,2]{1,0:T(1,128)S(1)}, f32[1,2]{1,0:T(1,128)}, u32[]{:S(2)}) copy-start(f32[1,2]{1,0:T(1,128)} %shift_ref.1) | copy-start | bytes 28
  9.1 5.7 %collective-permute-start.1 = (bf16[128,128]{1,0:T(8,128)(2,1)S(1)}, bf16[128,128]{1,0:T(8,128)(2,1)S(1)}, u32[]{:S(2)}, u32[]{:S(2)}) collective-permute-start(bf16[128,128]{1,0:T(8,128)(2,1)S(1)} %get-tuple-element.41), channel_id=1, source_target_pairs={{0,1},{1,0},{2,3},{3,2},{4,5},{5,4},{6,7},{7,6},{8,9},{9,8},{10,11... | collective-permute-start | bytes 98312 | tf_op jit(solution)/shard_map/ppermute | solution.py:113
  9.3 8.1 %collective-permute-start.2 = (bf16[128,128]{1,0:T(8,128)(2,1)S(1)}, bf16[128,128]{1,0:T(8,128)(2,1)S(1)}, u32[]{:S(2)}, u32[]{:S(2)}) collective-permute-start(bf16[128,128]{1,0:T(8,128)(2,1)S(1)} %get-tuple-element.42), channel_id=1, source_target_pairs={{0,2},{1,3},{2,0},{3,1},{4,6},{5,7},{6,4},{7,5},{8,10},{9,11},{10,... | collective-permute-start | bytes 98312 | tf_op jit(solution)/shard_map/ppermute | solution.py:113
  10.8 8.0 %collective-permute-start.3 = (bf16[128,128]{1,0:T(8,128)(2,1)S(1)}, bf16[128,128]{1,0:T(8,128)(2,1)S(1)}, u32[]{:S(2)}, u32[]{:S(2)}) collective-permute-start(bf16[128,128]{1,0:T(8,128)(2,1)S(1)} %get-tuple-element.43), channel_id=1, source_target_pairs={{0,3},{1,2},{2,1},{3,0},{4,7},{5,6},{6,5},{7,4},{8,11},{9,10},{10,... | collective-permute-start | bytes 98312 | tf_op jit(solution)/shard_map/ppermute | solution.py:113
  11.0 14.6 %collective-permute-start.4 = (bf16[128,128]{1,0:T(8,128)(2,1)S(1)}, bf16[128,128]{1,0:T(8,128)(2,1)S(1)}, u32[]{:S(2)}, u32[]{:S(2)}) collective-permute-start(bf16[128,128]{1,0:T(8,128)(2,1)S(1)} %get-tuple-element.44), channel_id=1, source_target_pairs={{0,4},{1,5},{2,6},{3,7},{4,0},{5,1},{6,2},{7,3},{8,12},{9,13},{10,... | collective-permute-start | bytes 98312 | tf_op jit(solution)/shard_map/ppermute | solution.py:113
  14.8 10.8 %collective-permute-start.5 = (bf16[128,128]{1,0:T(8,128)(2,1)S(1)}, bf16[128,128]{1,0:T(8,128)(2,1)S(1)}, u32[]{:S(2)}, u32[]{:S(2)}) collective-permute-start(bf16[128,128]{1,0:T(8,128)(2,1)S(1)} %get-tuple-element.45), channel_id=1, source_target_pairs={{0,5},{1,4},{2,7},{3,6},{4,1},{5,0},{6,3},{7,2},{8,13},{9,12},{10,... | collective-permute-start | bytes 98312 | tf_op jit(solution)/shard_map/ppermute | solution.py:113
  14.8 13.0 %collective-permute-start.6 = (bf16[128,128]{1,0:T(8,128)(2,1)S(1)}, bf16[128,128]{1,0:T(8,128)(2,1)S(1)}, u32[]{:S(2)}, u32[]{:S(2)}) collective-permute-start(bf16[128,128]{1,0:T(8,128)(2,1)S(1)} %get-tuple-element.46), channel_id=1, source_target_pairs={{0,6},{1,7},{2,4},{3,5},{4,2},{5,3},{6,0},{7,1},{8,14},{9,15},{10,... | collective-permute-start | bytes 98312 | tf_op jit(solution)/shard_map/ppermute | solution.py:113
  17.4 10.4 %collective-permute-start.7 = (bf16[128,128]{1,0:T(8,128)(2,1)S(1)}, bf16[128,128]{1,0:T(8,128)(2,1)S(1)}, u32[]{:S(2)}, u32[]{:S(2)}) collective-permute-start(bf16[128,128]{1,0:T(8,128)(2,1)S(1)} %get-tuple-element.47), channel_id=1, source_target_pairs={{0,7},{1,6},{2,5},{3,4},{4,3},{5,2},{6,1},{7,0},{8,15},{9,14},{10,... | collective-permute-start | bytes 98312 | tf_op jit(solution)/shard_map/ppermute | solution.py:113
  29.2 0.6 %copy-start.3 = (bf16[256,128]{1,0:T(8,128)(2,1)}, bf16[256,128]{1,0:T(8,128)(2,1)S(1)}, u32[]{:S(2)}) copy-start(bf16[256,128]{1,0:T(8,128)(2,1)S(1)} %get-tuple-element.54) | copy-start | bytes 196612
  29.9 6.5 %collective-permute-start.8 = (bf16[2,256,128]{2,1,0:T(8,128)(2,1)}, bf16[2,256,128]{2,1,0:T(8,128)(2,1)S(1)}, u32[]{:S(2)}, u32[]{:S(2)}) collective-permute-start(bf16[2,256,128]{2,1,0:T(8,128)(2,1)} %get-tuple-element.48), channel_id=1, source_target_pairs={{0,16},{16,0},{1,17},{17,1},{2,18},{18,2},{3,19},{19,3},{4,20},{20... | collective-permute-start | bytes 393224 | tf_op jit(solution)/shard_map/ppermute | solution.py:530
  32.0 13.8 %collective-permute-start.9 = (bf16[2,256,384]{2,1,0:T(8,128)(2,1)S(1)}, bf16[2,256,384]{2,1,0:T(8,128)(2,1)S(1)}, u32[]{:S(2)}, u32[]{:S(2)}) collective-permute-start(bf16[2,256,384]{2,1,0:T(8,128)(2,1)S(1)} %shard_map.68), channel_id=1, source_target_pairs={{0,16},{16,0},{1,17},{17,1},{2,18},{18,2},{3,19},{19,3},{4,20},{20... | collective-permute-start | bytes 1179656 | tf_op jit(solution)/shard_map/ppermute | solution.py:530
  36.4 5.7 %collective-permute-start.10 = (bf16[256,128]{1,0:T(8,128)(2,1)}, bf16[256,128]{1,0:T(8,128)(2,1)S(1)}, u32[]{:S(2)}, u32[]{:S(2)}) collective-permute-start(bf16[256,128]{1,0:T(8,128)(2,1)} %copy-done.3), channel_id=1, source_target_pairs={{0,1},{2,3},{4,5},{6,7},{8,9},{10,11},{12,13},{14,15},{1,0},{3,2},... | collective-permute-start | bytes 196616 | tf_op jit(solution)/shard_map/ppermute | solution.py:361
  36.4 6.6 %collective-permute-start.11 = (bf16[256,128]{1,0:T(8,128)(2,1)S(1)}, bf16[256,128]{1,0:T(8,128)(2,1)S(1)}, u32[]{:S(2)}, u32[]{:S(2)}) collective-permute-start(bf16[256,128]{1,0:T(8,128)(2,1)S(1)} %get-tuple-element.59), channel_id=1, source_target_pairs={{1,2},{3,4},{5,6},{7,8},{9,10},{11,12},{13,14},{2,1},{4,3},{6,5},{... | collective-permute-start | bytes 196616 | tf_op jit(solution)/shard_map/ppermute | solution.py:361
  43.1 4.7 %collective-permute-start.12 = (bf16[256,128]{1,0:T(8,128)(2,1)S(1)}, bf16[256,128]{1,0:T(8,128)(2,1)S(1)}, u32[]{:S(2)}, u32[]{:S(2)}) collective-permute-start(bf16[256,128]{1,0:T(8,128)(2,1)S(1)} %get-tuple-element.65), channel_id=1, source_target_pairs={{0,16},{16,0},{1,17},{17,1},{2,18},{18,2},{3,19},{19,3},{4,20},{20... | collective-permute-start | bytes 196616 | tf_op jit(solution)/shard_map/ppermute | solution.py:530

commit v11 on v9

--- a/solution.py
+++ b/solution.py
@@ -577,7 +577,7 @@
     far = [from_partner(value, 1) for value in (out_outer, out_inner)]
     edges = [after(edge, out_inner) for edge in edges]
     edges = exchanged(edges[0], 0), exchanged(edges[1], 1)
-    pulses = after(pulses, far[0], *edges)
+    pulses = after(pulses, far[0])
     own_kernel = functools.partial(own_rows_kernel, local_pulses)
     own = inner_image(own_kernel, angles, matrix, pulses, (own_outer,))
     rims, out_rims = sorted_rims(own_side, *edges)

time: 48.9 us -> 47.9 us (0.980)
  waiting for transfers between devices: 13.1 us -> 12.2 us
    ppermute x2, waiting for transfers between devices: 2.96 us -> 2 us  [exchanged(): return lax.ppermute(value, 'rng', pairs + [(j, i) for i, j in pairs] + ends)]
where the time goes in v11:
time: 47.9 us; the launch traced here: 47.3 us
  starting transfers between devices  21.3 us (44%)
  Pallas kernels  12.2 us (25%)
  waiting for transfers between devices  12.2 us (25%)
  local copies, waits for them, and re-layouts  1.44 us (3%)
    ppermute x8, waiting for transfers between devices, across(): return lax.ppermute(value, 'rng', [(i, i ^ mask) for i in range(devices)])  8.98 us
    ppermute x8, starting transfers between devices, across(): return lax.ppermute(value, 'rng', [(i, i ^ mask) for i in range(devices)])  8.48 us
    all_to_all x1, starting transfers between devices, on_device(): lax.all_to_all(blocks, 'rng', split_axis=0, concat_axis=0, tiled=True)  6.72 us
    ppermute x3, starting transfers between devices, from_partner(): return lax.ppermute(value, 'sub', pairs)  3.74 us
    pallas_call x1, Pallas kernels, merge_tables(): pl.pallas_call(functools.partial(merge_table_kernel, level, stride), out_...  2.8 us
    ppermute x2, starting transfers between devices, exchanged(): return lax.ppermute(value, 'rng', pairs + [(j, i) for i, j in pairs] + ends)  2.34 us
    ppermute x2, waiting for transfers between devices, exchanged(): return lax.ppermute(value, 'rng', pairs + [(j, i) for i, j in pairs] + ends)  2 us
    pallas_call x1, Pallas kernels, merged_image(): pl.pallas_call(middle_kernel, out_shape=[image, jax.ShapeDtypeStruct((ang...  1.99 us
  transfers between devices with their start and end apart: 14, of which 4 were waited for; matrix products, arithmetic and copies ran while one was open for 0% of the time, Pallas kernels for 20%

profile of v11, /device:TPU:16, one launch (start us, length us, event | category | flops | bytes accessed | tf_op | source)
XLA Modules:
  0.0 47.3 jit_solution(5190927295858741541)
XLA Ops:
  0.0 0.0 copy-start
  0.0 1.2 %copy-done = bf16[2,32,8192]{2,1,0:T(8,128)(2,1)S(1)} copy-done((bf16[2,32,8192]{2,1,0:T(8,128)(2,1)S(1)}, bf16[2,32,8192]{2,1,0:T(8,128)(2,1)}, u32[]{:S(2)}) %copy-start) | copy-done | bytes 1048600
  1.2 1.0 %shard_map.64 = (bf16[8,64,128]{2,1,0:T(8,128)(2,1)S(1)}, bf16[8,64,128]{2,1,0:T(8,128)(2,1)S(1)}, bf16[16,64,384]{2,1,0:T(8,128)(2,1)}) custom-call(bf16[64,8192]{1,0:T(8,128)(2,1)S(1)} %bitcast.4), custom_call_target="tpu_custom_call" | custom-call | bytes 2097152 | tf_op jit(solution)/shard_map/pallas_call | solution.py:81
  2.3 0.0 collective-permute-start
  2.3 6.7 %all-to-all-start = ((bf16[16,64,384]{2,1,0:T(8,128)(2,1)}), bf16[16,64,384]{2,1,0:T(8,128)(2,1)S(1)}, u32[]{:S(2)}, u32[]{:S(2)}) async-start(bf16[16,64,384]{2,1,0:T(8,128)(2,1)} %get-tuple-element.48), calls=%async_computation | async-start | bytes 1572864 | tf_op jit(solution)/shard_map/all_to_all | solution.py:568
  9.0 0.0 collective-permute-done.relay_ref
  9.0 0.0 copy-start.4
  9.0 0.0 copy-start.5
  9.0 0.2 collective-permute-start.1
  9.3 1.5 %collective-permute-start.2 = (bf16[128,128]{1,0:T(8,128)(2,1)S(1)}, bf16[128,128]{1,0:T(8,128)(2,1)S(1)}, u32[]{:S(2)}, u32[]{:S(2)}) collective-permute-start(bf16[128,128]{1,0:T(8,128)(2,1)S(1)} %get-tuple-element.41), channel_id=1, source_target_pairs={{0,2},{1,3},{2,0},{3,1},{4,6},{5,7},{6,4},{7,5},{8,10},{9,11},{10,... | collective-permute-start | bytes 98312 | tf_op jit(solution)/shard_map/ppermute | solution.py:113
  10.7 0.2 collective-permute-start.3
  11.0 3.8 %collective-permute-start.4 = (bf16[128,128]{1,0:T(8,128)(2,1)S(1)}, bf16[128,128]{1,0:T(8,128)(2,1)S(1)}, u32[]{:S(2)}, u32[]{:S(2)}) collective-permute-start(bf16[128,128]{1,0:T(8,128)(2,1)S(1)} %get-tuple-element.43), channel_id=1, source_target_pairs={{0,4},{1,5},{2,6},{3,7},{4,0},{5,1},{6,2},{7,3},{8,12},{9,13},{10,... | collective-permute-start | bytes 98312 | tf_op jit(solution)/shard_map/ppermute | solution.py:113
  14.7 0.0 collective-permute-start.5
  14.7 0.0 collective-permute-done.1.refs_1_
  14.8 2.6 %collective-permute-start.6 = (bf16[128,128]{1,0:T(8,128)(2,1)S(1)}, bf16[128,128]{1,0:T(8,128)(2,1)S(1)}, u32[]{:S(2)}, u32[]{:S(2)}) collective-permute-start(bf16[128,128]{1,0:T(8,128)(2,1)S(1)} %get-tuple-element.45), channel_id=1, source_target_pairs={{0,6},{1,7},{2,4},{3,5},{4,2},{5,3},{6,0},{7,1},{8,14},{9,15},{10,... | collective-permute-start | bytes 98312 | tf_op jit(solution)/shard_map/ppermute | solution.py:113
  17.4 0.0 collective-permute-done.2.refs_2_
  17.4 0.2 collective-permute-start.7
  17.5 0.0 copy-done.4
  17.5 0.1 copy.8.flag_ref
  17.6 1.2 %shard_map.66 = (bf16[256,1024]{1,0:T(8,128)(2,1)S(1)}, f32[8,128]{1,0:T(8,128)S(1)}) custom-call(s32[1,2,1]{2,1,0:T(2,128)S(1)} %copy.8.flag_ref, bf16[128,128]{1,0:T(8,128)(2,1)S(1)} %get-tuple-element.37.after_ref.refs_0_), custom_call_target="tpu_custom_call" | custom-call | flops 9000000 | bytes 4194304 | tf_op jit(solution)/shard_map/pallas_call | solution.py:152
  18.8 0.0 collective-permute-done.3.refs_3_
  18.8 6.8 %collective-permute-done.4.refs_4_ = bf16[128,128]{1,0:T(8,128)(2,1)S(1)} collective-permute-done((bf16[128,128]{1,0:T(8,128)(2,1)S(1)}, bf16[128,128]{1,0:T(8,128)(2,1)S(1)}, u32[]{:S(2)}, u32[]{:S(2)}) %collective-permute-start.4) | collective-permute-done | bytes 32800 | tf_op jit(solution)/shard_map/ppermute | solution.py:113
  25.6 0.0 collective-permute-done.5.refs_5_
  25.6 2.2 %collective-permute-done.6.refs_6_ = bf16[128,128]{1,0:T(8,128)(2,1)S(1)} collective-permute-done((bf16[128,128]{1,0:T(8,128)(2,1)S(1)}, bf16[128,128]{1,0:T(8,128)(2,1)S(1)}, u32[]{:S(2)}, u32[]{:S(2)}) %collective-permute-start.6) | collective-permute-done | bytes 32800 | tf_op jit(solution)/shard_map/ppermute | solution.py:113
  27.8 0.0 collective-permute-done.7.refs_7_
  27.8 0.8 %shard_map.67 = (bf16[2,256,128]{2,1,0:T(8,128)(2,1)S(1)}, bf16[2,256,128]{2,1,0:T(8,128)(2,1)S(1)}, bf16[256,128]{1,0:T(8,128)(2,1)S(1)}, bf16[256,128]{1,0:T(8,128)(2,1)S(1)}) custom-call(f32[8,128]{1,0:T(8,128)S(1)} %get-tuple-element.38.side_ref, bf16[256,1024]{1,0:T(8,128)(2,1)S(1)} %get-tuple-element.39.rows_ref, ...), custom_call_target="tpu_custom_call" | custom-call | flops 268435456 | bytes 3145728 | tf_op jit(solution)/shard_map/pallas_call | solution.py:312
  28.6 0.0 copy-start.1
  28.6 0.0 copy-start.3
  28.6 1.6 %collective-permute-start.8 = (bf16[2,256,128]{2,1,0:T(8,128)(2,1)S(1)}, bf16[2,256,128]{2,1,0:T(8,128)(2,1)S(1)}, u32[]{:S(2)}, u32[]{:S(2)}) collective-permute-start(bf16[2,256,128]{2,1,0:T(8,128)(2,1)S(1)} %get-tuple-element.47), channel_id=1, source_target_pairs={{0,16},{16,0},{1,17},{17,1},{2,18},{18,2},{3,19},{19,3},{4,20},{20... | collective-permute-start | bytes 393224 | tf_op jit(solution)/shard_map/ppermute | solution.py:530
  30.2 0.0 all-to-all-done
  30.2 0.6 %shard_map.68 = bf16[2,256,384]{2,1,0:T(8,128)(2,1)S(1)} custom-call(bf16[256,1024]{1,0:T(8,128)(2,1)S(1)} %get-tuple-element.39.rows_ref, bf16[1024,384]{1,0:T(8,128)(2,1)S(1)} %bitcast.2), custom_call_target="tpu_custom_call" | custom-call | flops 402653184 | bytes 3145728 | tf_op jit(solution)/shard_map/pallas_call | solution.py:345
  30.8 0.6 %collective-permute-start.9 = (bf16[2,256,384]{2,1,0:T(8,128)(2,1)S(1)}, bf16[2,256,384]{2,1,0:T(8,128)(2,1)S(1)}, u32[]{:S(2)}, u32[]{:S(2)}) collective-permute-start(bf16[2,256,384]{2,1,0:T(8,128)(2,1)S(1)} %shard_map.68), channel_id=1, source_target_pairs={{0,16},{16,0},{1,17},{17,1},{2,18},{18,2},{3,19},{19,3},{4,20},{20... | collective-permute-start | bytes 1179656 | tf_op jit(solution)/shard_map/ppermute | solution.py:530
  31.4 0.0 collective-permute-start.10
  31.4 2.3 %collective-permute-start.11 = (bf16[256,128]{1,0:T(8,128)(2,1)S(1)}, bf16[256,128]{1,0:T(8,128)(2,1)S(1)}, u32[]{:S(2)}, u32[]{:S(2)}) collective-permute-start(bf16[256,128]{1,0:T(8,128)(2,1)S(1)} %get-tuple-element.55), channel_id=1, source_target_pairs={{1,2},{3,4},{5,6},{7,8},{9,10},{11,12},{13,14},{2,1},{4,3},{6,5},{... | collective-permute-start | bytes 196616 | tf_op jit(solution)/shard_map/ppermute | solution.py:361
  33.7 0.0 copy-done.5
  33.7 0.1 copy.10.offset_ref
  33.8 0.0 copy-start.2
  33.8 1.2 %collective-permute-done.8.far_outer = bf16[2,256,128]{2,1,0:T(8,128)(2,1)S(1)} collective-permute-done((bf16[2,256,128]{2,1,0:T(8,128)(2,1)S(1)}, bf16[2,256,128]{2,1,0:T(8,128)(2,1)S(1)}, u32[]{:S(2)}, u32[]{:S(2)}) %collective-permute-start.8) | collective-permute-done | bytes 131104 | tf_op jit(solution)/shard_map/ppermute | solution.py:530
  35.0 0.9 %shard_map.69.own_ref = bf16[2,256,512]{2,1,0:T(8,128)(2,1)S(1)} custom-call(bf16[256,1024]{1,0:T(8,128)(2,1)S(1)} %get-tuple-element.39.rows_ref, bf16[1024,384]{1,0:T(8,128)(2,1)S(1)} %bitcast.3, bf16[2,256,128]{2,1,0:T(8,128)(2,1)S(1)} %get-tuple-element.51.outer_ref), custom_call_target="tpu_custom_call" | custom-call | flops 402653184 | bytes 3145728 | tf_op jit(solution)/shard_map/pallas_call | solution.py:345
  35.9 0.0 collective-permute-done.10.first_ref
  35.9 2.0 %collective-permute-done.11.second_ref = bf16[256,128]{1,0:T(8,128)(2,1)S(1)} collective-permute-done((bf16[256,128]{1,0:T(8,128)(2,1)S(1)}, bf16[256,128]{1,0:T(8,128)(2,1)S(1)}, u32[]{:S(2)}, u32[]{:S(2)}) %collective-permute-start.11) | collective-permute-done | bytes 65568 | tf_op jit(solution)/shard_map/ppermute | solution.py:361
  37.9 0.2 shard_map.70
  38.1 1.6 %collective-permute-start.12 = (bf16[256,128]{1,0:T(8,128)(2,1)S(1)}, bf16[256,128]{1,0:T(8,128)(2,1)S(1)}, u32[]{:S(2)}, u32[]{:S(2)}) collective-permute-start(bf16[256,128]{1,0:T(8,128)(2,1)S(1)} %get-tuple-element.58.after_ref), channel_id=1, source_target_pairs={{0,16},{16,0},{1,17},{17,1},{2,18},{18,2},{3,19},{19,3},{4,20},{20... | collective-permute-start | bytes 196616 | tf_op jit(solution)/shard_map/ppermute | solution.py:530
  39.7 0.0 copy-done.1
  39.7 0.0 copy-done.3
  39.7 0.0 copy-done.2
  39.7 2.8 %shard_map.71 = (bf16[2,512,512]{2,1,0:T(8,128)(2,1)S(1)}, bf16[2,2,128,512]{3,2,1,0:T(8,128)(2,1)S(1)}, f32[2,2,512,512]{3,2,1,0:T(8,128)S(1)}, bf16[2,512,256]{2,1,0:T(8,128)(2,1)S(1)}, f32[8,128]{1,0:T(8,128)}) custom-call(s32[1,2,1]{2,1,0:T(2,128)S(1)} %copy.8.flag_ref, s32[1,2,1]{2,1,0:T(2,128)S(1)} %copy.10.offset_ref, f32[1,2]{1,0:T(1,128)S(1)} %copy-done.3, ...), custom_call_target="tpu_custom_call" | custom-call | flops 2300000000 | bytes 7340032 | tf_op jit(solution)/shard_map/pallas_call | solution.py:238
  42.5 1.1 %shard_map.72.merged_ref = f32[2,512,512]{2,1,0:T(8,128)S(1)} custom-call(bf16[2,256,512]{2,1,0:T(8,128)(2,1)S(1)} %shard_map.69.own_ref, bf16[256,128]{1,0:T(8,128)(2,1)S(1)} %get-tuple-element.56.rims_ref, bf16[2,512,512]{2,1,0:T(8,128)(2,1)S(1)} %get-tuple-element.59.centre_ref, bf16[2,2,128,512]{3,2,1,0:T(8,128)(2,1)S(1)} %get-tuple-element.60.rim_ref, ...), custom_call_target="tpu_custom_call" | custom-call | flops 536870912 | bytes 8388608 | tf_op jit(solution)/shard_map/pallas_call | solution.py:486
  43.6 0.0 collective-permute-done.9.far_inner
  43.6 2.0 %shard_map.73 = (f32[2,512,512]{2,1,0:T(8,128)}, f32[512,256]{1,0:T(8,128)S(1)}) custom-call(bf16[2,256,384]{2,1,0:T(8,128)(2,1)S(1)} %collective-permute-done.9.far_inner, f32[2,512,512]{2,1,0:T(8,128)S(1)} %shard_map.72.merged_ref, bf16[2,512,512]{2,1,0:T(8,128)(2,1)S(1)} %get-tuple-element.59.centre_ref, ...), custom_call_target="tpu_custom_call" | custom-call | flops 536870912 | bytes 8388608 | tf_op jit(solution)/shard_map/pallas_call | solution.py:497
  45.6 0.0 collective-permute-done.12.rims_ref
  45.6 1.6 %shard_map.74 = f32[2,512,512]{2,1,0:T(8,128)} custom-call(bf16[2,256,128]{2,1,0:T(8,128)(2,1)S(1)} %collective-permute-done.8.far_outer, f32[512,256]{1,0:T(8,128)S(1)} %get-tuple-element.63.partial_ref, bf16[256,128]{1,0:T(8,128)(2,1)S(1)} %collective-permute-done.12.rims_ref, ...), custom_call_target="tpu_custom_call", output_to_operand_aliasing={{}: (8, {})} | custom-call | flops 536870912 | bytes 8388608 | tf_op jit(solution)/shard_map/pallas_call | solution.py:509
  (1 shorter events, 0.0 us)
Async XLA Ops:
  0.0 1.2 %copy-start = (bf16[2,32,8192]{2,1,0:T(8,128)(2,1)S(1)}, bf16[2,32,8192]{2,1,0:T(8,128)(2,1)}, u32[]{:S(2)}) copy-start(bf16[2,32,8192]{2,1,0:T(8,128)(2,1)} %param.6) | copy-start | bytes 3145732
  2.3 6.7 %collective-permute-start = (bf16[8,64,128]{2,1,0:T(8,128)(2,1)S(1)}, bf16[8,64,128]{2,1,0:T(8,128)(2,1)S(1)}, u32[]{:S(2)}, u32[]{:S(2)}) collective-permute-start(bf16[8,64,128]{2,1,0:T(8,128)(2,1)S(1)} %get-tuple-element.36), channel_id=1, source_target_pairs={{0,8},{1,9},{2,10},{3,11},{4,12},{5,13},{6,14},{7,15},{8,0},{9,1},... | collective-permute-start | bytes 393224 | tf_op jit(solution)/shard_map/ppermute | solution.py:113
  2.3 28.0 %all-to-all-start = ((bf16[16,64,384]{2,1,0:T(8,128)(2,1)}), bf16[16,64,384]{2,1,0:T(8,128)(2,1)S(1)}, u32[]{:S(2)}, u32[]{:S(2)}) async-start(bf16[16,64,384]{2,1,0:T(8,128)(2,1)} %get-tuple-element.48), calls=%async_computation | async-start | bytes 1572864 | tf_op jit(solution)/shard_map/all_to_all | solution.py:568
  9.0 8.6 %copy-start.4 = (s32[1,2,1]{1,2,0:T(1,128)S(1)}, s32[1,2,1]{1,2,0:T(1,128)}, u32[]{:S(2)}) copy-start(s32[1,2,1]{1,2,0:T(1,128)} %param.7) | copy-start | bytes 28
  9.0 24.7 %copy-start.5 = (s32[1,2,1]{1,2,0:T(1,128)S(1)}, s32[1,2,1]{1,2,0:T(1,128)}, u32[]{:S(2)}) copy-start(s32[1,2,1]{1,2,0:T(1,128)} %param.8) | copy-start | bytes 28
  9.0 5.7 %collective-permute-start.1 = (bf16[128,128]{1,0:T(8,128)(2,1)S(1)}, bf16[128,128]{1,0:T(8,128)(2,1)S(1)}, u32[]{:S(2)}, u32[]{:S(2)}) collective-permute-start(bf16[128,128]{1,0:T(8,128)(2,1)S(1)} %get-tuple-element.40), channel_id=1, source_target_pairs={{0,1},{1,0},{2,3},{3,2},{4,5},{5,4},{6,7},{7,6},{8,9},{9,8},{10,11... | collective-permute-start | bytes 98312 | tf_op jit(solution)/shard_map/ppermute | solution.py:113
  9.3 8.1 %collective-permute-start.2 = (bf16[128,128]{1,0:T(8,128)(2,1)S(1)}, bf16[128,128]{1,0:T(8,128)(2,1)S(1)}, u32[]{:S(2)}, u32[]{:S(2)}) collective-permute-start(bf16[128,128]{1,0:T(8,128)(2,1)S(1)} %get-tuple-element.41), channel_id=1, source_target_pairs={{0,2},{1,3},{2,0},{3,1},{4,6},{5,7},{6,4},{7,5},{8,10},{9,11},{10,... | collective-permute-start | bytes 98312 | tf_op jit(solution)/shard_map/ppermute | solution.py:113
  10.7 8.1 %collective-permute-start.3 = (bf16[128,128]{1,0:T(8,128)(2,1)S(1)}, bf16[128,128]{1,0:T(8,128)(2,1)S(1)}, u32[]{:S(2)}, u32[]{:S(2)}) collective-permute-start(bf16[128,128]{1,0:T(8,128)(2,1)S(1)} %get-tuple-element.42), channel_id=1, source_target_pairs={{0,3},{1,2},{2,1},{3,0},{4,7},{5,6},{6,5},{7,4},{8,11},{9,10},{10,... | collective-permute-start | bytes 98312 | tf_op jit(solution)/shard_map/ppermute | solution.py:113
  11.0 14.6 %collective-permute-start.4 = (bf16[128,128]{1,0:T(8,128)(2,1)S(1)}, bf16[128,128]{1,0:T(8,128)(2,1)S(1)}, u32[]{:S(2)}, u32[]{:S(2)}) collective-permute-start(bf16[128,128]{1,0:T(8,128)(2,1)S(1)} %get-tuple-element.43), channel_id=1, source_target_pairs={{0,4},{1,5},{2,6},{3,7},{4,0},{5,1},{6,2},{7,3},{8,12},{9,13},{10,... | collective-permute-start | bytes 98312 | tf_op jit(solution)/shard_map/ppermute | solution.py:113
  14.7 10.8 %collective-permute-start.5 = (bf16[128,128]{1,0:T(8,128)(2,1)S(1)}, bf16[128,128]{1,0:T(8,128)(2,1)S(1)}, u32[]{:S(2)}, u32[]{:S(2)}) collective-permute-start(bf16[128,128]{1,0:T(8,128)(2,1)S(1)} %get-tuple-element.44), channel_id=1, source_target_pairs={{0,5},{1,4},{2,7},{3,6},{4,1},{5,0},{6,3},{7,2},{8,13},{9,12},{10,... | collective-permute-start | bytes 98312 | tf_op jit(solution)/shard_map/ppermute | solution.py:113
  14.8 13.0 %collective-permute-start.6 = (bf16[128,128]{1,0:T(8,128)(2,1)S(1)}, bf16[128,128]{1,0:T(8,128)(2,1)S(1)}, u32[]{:S(2)}, u32[]{:S(2)}) collective-permute-start(bf16[128,128]{1,0:T(8,128)(2,1)S(1)} %get-tuple-element.45), channel_id=1, source_target_pairs={{0,6},{1,7},{2,4},{3,5},{4,2},{5,3},{6,0},{7,1},{8,14},{9,15},{10,... | collective-permute-start | bytes 98312 | tf_op jit(solution)/shard_map/ppermute | solution.py:113
  17.4 10.4 %collective-permute-start.7 = (bf16[128,128]{1,0:T(8,128)(2,1)S(1)}, bf16[128,128]{1,0:T(8,128)(2,1)S(1)}, u32[]{:S(2)}, u32[]{:S(2)}) collective-permute-start(bf16[128,128]{1,0:T(8,128)(2,1)S(1)} %get-tuple-element.46), channel_id=1, source_target_pairs={{0,7},{1,6},{2,5},{3,4},{4,3},{5,2},{6,1},{7,0},{8,15},{9,14},{10,... | collective-permute-start | bytes 98312 | tf_op jit(solution)/shard_map/ppermute | solution.py:113
  28.6 11.1 %copy-start.1 = (bf16[1,544,512]{2,1,0:T(8,128)(2,1)S(1)}, bf16[1,544,512]{2,1,0:T(8,128)(2,1)}, u32[]{:S(2)}) copy-start(bf16[1,544,512]{2,1,0:T(8,128)(2,1)} %range_ref.1) | copy-start | bytes 1671172
  28.6 11.1 %copy-start.3 = (f32[1,2]{1,0:T(1,128)S(1)}, f32[1,2]{1,0:T(1,128)}, u32[]{:S(2)}) copy-start(f32[1,2]{1,0:T(1,128)} %shift_ref.1) | copy-start | bytes 28
  28.6 6.4 %collective-permute-start.8 = (bf16[2,256,128]{2,1,0:T(8,128)(2,1)S(1)}, bf16[2,256,128]{2,1,0:T(8,128)(2,1)S(1)}, u32[]{:S(2)}, u32[]{:S(2)}) collective-permute-start(bf16[2,256,128]{2,1,0:T(8,128)(2,1)S(1)} %get-tuple-element.47), channel_id=1, source_target_pairs={{0,16},{16,0},{1,17},{17,1},{2,18},{18,2},{3,19},{19,3},{4,20},{20... | collective-permute-start | bytes 393224 | tf_op jit(solution)/shard_map/ppermute | solution.py:530
  30.8 12.8 %collective-permute-start.9 = (bf16[2,256,384]{2,1,0:T(8,128)(2,1)S(1)}, bf16[2,256,384]{2,1,0:T(8,128)(2,1)S(1)}, u32[]{:S(2)}, u32[]{:S(2)}) collective-permute-start(bf16[2,256,384]{2,1,0:T(8,128)(2,1)S(1)} %shard_map.68), channel_id=1, source_target_pairs={{0,16},{16,0},{1,17},{17,1},{2,18},{18,2},{3,19},{19,3},{4,20},{20... | collective-permute-start | bytes 1179656 | tf_op jit(solution)/shard_map/ppermute | solution.py:530
  31.4 4.6 %collective-permute-start.10 = (bf16[256,128]{1,0:T(8,128)(2,1)S(1)}, bf16[256,128]{1,0:T(8,128)(2,1)S(1)}, u32[]{:S(2)}, u32[]{:S(2)}) collective-permute-start(bf16[256,128]{1,0:T(8,128)(2,1)S(1)} %get-tuple-element.53), channel_id=1, source_target_pairs={{0,1},{2,3},{4,5},{6,7},{8,9},{10,11},{12,13},{14,15},{1,0},{3,2},... | collective-permute-start | bytes 196616 | tf_op jit(solution)/shard_map/ppermute | solution.py:361
  31.4 6.6 %collective-permute-start.11 = (bf16[256,128]{1,0:T(8,128)(2,1)S(1)}, bf16[256,128]{1,0:T(8,128)(2,1)S(1)}, u32[]{:S(2)}, u32[]{:S(2)}) collective-permute-start(bf16[256,128]{1,0:T(8,128)(2,1)S(1)} %get-tuple-element.55), channel_id=1, source_target_pairs={{1,2},{3,4},{5,6},{7,8},{9,10},{11,12},{13,14},{2,1},{4,3},{6,5},{... | collective-permute-start | bytes 196616 | tf_op jit(solution)/shard_map/ppermute | solution.py:361
  33.8 5.9 %copy-start.2 = (bf16[1,2,512,256]{3,2,1,0:T(8,128)(2,1)S(1)}, bf16[1,2,512,256]{3,2,1,0:T(8,128)(2,1)}, u32[]{:S(2)}) copy-start(bf16[1,2,512,256]{3,2,1,0:T(8,128)(2,1)} %interp_ref.1) | copy-start | bytes 1572868
  38.1 7.5 %collective-permute-start.12 = (bf16[256,128]{1,0:T(8,128)(2,1)S(1)}, bf16[256,128]{1,0:T(8,128)(2,1)S(1)}, u32[]{:S(2)}, u32[]{:S(2)}) collective-permute-start(bf16[256,128]{1,0:T(8,128)(2,1)S(1)} %get-tuple-element.58.after_ref), channel_id=1, source_target_pairs={{0,16},{16,0},{1,17},{17,1},{2,18},{18,2},{3,19},{19,3},{4,20},{20... | collective-permute-start | bytes 196616 | tf_op jit(solution)/shard_map/ppermute | solution.py:530

commit v12 on v5

--- a/solution.py
+++ b/solution.py
@@ -116,8 +116,8 @@
 def filter_table_kernel(local_pulses, flag_ref, after_ref, rows_ref, side_ref, cos_ref, sin_ref):
     own_flag = flag_ref[0, lax.axis_index("sub"), 0]
     side_ref[...] = jnp.full(side_ref.shape, own_flag.astype(F32))
-    angles, columns = rows_ref.shape
-    half = angles // 2
+    half, columns = rows_ref.shape
+    angles = 2 * half
     first = (1 - own_flag) * half
     base = cos_ref.shape[0]
     scale = 1.0 / math.sqrt(columns // 2)
@@ -136,25 +136,22 @@
     step = cos_sin_pi(per_angle * (2 * base))
     for j in range(half // base):
         for i in range(base // 16):
-            pair = [], []
+            pair = []
             for k in (2 * i, 2 * i + 1):
                 here = slice(8 * k, 8 * k + 8)
                 now = cos_ref[here, :], sin_ref[here, :]
-                pair[0].append(now[0])
-                pair[1].append(-now[1])
+                pair.append(now[0])
                 if j + 1 < half // base:
                     cos_ref[here, :], sin_ref[here, :] = rotated(now, step)
             begin = j * base + 16 * i
-            rows_ref[begin : begin + 16, :] = jnp.concatenate(pair[0]).astype(BF16)
-            begin += half
-            rows_ref[begin : begin + 16, :] = jnp.concatenate(pair[1]).astype(BF16)
+            rows_ref[begin : begin + 16, :] = jnp.concatenate(pair).astype(BF16)
 
 
 def filter_table(fore_flag, angles, local_pulses, earlier):
     side = 2 * local_pulses * lax.axis_size("rng")
     return pl.pallas_call(
         functools.partial(filter_table_kernel, local_pulses),
-        out_shape=[jax.ShapeDtypeStruct((angles, side), BF16), SIDE],
+        out_shape=[jax.ShapeDtypeStruct((angles // 2, side), BF16), SIDE],
         in_specs=[SMEM, ANY],
         out_specs=[VMEM] * 2,
         scratch_shapes=[pltpu.VMEM((64, side), F32)] * 2,
@@ -195,11 +192,10 @@
         hot = jnp.where(tap == bin_id, 1.0, 0.0).astype(BF16)
         return dot(hot, kernel_ref[...]).astype(BF16)
 
-    row = lax.broadcasted_iota(jnp.int32, (bins, 1), 0)
-    upper = row + (bins - 2 * LANES)
-    own_bin = jnp.where(row % LANES < LANES // 2, row, upper + LANES)
-    own_bin = jnp.where(row >= LANES, jnp.where(row % LANES < LANES // 2, upper, row - LANES), own_bin)
-    own_bin = jnp.where(row >= 2 * LANES, row - LANES, own_bin)
+    piece = LANES // 2
+    starts = [0, bins - piece, bins - 2 * piece, piece, *range(2 * piece, bins - 2 * piece, piece)]
+    line_bin = lax.broadcasted_iota(jnp.int32, (piece, 1), 0)
+    line_tap = lax.broadcasted_iota(jnp.int32, (piece, piece + taps - bins), 1)
     rim_row = lax.broadcasted_iota(jnp.int32, (2 * rim, 1), 0)
     rim_bin = jnp.where(rim_row < rim, rim_row - rim, rim_row - rim + bins)
     rim_ref[...] = jnp.zeros(rim_ref.shape, BF16)
@@ -224,7 +220,10 @@
         copy.wait()
     for child, member in enumerate(members):
         lead = band - offset_ref[level, member, 0]
-        centre_ref[child] = moved(own_bin + lead)
+        hot = jnp.where(line_tap == line_bin + lead, 1.0, 0.0).astype(BF16)
+        for i, start in enumerate(starts):
+            some = kernel_ref[start : start + piece + taps - bins, :]
+            centre_ref[child, i * piece : (i + 1) * piece, :] = dot(hot, some).astype(BF16)
         ends = moved(rim_bin + lead)
         for part in range(2):
             for side in range(2):
@@ -260,7 +259,15 @@
 def alternating(pulses, local_pulses):
     row = lax.broadcasted_iota(jnp.int32, (pulses.shape[0], 1), 0)
     pulse = row // (2 * local_pulses) * local_pulses + row % local_pulses
-    return jnp.where(pulse % 2 == 1, -pulses.astype(F32), pulses.astype(F32)).astype(BF16)
+    return jnp.where(pulse % 2 == 1, -pulses, pulses)
+
+
+def both_parts(pulses, local_pulses):
+    count = pulses.shape[0]
+    second = lax.broadcasted_iota(jnp.int32, (count, 1), 0) // local_pulses % 2 == 1
+    ahead, behind = pltpu.roll(pulses, count - local_pulses, 0), pltpu.roll(pulses, local_pulses, 0)
+    turned = jnp.where(second, -behind, ahead)
+    return jnp.concatenate([pulses, turned], axis=1).astype(BF16)
 
 
 def outer_kernel(pieces, side_ref, rows_ref, *refs):
@@ -274,14 +281,17 @@
             place = pl.multiple_of((me ^ (d + t * pieces)) * rows, rows)
             pulses_ref[pl.ds(place, rows), :] = ref[t * rows : (t + 1) * rows, :]
     pulses = pulses_ref[...]
-    own_parts = dot(rows_ref[...], alternating(pulses, rows // 2))
-    out_parts = dot(rows_ref[...], pulses)
+    pulses = pulses.astype(F32)
+    images = [
+        dot(rows_ref[...], both_parts(value, rows // 2))
+        for value in (alternating(pulses, rows // 2), pulses)
+    ]
     half = own_ref.shape[1]
     rim = LANES // 4
     lane = lax.broadcasted_iota(jnp.int32, (1, LANES), 1)
     edges = [0.0, 0.0]
     for part in range(2):
-        own, out = (value[part * half : (part + 1) * half] for value in (own_parts, out_parts))
+        own, out = (image[:, part * LANES : (part + 1) * LANES] for image in images)
         own_ref[part] = own.astype(BF16)
         out_ref[part] = out.astype(BF16)
         for side in range(2):
@@ -297,7 +307,8 @@
 
 
 def outer_image(own_side, rows, pieces):
-    angles, side = rows.shape
+    half, side = rows.shape
+    angles = 2 * half
     image = jax.ShapeDtypeStruct((2, angles // 2, LANES), BF16)
     edge = jax.ShapeDtypeStruct((angles // 2, LANES), BF16)
     return pl.pallas_call(
@@ -313,16 +324,21 @@
     )(own_side, rows, *pieces)
 
 
-def partner_rows_kernel(rows_ref, pulses_ref, image_ref):
-    image = dot(rows_ref[...], pulses_ref[...])
-    image_ref[...] = image.astype(BF16).reshape(image_ref.shape)
+def partner_rows_kernel(local_pulses, rows_ref, pulses_ref, image_ref):
+    count = pulses_ref.shape[1]
+    image = dot(rows_ref[...], both_parts(pulses_ref[...].astype(F32), local_pulses))
+    for part in range(2):
+        image_ref[part] = image[:, part * count : (part + 1) * count].astype(BF16)
 
 
 def own_rows_kernel(local_pulses, rows_ref, pulses_ref, outer_ref, image_ref):
-    image = dot(rows_ref[...], alternating(pulses_ref[...], local_pulses))
-    parts, half, count = outer_ref.shape
+    inner = pulses_ref.shape[1]
+    pulses = alternating(pulses_ref[...].astype(F32), local_pulses)
+    image = dot(rows_ref[...], both_parts(pulses, local_pulses))
+    count = outer_ref.shape[2]
     image_ref[:, :, :count] = outer_ref[...]
-    image_ref[:, :, count:] = image.astype(BF16).reshape(parts, half, image.shape[1])
+    for part in range(2):
+        image_ref[part, :, count:] = image[:, part * inner : (part + 1) * inner].astype(BF16)
 
 
 def inner_image(kernel, angles, rows, pulses, outer=()):
@@ -504,16 +520,19 @@
     sends = joined(near_blocks, relay)
     pieces = [across(value, d) if d else value for d, value in enumerate(sends)]
     matrix, own_side = filter_table(fore_flag, angles, local_pulses, sends[0])
-    pulses = after(pulses, *pieces[1:]).reshape(2 * local_pulses * devices, bins - LANES)
-    out_inner = inner_image(partner_rows_kernel, angles, matrix, pulses)
-    pieces[0] = after(pieces[0], out_inner)
     own_outer, out_outer, *edges = outer_image(own_side, matrix, pieces)
+
+    pulses = after(pulses, out_outer).reshape(2 * local_pulses * devices, bins - LANES)
+    out_kernel = functools.partial(partner_rows_kernel, local_pulses)
+    out_inner = inner_image(out_kernel, angles, matrix, pulses)
     far = [from_partner(value, 1) for value in (out_outer, out_inner)]
+    edges = [after(edge, out_inner) for edge in edges]
     edges = exchanged(edges[0], 0), exchanged(edges[1], 1)
+    pulses = after(pulses, far[0])
     own_kernel = functools.partial(own_rows_kernel, local_pulses)
     own = inner_image(own_kernel, angles, matrix, pulses, (own_outer,))
-    tables = merge_tables(0, 1, *settings, own)
-    edges = after(edges[0], tables[0]), edges[1]
+    rims, out_rims = sorted_rims(own_side, *edges)
+    tables = merge_tables(0, 1, *settings, after(out_rims, own))
     for level in range(levels):
         stride = 2**level
         if level > 0:
@@ -521,8 +540,7 @@
             own, out, edges = split_image(level, image, fore_flag, rim)
             far = [from_partner(value, stride) for value in (out[..., :LANES], out[..., LANES:])]
             edges = exchanged(edges[0], 0), exchanged(edges[1], 1)
-            own_side = tables[-1]
-        rims, out_rims = sorted_rims(own_side, *edges)
+            rims, out_rims = sorted_rims(tables[-1], *edges)
         far_rims = from_partner(out_rims, stride)
         image = merged_image(own, rims, far, far_rims, tables, BF16 if level + 1 < levels else F32)
     return image

time: 47.8 us -> 46.8 us (0.979)
  Pallas kernels: 11 us -> 10.2 us
    ppermute x2, waiting for transfers between devices: 0.02 us -> 2 us  [exchanged(): return lax.ppermute(value, 'rng', pairs + [(j, i) for i, j in pairs] + ends)]
    all_to_all x1, waiting for transfers between devices: 1.4 us -> 0.01 us  [on_device(): lax.all_to_all(blocks, 'rng', split_axis=0, concat_axis=0, tiled=True)]
    pallas_call x1, Pallas kernels: 2.8 us -> 2.23 us  [merge_tables(): pl.pallas_call(functools.partial(merge_table_kernel, level, stride), out_...]
    ppermute x3, waiting for transfers between devices: 3.04 us -> 2.51 us  [from_partner(): return lax.ppermute(value, 'sub', pairs)]
where the time goes in v12:
time: 46.8 us; the launch traced here: 46.6 us
  starting transfers between devices  21.3 us (46%)
  waiting for transfers between devices  13.5 us (29%)
  Pallas kernels  10.2 us (22%)
  local copies, waits for them, and re-layouts  1.44 us (3%)
    ppermute x8, waiting for transfers between devices, across(): return lax.ppermute(value, 'rng', [(i, i ^ mask) for i in range(devices)])  8.98 us
    ppermute x8, starting transfers between devices, across(): return lax.ppermute(value, 'rng', [(i, i ^ mask) for i in range(devices)])  8.48 us
    all_to_all x1, starting transfers between devices, on_device(): lax.all_to_all(blocks, 'rng', split_axis=0, concat_axis=0, tiled=True)  6.72 us
    ppermute x3, starting transfers between devices, from_partner(): return lax.ppermute(value, 'sub', pairs)  3.74 us
    ppermute x3, waiting for transfers between devices, from_partner(): return lax.ppermute(value, 'sub', pairs)  2.51 us
    ppermute x2, starting transfers between devices, exchanged(): return lax.ppermute(value, 'rng', pairs + [(j, i) for i, j in pairs] + ends)  2.34 us
    pallas_call x1, Pallas kernels, merge_tables(): pl.pallas_call(functools.partial(merge_table_kernel, level, stride), out_...  2.23 us
    pallas_call x1, Pallas kernels, merged_image(): pl.pallas_call(late_kernel, out_shape=jax.ShapeDtypeStruct((2, angles, bi...  2.18 us
  transfers between devices with their start and end apart: 14, of which 5 were waited for; matrix products, arithmetic and copies ran while one was open for 0% of the time, Pallas kernels for 15%

profile of v12, /device:TPU:16, one launch (start us, length us, event | category | flops | bytes accessed | tf_op | source)
XLA Modules:
  0.0 46.6 jit_solution(13677433203692757540)
XLA Ops:
  0.0 0.0 copy-start
  0.0 1.2 %copy-done = bf16[2,32,8192]{2,1,0:T(8,128)(2,1)S(1)} copy-done((bf16[2,32,8192]{2,1,0:T(8,128)(2,1)S(1)}, bf16[2,32,8192]{2,1,0:T(8,128)(2,1)}, u32[]{:S(2)}) %copy-start) | copy-done | bytes 1048600
  1.2 1.0 %shard_map.64 = (bf16[8,64,128]{2,1,0:T(8,128)(2,1)S(1)}, bf16[8,64,128]{2,1,0:T(8,128)(2,1)S(1)}, bf16[16,64,384]{2,1,0:T(8,128)(2,1)}) custom-call(bf16[64,8192]{1,0:T(8,128)(2,1)S(1)} %bitcast.4), custom_call_target="tpu_custom_call" | custom-call | bytes 2097152 | tf_op jit(solution)/shard_map/pallas_call | solution.py:81
  2.3 0.0 collective-permute-start
  2.3 6.7 %all-to-all-start = ((bf16[16,64,384]{2,1,0:T(8,128)(2,1)}), bf16[16,64,384]{2,1,0:T(8,128)(2,1)S(1)}, u32[]{:S(2)}, u32[]{:S(2)}) async-start(bf16[16,64,384]{2,1,0:T(8,128)(2,1)} %get-tuple-element.46), calls=%async_computation | async-start | bytes 1572864 | tf_op jit(solution)/shard_map/all_to_all | solution.py:519
  9.0 0.0 collective-permute-done.relay_ref
  9.0 0.0 copy-start.4
  9.0 0.0 copy-start.5
  9.0 0.2 collective-permute-start.1
  9.3 1.5 %collective-permute-start.2 = (bf16[128,128]{1,0:T(8,128)(2,1)S(1)}, bf16[128,128]{1,0:T(8,128)(2,1)S(1)}, u32[]{:S(2)}, u32[]{:S(2)}) collective-permute-start(bf16[128,128]{1,0:T(8,128)(2,1)S(1)} %get-tuple-element.39), channel_id=1, source_target_pairs={{0,2},{1,3},{2,0},{3,1},{4,6},{5,7},{6,4},{7,5},{8,10},{9,11},{10,... | collective-permute-start | bytes 98312 | tf_op jit(solution)/shard_map/ppermute | solution.py:113
  10.7 0.2 collective-permute-start.3
  11.0 3.8 %collective-permute-start.4 = (bf16[128,128]{1,0:T(8,128)(2,1)S(1)}, bf16[128,128]{1,0:T(8,128)(2,1)S(1)}, u32[]{:S(2)}, u32[]{:S(2)}) collective-permute-start(bf16[128,128]{1,0:T(8,128)(2,1)S(1)} %get-tuple-element.41), channel_id=1, source_target_pairs={{0,4},{1,5},{2,6},{3,7},{4,0},{5,1},{6,2},{7,3},{8,12},{9,13},{10,... | collective-permute-start | bytes 98312 | tf_op jit(solution)/shard_map/ppermute | solution.py:113
  14.7 0.0 collective-permute-start.5
  14.7 0.0 collective-permute-done.1.refs_1_
  14.8 2.6 %collective-permute-start.6 = (bf16[128,128]{1,0:T(8,128)(2,1)S(1)}, bf16[128,128]{1,0:T(8,128)(2,1)S(1)}, u32[]{:S(2)}, u32[]{:S(2)}) collective-permute-start(bf16[128,128]{1,0:T(8,128)(2,1)S(1)} %get-tuple-element.43), channel_id=1, source_target_pairs={{0,6},{1,7},{2,4},{3,5},{4,2},{5,3},{6,0},{7,1},{8,14},{9,15},{10,... | collective-permute-start | bytes 98312 | tf_op jit(solution)/shard_map/ppermute | solution.py:113
  17.4 0.0 collective-permute-done.2.refs_2_
  17.4 0.2 collective-permute-start.7
  17.5 0.0 copy-done.4
  17.5 0.1 copy.7.flag_ref
  17.6 1.2 %shard_map.66 = (bf16[256,1024]{1,0:T(8,128)(2,1)S(1)}, f32[8,128]{1,0:T(8,128)S(1)}) custom-call(s32[1,2,1]{2,1,0:T(2,128)S(1)} %copy.7.flag_ref, bf16[128,128]{1,0:T(8,128)(2,1)S(1)} %get-tuple-element.35.after_ref.refs_0_), custom_call_target="tpu_custom_call" | custom-call | flops 9000000 | bytes 4194304 | tf_op jit(solution)/shard_map/pallas_call | solution.py:152
  18.8 0.0 collective-permute-done.3.refs_3_
  18.8 6.8 %collective-permute-done.4.refs_4_ = bf16[128,128]{1,0:T(8,128)(2,1)S(1)} collective-permute-done((bf16[128,128]{1,0:T(8,128)(2,1)S(1)}, bf16[128,128]{1,0:T(8,128)(2,1)S(1)}, u32[]{:S(2)}, u32[]{:S(2)}) %collective-permute-start.4) | collective-permute-done | bytes 32800 | tf_op jit(solution)/shard_map/ppermute | solution.py:113
  25.6 0.0 collective-permute-done.5.refs_5_
  25.6 2.2 %collective-permute-done.6.refs_6_ = bf16[128,128]{1,0:T(8,128)(2,1)S(1)} collective-permute-done((bf16[128,128]{1,0:T(8,128)(2,1)S(1)}, bf16[128,128]{1,0:T(8,128)(2,1)S(1)}, u32[]{:S(2)}, u32[]{:S(2)}) %collective-permute-start.6) | collective-permute-done | bytes 32800 | tf_op jit(solution)/shard_map/ppermute | solution.py:113
  27.8 0.0 collective-permute-done.7.refs_7_
  27.8 0.8 %shard_map.67 = (bf16[2,256,128]{2,1,0:T(8,128)(2,1)S(1)}, bf16[2,256,128]{2,1,0:T(8,128)(2,1)S(1)}, bf16[256,128]{1,0:T(8,128)(2,1)S(1)}, bf16[256,128]{1,0:T(8,128)(2,1)S(1)}) custom-call(f32[8,128]{1,0:T(8,128)S(1)} %get-tuple-element.36.side_ref, bf16[256,1024]{1,0:T(8,128)(2,1)S(1)} %get-tuple-element.37.rows_ref, ...), custom_call_target="tpu_custom_call" | custom-call | flops 268435456 | bytes 3145728 | tf_op jit(solution)/shard_map/pallas_call | solution.py:314
  28.6 0.0 copy-start.1
  28.6 0.0 copy-start.3
  28.6 1.6 %collective-permute-start.8 = (bf16[2,256,128]{2,1,0:T(8,128)(2,1)S(1)}, bf16[2,256,128]{2,1,0:T(8,128)(2,1)S(1)}, u32[]{:S(2)}, u32[]{:S(2)}) collective-permute-start(bf16[2,256,128]{2,1,0:T(8,128)(2,1)S(1)} %get-tuple-element.45), channel_id=1, source_target_pairs={{0,16},{16,0},{1,17},{17,1},{2,18},{18,2},{3,19},{19,3},{4,20},{20... | collective-permute-start | bytes 393224 | tf_op jit(solution)/shard_map/ppermute | solution.py:481
  30.2 0.0 all-to-all-done
  30.2 0.6 %shard_map.68 = bf16[2,256,384]{2,1,0:T(8,128)(2,1)S(1)} custom-call(bf16[256,1024]{1,0:T(8,128)(2,1)S(1)} %get-tuple-element.37.rows_ref, bf16[1024,384]{1,0:T(8,128)(2,1)S(1)} %bitcast.2), custom_call_target="tpu_custom_call" | custom-call | flops 402653184 | bytes 3145728 | tf_op jit(solution)/shard_map/pallas_call | solution.py:347
  30.8 0.6 %collective-permute-start.9 = (bf16[2,256,384]{2,1,0:T(8,128)(2,1)S(1)}, bf16[2,256,384]{2,1,0:T(8,128)(2,1)S(1)}, u32[]{:S(2)}, u32[]{:S(2)}) collective-permute-start(bf16[2,256,384]{2,1,0:T(8,128)(2,1)S(1)} %shard_map.68), channel_id=1, source_target_pairs={{0,16},{16,0},{1,17},{17,1},{2,18},{18,2},{3,19},{19,3},{4,20},{20... | collective-permute-start | bytes 1179656 | tf_op jit(solution)/shard_map/ppermute | solution.py:481
  31.4 0.0 collective-permute-start.10
  31.4 2.3 %collective-permute-start.11 = (bf16[256,128]{1,0:T(8,128)(2,1)S(1)}, bf16[256,128]{1,0:T(8,128)(2,1)S(1)}, u32[]{:S(2)}, u32[]{:S(2)}) collective-permute-start(bf16[256,128]{1,0:T(8,128)(2,1)S(1)} %get-tuple-element.51), channel_id=1, source_target_pairs={{1,2},{3,4},{5,6},{7,8},{9,10},{11,12},{13,14},{2,1},{4,3},{6,5},{... | collective-permute-start | bytes 196616 | tf_op jit(solution)/shard_map/ppermute | solution.py:363
  33.7 0.0 copy-done.5
  33.7 0.1 copy.9.offset_ref
  33.8 0.0 copy-start.2
  33.8 1.2 %collective-permute-done.8.far_outer = bf16[2,256,128]{2,1,0:T(8,128)(2,1)S(1)} collective-permute-done((bf16[2,256,128]{2,1,0:T(8,128)(2,1)S(1)}, bf16[2,256,128]{2,1,0:T(8,128)(2,1)S(1)}, u32[]{:S(2)}, u32[]{:S(2)}) %collective-permute-start.8) | collective-permute-done | bytes 131104 | tf_op jit(solution)/shard_map/ppermute | solution.py:481
  35.0 0.9 %shard_map.70.own_ref = bf16[2,256,512]{2,1,0:T(8,128)(2,1)S(1)} custom-call(bf16[256,1024]{1,0:T(8,128)(2,1)S(1)} %get-tuple-element.37.rows_ref, bf16[1024,384]{1,0:T(8,128)(2,1)S(1)} %bitcast.3, bf16[2,256,128]{2,1,0:T(8,128)(2,1)S(1)} %get-tuple-element.54.outer_ref), custom_call_target="tpu_custom_call" | custom-call | flops 402653184 | bytes 3145728 | tf_op jit(solution)/shard_map/pallas_call | solution.py:347
  35.9 0.0 collective-permute-done.10.first_ref
  35.9 2.0 %collective-permute-done.11.second_ref = bf16[256,128]{1,0:T(8,128)(2,1)S(1)} collective-permute-done((bf16[256,128]{1,0:T(8,128)(2,1)S(1)}, bf16[256,128]{1,0:T(8,128)(2,1)S(1)}, u32[]{:S(2)}, u32[]{:S(2)}) %collective-permute-start.11) | collective-permute-done | bytes 65568 | tf_op jit(solution)/shard_map/ppermute | solution.py:363
  37.9 0.2 shard_map.69
  38.1 1.6 %collective-permute-start.12 = (bf16[256,128]{1,0:T(8,128)(2,1)S(1)}, bf16[256,128]{1,0:T(8,128)(2,1)S(1)}, u32[]{:S(2)}, u32[]{:S(2)}) collective-permute-start(bf16[256,128]{1,0:T(8,128)(2,1)S(1)} %get-tuple-element.56.after_ref), channel_id=1, source_target_pairs={{0,16},{16,0},{1,17},{17,1},{2,18},{18,2},{3,19},{19,3},{4,20},{20... | collective-permute-start | bytes 196616 | tf_op jit(solution)/shard_map/ppermute | solution.py:481
  39.7 0.0 copy-done.1
  39.7 0.0 copy-done.3
  39.7 0.0 copy-done.2
  39.7 2.2 %shard_map.71 = (bf16[2,512,512]{2,1,0:T(8,128)(2,1)S(1)}, bf16[2,2,128,512]{3,2,1,0:T(8,128)(2,1)S(1)}, f32[2,2,512,512]{3,2,1,0:T(8,128)S(1)}, bf16[2,512,256]{2,1,0:T(8,128)(2,1)S(1)}, f32[8,128]{1,0:T(8,128)}) custom-call(s32[1,2,1]{2,1,0:T(2,128)S(1)} %copy.7.flag_ref, s32[1,2,1]{2,1,0:T(2,128)S(1)} %copy.9.offset_ref, f32[1,2]{1,0:T(1,128)S(1)} %copy-done.3, ...), custom_call_target="tpu_custom_call" | custom-call | flops 2300000000 | bytes 7340032 | tf_op jit(solution)/shard_map/pallas_call | solution.py:240
  42.0 1.1 %shard_map.72.merged_ref = f32[2,512,512]{2,1,0:T(8,128)S(1)} custom-call(bf16[2,256,512]{2,1,0:T(8,128)(2,1)S(1)} %shard_map.70.own_ref, bf16[256,128]{1,0:T(8,128)(2,1)S(1)} %get-tuple-element.55.rims_ref, bf16[2,512,512]{2,1,0:T(8,128)(2,1)S(1)} %get-tuple-element.57.centre_ref, bf16[2,2,128,512]{3,2,1,0:T(8,128)(2,1)S(1)} %get-tuple-element.58.rim_ref, ...), custom_call_target="tpu_custom_call" | custom-call | flops 536870912 | bytes 8388608 | tf_op jit(solution)/shard_map/pallas_call | solution.py:451
  43.0 1.3 %collective-permute-done.12.rims_ref = bf16[256,128]{1,0:T(8,128)(2,1)S(1)} collective-permute-done((bf16[256,128]{1,0:T(8,128)(2,1)S(1)}, bf16[256,128]{1,0:T(8,128)(2,1)S(1)}, u32[]{:S(2)}, u32[]{:S(2)}) %collective-permute-start.12) | collective-permute-done | bytes 65568 | tf_op jit(solution)/shard_map/ppermute | solution.py:481
  44.4 0.0 collective-permute-done.9.far_inner
  44.4 2.2 %shard_map.73 = f32[2,512,512]{2,1,0:T(8,128)} custom-call(bf16[2,256,128]{2,1,0:T(8,128)(2,1)S(1)} %collective-permute-done.8.far_outer, bf16[2,256,384]{2,1,0:T(8,128)(2,1)S(1)} %collective-permute-done.9.far_inner, bf16[256,128]{1,0:T(8,128)(2,1)S(1)} %collective-permute-done.12.rims_ref, f32[2,512,512]{2,1,0:T(8,128)S(1)} %shard_map.72.merged_ref, ...), custom_call_target="tpu_custom_call" | custom-call | flops 536870912 | bytes 8388608 | tf_op jit(solution)/shard_map/pallas_call | solution.py:460
  (1 shorter events, 0.0 us)
Async XLA Ops:
  0.0 1.2 %copy-start = (bf16[2,32,8192]{2,1,0:T(8,128)(2,1)S(1)}, bf16[2,32,8192]{2,1,0:T(8,128)(2,1)}, u32[]{:S(2)}) copy-start(bf16[2,32,8192]{2,1,0:T(8,128)(2,1)} %param.6) | copy-start | bytes 3145732
  2.3 6.7 %collective-permute-start = (bf16[8,64,128]{2,1,0:T(8,128)(2,1)S(1)}, bf16[8,64,128]{2,1,0:T(8,128)(2,1)S(1)}, u32[]{:S(2)}, u32[]{:S(2)}) collective-permute-start(bf16[8,64,128]{2,1,0:T(8,128)(2,1)S(1)} %get-tuple-element.34), channel_id=1, source_target_pairs={{0,8},{1,9},{2,10},{3,11},{4,12},{5,13},{6,14},{7,15},{8,0},{9,1},... | collective-permute-start | bytes 393224 | tf_op jit(solution)/shard_map/ppermute | solution.py:113
  2.3 28.0 %all-to-all-start = ((bf16[16,64,384]{2,1,0:T(8,128)(2,1)}), bf16[16,64,384]{2,1,0:T(8,128)(2,1)S(1)}, u32[]{:S(2)}, u32[]{:S(2)}) async-start(bf16[16,64,384]{2,1,0:T(8,128)(2,1)} %get-tuple-element.46), calls=%async_computation | async-start | bytes 1572864 | tf_op jit(solution)/shard_map/all_to_all | solution.py:519
  9.0 8.6 %copy-start.4 = (s32[1,2,1]{1,2,0:T(1,128)S(1)}, s32[1,2,1]{1,2,0:T(1,128)}, u32[]{:S(2)}) copy-start(s32[1,2,1]{1,2,0:T(1,128)} %param.7) | copy-start | bytes 28
  9.0 24.7 %copy-start.5 = (s32[1,2,1]{1,2,0:T(1,128)S(1)}, s32[1,2,1]{1,2,0:T(1,128)}, u32[]{:S(2)}) copy-start(s32[1,2,1]{1,2,0:T(1,128)} %param.8) | copy-start | bytes 28
  9.0 5.7 %collective-permute-start.1 = (bf16[128,128]{1,0:T(8,128)(2,1)S(1)}, bf16[128,128]{1,0:T(8,128)(2,1)S(1)}, u32[]{:S(2)}, u32[]{:S(2)}) collective-permute-start(bf16[128,128]{1,0:T(8,128)(2,1)S(1)} %get-tuple-element.38), channel_id=1, source_target_pairs={{0,1},{1,0},{2,3},{3,2},{4,5},{5,4},{6,7},{7,6},{8,9},{9,8},{10,11... | collective-permute-start | bytes 98312 | tf_op jit(solution)/shard_map/ppermute | solution.py:113
  9.3 8.1 %collective-permute-start.2 = (bf16[128,128]{1,0:T(8,128)(2,1)S(1)}, bf16[128,128]{1,0:T(8,128)(2,1)S(1)}, u32[]{:S(2)}, u32[]{:S(2)}) collective-permute-start(bf16[128,128]{1,0:T(8,128)(2,1)S(1)} %get-tuple-element.39), channel_id=1, source_target_pairs={{0,2},{1,3},{2,0},{3,1},{4,6},{5,7},{6,4},{7,5},{8,10},{9,11},{10,... | collective-permute-start | bytes 98312 | tf_op jit(solution)/shard_map/ppermute | solution.py:113
  10.7 8.1 %collective-permute-start.3 = (bf16[128,128]{1,0:T(8,128)(2,1)S(1)}, bf16[128,128]{1,0:T(8,128)(2,1)S(1)}, u32[]{:S(2)}, u32[]{:S(2)}) collective-permute-start(bf16[128,128]{1,0:T(8,128)(2,1)S(1)} %get-tuple-element.40), channel_id=1, source_target_pairs={{0,3},{1,2},{2,1},{3,0},{4,7},{5,6},{6,5},{7,4},{8,11},{9,10},{10,... | collective-permute-start | bytes 98312 | tf_op jit(solution)/shard_map/ppermute | solution.py:113
  11.0 14.6 %collective-permute-start.4 = (bf16[128,128]{1,0:T(8,128)(2,1)S(1)}, bf16[128,128]{1,0:T(8,128)(2,1)S(1)}, u32[]{:S(2)}, u32[]{:S(2)}) collective-permute-start(bf16[128,128]{1,0:T(8,128)(2,1)S(1)} %get-tuple-element.41), channel_id=1, source_target_pairs={{0,4},{1,5},{2,6},{3,7},{4,0},{5,1},{6,2},{7,3},{8,12},{9,13},{10,... | collective-permute-start | bytes 98312 | tf_op jit(solution)/shard_map/ppermute | solution.py:113
  14.7 10.8 %collective-permute-start.5 = (bf16[128,128]{1,0:T(8,128)(2,1)S(1)}, bf16[128,128]{1,0:T(8,128)(2,1)S(1)}, u32[]{:S(2)}, u32[]{:S(2)}) collective-permute-start(bf16[128,128]{1,0:T(8,128)(2,1)S(1)} %get-tuple-element.42), channel_id=1, source_target_pairs={{0,5},{1,4},{2,7},{3,6},{4,1},{5,0},{6,3},{7,2},{8,13},{9,12},{10,... | collective-permute-start | bytes 98312 | tf_op jit(solution)/shard_map/ppermute | solution.py:113
  14.8 13.0 %collective-permute-start.6 = (bf16[128,128]{1,0:T(8,128)(2,1)S(1)}, bf16[128,128]{1,0:T(8,128)(2,1)S(1)}, u32[]{:S(2)}, u32[]{:S(2)}) collective-permute-start(bf16[128,128]{1,0:T(8,128)(2,1)S(1)} %get-tuple-element.43), channel_id=1, source_target_pairs={{0,6},{1,7},{2,4},{3,5},{4,2},{5,3},{6,0},{7,1},{8,14},{9,15},{10,... | collective-permute-start | bytes 98312 | tf_op jit(solution)/shard_map/ppermute | solution.py:113
  17.4 10.4 %collective-permute-start.7 = (bf16[128,128]{1,0:T(8,128)(2,1)S(1)}, bf16[128,128]{1,0:T(8,128)(2,1)S(1)}, u32[]{:S(2)}, u32[]{:S(2)}) collective-permute-start(bf16[128,128]{1,0:T(8,128)(2,1)S(1)} %get-tuple-element.44), channel_id=1, source_target_pairs={{0,7},{1,6},{2,5},{3,4},{4,3},{5,2},{6,1},{7,0},{8,15},{9,14},{10,... | collective-permute-start | bytes 98312 | tf_op jit(solution)/shard_map/ppermute | solution.py:113
  28.6 11.1 %copy-start.1 = (bf16[1,544,512]{2,1,0:T(8,128)(2,1)S(1)}, bf16[1,544,512]{2,1,0:T(8,128)(2,1)}, u32[]{:S(2)}) copy-start(bf16[1,544,512]{2,1,0:T(8,128)(2,1)} %range_ref.1) | copy-start | bytes 1671172
  28.6 11.1 %copy-start.3 = (f32[1,2]{1,0:T(1,128)S(1)}, f32[1,2]{1,0:T(1,128)}, u32[]{:S(2)}) copy-start(f32[1,2]{1,0:T(1,128)} %shift_ref.1) | copy-start | bytes 28
  28.6 6.4 %collective-permute-start.8 = (bf16[2,256,128]{2,1,0:T(8,128)(2,1)S(1)}, bf16[2,256,128]{2,1,0:T(8,128)(2,1)S(1)}, u32[]{:S(2)}, u32[]{:S(2)}) collective-permute-start(bf16[2,256,128]{2,1,0:T(8,128)(2,1)S(1)} %get-tuple-element.45), channel_id=1, source_target_pairs={{0,16},{16,0},{1,17},{17,1},{2,18},{18,2},{3,19},{19,3},{4,20},{20... | collective-permute-start | bytes 393224 | tf_op jit(solution)/shard_map/ppermute | solution.py:481
  30.8 13.6 %collective-permute-start.9 = (bf16[2,256,384]{2,1,0:T(8,128)(2,1)S(1)}, bf16[2,256,384]{2,1,0:T(8,128)(2,1)S(1)}, u32[]{:S(2)}, u32[]{:S(2)}) collective-permute-start(bf16[2,256,384]{2,1,0:T(8,128)(2,1)S(1)} %shard_map.68), channel_id=1, source_target_pairs={{0,16},{16,0},{1,17},{17,1},{2,18},{18,2},{3,19},{19,3},{4,20},{20... | collective-permute-start | bytes 1179656 | tf_op jit(solution)/shard_map/ppermute | solution.py:481
  31.4 4.6 %collective-permute-start.10 = (bf16[256,128]{1,0:T(8,128)(2,1)S(1)}, bf16[256,128]{1,0:T(8,128)(2,1)S(1)}, u32[]{:S(2)}, u32[]{:S(2)}) collective-permute-start(bf16[256,128]{1,0:T(8,128)(2,1)S(1)} %get-tuple-element.49), channel_id=1, source_target_pairs={{0,1},{2,3},{4,5},{6,7},{8,9},{10,11},{12,13},{14,15},{1,0},{3,2},... | collective-permute-start | bytes 196616 | tf_op jit(solution)/shard_map/ppermute | solution.py:363
  31.4 6.6 %collective-permute-start.11 = (bf16[256,128]{1,0:T(8,128)(2,1)S(1)}, bf16[256,128]{1,0:T(8,128)(2,1)S(1)}, u32[]{:S(2)}, u32[]{:S(2)}) collective-permute-start(bf16[256,128]{1,0:T(8,128)(2,1)S(1)} %get-tuple-element.51), channel_id=1, source_target_pairs={{1,2},{3,4},{5,6},{7,8},{9,10},{11,12},{13,14},{2,1},{4,3},{6,5},{... | collective-permute-start | bytes 196616 | tf_op jit(solution)/shard_map/ppermute | solution.py:363
  33.8 5.9 %copy-start.2 = (bf16[1,2,512,256]{3,2,1,0:T(8,128)(2,1)S(1)}, bf16[1,2,512,256]{3,2,1,0:T(8,128)(2,1)}, u32[]{:S(2)}) copy-start(bf16[1,2,512,256]{3,2,1,0:T(8,128)(2,1)} %interp_ref.1) | copy-start | bytes 1572868
  38.1 6.3 %collective-permute-start.12 = (bf16[256,128]{1,0:T(8,128)(2,1)S(1)}, bf16[256,128]{1,0:T(8,128)(2,1)S(1)}, u32[]{:S(2)}, u32[]{:S(2)}) collective-permute-start(bf16[256,128]{1,0:T(8,128)(2,1)S(1)} %get-tuple-element.56.after_ref), channel_id=1, source_target_pairs={{0,16},{16,0},{1,17},{17,1},{2,18},{18,2},{3,19},{19,3},{4,20},{20... | collective-permute-start | bytes 196616 | tf_op jit(solution)/shard_map/ppermute | solution.py:481

commit v13 on v12

--- a/solution.py
+++ b/solution.py
@@ -270,13 +270,14 @@
     return jnp.concatenate([pulses, turned], axis=1).astype(BF16)
 
 
-def outer_kernel(pieces, side_ref, rows_ref, *refs):
+def outer_kernel(order, side_ref, rows_ref, *refs):
     own_side = side_ref[:1, :]
     me = lax.axis_index("rng")
+    pieces = len(order)
     own_ref, out_ref, *edge_refs = refs[pieces:-1]
     pulses_ref = refs[-1]
     rows = refs[0].shape[0] // 2
-    for d, ref in enumerate(refs[:pieces]):
+    for d, ref in zip(order, refs[:pieces]):
         for t in range(2):
             place = pl.multiple_of((me ^ (d + t * pieces)) * rows, rows)
             pulses_ref[pl.ds(place, rows), :] = ref[t * rows : (t + 1) * rows, :]
@@ -308,11 +309,13 @@
 
 def outer_image(own_side, rows, pieces):
     half, side = rows.shape
+    middle = len(pieces) // 2
+    order = [0, 1, 2, *range(middle, len(pieces)), *range(3, middle)]
     angles = 2 * half
     image = jax.ShapeDtypeStruct((2, angles // 2, LANES), BF16)
     edge = jax.ShapeDtypeStruct((angles // 2, LANES), BF16)
     return pl.pallas_call(
-        functools.partial(outer_kernel, len(pieces)),
+        functools.partial(outer_kernel, order),
         out_shape=[image, image, edge, edge],
         in_specs=[VMEM] * (2 + len(pieces)),
         out_specs=[VMEM] * 4,
@@ -321,7 +324,7 @@
         cost_estimate=pl.CostEstimate(
             flops=4 * angles * side * LANES, bytes_accessed=3 * MIB, transcendentals=0
         ),
-    )(own_side, rows, *pieces)
+    )(own_side, rows, *(pieces[d] for d in order))
 
 
 def partner_rows_kernel(local_pulses, rows_ref, pulses_ref, image_ref):

time: 46.8 us -> 46.8 us (level)
  no operation moved by 1% of the time
where the time goes in v13:
time: 46.8 us; the launch traced here: 46.6 us
  starting transfers between devices  21.4 us (46%)
  waiting for transfers between devices  13.4 us (29%)
  Pallas kernels  10.2 us (22%)
  local copies, waits for them, and re-layouts  1.44 us (3%)
    ppermute x8, waiting for transfers between devices, across(): return lax.ppermute(value, 'rng', [(i, i ^ mask) for i in range(devices)])  8.9 us
    ppermute x8, starting transfers between devices, across(): return lax.ppermute(value, 'rng', [(i, i ^ mask) for i in range(devices)])  8.57 us
    all_to_all x1, starting transfers between devices, on_device(): lax.all_to_all(blocks, 'rng', split_axis=0, concat_axis=0, tiled=True)  6.72 us
    ppermute x3, starting transfers between devices, from_partner(): return lax.ppermute(value, 'sub', pairs)  3.74 us
    ppermute x3, waiting for transfers between devices, from_partner(): return lax.ppermute(value, 'sub', pairs)  2.51 us
    ppermute x2, starting transfers between devices, exchanged(): return lax.ppermute(value, 'rng', pairs + [(j, i) for i, j in pairs] + ends)  2.33 us
    pallas_call x1, Pallas kernels, merge_tables(): pl.pallas_call(functools.partial(merge_table_kernel, level, stride), out_...  2.24 us
    pallas_call x1, Pallas kernels, merged_image(): pl.pallas_call(late_kernel, out_shape=jax.ShapeDtypeStruct((2, angles, bi...  2.18 us
  transfers between devices with their start and end apart: 14, of which 5 were waited for; matrix products, arithmetic and copies ran while one was open for 0% of the time, Pallas kernels for 15%

profile of v13, /device:TPU:16, one launch (start us, length us, event | category | flops | bytes accessed | tf_op | source)
XLA Modules:
  0.0 46.6 jit_solution(11286954853318499359)
XLA Ops:
  0.0 0.0 copy-start
  0.0 1.2 %copy-done = bf16[2,32,8192]{2,1,0:T(8,128)(2,1)S(1)} copy-done((bf16[2,32,8192]{2,1,0:T(8,128)(2,1)S(1)}, bf16[2,32,8192]{2,1,0:T(8,128)(2,1)}, u32[]{:S(2)}) %copy-start) | copy-done | bytes 1048600
  1.2 1.0 %shard_map.64 = (bf16[8,64,128]{2,1,0:T(8,128)(2,1)S(1)}, bf16[8,64,128]{2,1,0:T(8,128)(2,1)S(1)}, bf16[16,64,384]{2,1,0:T(8,128)(2,1)}) custom-call(bf16[64,8192]{1,0:T(8,128)(2,1)S(1)} %bitcast.4), custom_call_target="tpu_custom_call" | custom-call | bytes 2097152 | tf_op jit(solution)/shard_map/pallas_call | solution.py:81
  2.3 0.0 collective-permute-start
  2.3 6.7 %all-to-all-start = ((bf16[16,64,384]{2,1,0:T(8,128)(2,1)}), bf16[16,64,384]{2,1,0:T(8,128)(2,1)S(1)}, u32[]{:S(2)}, u32[]{:S(2)}) async-start(bf16[16,64,384]{2,1,0:T(8,128)(2,1)} %get-tuple-element.46), calls=%async_computation | async-start | bytes 1572864 | tf_op jit(solution)/shard_map/all_to_all | solution.py:522
  9.0 0.0 collective-permute-done.relay_ref
  9.0 0.0 copy-start.4
  9.0 0.0 copy-start.5
  9.0 0.2 collective-permute-start.1
  9.3 1.5 %collective-permute-start.2 = (bf16[128,128]{1,0:T(8,128)(2,1)S(1)}, bf16[128,128]{1,0:T(8,128)(2,1)S(1)}, u32[]{:S(2)}, u32[]{:S(2)}) collective-permute-start(bf16[128,128]{1,0:T(8,128)(2,1)S(1)} %get-tuple-element.39), channel_id=1, source_target_pairs={{0,2},{1,3},{2,0},{3,1},{4,6},{5,7},{6,4},{7,5},{8,10},{9,11},{10,... | collective-permute-start | bytes 98312 | tf_op jit(solution)/shard_map/ppermute | solution.py:113
  10.7 3.7 %collective-permute-start.3 = (bf16[128,128]{1,0:T(8,128)(2,1)S(1)}, bf16[128,128]{1,0:T(8,128)(2,1)S(1)}, u32[]{:S(2)}, u32[]{:S(2)}) collective-permute-start(bf16[128,128]{1,0:T(8,128)(2,1)S(1)} %get-tuple-element.40), channel_id=1, source_target_pairs={{0,4},{1,5},{2,6},{3,7},{4,0},{5,1},{6,2},{7,3},{8,12},{9,13},{10,... | collective-permute-start | bytes 98312 | tf_op jit(solution)/shard_map/ppermute | solution.py:113
  14.4 0.0 collective-permute-start.4
  14.4 1.5 %collective-permute-start.5 = (bf16[128,128]{1,0:T(8,128)(2,1)S(1)}, bf16[128,128]{1,0:T(8,128)(2,1)S(1)}, u32[]{:S(2)}, u32[]{:S(2)}) collective-permute-start(bf16[128,128]{1,0:T(8,128)(2,1)S(1)} %get-tuple-element.42), channel_id=1, source_target_pairs={{0,6},{1,7},{2,4},{3,5},{4,2},{5,3},{6,0},{7,1},{8,14},{9,15},{10,... | collective-permute-start | bytes 98312 | tf_op jit(solution)/shard_map/ppermute | solution.py:113
  15.9 0.0 collective-permute-done.1.refs_1_
  15.9 0.9 %collective-permute-start.6 = (bf16[128,128]{1,0:T(8,128)(2,1)S(1)}, bf16[128,128]{1,0:T(8,128)(2,1)S(1)}, u32[]{:S(2)}, u32[]{:S(2)}) collective-permute-start(bf16[128,128]{1,0:T(8,128)(2,1)S(1)} %get-tuple-element.43), channel_id=1, source_target_pairs={{0,7},{1,6},{2,5},{3,4},{4,3},{5,2},{6,1},{7,0},{8,15},{9,14},{10,... | collective-permute-start | bytes 98312 | tf_op jit(solution)/shard_map/ppermute | solution.py:113
  16.8 0.0 collective-permute-done.2.refs_2_
  16.8 0.8 %collective-permute-start.7 = (bf16[128,128]{1,0:T(8,128)(2,1)S(1)}, bf16[128,128]{1,0:T(8,128)(2,1)S(1)}, u32[]{:S(2)}, u32[]{:S(2)}) collective-permute-start(bf16[128,128]{1,0:T(8,128)(2,1)S(1)} %get-tuple-element.44), channel_id=1, source_target_pairs={{0,3},{1,2},{2,1},{3,0},{4,7},{5,6},{6,5},{7,4},{8,11},{9,10},{10,... | collective-permute-start | bytes 98312 | tf_op jit(solution)/shard_map/ppermute | solution.py:113
  17.6 0.0 copy-done.4
  17.6 0.1 copy.7.flag_ref
  17.7 1.2 %shard_map.66 = (bf16[256,1024]{1,0:T(8,128)(2,1)S(1)}, f32[8,128]{1,0:T(8,128)S(1)}) custom-call(s32[1,2,1]{2,1,0:T(2,128)S(1)} %copy.7.flag_ref, bf16[128,128]{1,0:T(8,128)(2,1)S(1)} %get-tuple-element.35.after_ref.refs_0_), custom_call_target="tpu_custom_call" | custom-call | flops 9000000 | bytes 4194304 | tf_op jit(solution)/shard_map/pallas_call | solution.py:152
  18.9 6.7 %collective-permute-done.3.refs_3_ = bf16[128,128]{1,0:T(8,128)(2,1)S(1)} collective-permute-done((bf16[128,128]{1,0:T(8,128)(2,1)S(1)}, bf16[128,128]{1,0:T(8,128)(2,1)S(1)}, u32[]{:S(2)}, u32[]{:S(2)}) %collective-permute-start.3) | collective-permute-done | bytes 32800 | tf_op jit(solution)/shard_map/ppermute | solution.py:113
  25.6 0.0 collective-permute-done.4.refs_4_
  25.6 2.2 %collective-permute-done.5.refs_5_ = bf16[128,128]{1,0:T(8,128)(2,1)S(1)} collective-permute-done((bf16[128,128]{1,0:T(8,128)(2,1)S(1)}, bf16[128,128]{1,0:T(8,128)(2,1)S(1)}, u32[]{:S(2)}, u32[]{:S(2)}) %collective-permute-start.5) | collective-permute-done | bytes 32800 | tf_op jit(solution)/shard_map/ppermute | solution.py:113
  27.8 0.0 collective-permute-done.6.refs_6_
  27.8 0.0 collective-permute-done.7.refs_7_
  27.8 0.8 %shard_map.67 = (bf16[2,256,128]{2,1,0:T(8,128)(2,1)S(1)}, bf16[2,256,128]{2,1,0:T(8,128)(2,1)S(1)}, bf16[256,128]{1,0:T(8,128)(2,1)S(1)}, bf16[256,128]{1,0:T(8,128)(2,1)S(1)}) custom-call(f32[8,128]{1,0:T(8,128)S(1)} %get-tuple-element.36.side_ref, bf16[256,1024]{1,0:T(8,128)(2,1)S(1)} %get-tuple-element.37.rows_ref, ...), custom_call_target="tpu_custom_call" | custom-call | flops 268435456 | bytes 3145728 | tf_op jit(solution)/shard_map/pallas_call | solution.py:317
  28.6 0.0 copy-start.1
  28.6 0.0 copy-start.3
  28.6 1.6 %collective-permute-start.8 = (bf16[2,256,128]{2,1,0:T(8,128)(2,1)S(1)}, bf16[2,256,128]{2,1,0:T(8,128)(2,1)S(1)}, u32[]{:S(2)}, u32[]{:S(2)}) collective-permute-start(bf16[2,256,128]{2,1,0:T(8,128)(2,1)S(1)} %get-tuple-element.45), channel_id=1, source_target_pairs={{0,16},{16,0},{1,17},{17,1},{2,18},{18,2},{3,19},{19,3},{4,20},{20... | collective-permute-start | bytes 393224 | tf_op jit(solution)/shard_map/ppermute | solution.py:484
  30.2 0.0 all-to-all-done
  30.2 0.6 %shard_map.68 = bf16[2,256,384]{2,1,0:T(8,128)(2,1)S(1)} custom-call(bf16[256,1024]{1,0:T(8,128)(2,1)S(1)} %get-tuple-element.37.rows_ref, bf16[1024,384]{1,0:T(8,128)(2,1)S(1)} %bitcast.2), custom_call_target="tpu_custom_call" | custom-call | flops 402653184 | bytes 3145728 | tf_op jit(solution)/shard_map/pallas_call | solution.py:350
  30.8 0.6 %collective-permute-start.9 = (bf16[2,256,384]{2,1,0:T(8,128)(2,1)S(1)}, bf16[2,256,384]{2,1,0:T(8,128)(2,1)S(1)}, u32[]{:S(2)}, u32[]{:S(2)}) collective-permute-start(bf16[2,256,384]{2,1,0:T(8,128)(2,1)S(1)} %shard_map.68), channel_id=1, source_target_pairs={{0,16},{16,0},{1,17},{17,1},{2,18},{18,2},{3,19},{19,3},{4,20},{20... | collective-permute-start | bytes 1179656 | tf_op jit(solution)/shard_map/ppermute | solution.py:484
  31.4 0.0 collective-permute-start.10
  31.4 2.3 %collective-permute-start.11 = (bf16[256,128]{1,0:T(8,128)(2,1)S(1)}, bf16[256,128]{1,0:T(8,128)(2,1)S(1)}, u32[]{:S(2)}, u32[]{:S(2)}) collective-permute-start(bf16[256,128]{1,0:T(8,128)(2,1)S(1)} %get-tuple-element.51), channel_id=1, source_target_pairs={{1,2},{3,4},{5,6},{7,8},{9,10},{11,12},{13,14},{2,1},{4,3},{6,5},{... | collective-permute-start | bytes 196616 | tf_op jit(solution)/shard_map/ppermute | solution.py:366
  33.7 0.0 copy-done.5
  33.7 0.1 copy.9.offset_ref
  33.8 0.0 copy-start.2
  33.8 1.2 %collective-permute-done.8.far_outer = bf16[2,256,128]{2,1,0:T(8,128)(2,1)S(1)} collective-permute-done((bf16[2,256,128]{2,1,0:T(8,128)(2,1)S(1)}, bf16[2,256,128]{2,1,0:T(8,128)(2,1)S(1)}, u32[]{:S(2)}, u32[]{:S(2)}) %collective-permute-start.8) | collective-permute-done | bytes 131104 | tf_op jit(solution)/shard_map/ppermute | solution.py:484
  35.0 0.9 %shard_map.70.own_ref = bf16[2,256,512]{2,1,0:T(8,128)(2,1)S(1)} custom-call(bf16[256,1024]{1,0:T(8,128)(2,1)S(1)} %get-tuple-element.37.rows_ref, bf16[1024,384]{1,0:T(8,128)(2,1)S(1)} %bitcast.3, bf16[2,256,128]{2,1,0:T(8,128)(2,1)S(1)} %get-tuple-element.54.outer_ref), custom_call_target="tpu_custom_call" | custom-call | flops 402653184 | bytes 3145728 | tf_op jit(solution)/shard_map/pallas_call | solution.py:350
  35.9 0.0 collective-permute-done.10.first_ref
  36.0 2.0 %collective-permute-done.11.second_ref = bf16[256,128]{1,0:T(8,128)(2,1)S(1)} collective-permute-done((bf16[256,128]{1,0:T(8,128)(2,1)S(1)}, bf16[256,128]{1,0:T(8,128)(2,1)S(1)}, u32[]{:S(2)}, u32[]{:S(2)}) %collective-permute-start.11) | collective-permute-done | bytes 65568 | tf_op jit(solution)/shard_map/ppermute | solution.py:366
  38.0 0.2 shard_map.69
  38.1 1.6 %collective-permute-start.12 = (bf16[256,128]{1,0:T(8,128)(2,1)S(1)}, bf16[256,128]{1,0:T(8,128)(2,1)S(1)}, u32[]{:S(2)}, u32[]{:S(2)}) collective-permute-start(bf16[256,128]{1,0:T(8,128)(2,1)S(1)} %get-tuple-element.56.after_ref), channel_id=1, source_target_pairs={{0,16},{16,0},{1,17},{17,1},{2,18},{18,2},{3,19},{19,3},{4,20},{20... | collective-permute-start | bytes 196616 | tf_op jit(solution)/shard_map/ppermute | solution.py:484
  39.7 0.0 copy-done.1
  39.7 0.0 copy-done.3
  39.7 0.0 copy-done.2
  39.7 2.2 %shard_map.71 = (bf16[2,512,512]{2,1,0:T(8,128)(2,1)S(1)}, bf16[2,2,128,512]{3,2,1,0:T(8,128)(2,1)S(1)}, f32[2,2,512,512]{3,2,1,0:T(8,128)S(1)}, bf16[2,512,256]{2,1,0:T(8,128)(2,1)S(1)}, f32[8,128]{1,0:T(8,128)}) custom-call(s32[1,2,1]{2,1,0:T(2,128)S(1)} %copy.7.flag_ref, s32[1,2,1]{2,1,0:T(2,128)S(1)} %copy.9.offset_ref, f32[1,2]{1,0:T(1,128)S(1)} %copy-done.3, ...), custom_call_target="tpu_custom_call" | custom-call | flops 2300000000 | bytes 7340032 | tf_op jit(solution)/shard_map/pallas_call | solution.py:240
  42.0 1.1 %shard_map.72.merged_ref = f32[2,512,512]{2,1,0:T(8,128)S(1)} custom-call(bf16[2,256,512]{2,1,0:T(8,128)(2,1)S(1)} %shard_map.70.own_ref, bf16[256,128]{1,0:T(8,128)(2,1)S(1)} %get-tuple-element.55.rims_ref, bf16[2,512,512]{2,1,0:T(8,128)(2,1)S(1)} %get-tuple-element.57.centre_ref, bf16[2,2,128,512]{3,2,1,0:T(8,128)(2,1)S(1)} %get-tuple-element.58.rim_ref, ...), custom_call_target="tpu_custom_call" | custom-call | flops 536870912 | bytes 8388608 | tf_op jit(solution)/shard_map/pallas_call | solution.py:454
  43.1 1.3 %collective-permute-done.12.rims_ref = bf16[256,128]{1,0:T(8,128)(2,1)S(1)} collective-permute-done((bf16[256,128]{1,0:T(8,128)(2,1)S(1)}, bf16[256,128]{1,0:T(8,128)(2,1)S(1)}, u32[]{:S(2)}, u32[]{:S(2)}) %collective-permute-start.12) | collective-permute-done | bytes 65568 | tf_op jit(solution)/shard_map/ppermute | solution.py:484
  44.4 0.0 collective-permute-done.9.far_inner
  44.4 2.2 %shard_map.73 = f32[2,512,512]{2,1,0:T(8,128)} custom-call(bf16[2,256,128]{2,1,0:T(8,128)(2,1)S(1)} %collective-permute-done.8.far_outer, bf16[2,256,384]{2,1,0:T(8,128)(2,1)S(1)} %collective-permute-done.9.far_inner, bf16[256,128]{1,0:T(8,128)(2,1)S(1)} %collective-permute-done.12.rims_ref, f32[2,512,512]{2,1,0:T(8,128)S(1)} %shard_map.72.merged_ref, ...), custom_call_target="tpu_custom_call" | custom-call | flops 536870912 | bytes 8388608 | tf_op jit(solution)/shard_map/pallas_call | solution.py:463
  (1 shorter events, 0.0 us)
Async XLA Ops:
  0.0 1.2 %copy-start = (bf16[2,32,8192]{2,1,0:T(8,128)(2,1)S(1)}, bf16[2,32,8192]{2,1,0:T(8,128)(2,1)}, u32[]{:S(2)}) copy-start(bf16[2,32,8192]{2,1,0:T(8,128)(2,1)} %param.6) | copy-start | bytes 3145732
  2.3 6.7 %collective-permute-start = (bf16[8,64,128]{2,1,0:T(8,128)(2,1)S(1)}, bf16[8,64,128]{2,1,0:T(8,128)(2,1)S(1)}, u32[]{:S(2)}, u32[]{:S(2)}) collective-permute-start(bf16[8,64,128]{2,1,0:T(8,128)(2,1)S(1)} %get-tuple-element.34), channel_id=1, source_target_pairs={{0,8},{1,9},{2,10},{3,11},{4,12},{5,13},{6,14},{7,15},{8,0},{9,1},... | collective-permute-start | bytes 393224 | tf_op jit(solution)/shard_map/ppermute | solution.py:113
  2.3 28.0 %all-to-all-start = ((bf16[16,64,384]{2,1,0:T(8,128)(2,1)}), bf16[16,64,384]{2,1,0:T(8,128)(2,1)S(1)}, u32[]{:S(2)}, u32[]{:S(2)}) async-start(bf16[16,64,384]{2,1,0:T(8,128)(2,1)} %get-tuple-element.46), calls=%async_computation | async-start | bytes 1572864 | tf_op jit(solution)/shard_map/all_to_all | solution.py:522
  9.0 8.6 %copy-start.4 = (s32[1,2,1]{1,2,0:T(1,128)S(1)}, s32[1,2,1]{1,2,0:T(1,128)}, u32[]{:S(2)}) copy-start(s32[1,2,1]{1,2,0:T(1,128)} %param.7) | copy-start | bytes 28
  9.0 24.7 %copy-start.5 = (s32[1,2,1]{1,2,0:T(1,128)S(1)}, s32[1,2,1]{1,2,0:T(1,128)}, u32[]{:S(2)}) copy-start(s32[1,2,1]{1,2,0:T(1,128)} %param.8) | copy-start | bytes 28
  9.0 6.9 %collective-permute-start.1 = (bf16[128,128]{1,0:T(8,128)(2,1)S(1)}, bf16[128,128]{1,0:T(8,128)(2,1)S(1)}, u32[]{:S(2)}, u32[]{:S(2)}) collective-permute-start(bf16[128,128]{1,0:T(8,128)(2,1)S(1)} %get-tuple-element.38), channel_id=1, source_target_pairs={{0,1},{1,0},{2,3},{3,2},{4,5},{5,4},{6,7},{7,6},{8,9},{9,8},{10,11... | collective-permute-start | bytes 98312 | tf_op jit(solution)/shard_map/ppermute | solution.py:113
  9.3 7.6 %collective-permute-start.2 = (bf16[128,128]{1,0:T(8,128)(2,1)S(1)}, bf16[128,128]{1,0:T(8,128)(2,1)S(1)}, u32[]{:S(2)}, u32[]{:S(2)}) collective-permute-start(bf16[128,128]{1,0:T(8,128)(2,1)S(1)} %get-tuple-element.39), channel_id=1, source_target_pairs={{0,2},{1,3},{2,0},{3,1},{4,6},{5,7},{6,4},{7,5},{8,10},{9,11},{10,... | collective-permute-start | bytes 98312 | tf_op jit(solution)/shard_map/ppermute | solution.py:113
  10.7 14.9 %collective-permute-start.3 = (bf16[128,128]{1,0:T(8,128)(2,1)S(1)}, bf16[128,128]{1,0:T(8,128)(2,1)S(1)}, u32[]{:S(2)}, u32[]{:S(2)}) collective-permute-start(bf16[128,128]{1,0:T(8,128)(2,1)S(1)} %get-tuple-element.40), channel_id=1, source_target_pairs={{0,4},{1,5},{2,6},{3,7},{4,0},{5,1},{6,2},{7,3},{8,12},{9,13},{10,... | collective-permute-start | bytes 98312 | tf_op jit(solution)/shard_map/ppermute | solution.py:113
  14.4 11.2 %collective-permute-start.4 = (bf16[128,128]{1,0:T(8,128)(2,1)S(1)}, bf16[128,128]{1,0:T(8,128)(2,1)S(1)}, u32[]{:S(2)}, u32[]{:S(2)}) collective-permute-start(bf16[128,128]{1,0:T(8,128)(2,1)S(1)} %get-tuple-element.41), channel_id=1, source_target_pairs={{0,5},{1,4},{2,7},{3,6},{4,1},{5,0},{6,3},{7,2},{8,13},{9,12},{10,... | collective-permute-start | bytes 98312 | tf_op jit(solution)/shard_map/ppermute | solution.py:113
  14.4 13.3 %collective-permute-start.5 = (bf16[128,128]{1,0:T(8,128)(2,1)S(1)}, bf16[128,128]{1,0:T(8,128)(2,1)S(1)}, u32[]{:S(2)}, u32[]{:S(2)}) collective-permute-start(bf16[128,128]{1,0:T(8,128)(2,1)S(1)} %get-tuple-element.42), channel_id=1, source_target_pairs={{0,6},{1,7},{2,4},{3,5},{4,2},{5,3},{6,0},{7,1},{8,14},{9,15},{10,... | collective-permute-start | bytes 98312 | tf_op jit(solution)/shard_map/ppermute | solution.py:113
  15.9 11.9 %collective-permute-start.6 = (bf16[128,128]{1,0:T(8,128)(2,1)S(1)}, bf16[128,128]{1,0:T(8,128)(2,1)S(1)}, u32[]{:S(2)}, u32[]{:S(2)}) collective-permute-start(bf16[128,128]{1,0:T(8,128)(2,1)S(1)} %get-tuple-element.43), channel_id=1, source_target_pairs={{0,7},{1,6},{2,5},{3,4},{4,3},{5,2},{6,1},{7,0},{8,15},{9,14},{10,... | collective-permute-start | bytes 98312 | tf_op jit(solution)/shard_map/ppermute | solution.py:113
  16.8 10.9 %collective-permute-start.7 = (bf16[128,128]{1,0:T(8,128)(2,1)S(1)}, bf16[128,128]{1,0:T(8,128)(2,1)S(1)}, u32[]{:S(2)}, u32[]{:S(2)}) collective-permute-start(bf16[128,128]{1,0:T(8,128)(2,1)S(1)} %get-tuple-element.44), channel_id=1, source_target_pairs={{0,3},{1,2},{2,1},{3,0},{4,7},{5,6},{6,5},{7,4},{8,11},{9,10},{10,... | collective-permute-start | bytes 98312 | tf_op jit(solution)/shard_map/ppermute | solution.py:113
  28.6 11.1 %copy-start.1 = (bf16[1,544,512]{2,1,0:T(8,128)(2,1)S(1)}, bf16[1,544,512]{2,1,0:T(8,128)(2,1)}, u32[]{:S(2)}) copy-start(bf16[1,544,512]{2,1,0:T(8,128)(2,1)} %range_ref.1) | copy-start | bytes 1671172
  28.6 11.1 %copy-start.3 = (f32[1,2]{1,0:T(1,128)S(1)}, f32[1,2]{1,0:T(1,128)}, u32[]{:S(2)}) copy-start(f32[1,2]{1,0:T(1,128)} %shift_ref.1) | copy-start | bytes 28
  28.6 6.4 %collective-permute-start.8 = (bf16[2,256,128]{2,1,0:T(8,128)(2,1)S(1)}, bf16[2,256,128]{2,1,0:T(8,128)(2,1)S(1)}, u32[]{:S(2)}, u32[]{:S(2)}) collective-permute-start(bf16[2,256,128]{2,1,0:T(8,128)(2,1)S(1)} %get-tuple-element.45), channel_id=1, source_target_pairs={{0,16},{16,0},{1,17},{17,1},{2,18},{18,2},{3,19},{19,3},{4,20},{20... | collective-permute-start | bytes 393224 | tf_op jit(solution)/shard_map/ppermute | solution.py:484
  30.8 13.6 %collective-permute-start.9 = (bf16[2,256,384]{2,1,0:T(8,128)(2,1)S(1)}, bf16[2,256,384]{2,1,0:T(8,128)(2,1)S(1)}, u32[]{:S(2)}, u32[]{:S(2)}) collective-permute-start(bf16[2,256,384]{2,1,0:T(8,128)(2,1)S(1)} %shard_map.68), channel_id=1, source_target_pairs={{0,16},{16,0},{1,17},{17,1},{2,18},{18,2},{3,19},{19,3},{4,20},{20... | collective-permute-start | bytes 1179656 | tf_op jit(solution)/shard_map/ppermute | solution.py:484
  31.4 4.6 %collective-permute-start.10 = (bf16[256,128]{1,0:T(8,128)(2,1)S(1)}, bf16[256,128]{1,0:T(8,128)(2,1)S(1)}, u32[]{:S(2)}, u32[]{:S(2)}) collective-permute-start(bf16[256,128]{1,0:T(8,128)(2,1)S(1)} %get-tuple-element.49), channel_id=1, source_target_pairs={{0,1},{2,3},{4,5},{6,7},{8,9},{10,11},{12,13},{14,15},{1,0},{3,2},... | collective-permute-start | bytes 196616 | tf_op jit(solution)/shard_map/ppermute | solution.py:366
  31.4 6.6 %collective-permute-start.11 = (bf16[256,128]{1,0:T(8,128)(2,1)S(1)}, bf16[256,128]{1,0:T(8,128)(2,1)S(1)}, u32[]{:S(2)}, u32[]{:S(2)}) collective-permute-start(bf16[256,128]{1,0:T(8,128)(2,1)S(1)} %get-tuple-element.51), channel_id=1, source_target_pairs={{1,2},{3,4},{5,6},{7,8},{9,10},{11,12},{13,14},{2,1},{4,3},{6,5},{... | collective-permute-start | bytes 196616 | tf_op jit(solution)/shard_map/ppermute | solution.py:366
  33.8 5.9 %copy-start.2 = (bf16[1,2,512,256]{3,2,1,0:T(8,128)(2,1)S(1)}, bf16[1,2,512,256]{3,2,1,0:T(8,128)(2,1)}, u32[]{:S(2)}) copy-start(bf16[1,2,512,256]{3,2,1,0:T(8,128)(2,1)} %interp_ref.1) | copy-start | bytes 1572868
  38.1 6.3 %collective-permute-start.12 = (bf16[256,128]{1,0:T(8,128)(2,1)S(1)}, bf16[256,128]{1,0:T(8,128)(2,1)S(1)}, u32[]{:S(2)}, u32[]{:S(2)}) collective-permute-start(bf16[256,128]{1,0:T(8,128)(2,1)S(1)} %get-tuple-element.56.after_ref), channel_id=1, source_target_pairs={{0,16},{16,0},{1,17},{17,1},{2,18},{18,2},{3,19},{19,3},{4,20},{20... | collective-permute-start | bytes 196616 | tf_op jit(solution)/shard_map/ppermute | solution.py:484

commit v14 on v12

--- a/solution.py
+++ b/solution.py
@@ -423,22 +423,18 @@
     parts = len(rows)
     block = LANES
     copies = []
-    for first in range(0, matrix_ref.shape[1], 2 * block):
-        matrix = matrix_ref[1, first : first + 2 * block]
-        terms = dot(matrix, rows[0]), dot(matrix, rows[1])
-        for step in range(2):
-            here = slice(first + step * block, first + (step + 1) * block)
-            there = slice(step * block, (step + 1) * block)
-            turned = rotated(
-                (terms[0][there], terms[1][there]), (turn_ref[1, 0, here], turn_ref[1, 1, here])
-            )
-            for part in range(parts):
-                buffer[part, here] = (merged_ref[part, here] + turned[part]).astype(buffer.dtype)
-            copy = pltpu.make_async_copy(
-                buffer.at[:, here], out_ref.at[:, here], sems.at[len(copies)]
-            )
-            copy.start()
-            copies.append(copy)
+    for first in range(0, matrix_ref.shape[1], block):
+        here = slice(first, first + block)
+        matrix = matrix_ref[1, here]
+        turned = rotated(
+            (dot(matrix, rows[0]), dot(matrix, rows[1])),
+            (turn_ref[1, 0, here], turn_ref[1, 1, here]),
+        )
+        for part in range(parts):
+            buffer[part, here] = (merged_ref[part, here] + turned[part]).astype(buffer.dtype)
+        copy = pltpu.make_async_copy(buffer.at[:, here], out_ref.at[:, here], sems.at[len(copies)])
+        copy.start()
+        copies.append(copy)
     for copy in copies:
         copy.wait()
 

time: 46.8 us -> 46.8 us (level)
  no operation moved by 1% of the time
where the time goes in v14:
time: 46.8 us; the launch traced here: 46.6 us
  starting transfers between devices  21.3 us (46%)
  waiting for transfers between devices  13.5 us (29%)
  Pallas kernels  10.2 us (22%)
  local copies, waits for them, and re-layouts  1.44 us (3%)
    ppermute x8, waiting for transfers between devices, across(): return lax.ppermute(value, 'rng', [(i, i ^ mask) for i in range(devices)])  8.98 us
    ppermute x8, starting transfers between devices, across(): return lax.ppermute(value, 'rng', [(i, i ^ mask) for i in range(devices)])  8.48 us
    all_to_all x1, starting transfers between devices, on_device(): lax.all_to_all(blocks, 'rng', split_axis=0, concat_axis=0, tiled=True)  6.72 us
    ppermute x3, starting transfers between devices, from_partner(): return lax.ppermute(value, 'sub', pairs)  3.74 us
    ppermute x3, waiting for transfers between devices, from_partner(): return lax.ppermute(value, 'sub', pairs)  2.51 us
    ppermute x2, starting transfers between devices, exchanged(): return lax.ppermute(value, 'rng', pairs + [(j, i) for i, j in pairs] + ends)  2.34 us
    pallas_call x1, Pallas kernels, merge_tables(): pl.pallas_call(functools.partial(merge_table_kernel, level, stride), out_...  2.23 us
    pallas_call x1, Pallas kernels, merged_image(): pl.pallas_call(late_kernel, out_shape=jax.ShapeDtypeStruct((2, angles, bi...  2.2 us
  transfers between devices with their start and end apart: 14, of which 5 were waited for; matrix products, arithmetic and copies ran while one was open for 0% of the time, Pallas kernels for 15%

profile of v14, /device:TPU:16, one launch (start us, length us, event | category | flops | bytes accessed | tf_op | source)
XLA Modules:
  0.0 46.6 jit_solution(8773617994085653826)
XLA Ops:
  0.0 0.0 copy-start
  0.0 1.2 %copy-done = bf16[2,32,8192]{2,1,0:T(8,128)(2,1)S(1)} copy-done((bf16[2,32,8192]{2,1,0:T(8,128)(2,1)S(1)}, bf16[2,32,8192]{2,1,0:T(8,128)(2,1)}, u32[]{:S(2)}) %copy-start) | copy-done | bytes 1048600
  1.2 1.0 %shard_map.64 = (bf16[8,64,128]{2,1,0:T(8,128)(2,1)S(1)}, bf16[8,64,128]{2,1,0:T(8,128)(2,1)S(1)}, bf16[16,64,384]{2,1,0:T(8,128)(2,1)}) custom-call(bf16[64,8192]{1,0:T(8,128)(2,1)S(1)} %bitcast.4), custom_call_target="tpu_custom_call" | custom-call | bytes 2097152 | tf_op jit(solution)/shard_map/pallas_call | solution.py:81
  2.3 0.0 collective-permute-start
  2.3 6.7 %all-to-all-start = ((bf16[16,64,384]{2,1,0:T(8,128)(2,1)}), bf16[16,64,384]{2,1,0:T(8,128)(2,1)S(1)}, u32[]{:S(2)}, u32[]{:S(2)}) async-start(bf16[16,64,384]{2,1,0:T(8,128)(2,1)} %get-tuple-element.46), calls=%async_computation | async-start | bytes 1572864 | tf_op jit(solution)/shard_map/all_to_all | solution.py:515
  9.0 0.0 collective-permute-done.relay_ref
  9.0 0.0 copy-start.4
  9.0 0.0 copy-start.5
  9.0 0.2 collective-permute-start.1
  9.3 1.5 %collective-permute-start.2 = (bf16[128,128]{1,0:T(8,128)(2,1)S(1)}, bf16[128,128]{1,0:T(8,128)(2,1)S(1)}, u32[]{:S(2)}, u32[]{:S(2)}) collective-permute-start(bf16[128,128]{1,0:T(8,128)(2,1)S(1)} %get-tuple-element.39), channel_id=1, source_target_pairs={{0,2},{1,3},{2,0},{3,1},{4,6},{5,7},{6,4},{7,5},{8,10},{9,11},{10,... | collective-permute-start | bytes 98312 | tf_op jit(solution)/shard_map/ppermute | solution.py:113
  10.7 0.2 collective-permute-start.3
  11.0 3.8 %collective-permute-start.4 = (bf16[128,128]{1,0:T(8,128)(2,1)S(1)}, bf16[128,128]{1,0:T(8,128)(2,1)S(1)}, u32[]{:S(2)}, u32[]{:S(2)}) collective-permute-start(bf16[128,128]{1,0:T(8,128)(2,1)S(1)} %get-tuple-element.41), channel_id=1, source_target_pairs={{0,4},{1,5},{2,6},{3,7},{4,0},{5,1},{6,2},{7,3},{8,12},{9,13},{10,... | collective-permute-start | bytes 98312 | tf_op jit(solution)/shard_map/ppermute | solution.py:113
  14.7 0.0 collective-permute-start.5
  14.7 0.0 collective-permute-done.1.refs_1_
  14.8 2.6 %collective-permute-start.6 = (bf16[128,128]{1,0:T(8,128)(2,1)S(1)}, bf16[128,128]{1,0:T(8,128)(2,1)S(1)}, u32[]{:S(2)}, u32[]{:S(2)}) collective-permute-start(bf16[128,128]{1,0:T(8,128)(2,1)S(1)} %get-tuple-element.43), channel_id=1, source_target_pairs={{0,6},{1,7},{2,4},{3,5},{4,2},{5,3},{6,0},{7,1},{8,14},{9,15},{10,... | collective-permute-start | bytes 98312 | tf_op jit(solution)/shard_map/ppermute | solution.py:113
  17.4 0.0 collective-permute-done.2.refs_2_
  17.4 0.2 collective-permute-start.7
  17.5 0.0 copy-done.4
  17.5 0.1 copy.7.flag_ref
  17.6 1.2 %shard_map.66 = (bf16[256,1024]{1,0:T(8,128)(2,1)S(1)}, f32[8,128]{1,0:T(8,128)S(1)}) custom-call(s32[1,2,1]{2,1,0:T(2,128)S(1)} %copy.7.flag_ref, bf16[128,128]{1,0:T(8,128)(2,1)S(1)} %get-tuple-element.35.after_ref.refs_0_), custom_call_target="tpu_custom_call" | custom-call | flops 9000000 | bytes 4194304 | tf_op jit(solution)/shard_map/pallas_call | solution.py:152
  18.8 0.0 collective-permute-done.3.refs_3_
  18.8 6.8 %collective-permute-done.4.refs_4_ = bf16[128,128]{1,0:T(8,128)(2,1)S(1)} collective-permute-done((bf16[128,128]{1,0:T(8,128)(2,1)S(1)}, bf16[128,128]{1,0:T(8,128)(2,1)S(1)}, u32[]{:S(2)}, u32[]{:S(2)}) %collective-permute-start.4) | collective-permute-done | bytes 32800 | tf_op jit(solution)/shard_map/ppermute | solution.py:113
  25.6 0.0 collective-permute-done.5.refs_5_
  25.6 2.2 %collective-permute-done.6.refs_6_ = bf16[128,128]{1,0:T(8,128)(2,1)S(1)} collective-permute-done((bf16[128,128]{1,0:T(8,128)(2,1)S(1)}, bf16[128,128]{1,0:T(8,128)(2,1)S(1)}, u32[]{:S(2)}, u32[]{:S(2)}) %collective-permute-start.6) | collective-permute-done | bytes 32800 | tf_op jit(solution)/shard_map/ppermute | solution.py:113
  27.8 0.0 collective-permute-done.7.refs_7_
  27.8 0.8 %shard_map.67 = (bf16[2,256,128]{2,1,0:T(8,128)(2,1)S(1)}, bf16[2,256,128]{2,1,0:T(8,128)(2,1)S(1)}, bf16[256,128]{1,0:T(8,128)(2,1)S(1)}, bf16[256,128]{1,0:T(8,128)(2,1)S(1)}) custom-call(f32[8,128]{1,0:T(8,128)S(1)} %get-tuple-element.36.side_ref, bf16[256,1024]{1,0:T(8,128)(2,1)S(1)} %get-tuple-element.37.rows_ref, ...), custom_call_target="tpu_custom_call" | custom-call | flops 268435456 | bytes 3145728 | tf_op jit(solution)/shard_map/pallas_call | solution.py:314
  28.6 0.0 copy-start.1
  28.6 0.0 copy-start.3
  28.6 1.6 %collective-permute-start.8 = (bf16[2,256,128]{2,1,0:T(8,128)(2,1)S(1)}, bf16[2,256,128]{2,1,0:T(8,128)(2,1)S(1)}, u32[]{:S(2)}, u32[]{:S(2)}) collective-permute-start(bf16[2,256,128]{2,1,0:T(8,128)(2,1)S(1)} %get-tuple-element.45), channel_id=1, source_target_pairs={{0,16},{16,0},{1,17},{17,1},{2,18},{18,2},{3,19},{19,3},{4,20},{20... | collective-permute-start | bytes 393224 | tf_op jit(solution)/shard_map/ppermute | solution.py:477
  30.2 0.0 all-to-all-done
  30.2 0.6 %shard_map.68 = bf16[2,256,384]{2,1,0:T(8,128)(2,1)S(1)} custom-call(bf16[256,1024]{1,0:T(8,128)(2,1)S(1)} %get-tuple-element.37.rows_ref, bf16[1024,384]{1,0:T(8,128)(2,1)S(1)} %bitcast.2), custom_call_target="tpu_custom_call" | custom-call | flops 402653184 | bytes 3145728 | tf_op jit(solution)/shard_map/pallas_call | solution.py:347
  30.8 0.6 %collective-permute-start.9 = (bf16[2,256,384]{2,1,0:T(8,128)(2,1)S(1)}, bf16[2,256,384]{2,1,0:T(8,128)(2,1)S(1)}, u32[]{:S(2)}, u32[]{:S(2)}) collective-permute-start(bf16[2,256,384]{2,1,0:T(8,128)(2,1)S(1)} %shard_map.68), channel_id=1, source_target_pairs={{0,16},{16,0},{1,17},{17,1},{2,18},{18,2},{3,19},{19,3},{4,20},{20... | collective-permute-start | bytes 1179656 | tf_op jit(solution)/shard_map/ppermute | solution.py:477
  31.4 0.0 collective-permute-start.10
  31.4 2.3 %collective-permute-start.11 = (bf16[256,128]{1,0:T(8,128)(2,1)S(1)}, bf16[256,128]{1,0:T(8,128)(2,1)S(1)}, u32[]{:S(2)}, u32[]{:S(2)}) collective-permute-start(bf16[256,128]{1,0:T(8,128)(2,1)S(1)} %get-tuple-element.51), channel_id=1, source_target_pairs={{1,2},{3,4},{5,6},{7,8},{9,10},{11,12},{13,14},{2,1},{4,3},{6,5},{... | collective-permute-start | bytes 196616 | tf_op jit(solution)/shard_map/ppermute | solution.py:363
  33.7 0.0 copy-done.5
  33.7 0.1 copy.9.offset_ref
  33.8 0.0 copy-start.2
  33.8 1.2 %collective-permute-done.8.far_outer = bf16[2,256,128]{2,1,0:T(8,128)(2,1)S(1)} collective-permute-done((bf16[2,256,128]{2,1,0:T(8,128)(2,1)S(1)}, bf16[2,256,128]{2,1,0:T(8,128)(2,1)S(1)}, u32[]{:S(2)}, u32[]{:S(2)}) %collective-permute-start.8) | collective-permute-done | bytes 131104 | tf_op jit(solution)/shard_map/ppermute | solution.py:477
  35.0 0.9 %shard_map.70.own_ref = bf16[2,256,512]{2,1,0:T(8,128)(2,1)S(1)} custom-call(bf16[256,1024]{1,0:T(8,128)(2,1)S(1)} %get-tuple-element.37.rows_ref, bf16[1024,384]{1,0:T(8,128)(2,1)S(1)} %bitcast.3, bf16[2,256,128]{2,1,0:T(8,128)(2,1)S(1)} %get-tuple-element.54.outer_ref), custom_call_target="tpu_custom_call" | custom-call | flops 402653184 | bytes 3145728 | tf_op jit(solution)/shard_map/pallas_call | solution.py:347
  35.9 0.0 collective-permute-done.10.first_ref
  35.9 2.0 %collective-permute-done.11.second_ref = bf16[256,128]{1,0:T(8,128)(2,1)S(1)} collective-permute-done((bf16[256,128]{1,0:T(8,128)(2,1)S(1)}, bf16[256,128]{1,0:T(8,128)(2,1)S(1)}, u32[]{:S(2)}, u32[]{:S(2)}) %collective-permute-start.11) | collective-permute-done | bytes 65568 | tf_op jit(solution)/shard_map/ppermute | solution.py:363
  37.9 0.2 shard_map.69
  38.1 1.6 %collective-permute-start.12 = (bf16[256,128]{1,0:T(8,128)(2,1)S(1)}, bf16[256,128]{1,0:T(8,128)(2,1)S(1)}, u32[]{:S(2)}, u32[]{:S(2)}) collective-permute-start(bf16[256,128]{1,0:T(8,128)(2,1)S(1)} %get-tuple-element.56.after_ref), channel_id=1, source_target_pairs={{0,16},{16,0},{1,17},{17,1},{2,18},{18,2},{3,19},{19,3},{4,20},{20... | collective-permute-start | bytes 196616 | tf_op jit(solution)/shard_map/ppermute | solution.py:477
  39.7 0.0 copy-done.1
  39.7 0.0 copy-done.3
  39.7 0.0 copy-done.2
  39.7 2.2 %shard_map.71 = (bf16[2,512,512]{2,1,0:T(8,128)(2,1)S(1)}, bf16[2,2,128,512]{3,2,1,0:T(8,128)(2,1)S(1)}, f32[2,2,512,512]{3,2,1,0:T(8,128)S(1)}, bf16[2,512,256]{2,1,0:T(8,128)(2,1)S(1)}, f32[8,128]{1,0:T(8,128)}) custom-call(s32[1,2,1]{2,1,0:T(2,128)S(1)} %copy.7.flag_ref, s32[1,2,1]{2,1,0:T(2,128)S(1)} %copy.9.offset_ref, f32[1,2]{1,0:T(1,128)S(1)} %copy-done.3, ...), custom_call_target="tpu_custom_call" | custom-call | flops 2300000000 | bytes 7340032 | tf_op jit(solution)/shard_map/pallas_call | solution.py:240
  42.0 1.1 %shard_map.72.merged_ref = f32[2,512,512]{2,1,0:T(8,128)S(1)} custom-call(bf16[2,256,512]{2,1,0:T(8,128)(2,1)S(1)} %shard_map.70.own_ref, bf16[256,128]{1,0:T(8,128)(2,1)S(1)} %get-tuple-element.55.rims_ref, bf16[2,512,512]{2,1,0:T(8,128)(2,1)S(1)} %get-tuple-element.57.centre_ref, bf16[2,2,128,512]{3,2,1,0:T(8,128)(2,1)S(1)} %get-tuple-element.58.rim_ref, ...), custom_call_target="tpu_custom_call" | custom-call | flops 536870912 | bytes 8388608 | tf_op jit(solution)/shard_map/pallas_call | solution.py:447
  43.0 1.3 %collective-permute-done.12.rims_ref = bf16[256,128]{1,0:T(8,128)(2,1)S(1)} collective-permute-done((bf16[256,128]{1,0:T(8,128)(2,1)S(1)}, bf16[256,128]{1,0:T(8,128)(2,1)S(1)}, u32[]{:S(2)}, u32[]{:S(2)}) %collective-permute-start.12) | collective-permute-done | bytes 65568 | tf_op jit(solution)/shard_map/ppermute | solution.py:477
  44.4 0.0 collective-permute-done.9.far_inner
  44.4 2.2 %shard_map.73 = f32[2,512,512]{2,1,0:T(8,128)} custom-call(bf16[2,256,128]{2,1,0:T(8,128)(2,1)S(1)} %collective-permute-done.8.far_outer, bf16[2,256,384]{2,1,0:T(8,128)(2,1)S(1)} %collective-permute-done.9.far_inner, bf16[256,128]{1,0:T(8,128)(2,1)S(1)} %collective-permute-done.12.rims_ref, f32[2,512,512]{2,1,0:T(8,128)S(1)} %shard_map.72.merged_ref, ...), custom_call_target="tpu_custom_call" | custom-call | flops 536870912 | bytes 8388608 | tf_op jit(solution)/shard_map/pallas_call | solution.py:456
  (1 shorter events, 0.0 us)
Async XLA Ops:
  0.0 1.2 %copy-start = (bf16[2,32,8192]{2,1,0:T(8,128)(2,1)S(1)}, bf16[2,32,8192]{2,1,0:T(8,128)(2,1)}, u32[]{:S(2)}) copy-start(bf16[2,32,8192]{2,1,0:T(8,128)(2,1)} %param.6) | copy-start | bytes 3145732
  2.3 6.7 %collective-permute-start = (bf16[8,64,128]{2,1,0:T(8,128)(2,1)S(1)}, bf16[8,64,128]{2,1,0:T(8,128)(2,1)S(1)}, u32[]{:S(2)}, u32[]{:S(2)}) collective-permute-start(bf16[8,64,128]{2,1,0:T(8,128)(2,1)S(1)} %get-tuple-element.34), channel_id=1, source_target_pairs={{0,8},{1,9},{2,10},{3,11},{4,12},{5,13},{6,14},{7,15},{8,0},{9,1},... | collective-permute-start | bytes 393224 | tf_op jit(solution)/shard_map/ppermute | solution.py:113
  2.3 28.0 %all-to-all-start = ((bf16[16,64,384]{2,1,0:T(8,128)(2,1)}), bf16[16,64,384]{2,1,0:T(8,128)(2,1)S(1)}, u32[]{:S(2)}, u32[]{:S(2)}) async-start(bf16[16,64,384]{2,1,0:T(8,128)(2,1)} %get-tuple-element.46), calls=%async_computation | async-start | bytes 1572864 | tf_op jit(solution)/shard_map/all_to_all | solution.py:515
  9.0 8.6 %copy-start.4 = (s32[1,2,1]{1,2,0:T(1,128)S(1)}, s32[1,2,1]{1,2,0:T(1,128)}, u32[]{:S(2)}) copy-start(s32[1,2,1]{1,2,0:T(1,128)} %param.7) | copy-start | bytes 28
  9.0 24.7 %copy-start.5 = (s32[1,2,1]{1,2,0:T(1,128)S(1)}, s32[1,2,1]{1,2,0:T(1,128)}, u32[]{:S(2)}) copy-start(s32[1,2,1]{1,2,0:T(1,128)} %param.8) | copy-start | bytes 28
  9.0 5.7 %collective-permute-start.1 = (bf16[128,128]{1,0:T(8,128)(2,1)S(1)}, bf16[128,128]{1,0:T(8,128)(2,1)S(1)}, u32[]{:S(2)}, u32[]{:S(2)}) collective-permute-start(bf16[128,128]{1,0:T(8,128)(2,1)S(1)} %get-tuple-element.38), channel_id=1, source_target_pairs={{0,1},{1,0},{2,3},{3,2},{4,5},{5,4},{6,7},{7,6},{8,9},{9,8},{10,11... | collective-permute-start | bytes 98312 | tf_op jit(solution)/shard_map/ppermute | solution.py:113
  9.3 8.1 %collective-permute-start.2 = (bf16[128,128]{1,0:T(8,128)(2,1)S(1)}, bf16[128,128]{1,0:T(8,128)(2,1)S(1)}, u32[]{:S(2)}, u32[]{:S(2)}) collective-permute-start(bf16[128,128]{1,0:T(8,128)(2,1)S(1)} %get-tuple-element.39), channel_id=1, source_target_pairs={{0,2},{1,3},{2,0},{3,1},{4,6},{5,7},{6,4},{7,5},{8,10},{9,11},{10,... | collective-permute-start | bytes 98312 | tf_op jit(solution)/shard_map/ppermute | solution.py:113
  10.7 8.1 %collective-permute-start.3 = (bf16[128,128]{1,0:T(8,128)(2,1)S(1)}, bf16[128,128]{1,0:T(8,128)(2,1)S(1)}, u32[]{:S(2)}, u32[]{:S(2)}) collective-permute-start(bf16[128,128]{1,0:T(8,128)(2,1)S(1)} %get-tuple-element.40), channel_id=1, source_target_pairs={{0,3},{1,2},{2,1},{3,0},{4,7},{5,6},{6,5},{7,4},{8,11},{9,10},{10,... | collective-permute-start | bytes 98312 | tf_op jit(solution)/shard_map/ppermute | solution.py:113
  11.0 14.6 %collective-permute-start.4 = (bf16[128,128]{1,0:T(8,128)(2,1)S(1)}, bf16[128,128]{1,0:T(8,128)(2,1)S(1)}, u32[]{:S(2)}, u32[]{:S(2)}) collective-permute-start(bf16[128,128]{1,0:T(8,128)(2,1)S(1)} %get-tuple-element.41), channel_id=1, source_target_pairs={{0,4},{1,5},{2,6},{3,7},{4,0},{5,1},{6,2},{7,3},{8,12},{9,13},{10,... | collective-permute-start | bytes 98312 | tf_op jit(solution)/shard_map/ppermute | solution.py:113
  14.7 10.8 %collective-permute-start.5 = (bf16[128,128]{1,0:T(8,128)(2,1)S(1)}, bf16[128,128]{1,0:T(8,128)(2,1)S(1)}, u32[]{:S(2)}, u32[]{:S(2)}) collective-permute-start(bf16[128,128]{1,0:T(8,128)(2,1)S(1)} %get-tuple-element.42), channel_id=1, source_target_pairs={{0,5},{1,4},{2,7},{3,6},{4,1},{5,0},{6,3},{7,2},{8,13},{9,12},{10,... | collective-permute-start | bytes 98312 | tf_op jit(solution)/shard_map/ppermute | solution.py:113
  14.8 13.0 %collective-permute-start.6 = (bf16[128,128]{1,0:T(8,128)(2,1)S(1)}, bf16[128,128]{1,0:T(8,128)(2,1)S(1)}, u32[]{:S(2)}, u32[]{:S(2)}) collective-permute-start(bf16[128,128]{1,0:T(8,128)(2,1)S(1)} %get-tuple-element.43), channel_id=1, source_target_pairs={{0,6},{1,7},{2,4},{3,5},{4,2},{5,3},{6,0},{7,1},{8,14},{9,15},{10,... | collective-permute-start | bytes 98312 | tf_op jit(solution)/shard_map/ppermute | solution.py:113
  17.4 10.4 %collective-permute-start.7 = (bf16[128,128]{1,0:T(8,128)(2,1)S(1)}, bf16[128,128]{1,0:T(8,128)(2,1)S(1)}, u32[]{:S(2)}, u32[]{:S(2)}) collective-permute-start(bf16[128,128]{1,0:T(8,128)(2,1)S(1)} %get-tuple-element.44), channel_id=1, source_target_pairs={{0,7},{1,6},{2,5},{3,4},{4,3},{5,2},{6,1},{7,0},{8,15},{9,14},{10,... | collective-permute-start | bytes 98312 | tf_op jit(solution)/shard_map/ppermute | solution.py:113
  28.6 11.1 %copy-start.1 = (bf16[1,544,512]{2,1,0:T(8,128)(2,1)S(1)}, bf16[1,544,512]{2,1,0:T(8,128)(2,1)}, u32[]{:S(2)}) copy-start(bf16[1,544,512]{2,1,0:T(8,128)(2,1)} %range_ref.1) | copy-start | bytes 1671172
  28.6 11.1 %copy-start.3 = (f32[1,2]{1,0:T(1,128)S(1)}, f32[1,2]{1,0:T(1,128)}, u32[]{:S(2)}) copy-start(f32[1,2]{1,0:T(1,128)} %shift_ref.1) | copy-start | bytes 28
  28.6 6.4 %collective-permute-start.8 = (bf16[2,256,128]{2,1,0:T(8,128)(2,1)S(1)}, bf16[2,256,128]{2,1,0:T(8,128)(2,1)S(1)}, u32[]{:S(2)}, u32[]{:S(2)}) collective-permute-start(bf16[2,256,128]{2,1,0:T(8,128)(2,1)S(1)} %get-tuple-element.45), channel_id=1, source_target_pairs={{0,16},{16,0},{1,17},{17,1},{2,18},{18,2},{3,19},{19,3},{4,20},{20... | collective-permute-start | bytes 393224 | tf_op jit(solution)/shard_map/ppermute | solution.py:477
  30.8 13.6 %collective-permute-start.9 = (bf16[2,256,384]{2,1,0:T(8,128)(2,1)S(1)}, bf16[2,256,384]{2,1,0:T(8,128)(2,1)S(1)}, u32[]{:S(2)}, u32[]{:S(2)}) collective-permute-start(bf16[2,256,384]{2,1,0:T(8,128)(2,1)S(1)} %shard_map.68), channel_id=1, source_target_pairs={{0,16},{16,0},{1,17},{17,1},{2,18},{18,2},{3,19},{19,3},{4,20},{20... | collective-permute-start | bytes 1179656 | tf_op jit(solution)/shard_map/ppermute | solution.py:477
  31.4 4.6 %collective-permute-start.10 = (bf16[256,128]{1,0:T(8,128)(2,1)S(1)}, bf16[256,128]{1,0:T(8,128)(2,1)S(1)}, u32[]{:S(2)}, u32[]{:S(2)}) collective-permute-start(bf16[256,128]{1,0:T(8,128)(2,1)S(1)} %get-tuple-element.49), channel_id=1, source_target_pairs={{0,1},{2,3},{4,5},{6,7},{8,9},{10,11},{12,13},{14,15},{1,0},{3,2},... | collective-permute-start | bytes 196616 | tf_op jit(solution)/shard_map/ppermute | solution.py:363
  31.4 6.6 %collective-permute-start.11 = (bf16[256,128]{1,0:T(8,128)(2,1)S(1)}, bf16[256,128]{1,0:T(8,128)(2,1)S(1)}, u32[]{:S(2)}, u32[]{:S(2)}) collective-permute-start(bf16[256,128]{1,0:T(8,128)(2,1)S(1)} %get-tuple-element.51), channel_id=1, source_target_pairs={{1,2},{3,4},{5,6},{7,8},{9,10},{11,12},{13,14},{2,1},{4,3},{6,5},{... | collective-permute-start | bytes 196616 | tf_op jit(solution)/shard_map/ppermute | solution.py:363
  33.8 5.9 %copy-start.2 = (bf16[1,2,512,256]{3,2,1,0:T(8,128)(2,1)S(1)}, bf16[1,2,512,256]{3,2,1,0:T(8,128)(2,1)}, u32[]{:S(2)}) copy-start(bf16[1,2,512,256]{3,2,1,0:T(8,128)(2,1)} %interp_ref.1) | copy-start | bytes 1572868
  38.1 6.3 %collective-permute-start.12 = (bf16[256,128]{1,0:T(8,128)(2,1)S(1)}, bf16[256,128]{1,0:T(8,128)(2,1)S(1)}, u32[]{:S(2)}, u32[]{:S(2)}) collective-permute-start(bf16[256,128]{1,0:T(8,128)(2,1)S(1)} %get-tuple-element.56.after_ref), channel_id=1, source_target_pairs={{0,16},{16,0},{1,17},{17,1},{2,18},{18,2},{3,19},{19,3},{4,20},{20... | collective-permute-start | bytes 196616 | tf_op jit(solution)/shard_map/ppermute | solution.py:477

commit v15 on v12

--- a/solution.py
+++ b/solution.py
@@ -397,10 +397,9 @@
 
 def resampled(image, rims_ref, centre_ref, rim_ref, value_ref, child):
     parts, half, bins = image.shape
-    value_ref[...] = dot(image.reshape(parts * half, bins), centre_ref[child])
     rims = rims_ref[...]
     return [
-        (value_ref[part * half : (part + 1) * half, :] + dot(rims, rim_ref[child, part])).astype(BF16)
+        (dot(image[part], centre_ref[child]) + dot(rims, rim_ref[child, part])).astype(BF16)
         for part in range(parts)
     ]
 

time: 46.8 us -> 46.8 us (level)
  no operation moved by 1% of the time
where the time goes in v15:
time: 46.8 us; the launch traced here: 46.6 us
  starting transfers between devices  21.3 us (46%)
  waiting for transfers between devices  13.6 us (29%)
  Pallas kernels  10.1 us (22%)
  local copies, waits for them, and re-layouts  1.44 us (3%)
    ppermute x8, waiting for transfers between devices, across(): return lax.ppermute(value, 'rng', [(i, i ^ mask) for i in range(devices)])  8.98 us
    ppermute x8, starting transfers between devices, across(): return lax.ppermute(value, 'rng', [(i, i ^ mask) for i in range(devices)])  8.48 us
    all_to_all x1, starting transfers between devices, on_device(): lax.all_to_all(blocks, 'rng', split_axis=0, concat_axis=0, tiled=True)  6.72 us
    ppermute x3, starting transfers between devices, from_partner(): return lax.ppermute(value, 'sub', pairs)  3.74 us
    ppermute x3, waiting for transfers between devices, from_partner(): return lax.ppermute(value, 'sub', pairs)  2.59 us
    ppermute x2, starting transfers between devices, exchanged(): return lax.ppermute(value, 'rng', pairs + [(j, i) for i, j in pairs] + ends)  2.34 us
    pallas_call x1, Pallas kernels, merge_tables(): pl.pallas_call(functools.partial(merge_table_kernel, level, stride), out_...  2.23 us
    pallas_call x1, Pallas kernels, merged_image(): pl.pallas_call(late_kernel, out_shape=jax.ShapeDtypeStruct((2, angles, bi...  2.17 us
  transfers between devices with their start and end apart: 14, of which 5 were waited for; matrix products, arithmetic and copies ran while one was open for 0% of the time, Pallas kernels for 15%

profile of v15, /device:TPU:16, one launch (start us, length us, event | category | flops | bytes accessed | tf_op | source)
XLA Modules:
  0.0 46.6 jit_solution(8681233473383131081)
XLA Ops:
  0.0 0.0 copy-start
  0.0 1.2 %copy-done = bf16[2,32,8192]{2,1,0:T(8,128)(2,1)S(1)} copy-done((bf16[2,32,8192]{2,1,0:T(8,128)(2,1)S(1)}, bf16[2,32,8192]{2,1,0:T(8,128)(2,1)}, u32[]{:S(2)}) %copy-start) | copy-done | bytes 1048600
  1.2 1.0 %shard_map.64 = (bf16[8,64,128]{2,1,0:T(8,128)(2,1)S(1)}, bf16[8,64,128]{2,1,0:T(8,128)(2,1)S(1)}, bf16[16,64,384]{2,1,0:T(8,128)(2,1)}) custom-call(bf16[64,8192]{1,0:T(8,128)(2,1)S(1)} %bitcast.4), custom_call_target="tpu_custom_call" | custom-call | bytes 2097152 | tf_op jit(solution)/shard_map/pallas_call | solution.py:81
  2.3 0.0 collective-permute-start
  2.3 6.7 %all-to-all-start = ((bf16[16,64,384]{2,1,0:T(8,128)(2,1)}), bf16[16,64,384]{2,1,0:T(8,128)(2,1)S(1)}, u32[]{:S(2)}, u32[]{:S(2)}) async-start(bf16[16,64,384]{2,1,0:T(8,128)(2,1)} %get-tuple-element.46), calls=%async_computation | async-start | bytes 1572864 | tf_op jit(solution)/shard_map/all_to_all | solution.py:518
  9.0 0.0 collective-permute-done.relay_ref
  9.0 0.0 copy-start.4
  9.0 0.0 copy-start.5
  9.0 0.2 collective-permute-start.1
  9.3 1.5 %collective-permute-start.2 = (bf16[128,128]{1,0:T(8,128)(2,1)S(1)}, bf16[128,128]{1,0:T(8,128)(2,1)S(1)}, u32[]{:S(2)}, u32[]{:S(2)}) collective-permute-start(bf16[128,128]{1,0:T(8,128)(2,1)S(1)} %get-tuple-element.39), channel_id=1, source_target_pairs={{0,2},{1,3},{2,0},{3,1},{4,6},{5,7},{6,4},{7,5},{8,10},{9,11},{10,... | collective-permute-start | bytes 98312 | tf_op jit(solution)/shard_map/ppermute | solution.py:113
  10.7 0.2 collective-permute-start.3
  11.0 3.8 %collective-permute-start.4 = (bf16[128,128]{1,0:T(8,128)(2,1)S(1)}, bf16[128,128]{1,0:T(8,128)(2,1)S(1)}, u32[]{:S(2)}, u32[]{:S(2)}) collective-permute-start(bf16[128,128]{1,0:T(8,128)(2,1)S(1)} %get-tuple-element.41), channel_id=1, source_target_pairs={{0,4},{1,5},{2,6},{3,7},{4,0},{5,1},{6,2},{7,3},{8,12},{9,13},{10,... | collective-permute-start | bytes 98312 | tf_op jit(solution)/shard_map/ppermute | solution.py:113
  14.7 0.0 collective-permute-start.5
  14.7 0.0 collective-permute-done.1.refs_1_
  14.8 2.6 %collective-permute-start.6 = (bf16[128,128]{1,0:T(8,128)(2,1)S(1)}, bf16[128,128]{1,0:T(8,128)(2,1)S(1)}, u32[]{:S(2)}, u32[]{:S(2)}) collective-permute-start(bf16[128,128]{1,0:T(8,128)(2,1)S(1)} %get-tuple-element.43), channel_id=1, source_target_pairs={{0,6},{1,7},{2,4},{3,5},{4,2},{5,3},{6,0},{7,1},{8,14},{9,15},{10,... | collective-permute-start | bytes 98312 | tf_op jit(solution)/shard_map/ppermute | solution.py:113
  17.4 0.0 collective-permute-done.2.refs_2_
  17.4 0.2 collective-permute-start.7
  17.5 0.0 copy-done.4
  17.5 0.1 copy.7.flag_ref
  17.6 1.2 %shard_map.66 = (bf16[256,1024]{1,0:T(8,128)(2,1)S(1)}, f32[8,128]{1,0:T(8,128)S(1)}) custom-call(s32[1,2,1]{2,1,0:T(2,128)S(1)} %copy.7.flag_ref, bf16[128,128]{1,0:T(8,128)(2,1)S(1)} %get-tuple-element.35.after_ref.refs_0_), custom_call_target="tpu_custom_call" | custom-call | flops 9000000 | bytes 4194304 | tf_op jit(solution)/shard_map/pallas_call | solution.py:152
  18.8 0.0 collective-permute-done.3.refs_3_
  18.8 6.8 %collective-permute-done.4.refs_4_ = bf16[128,128]{1,0:T(8,128)(2,1)S(1)} collective-permute-done((bf16[128,128]{1,0:T(8,128)(2,1)S(1)}, bf16[128,128]{1,0:T(8,128)(2,1)S(1)}, u32[]{:S(2)}, u32[]{:S(2)}) %collective-permute-start.4) | collective-permute-done | bytes 32800 | tf_op jit(solution)/shard_map/ppermute | solution.py:113
  25.6 0.0 collective-permute-done.5.refs_5_
  25.6 2.2 %collective-permute-done.6.refs_6_ = bf16[128,128]{1,0:T(8,128)(2,1)S(1)} collective-permute-done((bf16[128,128]{1,0:T(8,128)(2,1)S(1)}, bf16[128,128]{1,0:T(8,128)(2,1)S(1)}, u32[]{:S(2)}, u32[]{:S(2)}) %collective-permute-start.6) | collective-permute-done | bytes 32800 | tf_op jit(solution)/shard_map/ppermute | solution.py:113
  27.8 0.0 collective-permute-done.7.refs_7_
  27.8 0.8 %shard_map.67 = (bf16[2,256,128]{2,1,0:T(8,128)(2,1)S(1)}, bf16[2,256,128]{2,1,0:T(8,128)(2,1)S(1)}, bf16[256,128]{1,0:T(8,128)(2,1)S(1)}, bf16[256,128]{1,0:T(8,128)(2,1)S(1)}) custom-call(f32[8,128]{1,0:T(8,128)S(1)} %get-tuple-element.36.side_ref, bf16[256,1024]{1,0:T(8,128)(2,1)S(1)} %get-tuple-element.37.rows_ref, ...), custom_call_target="tpu_custom_call" | custom-call | flops 268435456 | bytes 3145728 | tf_op jit(solution)/shard_map/pallas_call | solution.py:314
  28.6 0.0 copy-start.1
  28.6 0.0 copy-start.3
  28.6 1.6 %collective-permute-start.8 = (bf16[2,256,128]{2,1,0:T(8,128)(2,1)S(1)}, bf16[2,256,128]{2,1,0:T(8,128)(2,1)S(1)}, u32[]{:S(2)}, u32[]{:S(2)}) collective-permute-start(bf16[2,256,128]{2,1,0:T(8,128)(2,1)S(1)} %get-tuple-element.45), channel_id=1, source_target_pairs={{0,16},{16,0},{1,17},{17,1},{2,18},{18,2},{3,19},{19,3},{4,20},{20... | collective-permute-start | bytes 393224 | tf_op jit(solution)/shard_map/ppermute | solution.py:480
  30.2 0.0 all-to-all-done
  30.2 0.6 %shard_map.68 = bf16[2,256,384]{2,1,0:T(8,128)(2,1)S(1)} custom-call(bf16[256,1024]{1,0:T(8,128)(2,1)S(1)} %get-tuple-element.37.rows_ref, bf16[1024,384]{1,0:T(8,128)(2,1)S(1)} %bitcast.2), custom_call_target="tpu_custom_call" | custom-call | flops 402653184 | bytes 3145728 | tf_op jit(solution)/shard_map/pallas_call | solution.py:347
  30.8 0.6 %collective-permute-start.9 = (bf16[2,256,384]{2,1,0:T(8,128)(2,1)S(1)}, bf16[2,256,384]{2,1,0:T(8,128)(2,1)S(1)}, u32[]{:S(2)}, u32[]{:S(2)}) collective-permute-start(bf16[2,256,384]{2,1,0:T(8,128)(2,1)S(1)} %shard_map.68), channel_id=1, source_target_pairs={{0,16},{16,0},{1,17},{17,1},{2,18},{18,2},{3,19},{19,3},{4,20},{20... | collective-permute-start | bytes 1179656 | tf_op jit(solution)/shard_map/ppermute | solution.py:480
  31.4 0.0 collective-permute-start.10
  31.4 2.3 %collective-permute-start.11 = (bf16[256,128]{1,0:T(8,128)(2,1)S(1)}, bf16[256,128]{1,0:T(8,128)(2,1)S(1)}, u32[]{:S(2)}, u32[]{:S(2)}) collective-permute-start(bf16[256,128]{1,0:T(8,128)(2,1)S(1)} %get-tuple-element.51), channel_id=1, source_target_pairs={{1,2},{3,4},{5,6},{7,8},{9,10},{11,12},{13,14},{2,1},{4,3},{6,5},{... | collective-permute-start | bytes 196616 | tf_op jit(solution)/shard_map/ppermute | solution.py:363
  33.7 0.0 copy-done.5
  33.7 0.1 copy.9.offset_ref
  33.8 0.0 copy-start.2
  33.8 1.2 %collective-permute-done.8.far_outer = bf16[2,256,128]{2,1,0:T(8,128)(2,1)S(1)} collective-permute-done((bf16[2,256,128]{2,1,0:T(8,128)(2,1)S(1)}, bf16[2,256,128]{2,1,0:T(8,128)(2,1)S(1)}, u32[]{:S(2)}, u32[]{:S(2)}) %collective-permute-start.8) | collective-permute-done | bytes 131104 | tf_op jit(solution)/shard_map/ppermute | solution.py:480
  35.0 0.9 %shard_map.70.own_ref = bf16[2,256,512]{2,1,0:T(8,128)(2,1)S(1)} custom-call(bf16[256,1024]{1,0:T(8,128)(2,1)S(1)} %get-tuple-element.37.rows_ref, bf16[1024,384]{1,0:T(8,128)(2,1)S(1)} %bitcast.3, bf16[2,256,128]{2,1,0:T(8,128)(2,1)S(1)} %get-tuple-element.54.outer_ref), custom_call_target="tpu_custom_call" | custom-call | flops 402653184 | bytes 3145728 | tf_op jit(solution)/shard_map/pallas_call | solution.py:347
  35.9 0.0 collective-permute-done.10.first_ref
  35.9 2.0 %collective-permute-done.11.second_ref = bf16[256,128]{1,0:T(8,128)(2,1)S(1)} collective-permute-done((bf16[256,128]{1,0:T(8,128)(2,1)S(1)}, bf16[256,128]{1,0:T(8,128)(2,1)S(1)}, u32[]{:S(2)}, u32[]{:S(2)}) %collective-permute-start.11) | collective-permute-done | bytes 65568 | tf_op jit(solution)/shard_map/ppermute | solution.py:363
  37.9 0.2 shard_map.69
  38.1 1.6 %collective-permute-start.12 = (bf16[256,128]{1,0:T(8,128)(2,1)S(1)}, bf16[256,128]{1,0:T(8,128)(2,1)S(1)}, u32[]{:S(2)}, u32[]{:S(2)}) collective-permute-start(bf16[256,128]{1,0:T(8,128)(2,1)S(1)} %get-tuple-element.56.after_ref), channel_id=1, source_target_pairs={{0,16},{16,0},{1,17},{17,1},{2,18},{18,2},{3,19},{19,3},{4,20},{20... | collective-permute-start | bytes 196616 | tf_op jit(solution)/shard_map/ppermute | solution.py:480
  39.7 0.0 copy-done.1
  39.7 0.0 copy-done.3
  39.7 0.0 copy-done.2
  39.7 2.2 %shard_map.71 = (bf16[2,512,512]{2,1,0:T(8,128)(2,1)S(1)}, bf16[2,2,128,512]{3,2,1,0:T(8,128)(2,1)S(1)}, f32[2,2,512,512]{3,2,1,0:T(8,128)S(1)}, bf16[2,512,256]{2,1,0:T(8,128)(2,1)S(1)}, f32[8,128]{1,0:T(8,128)}) custom-call(s32[1,2,1]{2,1,0:T(2,128)S(1)} %copy.7.flag_ref, s32[1,2,1]{2,1,0:T(2,128)S(1)} %copy.9.offset_ref, f32[1,2]{1,0:T(1,128)S(1)} %copy-done.3, ...), custom_call_target="tpu_custom_call" | custom-call | flops 2300000000 | bytes 7340032 | tf_op jit(solution)/shard_map/pallas_call | solution.py:240
  42.0 1.0 %shard_map.72.merged_ref = f32[2,512,512]{2,1,0:T(8,128)S(1)} custom-call(bf16[2,256,512]{2,1,0:T(8,128)(2,1)S(1)} %shard_map.70.own_ref, bf16[256,128]{1,0:T(8,128)(2,1)S(1)} %get-tuple-element.55.rims_ref, bf16[2,512,512]{2,1,0:T(8,128)(2,1)S(1)} %get-tuple-element.57.centre_ref, bf16[2,2,128,512]{3,2,1,0:T(8,128)(2,1)S(1)} %get-tuple-element.58.rim_ref, ...), custom_call_target="tpu_custom_call" | custom-call | flops 536870912 | bytes 8388608 | tf_op jit(solution)/shard_map/pallas_call | solution.py:450
  43.0 1.4 %collective-permute-done.12.rims_ref = bf16[256,128]{1,0:T(8,128)(2,1)S(1)} collective-permute-done((bf16[256,128]{1,0:T(8,128)(2,1)S(1)}, bf16[256,128]{1,0:T(8,128)(2,1)S(1)}, u32[]{:S(2)}, u32[]{:S(2)}) %collective-permute-start.12) | collective-permute-done | bytes 65568 | tf_op jit(solution)/shard_map/ppermute | solution.py:480
  44.4 0.0 collective-permute-done.9.far_inner
  44.4 2.2 %shard_map.73 = f32[2,512,512]{2,1,0:T(8,128)} custom-call(bf16[2,256,128]{2,1,0:T(8,128)(2,1)S(1)} %collective-permute-done.8.far_outer, bf16[2,256,384]{2,1,0:T(8,128)(2,1)S(1)} %collective-permute-done.9.far_inner, bf16[256,128]{1,0:T(8,128)(2,1)S(1)} %collective-permute-done.12.rims_ref, f32[2,512,512]{2,1,0:T(8,128)S(1)} %shard_map.72.merged_ref, ...), custom_call_target="tpu_custom_call" | custom-call | flops 536870912 | bytes 8388608 | tf_op jit(solution)/shard_map/pallas_call | solution.py:459
  (1 shorter events, 0.0 us)
Async XLA Ops:
  0.0 1.2 %copy-start = (bf16[2,32,8192]{2,1,0:T(8,128)(2,1)S(1)}, bf16[2,32,8192]{2,1,0:T(8,128)(2,1)}, u32[]{:S(2)}) copy-start(bf16[2,32,8192]{2,1,0:T(8,128)(2,1)} %param.6) | copy-start | bytes 3145732
  2.3 6.7 %collective-permute-start = (bf16[8,64,128]{2,1,0:T(8,128)(2,1)S(1)}, bf16[8,64,128]{2,1,0:T(8,128)(2,1)S(1)}, u32[]{:S(2)}, u32[]{:S(2)}) collective-permute-start(bf16[8,64,128]{2,1,0:T(8,128)(2,1)S(1)} %get-tuple-element.34), channel_id=1, source_target_pairs={{0,8},{1,9},{2,10},{3,11},{4,12},{5,13},{6,14},{7,15},{8,0},{9,1},... | collective-permute-start | bytes 393224 | tf_op jit(solution)/shard_map/ppermute | solution.py:113
  2.3 28.0 %all-to-all-start = ((bf16[16,64,384]{2,1,0:T(8,128)(2,1)}), bf16[16,64,384]{2,1,0:T(8,128)(2,1)S(1)}, u32[]{:S(2)}, u32[]{:S(2)}) async-start(bf16[16,64,384]{2,1,0:T(8,128)(2,1)} %get-tuple-element.46), calls=%async_computation | async-start | bytes 1572864 | tf_op jit(solution)/shard_map/all_to_all | solution.py:518
  9.0 8.6 %copy-start.4 = (s32[1,2,1]{1,2,0:T(1,128)S(1)}, s32[1,2,1]{1,2,0:T(1,128)}, u32[]{:S(2)}) copy-start(s32[1,2,1]{1,2,0:T(1,128)} %param.7) | copy-start | bytes 28
  9.0 24.7 %copy-start.5 = (s32[1,2,1]{1,2,0:T(1,128)S(1)}, s32[1,2,1]{1,2,0:T(1,128)}, u32[]{:S(2)}) copy-start(s32[1,2,1]{1,2,0:T(1,128)} %param.8) | copy-start | bytes 28
  9.0 5.7 %collective-permute-start.1 = (bf16[128,128]{1,0:T(8,128)(2,1)S(1)}, bf16[128,128]{1,0:T(8,128)(2,1)S(1)}, u32[]{:S(2)}, u32[]{:S(2)}) collective-permute-start(bf16[128,128]{1,0:T(8,128)(2,1)S(1)} %get-tuple-element.38), channel_id=1, source_target_pairs={{0,1},{1,0},{2,3},{3,2},{4,5},{5,4},{6,7},{7,6},{8,9},{9,8},{10,11... | collective-permute-start | bytes 98312 | tf_op jit(solution)/shard_map/ppermute | solution.py:113
  9.3 8.1 %collective-permute-start.2 = (bf16[128,128]{1,0:T(8,128)(2,1)S(1)}, bf16[128,128]{1,0:T(8,128)(2,1)S(1)}, u32[]{:S(2)}, u32[]{:S(2)}) collective-permute-start(bf16[128,128]{1,0:T(8,128)(2,1)S(1)} %get-tuple-element.39), channel_id=1, source_target_pairs={{0,2},{1,3},{2,0},{3,1},{4,6},{5,7},{6,4},{7,5},{8,10},{9,11},{10,... | collective-permute-start | bytes 98312 | tf_op jit(solution)/shard_map/ppermute | solution.py:113
  10.7 8.1 %collective-permute-start.3 = (bf16[128,128]{1,0:T(8,128)(2,1)S(1)}, bf16[128,128]{1,0:T(8,128)(2,1)S(1)}, u32[]{:S(2)}, u32[]{:S(2)}) collective-permute-start(bf16[128,128]{1,0:T(8,128)(2,1)S(1)} %get-tuple-element.40), channel_id=1, source_target_pairs={{0,3},{1,2},{2,1},{3,0},{4,7},{5,6},{6,5},{7,4},{8,11},{9,10},{10,... | collective-permute-start | bytes 98312 | tf_op jit(solution)/shard_map/ppermute | solution.py:113
  11.0 14.6 %collective-permute-start.4 = (bf16[128,128]{1,0:T(8,128)(2,1)S(1)}, bf16[128,128]{1,0:T(8,128)(2,1)S(1)}, u32[]{:S(2)}, u32[]{:S(2)}) collective-permute-start(bf16[128,128]{1,0:T(8,128)(2,1)S(1)} %get-tuple-element.41), channel_id=1, source_target_pairs={{0,4},{1,5},{2,6},{3,7},{4,0},{5,1},{6,2},{7,3},{8,12},{9,13},{10,... | collective-permute-start | bytes 98312 | tf_op jit(solution)/shard_map/ppermute | solution.py:113
  14.7 10.8 %collective-permute-start.5 = (bf16[128,128]{1,0:T(8,128)(2,1)S(1)}, bf16[128,128]{1,0:T(8,128)(2,1)S(1)}, u32[]{:S(2)}, u32[]{:S(2)}) collective-permute-start(bf16[128,128]{1,0:T(8,128)(2,1)S(1)} %get-tuple-element.42), channel_id=1, source_target_pairs={{0,5},{1,4},{2,7},{3,6},{4,1},{5,0},{6,3},{7,2},{8,13},{9,12},{10,... | collective-permute-start | bytes 98312 | tf_op jit(solution)/shard_map/ppermute | solution.py:113
  14.8 13.0 %collective-permute-start.6 = (bf16[128,128]{1,0:T(8,128)(2,1)S(1)}, bf16[128,128]{1,0:T(8,128)(2,1)S(1)}, u32[]{:S(2)}, u32[]{:S(2)}) collective-permute-start(bf16[128,128]{1,0:T(8,128)(2,1)S(1)} %get-tuple-element.43), channel_id=1, source_target_pairs={{0,6},{1,7},{2,4},{3,5},{4,2},{5,3},{6,0},{7,1},{8,14},{9,15},{10,... | collective-permute-start | bytes 98312 | tf_op jit(solution)/shard_map/ppermute | solution.py:113
  17.4 10.4 %collective-permute-start.7 = (bf16[128,128]{1,0:T(8,128)(2,1)S(1)}, bf16[128,128]{1,0:T(8,128)(2,1)S(1)}, u32[]{:S(2)}, u32[]{:S(2)}) collective-permute-start(bf16[128,128]{1,0:T(8,128)(2,1)S(1)} %get-tuple-element.44), channel_id=1, source_target_pairs={{0,7},{1,6},{2,5},{3,4},{4,3},{5,2},{6,1},{7,0},{8,15},{9,14},{10,... | collective-permute-start | bytes 98312 | tf_op jit(solution)/shard_map/ppermute | solution.py:113
  28.6 11.1 %copy-start.1 = (bf16[1,544,512]{2,1,0:T(8,128)(2,1)S(1)}, bf16[1,544,512]{2,1,0:T(8,128)(2,1)}, u32[]{:S(2)}) copy-start(bf16[1,544,512]{2,1,0:T(8,128)(2,1)} %range_ref.1) | copy-start | bytes 1671172
  28.6 11.1 %copy-start.3 = (f32[1,2]{1,0:T(1,128)S(1)}, f32[1,2]{1,0:T(1,128)}, u32[]{:S(2)}) copy-start(f32[1,2]{1,0:T(1,128)} %shift_ref.1) | copy-start | bytes 28
  28.6 6.4 %collective-permute-start.8 = (bf16[2,256,128]{2,1,0:T(8,128)(2,1)S(1)}, bf16[2,256,128]{2,1,0:T(8,128)(2,1)S(1)}, u32[]{:S(2)}, u32[]{:S(2)}) collective-permute-start(bf16[2,256,128]{2,1,0:T(8,128)(2,1)S(1)} %get-tuple-element.45), channel_id=1, source_target_pairs={{0,16},{16,0},{1,17},{17,1},{2,18},{18,2},{3,19},{19,3},{4,20},{20... | collective-permute-start | bytes 393224 | tf_op jit(solution)/shard_map/ppermute | solution.py:480
  30.8 13.6 %collective-permute-start.9 = (bf16[2,256,384]{2,1,0:T(8,128)(2,1)S(1)}, bf16[2,256,384]{2,1,0:T(8,128)(2,1)S(1)}, u32[]{:S(2)}, u32[]{:S(2)}) collective-permute-start(bf16[2,256,384]{2,1,0:T(8,128)(2,1)S(1)} %shard_map.68), channel_id=1, source_target_pairs={{0,16},{16,0},{1,17},{17,1},{2,18},{18,2},{3,19},{19,3},{4,20},{20... | collective-permute-start | bytes 1179656 | tf_op jit(solution)/shard_map/ppermute | solution.py:480
  31.4 4.6 %collective-permute-start.10 = (bf16[256,128]{1,0:T(8,128)(2,1)S(1)}, bf16[256,128]{1,0:T(8,128)(2,1)S(1)}, u32[]{:S(2)}, u32[]{:S(2)}) collective-permute-start(bf16[256,128]{1,0:T(8,128)(2,1)S(1)} %get-tuple-element.49), channel_id=1, source_target_pairs={{0,1},{2,3},{4,5},{6,7},{8,9},{10,11},{12,13},{14,15},{1,0},{3,2},... | collective-permute-start | bytes 196616 | tf_op jit(solution)/shard_map/ppermute | solution.py:363
  31.4 6.6 %collective-permute-start.11 = (bf16[256,128]{1,0:T(8,128)(2,1)S(1)}, bf16[256,128]{1,0:T(8,128)(2,1)S(1)}, u32[]{:S(2)}, u32[]{:S(2)}) collective-permute-start(bf16[256,128]{1,0:T(8,128)(2,1)S(1)} %get-tuple-element.51), channel_id=1, source_target_pairs={{1,2},{3,4},{5,6},{7,8},{9,10},{11,12},{13,14},{2,1},{4,3},{6,5},{... | collective-permute-start | bytes 196616 | tf_op jit(solution)/shard_map/ppermute | solution.py:363
  33.8 5.9 %copy-start.2 = (bf16[1,2,512,256]{3,2,1,0:T(8,128)(2,1)S(1)}, bf16[1,2,512,256]{3,2,1,0:T(8,128)(2,1)}, u32[]{:S(2)}) copy-start(bf16[1,2,512,256]{3,2,1,0:T(8,128)(2,1)} %interp_ref.1) | copy-start | bytes 1572868
  38.1 6.3 %collective-permute-start.12 = (bf16[256,128]{1,0:T(8,128)(2,1)S(1)}, bf16[256,128]{1,0:T(8,128)(2,1)S(1)}, u32[]{:S(2)}, u32[]{:S(2)}) collective-permute-start(bf16[256,128]{1,0:T(8,128)(2,1)S(1)} %get-tuple-element.56.after_ref), channel_id=1, source_target_pairs={{0,16},{16,0},{1,17},{17,1},{2,18},{18,2},{3,19},{19,3},{4,20},{20... | collective-permute-start | bytes 196616 | tf_op jit(solution)/shard_map/ppermute | solution.py:480
